TPU v7x, 32 devices: a whole 2x2x4 slice. The times are simulated.
32 devices in a mesh: fsdp: 8 (over y, x, core), tp: 4 (over z).
Axes of the slice: x: 2, y: 2, z: 4, core: 2. Of those that a mesh axis runs over, the one named last changes fastest.
Arguments:
- activations: bfloat16 [16384, 5120], P(('fsdp', 'tp')), may hold values from -6 to 6
- grad_out: bfloat16 [16384, 1024], P(('fsdp', 'tp')), may hold values from -6 to 6
- master_w: float32 [5120, 1024], P(('fsdp', 'tp')), may hold values from -0.078125 to 0.078125
- embed_table: bfloat16 [151936, 5120], P(('fsdp', 'tp')), may hold values from -6 to 6
- token_ids: int32 [64], replicated, may hold values from 0 to 151935
- queries: bfloat16 [64, 8192], P('fsdp', 'tp'), may hold values from -30 to 30
- cache_keys: bfloat16 [64, 512, 1024], P('fsdp', None, 'tp'), may hold values from -6 to 6
- cache_values: bfloat16 [64, 512, 1024], P('fsdp', None, 'tp'), may hold values from -6 to 6
- new_key: bfloat16 [64, 1024], P('fsdp', 'tp'), may hold values from -6 to 6
- first_value: bfloat16 [64, 1024], P('fsdp', 'tp'), may hold values from -6 to 6
- residual_mix: float32 [8], P('tp'), may hold values from 0.2 to 0.8
- lengths: int32 [64], P('fsdp'), may hold values from 1 to 512, 16384 in all
Outputs:
- w_next: float32 [5120, 1024], P(('fsdp', 'tp'))
- new_value: bfloat16 [64, 1024], P('fsdp', 'tp')
- attended: bfloat16 [64, 8192], P('fsdp', 'tp')
Inputs may be any that keep to these rules, and one draw needn't show every extreme that they name: `lengths`: some row holds exactly 512 positions.
All inputs are finite; a program needn't handle non-finite values. No bound on the sum of `lengths` on one device may be relied on, other than what follows from the above.
Results may differ from a plain program's by a relative error of at most 0.006.
Values may be sent and summed in bfloat16 or wider, within the bound.
No kernel may reach another device: no remote copies, remote signals or barrier semaphores. Data moves between devices by JAX's collectives and lax.ppermute only.
A program may use at most 128 MiB of HBM per device.

v0:
```python
import math

import jax
import jax.numpy as jnp
from jax import lax
from jax.sharding import PartitionSpec as P

HEADS = 64
KV = 8
HD = 128


def per_device(
    activations,
    grad_out,
    master_w,
    embed_table,
    token_ids,
    queries,
    cache_keys,
    cache_values,
    new_key,
    first_value,
    residual_mix,
    lengths,
):
    count_fsdp = lax.axis_size("fsdp")
    count_tp = lax.axis_size("tp")
    devices_all = count_fsdp * count_tp
    width = activations.shape[1]
    tokens_total = activations.shape[0] * devices_all
    grad_w = lax.psum_scatter(
        lax.dot_general(
            activations, grad_out, (((0,), (0,)), ((), ())), preferred_element_type=jnp.float32
        ),
        ("fsdp", "tp"),
        scatter_dimension=0,
        tiled=True,
    )
    coef = 1.0 / math.sqrt(tokens_total * width)
    w_next = master_w - coef * grad_w
    w_roll = w_next.astype(jnp.bfloat16)
    vocab_local = embed_table.shape[0]
    vocab_start = (lax.axis_index("fsdp") * count_tp + lax.axis_index("tp")) * vocab_local
    picked = token_ids - vocab_start
    onehot = (picked[:, None] == jnp.arange(vocab_local, dtype=jnp.int32)[None, :]).astype(
        jnp.bfloat16
    )
    own_rows = lax.psum_scatter(
        jnp.dot(onehot, embed_table, preferred_element_type=jnp.float32),
        ("fsdp", "tp"),
        scatter_dimension=0,
        tiled=True,
    ).astype(jnp.bfloat16)
    embedded = lax.all_gather(own_rows, "tp", axis=0, tiled=True)
    col_width = master_w.shape[1] // count_tp
    whole = lax.all_gather(w_roll, ("fsdp", "tp"), axis=0, tiled=True)
    local_w = lax.dynamic_slice_in_dim(whole, lax.axis_index("tp") * col_width, col_width, 1)
    own_value = jnp.dot(embedded, local_w, preferred_element_type=jnp.float32)
    share = jnp.repeat(residual_mix, HD)[None, :]
    new_value = (share * own_value + (1.0 - share) * first_value.astype(jnp.float32)).astype(
        jnp.bfloat16
    )
    rows = queries.shape[0]
    heads_kv = residual_mix.shape[0]
    group = HEADS // KV
    context = cache_keys.shape[1]
    scale = 1.0 / math.sqrt(HD)
    query_b = queries.reshape(rows, heads_kv, group, HD)
    keys_b = cache_keys.reshape(rows, context, heads_kv, HD)
    vals_b = cache_values.reshape(rows, context, heads_kv, HD)
    newk_b = new_key.reshape(rows, heads_kv, HD)
    newv_b = new_value.reshape(rows, heads_kv, HD)
    scores = (
        jnp.einsum("rkgd,rckd->rkgc", query_b, keys_b, preferred_element_type=jnp.float32) * scale
    )
    fresh = jnp.einsum("rkgd,rkd->rkg", query_b, newk_b, preferred_element_type=jnp.float32) * scale
    valid = jnp.arange(context, dtype=jnp.int32)[None, :] < lengths[:, None]
    scores = jnp.where(valid[:, None, None, :], scores, -1e30)
    peak = jnp.maximum(jnp.max(scores, axis=-1), fresh)
    expo = jnp.exp(scores - peak[..., None])
    expo_new = jnp.exp(fresh - peak)
    total = jnp.sum(expo, axis=-1) + expo_new
    probs = (expo / total[..., None]).astype(jnp.bfloat16)
    probs_new = (expo_new / total).astype(jnp.bfloat16)
    mixed = jnp.einsum("rkgc,rckd->rkgd", probs, vals_b, preferred_element_type=jnp.float32)
    mixed = (
        mixed + probs_new.astype(jnp.float32)[..., None] * newv_b.astype(jnp.float32)[:, :, None, :]
    )
    attended = mixed.reshape(rows, group * heads_kv * HD).astype(jnp.bfloat16)
    return (w_next, new_value, attended)


def solution(mesh):
    return jax.shard_map(
        per_device,
        mesh=mesh,
        in_specs=(
            P(("fsdp", "tp"), None),
            P(("fsdp", "tp"), None),
            P(("fsdp", "tp"), None),
            P(("fsdp", "tp"), None),
            P(),
            P("fsdp", "tp"),
            P("fsdp", None, "tp"),
            P("fsdp", None, "tp"),
            P("fsdp", "tp"),
            P("fsdp", "tp"),
            P("tp"),
            P("fsdp"),
        ),
        out_specs=(P(("fsdp", "tp"), None), P("fsdp", "tp"), P("fsdp", "tp")),
        check_vma=False,
    )
```

profile of v0, /device:TPU:0, one launch (start us, length us, event | category | flops | bytes accessed | tf_op | source)
XLA Modules:
  0.0 587.5 jit_solution(1477471216345414142)
XLA Ops:
  7.2 0.0 copy-start
  7.2 0.0 reduce-scatter.2.cloned.1.call-start
  7.2 12.1 %fusion.47 = f32[5120,1024]{1,0:T(8,128)} fusion(bf16[512,5120]{1,0:T(8,128)(2,1)} %param.12, bf16[512,1024]{1,0:T(8,128)(2,1)} %param.13), kind=kOutput, calls=%fused_computation.45 | convolution fusion | flops 5368709120 | bytes 27262976 | tf_op jit(solution)/shard_map/dot_general | solution.py:33
  19.3 0.0 copy-start.1
  19.3 0.0 reduce-scatter.2.cloned.1.call-update
  19.3 0.0 copy-start.7
  19.3 0.0 all-gather.3.cloned.1.call-start
  19.4 453.3 %reduce-scatter.2.cloned.1.call-done = f32[160,1024]{1,0:T(8,128)} async-done(((f32[5120,1024]{1,0:T(8,128)}), f32[160,1024]{1,0:T(8,128)}) %reduce-scatter.2.cloned.1.call-update) | async-done | bytes 655376 | tf_op jit(solution)/shard_map/reduce_scatter | solution.py:32
  472.7 0.0 copy-done.1
  472.7 2.1 fusion.45
  474.8 0.0 all-gather.3.cloned.1.call-update
  474.9 0.0 copy-done.7
  474.9 19.7 %fusion.8 = f32[64,5120]{1,0:T(8,128)S(1)} fusion(bf16[4748,5120]{1,0:T(8,128)(2,1)} %param.15, s32[64]{0:T(128)S(1)} %broadcast_subtract_fusion), kind=kOutput, calls=%fused_computation.9 | convolution fusion | flops 3111953152 | bytes 49930496 | tf_op jit(solution)/shard_map/dot_general | solution.py:50
  494.6 0.0 copy-start.4
  494.6 0.0 copy-start.2
  494.6 0.0 copy-start.6
  494.6 0.0 copy-start.8
  494.6 0.0 copy-start.3
  494.6 66.0 %all-reduce.2 = bf16[64,5120]{1,0:T(8,128)(2,1)} all-reduce(f32[64,5120]{1,0:T(8,128)S(1)} %fusion.8), channel_id=3, replica_groups=mesh['fsdp'=8,'tp'=4] {'fsdp','tp'}, use_global_device_ids=true, to_apply=%region_1.0.clone | all-reduce | flops 327680 | bytes 1966080
  560.6 0.9 fusion.40
  561.6 13.6 %all-gather = bf16[4,2,5120]{2,1,0:T(2,128)(2,1)S(1)} all-gather(bf16[1,2,5120]{2,1,0:T(2,128)(2,1)S(1)} %fusion.40), channel_id=1, replica_groups=mesh['fsdp'=8,'tp'=4] {'tp'}, dimensions={0}, use_global_device_ids=true | all-gather | bytes 102400 | tf_op jit(solution)/shard_map/all_gather | solution.py:55
  575.2 0.0 copy-done.4
  575.2 0.1 iota_compare_fusion.2
  575.3 0.0 copy-done.2
  575.3 0.0 copy-done.6
  575.3 0.1 fusion.37
  575.5 0.0 copy-done
  575.5 0.7 fusion.46
  576.2 0.2 fusion.34
  576.4 0.0 copy-done.8
  576.4 0.1 bitcast_subtract_fusion
  576.5 0.1 broadcast_bitcast_fusion
  576.6 0.0 all-gather.3.cloned.1.call-done
  576.6 0.0 copy-done.3
  576.6 0.0 copy-start.5
  576.7 2.9 bitcast_convert_fusion
  579.6 0.0 copy-done.5
  579.6 0.4 fusion.21
  580.1 0.6 copy.57
  (5 shorter events, 0.1 us)
Async XLA Ops:
  7.2 568.3 %copy-start = (bf16[8,512,256]{2,1,0:T(8,128)(2,1)S(1)}, bf16[8,512,256]{2,1,0:T(8,128)(2,1)}, u32[]{:S(2)}) copy-start(bf16[8,512,256]{2,1,0:T(8,128)(2,1)} %param.18) | copy-start | bytes 6291460
  7.2 465.5 %reduce-scatter.2.cloned.1.call-start = ((), (), s32[]{:S(2)}) async-start(), calls=%async_computation.1 | async-start | bytes 21626880 | tf_op jit(solution)/shard_map/reduce_scatter | solution.py:32
  19.3 453.4 %copy-start.1 = (f32[160,1024]{1,0:T(8,128)S(1)}, f32[160,1024]{1,0:T(8,128)}, u32[]{:S(2)}) copy-start(f32[160,1024]{1,0:T(8,128)} %param.14) | copy-start | bytes 1966084
  19.3 455.6 %copy-start.7 = (s32[64]{0:T(128)S(1)}, s32[64]{0:T(128)}, u32[]{:S(2)}) copy-start(s32[64]{0:T(128)} %param.16) | copy-start | bytes 772
  19.3 557.3 %all-gather.3.cloned.1.call-start = ((), (), s32[]{:S(2)}) async-start(), calls=%async_computation.2 | async-start | bytes 10813440 | tf_op jit(solution)/shard_map/all_gather | solution.py:57
  494.6 80.7 %copy-start.4 = (s32[8]{0:T(128)S(1)}, s32[8]{0:T(128)}, u32[]{:S(2)}) copy-start(s32[8]{0:T(128)} %param.23) | copy-start | bytes 100
  494.6 80.8 %copy-start.2 = (bf16[8,2048]{1,0:T(8,128)(2,1)S(1)}, bf16[8,2048]{1,0:T(8,128)(2,1)}, u32[]{:S(2)}) copy-start(bf16[8,2048]{1,0:T(8,128)(2,1)} %param.17) | copy-start | bytes 98308
  494.6 80.7 %copy-start.6 = (bf16[8,256]{1,0:T(8,128)(2,1)S(1)}, bf16[8,256]{1,0:T(8,128)(2,1)}, u32[]{:S(2)}) copy-start(bf16[8,256]{1,0:T(8,128)(2,1)} %param.20) | copy-start | bytes 12292
  494.6 81.8 %copy-start.8 = (f32[2]{0:T(128)S(1)}, f32[2]{0:T(128)}, u32[]{:S(2)}) copy-start(f32[2]{0:T(128)} %param.22) | copy-start | bytes 28
  494.6 82.0 %copy-start.3 = (bf16[8,256]{1,0:T(8,128)(2,1)S(1)}, bf16[8,256]{1,0:T(8,128)(2,1)}, u32[]{:S(2)}) copy-start(bf16[8,256]{1,0:T(8,128)(2,1)} %param.21) | copy-start | bytes 12292
  576.6 3.0 copy-start.5
Sparse Core Ops, SparseCore 0:
  19.4 453.2 reduce-scatter.1
  475.5 99.4 all-gather.2
where the time goes:
time: 588 us
  waiting for transfers between devices  453 us (77%)
  blocking collectives  79.7 us (14%)
  matrix products  36 us (6%)
  between operations  14.2 us (2%)
    reduce_scatter x1, waiting for transfers between devices, per_device(): lax.psum_scatter(lax.dot_general(activations, grad_out, (((0,), (0,)), ((...  453 us
    unnamed x1, blocking collectives  66 us
    dot_general x1, matrix products, per_device(): jnp.dot(onehot, embed_table, preferred_element_type=jnp.float32)  19.7 us
    all_gather x1, blocking collectives, per_device(): embedded = lax.all_gather(own_rows, 'tp', axis=0, tiled=True)  13.6 us
    dot_general x1, matrix products, per_device(): lax.dot_general(activations, grad_out, (((0,), (0,)), ((), ())), preferre...  12.1 us
  transfers between devices with their start and end apart: 2, of which 1 were waited for; matrix products, arithmetic and copies ran while one was open for 4% of the time, Pallas kernels for 0%

commit v1 on v0

--- a/solution.py
+++ b/solution.py
@@ -3,11 +3,93 @@
 import jax
 import jax.numpy as jnp
 from jax import lax
+from jax.experimental import pallas as pl
+from jax.experimental.pallas import tpu as pltpu
 from jax.sharding import PartitionSpec as P
 
 HEADS = 64
 KV = 8
 HD = 128
+LANES = 128
+SLAB = 16
+
+
+def exchange(value, axis, mask):
+    return lax.ppermute(value, axis, [(i, i ^ mask) for i in range(lax.axis_size(axis))])
+
+
+def transpose_block(order, block, out):
+    out[...] = block[...].T
+
+
+def pack(activations, order, width):
+    tokens = activations.shape[0]
+    count = len(order)
+    if width % LANES:
+        flipped = activations.T
+        return jnp.concatenate(
+            [lax.dynamic_slice_in_dim(flipped, place * width, width, 0) for place in order]
+        )
+    return pl.pallas_call(
+        transpose_block,
+        grid_spec=pltpu.PrefetchScalarGridSpec(
+            num_scalar_prefetch=1,
+            grid=(count,),
+            in_specs=[pl.BlockSpec((tokens, width), lambda j, order: (0, order[j]))],
+            out_specs=pl.BlockSpec((width, tokens), lambda j, order: (j, 0)),
+        ),
+        out_shape=jax.ShapeDtypeStruct((count * width, tokens), activations.dtype),
+        compiler_params=pltpu.CompilerParams(vmem_limit_bytes=32 << 20),
+        cost_estimate=pl.CostEstimate(
+            flops=0, bytes_accessed=4 * count * width * tokens, transcendentals=0
+        ),
+    )(jnp.stack(order).astype(jnp.int32), activations)
+
+
+def pick_rows(place, *refs):
+    slabs, out, held = refs[:SLAB], refs[SLAB], refs[SLAB + 1]
+    held[...] = jnp.zeros_like(held)
+    for k in range(SLAB):
+        inside = place[pl.program_id(0) * SLAB + k]
+
+        @pl.when(inside >= 0)
+        def _():
+            rows = slabs[k][...].astype(jnp.float32)
+            at = lax.broadcasted_iota(jnp.int32, rows.shape, 0)
+            chosen = jnp.where(at == lax.rem(inside, SLAB), rows, 0.0)
+            held[k : k + 1, :] = jnp.sum(chosen, axis=0, keepdims=True)
+
+    out[...] = held[...].astype(out.dtype)
+
+
+def lookup(embed_table, token_ids, start):
+    here, width = embed_table.shape
+    count = token_ids.shape[0]
+    inside = token_ids - start
+    place = jnp.where((inside >= 0) & (inside < here), inside, -1)
+
+    def slab_of(k):
+        return lambda i, place: (jnp.maximum(place[i * SLAB + k], 0) // SLAB, 0)
+
+    return pl.pallas_call(
+        pick_rows,
+        grid_spec=pltpu.PrefetchScalarGridSpec(
+            num_scalar_prefetch=1,
+            grid=(count // SLAB,),
+            in_specs=[pl.BlockSpec((SLAB, width), slab_of(k)) for k in range(SLAB)],
+            out_specs=pl.BlockSpec((SLAB, width), lambda i, place: (i, 0)),
+            scratch_shapes=[pltpu.VMEM((SLAB, width), jnp.float32)],
+        ),
+        out_shape=jax.ShapeDtypeStruct((count, width), embed_table.dtype),
+        compiler_params=pltpu.CompilerParams(vmem_limit_bytes=32 << 20),
+        cost_estimate=pl.CostEstimate(
+            flops=0, bytes_accessed=2 * count * SLAB * width, transcendentals=0
+        ),
+    )(place.astype(jnp.int32), *([embed_table] * SLAB))
+
+
+def dot32(left, right):
+    return jnp.dot(left, right, preferred_element_type=jnp.float32)
 
 
 def per_device(
@@ -29,34 +111,128 @@
     devices_all = count_fsdp * count_tp
     width = activations.shape[1]
     tokens_total = activations.shape[0] * devices_all
-    grad_w = lax.psum_scatter(
-        lax.dot_general(
-            activations, grad_out, (((0,), (0,)), ((), ())), preferred_element_type=jnp.float32
-        ),
-        ("fsdp", "tp"),
-        scatter_dimension=0,
-        tiled=True,
-    )
     coef = 1.0 / math.sqrt(tokens_total * width)
-    w_next = master_w - coef * grad_w
-    w_roll = w_next.astype(jnp.bfloat16)
-    vocab_local = embed_table.shape[0]
-    vocab_start = (lax.axis_index("fsdp") * count_tp + lax.axis_index("tp")) * vocab_local
-    picked = token_ids - vocab_start
-    onehot = (picked[:, None] == jnp.arange(vocab_local, dtype=jnp.int32)[None, :]).astype(
-        jnp.bfloat16
-    )
-    own_rows = lax.psum_scatter(
-        jnp.dot(onehot, embed_table, preferred_element_type=jnp.float32),
-        ("fsdp", "tp"),
-        scatter_dimension=0,
-        tiled=True,
-    ).astype(jnp.bfloat16)
-    embedded = lax.all_gather(own_rows, "tp", axis=0, tiled=True)
-    col_width = master_w.shape[1] // count_tp
-    whole = lax.all_gather(w_roll, ("fsdp", "tp"), axis=0, tiled=True)
-    local_w = lax.dynamic_slice_in_dim(whole, lax.axis_index("tp") * col_width, col_width, 1)
-    own_value = jnp.dot(embedded, local_w, preferred_element_type=jnp.float32)
+    f = lax.axis_index("fsdp")
+    t = lax.axis_index("tp")
+    core = f & 1
+    upper = f >> 1
+    upper_bits = count_fsdp.bit_length() - 2
+    uppers = 1 << upper_bits
+
+    block = width // count_fsdp
+    arranged = [r ^ (r >> 1) for r in range(uppers)][::-1]
+    grads = [grad_out, exchange(grad_out, "fsdp", 1)]
+    outgoing = pack(activations, [((r ^ upper) << 1) | (1 - core) for r in arranged], block)
+    incoming = exchange(outgoing, "fsdp", 1)
+    staying = pack(activations, [((r ^ upper) << 1) | core for r in arranged], block)
+    lefts = [staying, incoming]
+
+    def partial(wanted, first, last):
+        places = [arranged.index(r) for r in wanted]
+        runs = []
+        for place in places:
+            if runs and runs[-1][1] == place:
+                runs[-1][1] = place + 1
+            else:
+                runs.append([place, place + 1])
+        return [
+            sum(
+                dot32(left[low * block : high * block], grad[:, first:last])
+                for left, grad in zip(lefts, grads)
+            )
+            for low, high in runs
+        ]
+
+    columns = master_w.shape[1]
+    rows = master_w.shape[0]
+    quarter = columns // 4
+    eighth = columns // 8
+    sizes = [quarter, quarter, eighth, eighth, eighth, eighth]
+    chunks = []
+    first = 0
+    for index, size in enumerate(sizes):
+        order = list(range(upper_bits))
+        chunks.append((first, first + size, order if index % 2 == 0 else order[::-1]))
+        first += size
+
+    def reduce_chunk(first, last, order):
+        arrived = {r: [] for r in range(uppers)}
+        remaining = list(arranged)
+        for bit in order:
+            sent = [r for r in remaining if (r >> bit) & 1]
+            remaining = [r for r in remaining if not (r >> bit) & 1]
+            value = jnp.concatenate(partial(sent, first, last))
+            for step in range(len(arrived[sent[0]])):
+                value = value + jnp.concatenate([arrived[r][step] for r in sent]).astype(
+                    jnp.float32
+                )
+            got = exchange(value.astype(jnp.bfloat16), "fsdp", 2 << bit)
+            for at, r in enumerate(sent):
+                arrived[r ^ (1 << bit)].append(got[at * block : (at + 1) * block])
+        total = jnp.concatenate(partial([0], first, last))
+        for piece in arrived[0]:
+            total = total + piece.astype(jnp.float32)
+        grad = lax.dynamic_slice_in_dim(total, t * rows, rows, 0)
+        for step in range(1, count_tp):
+            away = lax.dynamic_slice_in_dim(total, (t ^ step) * rows, rows, 0)
+            grad = grad + exchange(away.astype(jnp.bfloat16), "tp", step).astype(jnp.float32)
+        return master_w[:, first:last] - coef * grad
+
+    w_next = jnp.concatenate([reduce_chunk(*chunk) for chunk in chunks], axis=1)
+
+    tokens_new = token_ids.shape[0]
+    half = tokens_new // 2
+    piece = half // count_tp
+    flat = f * count_tp + t
+    found = lookup(embed_table, token_ids, flat * embed_table.shape[0])
+    held = lax.dynamic_slice_in_dim(found, core * half, half, 0) + exchange(
+        lax.dynamic_slice_in_dim(found, (1 - core) * half, half, 0), "fsdp", 1
+    )
+    mine = lax.dynamic_slice_in_dim(held, t * piece, piece, 0)
+    for step in range(1, count_tp):
+        mine = mine + exchange(
+            lax.dynamic_slice_in_dim(held, (t ^ step) * piece, piece, 0), "tp", step
+        )
+    for bit in range(1, upper_bits + 1):
+        mine = mine + exchange(mine, "fsdp", 1 << bit)
+    near = jnp.concatenate([mine] + [exchange(mine, "tp", step) for step in range(1, count_tp)])
+    embedded = jnp.concatenate([near, exchange(near, "fsdp", 1)])
+
+    through = lax.dot_general(
+        embedded, activations, (((1,), (1,)), ((), ())), preferred_element_type=jnp.float32
+    )
+    high = through.astype(jnp.bfloat16)
+    low = (through - high.astype(jnp.float32)).astype(jnp.bfloat16)
+    own_columns = lax.dynamic_slice_in_dim(embedded, flat * rows, rows, 1).astype(jnp.float32)
+    share_own = jnp.dot(
+        own_columns,
+        master_w,
+        preferred_element_type=jnp.float32,
+        precision=lax.Precision.HIGHEST,
+    ) - coef * (dot32(high, grad_out) + dot32(low, grad_out))
+    rows_f = tokens_new // count_fsdp
+
+    def rows_of(j):
+        start = (f ^ j) * rows_f
+        at = start // piece
+        placed = ((at // count_tp) ^ core) * count_tp + ((at % count_tp) ^ t)
+        return lax.dynamic_slice_in_dim(share_own, placed * piece + start % piece, rows_f, 0)
+
+    parts = {j: rows_of(j) for j in range(count_fsdp)}
+    for bit in range(upper_bits + 1):
+        sent = [j for j in parts if (j >> bit) & 1]
+        got = exchange(jnp.concatenate([parts[j] for j in sent]), "fsdp", 1 << bit)
+        parts = {
+            j ^ (1 << bit): parts[j ^ (1 << bit)] + got[at * rows_f : (at + 1) * rows_f]
+            for at, j in enumerate(sent)
+        }
+    col_width = columns // count_tp
+    own_value = lax.dynamic_slice_in_dim(parts[0], t * col_width, col_width, 1)
+    for step in range(1, count_tp):
+        own_value = own_value + exchange(
+            lax.dynamic_slice_in_dim(parts[0], (t ^ step) * col_width, col_width, 1), "tp", step
+        )
+
     share = jnp.repeat(residual_mix, HD)[None, :]
     new_value = (share * own_value + (1.0 - share) * first_value.astype(jnp.float32)).astype(
         jnp.bfloat16

time: 588 us -> 214 us (0.36)
  waiting for transfers between devices: 453 us -> 39.9 us
  blocking collectives: 79.7 us -> 0 us
  starting transfers between devices: 0.08 us -> 64.9 us
  matrix products: 36 us -> 79.1 us
  between operations: 14.2 us -> 1.81 us
  Pallas kernels: 0 us -> 12.2 us
  local copies, waits for them, and re-layouts: 1.72 us -> 8.5 us
    reduce_scatter x1 -> x0, waiting for transfers between devices: 453 us -> none  [per_device(): lax.psum_scatter(lax.dot_general(activations, grad_out, (((0,), (0,)), ((...]
    unnamed x1 -> x0, blocking collectives: 66 us -> none
    ppermute x0 -> x48, starting transfers between devices: none -> 64.9 us  [exchange(): lax.ppermute(value, axis, [(i, i ^ mask) for i in range(lax.axis_size(axi...]
    dot_general x3 -> x40, matrix products: 34.7 us -> 75.4 us  [the longest x38 70.8 us: dot32(): return jnp.dot(left, right, preferred_element_type=jnp.float32)]
    ppermute x0 -> x48, waiting for transfers between devices: none -> 39.9 us  [exchange(): lax.ppermute(value, axis, [(i, i ^ mask) for i in range(lax.axis_size(axi...]
    all_gather x1 -> x0, blocking collectives: 13.6 us -> none  [per_device(): embedded = lax.all_gather(own_rows, 'tp', axis=0, tiled=True)]
    pallas_call x0 -> x3, Pallas kernels: none -> 12.2 us  [the longest x1 7.05 us: lookup(): pl.pallas_call(pick_rows, grid_spec=pltpu.PrefetchScalarGridSpec(num_scal...]
  transfers between devices with their start and end apart: 2 -> 48, of which waited for: 1 -> 22; matrix products, arithmetic and copies ran while one was open for 4% -> 40% of each run, Pallas kernels for 0% -> 4%
where the time goes in v1:
time: 214 us; the launch traced here: 213 us
  matrix products  79.1 us (37%)
  starting transfers between devices  64.9 us (30%)
  waiting for transfers between devices  39.9 us (19%)
  Pallas kernels  12.2 us (6%)
  local copies, waits for them, and re-layouts  8.5 us (4%)
  other arithmetic  6.47 us (3%)
    dot_general x38, matrix products, dot32(): return jnp.dot(left, right, preferred_element_type=jnp.float32)  70.8 us
    ppermute x48, starting transfers between devices, exchange(): lax.ppermute(value, axis, [(i, i ^ mask) for i in range(lax.axis_size(axi...  64.9 us
    ppermute x48, waiting for transfers between devices, exchange(): lax.ppermute(value, axis, [(i, i ^ mask) for i in range(lax.axis_size(axi...  39.9 us
    pallas_call x1, Pallas kernels, lookup(): pl.pallas_call(pick_rows, grid_spec=pltpu.PrefetchScalarGridSpec(num_scal...  7.05 us
    unnamed x72, local copies, waits for them, and re-layouts  6.73 us
    pallas_call x2, Pallas kernels, pack(): pl.pallas_call(transpose_block, grid_spec=pltpu.PrefetchScalarGridSpec(nu...  5.15 us
  transfers between devices with their start and end apart: 48, of which 22 were waited for; matrix products, arithmetic and copies ran while one was open for 40% of the time, Pallas kernels for 4%

profile of v1, /device:TPU:0, one launch (start us, length us, event | category | flops | bytes accessed | tf_op | source)
XLA Modules:
  0.0 212.9 jit_solution(6606316233810293804)
XLA Ops:
  0.7 2.6 %copy-done.1 = bf16[512,5120]{1,0:T(8,128)(2,1)S(1)} copy-done((bf16[512,5120]{1,0:T(8,128)(2,1)S(1)}, bf16[512,5120]{1,0:T(8,128)(2,1)}, u32[]{:S(2)}) %copy-start.1) | copy-done | bytes 5242904
  3.4 3.2 %shard_map.140 = bf16[2560,512]{1,0:T(8,128)(2,1)} custom-call(s32[4]{0:T(128)S(1)} %get-tuple-element.42.order, bf16[512,5120]{1,0:T(8,128)(2,1)S(1)} %copy-done.1), custom_call_target="tpu_custom_call" | custom-call | bytes 5242880 | tf_op jit(solution)/shard_map/pallas_call | solution.py:33
  7.1 7.0 %shard_map.141 = bf16[64,5120]{1,0:T(8,128)(2,1)S(1)} custom-call(s32[64]{0:T(128)S(1)} %and_select_fusion.place, bf16[4748,5120]{1,0:T(8,128)(2,1)} %refs_15_.1, bf16[4748,5120]{1,0:T(8,128)(2,1)} %refs_15_.1, bf16[4748,5120]{1,0:T(8,128)(2,1)} %refs_15_.1, bf16[4748,5120]{1,0:T(8,128)(2,1)} %refs_15_.1, bf16[4748,5120]{1,0:T(8,128)(2,1)} %refs_15_.1, ...), custom_call_target="tpu_custom_call" | custom-call | bytes 10485760 | tf_op jit(solution)/shard_map/pallas_call | solution.py:74
  15.0 2.5 %copy-done.2 = bf16[512,5120]{1,0:T(8,128)(2,1)S(1)} copy-done((bf16[512,5120]{1,0:T(8,128)(2,1)S(1)}, bf16[512,5120]{1,0:T(8,128)(2,1)}, u32[]{:S(2)}) %copy-start.2) | copy-done | bytes 5242904
  17.5 2.0 shard_map.139
  19.5 2.3 %fusion.104 = f32[640,256]{1,0:T(8,128)} fusion(bf16[2560,512]{1,0:T(8,128)(2,1)S(1)} %shard_map.139, bf16[512,1024]{1,0:T(8,128)(2,1)} %param.13), kind=kOutput, calls=%fused_computation.116 | convolution fusion | flops 167772160 | bytes 1572864 | tf_op jit(solution)/shard_map/dot_general | solution.py:92
  21.8 2.2 %fusion.86 = f32[640,256]{1,0:T(8,128)} fusion(bf16[2560,512]{1,0:T(8,128)(2,1)S(1)} %shard_map.139, bf16[512,1024]{1,0:T(8,128)(2,1)} %param.13), kind=kOutput, calls=%fused_computation.96 | convolution fusion | flops 167772160 | bytes 1572864 | tf_op jit(solution)/shard_map/dot_general | solution.py:92
  24.0 2.5 %fusion.68 = f32[1280,256]{1,0:T(8,128)} fusion(bf16[2560,512]{1,0:T(8,128)(2,1)S(1)} %shard_map.139, bf16[512,1024]{1,0:T(8,128)(2,1)} %param.13), kind=kOutput, calls=%fused_computation.78 | convolution fusion | flops 335544320 | bytes 2883584 | tf_op jit(solution)/shard_map/dot_general | solution.py:92
  26.5 2.1 fusion.102
  28.6 2.1 fusion.77
  30.7 1.9 fusion.100
  32.7 2.0 fusion.84
  34.6 2.2 %fusion.66 = f32[1280,128]{1,0:T(8,128)} fusion(bf16[2560,512]{1,0:T(8,128)(2,1)S(1)} %shard_map.139, bf16[512,1024]{1,0:T(8,128)(2,1)} %param.13), kind=kOutput, calls=%fused_computation.76 | convolution fusion | flops 167772160 | bytes 2097152 | tf_op jit(solution)/shard_map/dot_general | solution.py:92
  36.9 2.0 fusion.98
  38.8 2.0 fusion.75
  40.8 2.2 %fusion.57 = f32[1280,128]{1,0:T(8,128)} fusion(bf16[2560,512]{1,0:T(8,128)(2,1)S(1)} %shard_map.139, bf16[512,1024]{1,0:T(8,128)(2,1)} %param.13), kind=kOutput, calls=%fused_computation.67 | convolution fusion | flops 167772160 | bytes 2097152 | tf_op jit(solution)/shard_map/dot_general | solution.py:92
  43.0 2.0 fusion.96
  45.0 2.2 %fusion.64 = f32[1280,128]{1,0:T(8,128)} fusion(bf16[2560,512]{1,0:T(8,128)(2,1)S(1)} %shard_map.139, bf16[512,1024]{1,0:T(8,128)(2,1)} %param.13), kind=kOutput, calls=%fused_computation.74 | convolution fusion | flops 167772160 | bytes 2097152 | tf_op jit(solution)/shard_map/dot_general | solution.py:92
  47.3 2.3 %fusion.55 = f32[1280,128]{1,0:T(8,128)} fusion(bf16[2560,512]{1,0:T(8,128)(2,1)S(1)} %shard_map.139, bf16[512,1024]{1,0:T(8,128)(2,1)} %param.13), kind=kOutput, calls=%fused_computation.65 | convolution fusion | flops 167772160 | bytes 2097152 | tf_op jit(solution)/shard_map/dot_general | solution.py:92
  51.0 2.0 fusion.82
  52.9 2.9 %fusion.59 = f32[1280,256]{1,0:T(8,128)} fusion(bf16[2560,512]{1,0:T(8,128)(2,1)} %copy-done.3, bf16[512,1024]{1,0:T(8,128)(2,1)} %param.13), kind=kOutput, calls=%fused_computation.69 | convolution fusion | flops 335544320 | bytes 2883584 | tf_op jit(solution)/shard_map/dot_general | solution.py:92
  56.0 4.9 %collective-permute-start.35 = (bf16[8,5120]{1,0:T(8,128)(2,1)S(1)}, bf16[8,5120]{1,0:T(8,128)(2,1)S(1)}, u32[]{:S(2)}, u32[]{:S(2)}) collective-permute-start(bf16[8,5120]{1,0:T(8,128)(2,1)S(1)} %get-tuple-element.16), channel_id=1, source_target_pairs={{0,3},{1,2},{2,1},{3,0},{4,7},{5,6},{6,5},{7,4},{8,11},{9,10},{10,... | collective-permute-start | bytes 245768 | tf_op jit(solution)/shard_map/ppermute | solution.py:18
  61.6 2.2 %fusion.94 = f32[640,128]{1,0:T(8,128)} fusion(bf16[2560,512]{1,0:T(8,128)(2,1)} %copy-done.3, bf16[512,1024]{1,0:T(8,128)(2,1)} %param.13), kind=kOutput, calls=%fused_computation.106 | convolution fusion | flops 83886080 | bytes 1114112 | tf_op jit(solution)/shard_map/dot_general | solution.py:92
  64.3 3.5 %collective-permute-done.34 = bf16[8,5120]{1,0:T(8,128)(2,1)S(1)} collective-permute-done((bf16[8,5120]{1,0:T(8,128)(2,1)S(1)}, bf16[8,5120]{1,0:T(8,128)(2,1)S(1)}, u32[]{:S(2)}, u32[]{:S(2)}) %collective-permute-start.34) | collective-permute-done | bytes 81952 | tf_op jit(solution)/shard_map/ppermute | solution.py:18
  69.7 2.2 %fusion.73 = f32[640,128]{1,0:T(8,128)} fusion(bf16[2560,512]{1,0:T(8,128)(2,1)} %copy-done.3, bf16[512,1024]{1,0:T(8,128)(2,1)} %param.13), kind=kOutput, calls=%fused_computation.83 | convolution fusion | flops 83886080 | bytes 1114112 | tf_op jit(solution)/shard_map/dot_general | solution.py:92
  72.4 2.2 %collective-permute-start.37 = (bf16[8,5120]{1,0:T(8,128)(2,1)S(1)}, bf16[8,5120]{1,0:T(8,128)(2,1)S(1)}, u32[]{:S(2)}, u32[]{:S(2)}) collective-permute-start(bf16[8,5120]{1,0:T(8,128)(2,1)S(1)} %add.496), channel_id=1, source_target_pairs={{0,16},{4,20},{8,24},{12,28},{16,0},{20,4},{24,8},{28,12},{1,17},{... | collective-permute-start | bytes 245768 | tf_op jit(solution)/shard_map/ppermute | solution.py:18
  74.8 2.3 %collective-permute-done.37 = bf16[8,5120]{1,0:T(8,128)(2,1)S(1)} collective-permute-done((bf16[8,5120]{1,0:T(8,128)(2,1)S(1)}, bf16[8,5120]{1,0:T(8,128)(2,1)S(1)}, u32[]{:S(2)}, u32[]{:S(2)}) %collective-permute-start.37) | collective-permute-done | bytes 81952 | tf_op jit(solution)/shard_map/ppermute | solution.py:18
  82.0 2.8 %collective-permute-done.39 = bf16[8,5120]{1,0:T(8,128)(2,1)S(1)} collective-permute-done((bf16[8,5120]{1,0:T(8,128)(2,1)S(1)}, bf16[8,5120]{1,0:T(8,128)(2,1)S(1)}, u32[]{:S(2)}, u32[]{:S(2)}) %collective-permute-start.39) | collective-permute-done | bytes 81952 | tf_op jit(solution)/shard_map/ppermute | solution.py:18
  88.2 4.2 %fusion.165 = f32[64,512]{1,0:T(8,128)S(1)} fusion(bf16[64,5120]{1,0:T(8,128)(2,1)S(1)} %constant_dynamic-update-slice_fusion, bf16[512,5120]{1,0:T(8,128)(2,1)} %block.3), kind=kOutput, calls=%fused_computation.240 | convolution fusion | flops 335544320 | bytes 6029312 | tf_op jit(solution)/shard_map/dot_general | solution.py:201
  100.6 2.2 %collective-permute-done.43 = f32[16,1024]{1,0:T(8,128)} collective-permute-done((f32[16,1024]{1,0:T(8,128)}, f32[16,1024]{1,0:T(8,128)}, u32[]{:S(2)}, u32[]{:S(2)}) %collective-permute-start.43) | collective-permute-done | bytes 65568 | tf_op jit(solution)/shard_map/ppermute | solution.py:18
  106.6 1.9 collective-permute-done.44
  110.9 3.0 %collective-permute-start.45 = (f32[8,256]{1,0:T(8,128)S(1)}, f32[8,256]{1,0:T(8,128)S(1)}, u32[]{:S(2)}, u32[]{:S(2)}) collective-permute-start(f32[8,256]{1,0:T(8,128)S(1)} %get-tuple-element.34), channel_id=1, source_target_pairs={{0,1},{1,0},{2,3},{3,2},{4,5},{5,4},{6,7},{7,6},{8,9},{9,8},{10,11... | collective-permute-start | bytes 24584 | tf_op jit(solution)/shard_map/ppermute | solution.py:18
  116.8 2.1 %fusion.49 = bf16[1,8,16,128]{3,2,1,0:T(8,128)(2,1)S(1)} fusion(f32[8,2,8,512]{3,2,1,0:T(8,128)} %get-tuple-element.40, f32[8,2,8]{2,1,0:T(2,128)} %get-tuple-element.38, f32[8,2,8]{2,1,0:T(2,128)S(1)} %multiply_maximum_fusion, f32[8,2,128]{2,1,0:T(2,128)S(1)} %copy.18, f32[8,2,8]{2,1,0:T(2,128)} %get-tuple-element.37, bf16[8,512,256]{2,1,0:T(8,128)(2,1)} %param.19), kind=kOutput, calls=%fused_computation.61 | convolution fusion | flops 17022976 | bytes 2401792 | tf_op jit(solution)/shard_map/rkgc,rckd->rkgd/dot_general | solution.py:262
  119.6 1.8 fusion
  123.3 1.9 fusion.1
  137.1 8.3 %collective-permute-done.12 = bf16[1280,128]{1,0:T(8,128)(2,1)S(1)} collective-permute-done((bf16[1280,128]{1,0:T(8,128)(2,1)S(1)}, bf16[1280,128]{1,0:T(8,128)(2,1)S(1)}, u32[]{:S(2)}, u32[]{:S(2)}) %collective-permute-start.12) | collective-permute-done | bytes 327712 | tf_op jit(solution)/shard_map/ppermute | solution.py:18
  149.6 1.9 collective-permute-start.13
  160.8 2.3 %collective-permute-start.16 = (bf16[160,128]{1,0:T(8,128)(2,1)S(1)}, bf16[160,128]{1,0:T(8,128)(2,1)S(1)}, u32[]{:S(2)}, u32[]{:S(2)}) collective-permute-start(bf16[160,128]{1,0:T(8,128)(2,1)S(1)} %get-tuple-element.28), channel_id=1, source_target_pairs={{0,3},{1,2},{2,1},{3,0},{4,7},{5,6},{6,5},{7,4},{8,11},{9,10},{10,... | collective-permute-start | bytes 122888 | tf_op jit(solution)/shard_map/ppermute | solution.py:18
  173.7 3.5 %collective-permute-done.3 = bf16[640,256]{1,0:T(8,128)(2,1)S(1)} collective-permute-done((bf16[640,256]{1,0:T(8,128)(2,1)S(1)}, bf16[640,256]{1,0:T(8,128)(2,1)S(1)}, u32[]{:S(2)}, u32[]{:S(2)}) %collective-permute-start.3) | collective-permute-done | bytes 327712 | tf_op jit(solution)/shard_map/ppermute | solution.py:18
  188.9 2.7 %collective-permute-start.9 = (bf16[160,256]{1,0:T(8,128)(2,1)S(1)}, bf16[160,256]{1,0:T(8,128)(2,1)S(1)}, u32[]{:S(2)}, u32[]{:S(2)}) collective-permute-start(bf16[160,256]{1,0:T(8,128)(2,1)S(1)} %get-tuple-element.7), channel_id=1, source_target_pairs={{0,1},{1,0},{2,3},{3,2},{4,5},{5,4},{6,7},{7,6},{8,9},{9,8},{10,11... | collective-permute-start | bytes 245768 | tf_op jit(solution)/shard_map/ppermute | solution.py:18
  191.7 2.2 %collective-permute-start.14 = (bf16[160,128]{1,0:T(8,128)(2,1)S(1)}, bf16[160,128]{1,0:T(8,128)(2,1)S(1)}, u32[]{:S(2)}, u32[]{:S(2)}) collective-permute-start(bf16[160,128]{1,0:T(8,128)(2,1)S(1)} %get-tuple-element.27), channel_id=1, source_target_pairs={{0,1},{1,0},{2,3},{3,2},{4,5},{5,4},{6,7},{7,6},{8,9},{9,8},{10,11... | collective-permute-start | bytes 122888 | tf_op jit(solution)/shard_map/ppermute | solution.py:18
  193.9 2.1 collective-permute-done.10
  196.0 2.1 collective-permute-start.21
  198.1 2.3 %collective-permute-start.19 = (bf16[160,128]{1,0:T(8,128)(2,1)S(1)}, bf16[160,128]{1,0:T(8,128)(2,1)S(1)}, u32[]{:S(2)}, u32[]{:S(2)}) collective-permute-start(bf16[160,128]{1,0:T(8,128)(2,1)S(1)} %get-tuple-element.24), channel_id=1, source_target_pairs={{0,1},{1,0},{2,3},{3,2},{4,5},{5,4},{6,7},{7,6},{8,9},{9,8},{10,11... | collective-permute-start | bytes 122888 | tf_op jit(solution)/shard_map/ppermute | solution.py:18
  200.5 2.1 collective-permute-start.26
  202.6 2.3 %collective-permute-start.24 = (bf16[160,128]{1,0:T(8,128)(2,1)S(1)}, bf16[160,128]{1,0:T(8,128)(2,1)S(1)}, u32[]{:S(2)}, u32[]{:S(2)}) collective-permute-start(bf16[160,128]{1,0:T(8,128)(2,1)S(1)} %get-tuple-element.21), channel_id=1, source_target_pairs={{0,1},{1,0},{2,3},{3,2},{4,5},{5,4},{6,7},{7,6},{8,9},{9,8},{10,11... | collective-permute-start | bytes 122888 | tf_op jit(solution)/shard_map/ppermute | solution.py:18
  205.0 2.1 collective-permute-start.31
  207.1 2.3 %collective-permute-start.29 = (bf16[160,128]{1,0:T(8,128)(2,1)S(1)}, bf16[160,128]{1,0:T(8,128)(2,1)S(1)}, u32[]{:S(2)}, u32[]{:S(2)}) collective-permute-start(bf16[160,128]{1,0:T(8,128)(2,1)S(1)} %get-tuple-element.18), channel_id=1, source_target_pairs={{0,1},{1,0},{2,3},{3,2},{4,5},{5,4},{6,7},{7,6},{8,9},{9,8},{10,11... | collective-permute-start | bytes 122888 | tf_op jit(solution)/shard_map/ppermute | solution.py:18
  (203 shorter events, 85.4 us)
Async XLA Ops:
  6.5 113.1 %collective-permute-start = (bf16[2560,512]{1,0:T(8,128)(2,1)}, bf16[2560,512]{1,0:T(8,128)(2,1)}, u32[]{:S(2)}, u32[]{:S(2)}) collective-permute-start(bf16[2560,512]{1,0:T(8,128)(2,1)} %shard_map.140), channel_id=1, source_target_pairs={{0,4},{4,0},{8,12},{12,8},{16,20},{20,16},{24,28},{28,24},{1,5},{5... | collective-permute-start | bytes 7864328 | tf_op jit(solution)/shard_map/ppermute | solution.py:18
  7.0 112.6 %collective-permute-start.1 = (bf16[512,1024]{1,0:T(8,128)(2,1)}, bf16[512,1024]{1,0:T(8,128)(2,1)}, u32[]{:S(2)}, u32[]{:S(2)}) collective-permute-start(bf16[512,1024]{1,0:T(8,128)(2,1)} %param.13), channel_id=1, source_target_pairs={{0,4},{4,0},{8,12},{12,8},{16,20},{20,16},{24,28},{28,24},{1,5},{5... | collective-permute-start | bytes 3145736 | tf_op jit(solution)/shard_map/ppermute | solution.py:18
  14.9 41.0 %collective-permute-start.32 = (bf16[32,5120]{1,0:T(8,128)(2,1)}, bf16[32,5120]{1,0:T(8,128)(2,1)S(1)}, u32[]{:S(2)}, u32[]{:S(2)}) collective-permute-start(bf16[32,5120]{1,0:T(8,128)(2,1)} %constant_dynamic-slice_fusion.11), channel_id=1, source_target_pairs={{0,4},{4,0},{8,12},{12,8},{16,20},{20,16},{24,28},{28,24},{1,5},{5... | collective-permute-start | bytes 983048 | tf_op jit(solution)/shard_map/ppermute | solution.py:18
  56.0 8.3 %collective-permute-start.35 = (bf16[8,5120]{1,0:T(8,128)(2,1)S(1)}, bf16[8,5120]{1,0:T(8,128)(2,1)S(1)}, u32[]{:S(2)}, u32[]{:S(2)}) collective-permute-start(bf16[8,5120]{1,0:T(8,128)(2,1)S(1)} %get-tuple-element.16), channel_id=1, source_target_pairs={{0,3},{1,2},{2,1},{3,0},{4,7},{5,6},{6,5},{7,4},{8,11},{9,10},{10,... | collective-permute-start | bytes 245768 | tf_op jit(solution)/shard_map/ppermute | solution.py:18
  60.9 6.9 %collective-permute-start.34 = (bf16[8,5120]{1,0:T(8,128)(2,1)S(1)}, bf16[8,5120]{1,0:T(8,128)(2,1)S(1)}, u32[]{:S(2)}, u32[]{:S(2)}) collective-permute-start(bf16[8,5120]{1,0:T(8,128)(2,1)S(1)} %get-tuple-element.17), channel_id=1, source_target_pairs={{0,2},{1,3},{2,0},{3,1},{4,6},{5,7},{6,4},{7,5},{8,10},{9,11},{10,... | collective-permute-start | bytes 245768 | tf_op jit(solution)/shard_map/ppermute | solution.py:18
  60.9 6.9 %collective-permute-start.33 = (bf16[8,5120]{1,0:T(8,128)(2,1)S(1)}, bf16[8,5120]{1,0:T(8,128)(2,1)S(1)}, u32[]{:S(2)}, u32[]{:S(2)}) collective-permute-start(bf16[8,5120]{1,0:T(8,128)(2,1)S(1)} %get-tuple-element.15), channel_id=1, source_target_pairs={{0,1},{1,0},{2,3},{3,2},{4,5},{5,4},{6,7},{7,6},{8,9},{9,8},{10,11... | collective-permute-start | bytes 245768 | tf_op jit(solution)/shard_map/ppermute | solution.py:18
  67.9 4.5 %collective-permute-start.36 = (bf16[8,5120]{1,0:T(8,128)(2,1)S(1)}, bf16[8,5120]{1,0:T(8,128)(2,1)S(1)}, u32[]{:S(2)}, u32[]{:S(2)}) collective-permute-start(bf16[8,5120]{1,0:T(8,128)(2,1)S(1)} %add_add_fusion), channel_id=1, source_target_pairs={{0,8},{4,12},{8,0},{12,4},{16,24},{20,28},{24,16},{28,20},{1,9},{5... | collective-permute-start | bytes 245768 | tf_op jit(solution)/shard_map/ppermute | solution.py:18
  72.4 4.6 %collective-permute-start.37 = (bf16[8,5120]{1,0:T(8,128)(2,1)S(1)}, bf16[8,5120]{1,0:T(8,128)(2,1)S(1)}, u32[]{:S(2)}, u32[]{:S(2)}) collective-permute-start(bf16[8,5120]{1,0:T(8,128)(2,1)S(1)} %add.496), channel_id=1, source_target_pairs={{0,16},{4,20},{8,24},{12,28},{16,0},{20,4},{24,8},{28,12},{1,17},{... | collective-permute-start | bytes 245768 | tf_op jit(solution)/shard_map/ppermute | solution.py:18
  77.1 4.9 %collective-permute-start.38 = (bf16[8,5120]{1,0:T(8,128)(2,1)S(1)}, bf16[8,5120]{1,0:T(8,128)(2,1)S(1)}, u32[]{:S(2)}, u32[]{:S(2)}) collective-permute-start(bf16[8,5120]{1,0:T(8,128)(2,1)S(1)} %get-tuple-element.6), channel_id=1, source_target_pairs={{0,1},{1,0},{2,3},{3,2},{4,5},{5,4},{6,7},{7,6},{8,9},{9,8},{10,11... | collective-permute-start | bytes 245768 | tf_op jit(solution)/shard_map/ppermute | solution.py:18
  78.5 6.3 %collective-permute-start.39 = (bf16[8,5120]{1,0:T(8,128)(2,1)S(1)}, bf16[8,5120]{1,0:T(8,128)(2,1)S(1)}, u32[]{:S(2)}, u32[]{:S(2)}) collective-permute-start(bf16[8,5120]{1,0:T(8,128)(2,1)S(1)} %get-tuple-element.6), channel_id=1, source_target_pairs={{0,2},{1,3},{2,0},{3,1},{4,6},{5,7},{6,4},{7,5},{8,10},{9,11},{10,... | collective-permute-start | bytes 245768 | tf_op jit(solution)/shard_map/ppermute | solution.py:18
  80.2 6.2 %collective-permute-start.40 = (bf16[8,5120]{1,0:T(8,128)(2,1)S(1)}, bf16[8,5120]{1,0:T(8,128)(2,1)S(1)}, u32[]{:S(2)}, u32[]{:S(2)}) collective-permute-start(bf16[8,5120]{1,0:T(8,128)(2,1)S(1)} %get-tuple-element.6), channel_id=1, source_target_pairs={{0,3},{1,2},{2,1},{3,0},{4,7},{5,6},{6,5},{7,4},{8,11},{9,10},{10,... | collective-permute-start | bytes 245768 | tf_op jit(solution)/shard_map/ppermute | solution.py:18
  86.5 1.7 collective-permute-start.41
  96.1 1.4 collective-permute-start.42
  98.2 4.6 %collective-permute-start.43 = (f32[16,1024]{1,0:T(8,128)}, f32[16,1024]{1,0:T(8,128)}, u32[]{:S(2)}, u32[]{:S(2)}) collective-permute-start(f32[16,1024]{1,0:T(8,128)} %pad_maximum_fusion.2), channel_id=1, source_target_pairs={{0,8},{4,12},{8,0},{12,4},{16,24},{20,28},{24,16},{28,20},{1,9},{5... | collective-permute-start | bytes 196616 | tf_op jit(solution)/shard_map/ppermute | solution.py:18
  104.3 4.2 %collective-permute-start.44 = (f32[8,1024]{1,0:T(8,128)}, f32[8,1024]{1,0:T(8,128)}, u32[]{:S(2)}, u32[]{:S(2)}) collective-permute-start(f32[8,1024]{1,0:T(8,128)} %slice_add_fusion), channel_id=1, source_target_pairs={{0,16},{4,20},{8,24},{12,28},{16,0},{20,4},{24,8},{28,12},{1,17},{... | collective-permute-start | bytes 98312 | tf_op jit(solution)/shard_map/ppermute | solution.py:18
  109.4 5.5 %collective-permute-start.47 = (f32[8,256]{1,0:T(8,128)S(1)}, f32[8,256]{1,0:T(8,128)S(1)}, u32[]{:S(2)}, u32[]{:S(2)}) collective-permute-start(f32[8,256]{1,0:T(8,128)S(1)} %get-tuple-element.35), channel_id=1, source_target_pairs={{0,3},{1,2},{2,1},{3,0},{4,7},{5,6},{6,5},{7,4},{8,11},{9,10},{10,... | collective-permute-start | bytes 24584 | tf_op jit(solution)/shard_map/ppermute | solution.py:18
  110.9 4.5 %collective-permute-start.46 = (f32[8,256]{1,0:T(8,128)S(1)}, f32[8,256]{1,0:T(8,128)S(1)}, u32[]{:S(2)}, u32[]{:S(2)}) collective-permute-start(f32[8,256]{1,0:T(8,128)S(1)} %get-tuple-element.36), channel_id=1, source_target_pairs={{0,2},{1,3},{2,0},{3,1},{4,6},{5,7},{6,4},{7,5},{8,10},{9,11},{10,... | collective-permute-start | bytes 24584 | tf_op jit(solution)/shard_map/ppermute | solution.py:18
  110.9 4.7 %collective-permute-start.45 = (f32[8,256]{1,0:T(8,128)S(1)}, f32[8,256]{1,0:T(8,128)S(1)}, u32[]{:S(2)}, u32[]{:S(2)}) collective-permute-start(f32[8,256]{1,0:T(8,128)S(1)} %get-tuple-element.34), channel_id=1, source_target_pairs={{0,1},{1,0},{2,3},{3,2},{4,5},{5,4},{6,7},{7,6},{8,9},{9,8},{10,11... | collective-permute-start | bytes 24584 | tf_op jit(solution)/shard_map/ppermute | solution.py:18
  121.5 47.0 %collective-permute-start.2 = (bf16[1280,256]{1,0:T(8,128)(2,1)S(1)}, bf16[1280,256]{1,0:T(8,128)(2,1)S(1)}, u32[]{:S(2)}, u32[]{:S(2)}) collective-permute-start(bf16[1280,256]{1,0:T(8,128)(2,1)S(1)} %fusion), channel_id=1, source_target_pairs={{0,8},{4,12},{8,0},{12,4},{16,24},{20,28},{24,16},{28,20},{1,9},{5... | collective-permute-start | bytes 1966088 | tf_op jit(solution)/shard_map/ppermute | solution.py:18
  125.2 46.3 %collective-permute-start.7 = (bf16[1280,256]{1,0:T(8,128)(2,1)S(1)}, bf16[1280,256]{1,0:T(8,128)(2,1)S(1)}, u32[]{:S(2)}, u32[]{:S(2)}) collective-permute-start(bf16[1280,256]{1,0:T(8,128)(2,1)S(1)} %fusion.1), channel_id=1, source_target_pairs={{0,16},{4,20},{8,24},{12,28},{16,0},{20,4},{24,8},{28,12},{1,17},{... | collective-permute-start | bytes 1966088 | tf_op jit(solution)/shard_map/ppermute | solution.py:18
  128.7 16.7 %collective-permute-start.12 = (bf16[1280,128]{1,0:T(8,128)(2,1)S(1)}, bf16[1280,128]{1,0:T(8,128)(2,1)S(1)}, u32[]{:S(2)}, u32[]{:S(2)}) collective-permute-start(bf16[1280,128]{1,0:T(8,128)(2,1)S(1)} %fusion.2), channel_id=1, source_target_pairs={{0,8},{4,12},{8,0},{12,4},{16,24},{20,28},{24,16},{28,20},{1,9},{5... | collective-permute-start | bytes 983048 | tf_op jit(solution)/shard_map/ppermute | solution.py:18
  131.1 18.5 %collective-permute-start.17 = (bf16[1280,128]{1,0:T(8,128)(2,1)S(1)}, bf16[1280,128]{1,0:T(8,128)(2,1)S(1)}, u32[]{:S(2)}, u32[]{:S(2)}) collective-permute-start(bf16[1280,128]{1,0:T(8,128)(2,1)S(1)} %fusion.3), channel_id=1, source_target_pairs={{0,16},{4,20},{8,24},{12,28},{16,0},{20,4},{24,8},{28,12},{1,17},{... | collective-permute-start | bytes 983048 | tf_op jit(solution)/shard_map/ppermute | solution.py:18
  133.5 19.4 %collective-permute-start.22 = (bf16[1280,128]{1,0:T(8,128)(2,1)S(1)}, bf16[1280,128]{1,0:T(8,128)(2,1)S(1)}, u32[]{:S(2)}, u32[]{:S(2)}) collective-permute-start(bf16[1280,128]{1,0:T(8,128)(2,1)S(1)} %fusion.4), channel_id=1, source_target_pairs={{0,8},{4,12},{8,0},{12,4},{16,24},{20,28},{24,16},{28,20},{1,9},{5... | collective-permute-start | bytes 983048 | tf_op jit(solution)/shard_map/ppermute | solution.py:18
  145.4 10.1 %collective-permute-start.27 = (bf16[1280,128]{1,0:T(8,128)(2,1)S(1)}, bf16[1280,128]{1,0:T(8,128)(2,1)S(1)}, u32[]{:S(2)}, u32[]{:S(2)}) collective-permute-start(bf16[1280,128]{1,0:T(8,128)(2,1)S(1)} %fusion.5), channel_id=1, source_target_pairs={{0,16},{4,20},{8,24},{12,28},{16,0},{20,4},{24,8},{28,12},{1,17},{... | collective-permute-start | bytes 983048 | tf_op jit(solution)/shard_map/ppermute | solution.py:18
  149.6 9.0 %collective-permute-start.13 = (bf16[640,128]{1,0:T(8,128)(2,1)S(1)}, bf16[640,128]{1,0:T(8,128)(2,1)S(1)}, u32[]{:S(2)}, u32[]{:S(2)}) collective-permute-start(bf16[640,128]{1,0:T(8,128)(2,1)S(1)} %fusion.42), channel_id=1, source_target_pairs={{0,16},{4,20},{8,24},{12,28},{16,0},{20,4},{24,8},{28,12},{1,17},{... | collective-permute-start | bytes 491528 | tf_op jit(solution)/shard_map/ppermute | solution.py:18
  152.9 7.9 %collective-permute-start.18 = (bf16[640,128]{1,0:T(8,128)(2,1)S(1)}, bf16[640,128]{1,0:T(8,128)(2,1)S(1)}, u32[]{:S(2)}, u32[]{:S(2)}) collective-permute-start(bf16[640,128]{1,0:T(8,128)(2,1)S(1)} %fusion.41), channel_id=1, source_target_pairs={{0,8},{4,12},{8,0},{12,4},{16,24},{20,28},{24,16},{28,20},{1,9},{5... | collective-permute-start | bytes 491528 | tf_op jit(solution)/shard_map/ppermute | solution.py:18
  155.5 9.1 %collective-permute-start.23 = (bf16[640,128]{1,0:T(8,128)(2,1)S(1)}, bf16[640,128]{1,0:T(8,128)(2,1)S(1)}, u32[]{:S(2)}, u32[]{:S(2)}) collective-permute-start(bf16[640,128]{1,0:T(8,128)(2,1)S(1)} %fusion.40), channel_id=1, source_target_pairs={{0,16},{4,20},{8,24},{12,28},{16,0},{20,4},{24,8},{28,12},{1,17},{... | collective-permute-start | bytes 491528 | tf_op jit(solution)/shard_map/ppermute | solution.py:18
  158.6 8.3 %collective-permute-start.28 = (bf16[640,128]{1,0:T(8,128)(2,1)S(1)}, bf16[640,128]{1,0:T(8,128)(2,1)S(1)}, u32[]{:S(2)}, u32[]{:S(2)}) collective-permute-start(bf16[640,128]{1,0:T(8,128)(2,1)S(1)} %fusion.39), channel_id=1, source_target_pairs={{0,8},{4,12},{8,0},{12,4},{16,24},{20,28},{24,16},{28,20},{1,9},{5... | collective-permute-start | bytes 491528 | tf_op jit(solution)/shard_map/ppermute | solution.py:18
  160.8 37.3 %collective-permute-start.16 = (bf16[160,128]{1,0:T(8,128)(2,1)S(1)}, bf16[160,128]{1,0:T(8,128)(2,1)S(1)}, u32[]{:S(2)}, u32[]{:S(2)}) collective-permute-start(bf16[160,128]{1,0:T(8,128)(2,1)S(1)} %get-tuple-element.28), channel_id=1, source_target_pairs={{0,3},{1,2},{2,1},{3,0},{4,7},{5,6},{6,5},{7,4},{8,11},{9,10},{10,... | collective-permute-start | bytes 122888 | tf_op jit(solution)/shard_map/ppermute | solution.py:18
  164.6 35.9 %collective-permute-start.15 = (bf16[160,128]{1,0:T(8,128)(2,1)S(1)}, bf16[160,128]{1,0:T(8,128)(2,1)S(1)}, u32[]{:S(2)}, u32[]{:S(2)}) collective-permute-start(bf16[160,128]{1,0:T(8,128)(2,1)S(1)} %get-tuple-element.29), channel_id=1, source_target_pairs={{0,2},{1,3},{2,0},{3,1},{4,6},{5,7},{6,4},{7,5},{8,10},{9,11},{10,... | collective-permute-start | bytes 122888 | tf_op jit(solution)/shard_map/ppermute | solution.py:18
  170.0 7.1 %collective-permute-start.3 = (bf16[640,256]{1,0:T(8,128)(2,1)S(1)}, bf16[640,256]{1,0:T(8,128)(2,1)S(1)}, u32[]{:S(2)}, u32[]{:S(2)}) collective-permute-start(bf16[640,256]{1,0:T(8,128)(2,1)S(1)} %fusion.19), channel_id=1, source_target_pairs={{0,16},{4,20},{8,24},{12,28},{16,0},{20,4},{24,8},{28,12},{1,17},{... | collective-permute-start | bytes 983048 | tf_op jit(solution)/shard_map/ppermute | solution.py:18
  173.0 8.5 %collective-permute-start.8 = (bf16[640,256]{1,0:T(8,128)(2,1)S(1)}, bf16[640,256]{1,0:T(8,128)(2,1)S(1)}, u32[]{:S(2)}, u32[]{:S(2)}) collective-permute-start(bf16[640,256]{1,0:T(8,128)(2,1)S(1)} %fusion.18), channel_id=1, source_target_pairs={{0,8},{4,12},{8,0},{12,4},{16,24},{20,28},{24,16},{28,20},{1,9},{5... | collective-permute-start | bytes 983048 | tf_op jit(solution)/shard_map/ppermute | solution.py:18
  178.7 6.6 %collective-permute-start.6 = (bf16[160,256]{1,0:T(8,128)(2,1)S(1)}, bf16[160,256]{1,0:T(8,128)(2,1)S(1)}, u32[]{:S(2)}, u32[]{:S(2)}) collective-permute-start(bf16[160,256]{1,0:T(8,128)(2,1)S(1)} %get-tuple-element.11), channel_id=1, source_target_pairs={{0,3},{1,2},{2,1},{3,0},{4,7},{5,6},{6,5},{7,4},{8,11},{9,10},{10,... | collective-permute-start | bytes 245768 | tf_op jit(solution)/shard_map/ppermute | solution.py:18
  180.5 8.1 %collective-permute-start.5 = (bf16[160,256]{1,0:T(8,128)(2,1)S(1)}, bf16[160,256]{1,0:T(8,128)(2,1)S(1)}, u32[]{:S(2)}, u32[]{:S(2)}) collective-permute-start(bf16[160,256]{1,0:T(8,128)(2,1)S(1)} %get-tuple-element.12), channel_id=1, source_target_pairs={{0,2},{1,3},{2,0},{3,1},{4,6},{5,7},{6,4},{7,5},{8,10},{9,11},{10,... | collective-permute-start | bytes 245768 | tf_op jit(solution)/shard_map/ppermute | solution.py:18
  181.6 7.3 %collective-permute-start.4 = (bf16[160,256]{1,0:T(8,128)(2,1)S(1)}, bf16[160,256]{1,0:T(8,128)(2,1)S(1)}, u32[]{:S(2)}, u32[]{:S(2)}) collective-permute-start(bf16[160,256]{1,0:T(8,128)(2,1)S(1)} %get-tuple-element.10), channel_id=1, source_target_pairs={{0,1},{1,0},{2,3},{3,2},{4,5},{5,4},{6,7},{7,6},{8,9},{9,8},{10,11... | collective-permute-start | bytes 245768 | tf_op jit(solution)/shard_map/ppermute | solution.py:18
  185.3 6.4 %collective-permute-start.11 = (bf16[160,256]{1,0:T(8,128)(2,1)S(1)}, bf16[160,256]{1,0:T(8,128)(2,1)S(1)}, u32[]{:S(2)}, u32[]{:S(2)}) collective-permute-start(bf16[160,256]{1,0:T(8,128)(2,1)S(1)} %get-tuple-element.8), channel_id=1, source_target_pairs={{0,3},{1,2},{2,1},{3,0},{4,7},{5,6},{6,5},{7,4},{8,11},{9,10},{10,... | collective-permute-start | bytes 245768 | tf_op jit(solution)/shard_map/ppermute | solution.py:18
  188.6 7.3 %collective-permute-start.10 = (bf16[160,256]{1,0:T(8,128)(2,1)S(1)}, bf16[160,256]{1,0:T(8,128)(2,1)S(1)}, u32[]{:S(2)}, u32[]{:S(2)}) collective-permute-start(bf16[160,256]{1,0:T(8,128)(2,1)S(1)} %get-tuple-element.9), channel_id=1, source_target_pairs={{0,2},{1,3},{2,0},{3,1},{4,6},{5,7},{6,4},{7,5},{8,10},{9,11},{10,... | collective-permute-start | bytes 245768 | tf_op jit(solution)/shard_map/ppermute | solution.py:18
  188.9 9.2 %collective-permute-start.9 = (bf16[160,256]{1,0:T(8,128)(2,1)S(1)}, bf16[160,256]{1,0:T(8,128)(2,1)S(1)}, u32[]{:S(2)}, u32[]{:S(2)}) collective-permute-start(bf16[160,256]{1,0:T(8,128)(2,1)S(1)} %get-tuple-element.7), channel_id=1, source_target_pairs={{0,1},{1,0},{2,3},{3,2},{4,5},{5,4},{6,7},{7,6},{8,9},{9,8},{10,11... | collective-permute-start | bytes 245768 | tf_op jit(solution)/shard_map/ppermute | solution.py:18
  191.7 10.9 %collective-permute-start.14 = (bf16[160,128]{1,0:T(8,128)(2,1)S(1)}, bf16[160,128]{1,0:T(8,128)(2,1)S(1)}, u32[]{:S(2)}, u32[]{:S(2)}) collective-permute-start(bf16[160,128]{1,0:T(8,128)(2,1)S(1)} %get-tuple-element.27), channel_id=1, source_target_pairs={{0,1},{1,0},{2,3},{3,2},{4,5},{5,4},{6,7},{7,6},{8,9},{9,8},{10,11... | collective-permute-start | bytes 122888 | tf_op jit(solution)/shard_map/ppermute | solution.py:18
  196.0 6.7 %collective-permute-start.21 = (bf16[160,128]{1,0:T(8,128)(2,1)S(1)}, bf16[160,128]{1,0:T(8,128)(2,1)S(1)}, u32[]{:S(2)}, u32[]{:S(2)}) collective-permute-start(bf16[160,128]{1,0:T(8,128)(2,1)S(1)} %get-tuple-element.25), channel_id=1, source_target_pairs={{0,3},{1,2},{2,1},{3,0},{4,7},{5,6},{6,5},{7,4},{8,11},{9,10},{10,... | collective-permute-start | bytes 122888 | tf_op jit(solution)/shard_map/ppermute | solution.py:18
  198.1 6.9 %collective-permute-start.20 = (bf16[160,128]{1,0:T(8,128)(2,1)S(1)}, bf16[160,128]{1,0:T(8,128)(2,1)S(1)}, u32[]{:S(2)}, u32[]{:S(2)}) collective-permute-start(bf16[160,128]{1,0:T(8,128)(2,1)S(1)} %get-tuple-element.26), channel_id=1, source_target_pairs={{0,2},{1,3},{2,0},{3,1},{4,6},{5,7},{6,4},{7,5},{8,10},{9,11},{10,... | collective-permute-start | bytes 122888 | tf_op jit(solution)/shard_map/ppermute | solution.py:18
  198.1 9.0 %collective-permute-start.19 = (bf16[160,128]{1,0:T(8,128)(2,1)S(1)}, bf16[160,128]{1,0:T(8,128)(2,1)S(1)}, u32[]{:S(2)}, u32[]{:S(2)}) collective-permute-start(bf16[160,128]{1,0:T(8,128)(2,1)S(1)} %get-tuple-element.24), channel_id=1, source_target_pairs={{0,1},{1,0},{2,3},{3,2},{4,5},{5,4},{6,7},{7,6},{8,9},{9,8},{10,11... | collective-permute-start | bytes 122888 | tf_op jit(solution)/shard_map/ppermute | solution.py:18
  200.5 6.7 %collective-permute-start.26 = (bf16[160,128]{1,0:T(8,128)(2,1)S(1)}, bf16[160,128]{1,0:T(8,128)(2,1)S(1)}, u32[]{:S(2)}, u32[]{:S(2)}) collective-permute-start(bf16[160,128]{1,0:T(8,128)(2,1)S(1)} %get-tuple-element.22), channel_id=1, source_target_pairs={{0,3},{1,2},{2,1},{3,0},{4,7},{5,6},{6,5},{7,4},{8,11},{9,10},{10,... | collective-permute-start | bytes 122888 | tf_op jit(solution)/shard_map/ppermute | solution.py:18
  202.6 6.9 %collective-permute-start.25 = (bf16[160,128]{1,0:T(8,128)(2,1)S(1)}, bf16[160,128]{1,0:T(8,128)(2,1)S(1)}, u32[]{:S(2)}, u32[]{:S(2)}) collective-permute-start(bf16[160,128]{1,0:T(8,128)(2,1)S(1)} %get-tuple-element.23), channel_id=1, source_target_pairs={{0,2},{1,3},{2,0},{3,1},{4,6},{5,7},{6,4},{7,5},{8,10},{9,11},{10,... | collective-permute-start | bytes 122888 | tf_op jit(solution)/shard_map/ppermute | solution.py:18
  202.6 6.9 %collective-permute-start.24 = (bf16[160,128]{1,0:T(8,128)(2,1)S(1)}, bf16[160,128]{1,0:T(8,128)(2,1)S(1)}, u32[]{:S(2)}, u32[]{:S(2)}) collective-permute-start(bf16[160,128]{1,0:T(8,128)(2,1)S(1)} %get-tuple-element.21), channel_id=1, source_target_pairs={{0,1},{1,0},{2,3},{3,2},{4,5},{5,4},{6,7},{7,6},{8,9},{9,8},{10,11... | collective-permute-start | bytes 122888 | tf_op jit(solution)/shard_map/ppermute | solution.py:18
  205.0 5.8 %collective-permute-start.31 = (bf16[160,128]{1,0:T(8,128)(2,1)S(1)}, bf16[160,128]{1,0:T(8,128)(2,1)S(1)}, u32[]{:S(2)}, u32[]{:S(2)}) collective-permute-start(bf16[160,128]{1,0:T(8,128)(2,1)S(1)} %get-tuple-element.19), channel_id=1, source_target_pairs={{0,3},{1,2},{2,1},{3,0},{4,7},{5,6},{6,5},{7,4},{8,11},{9,10},{10,... | collective-permute-start | bytes 122888 | tf_op jit(solution)/shard_map/ppermute | solution.py:18
  207.1 4.9 %collective-permute-start.30 = (bf16[160,128]{1,0:T(8,128)(2,1)S(1)}, bf16[160,128]{1,0:T(8,128)(2,1)S(1)}, u32[]{:S(2)}, u32[]{:S(2)}) collective-permute-start(bf16[160,128]{1,0:T(8,128)(2,1)S(1)} %get-tuple-element.20), channel_id=1, source_target_pairs={{0,2},{1,3},{2,0},{3,1},{4,6},{5,7},{6,4},{7,5},{8,10},{9,11},{10,... | collective-permute-start | bytes 122888 | tf_op jit(solution)/shard_map/ppermute | solution.py:18
  207.1 4.9 %collective-permute-start.29 = (bf16[160,128]{1,0:T(8,128)(2,1)S(1)}, bf16[160,128]{1,0:T(8,128)(2,1)S(1)}, u32[]{:S(2)}, u32[]{:S(2)}) collective-permute-start(bf16[160,128]{1,0:T(8,128)(2,1)S(1)} %get-tuple-element.18), channel_id=1, source_target_pairs={{0,1},{1,0},{2,3},{3,2},{4,5},{5,4},{6,7},{7,6},{8,9},{9,8},{10,11... | collective-permute-start | bytes 122888 | tf_op jit(solution)/shard_map/ppermute | solution.py:18
  (34 other events, 390.6 us)

commit v2 on v1

v2 whole, which is shorter than its diff:
```python
import functools
import math

import jax
import jax.numpy as jnp
from jax import lax
from jax.experimental import pallas as pl
from jax.experimental.pallas import tpu as pltpu
from jax.sharding import PartitionSpec as P

HEADS = 64
KV = 8
HD = 128
LANES = 128
SLAB = 16
VMEM = 56 << 20


def exchange(value, axis, mask):
    return lax.ppermute(value, axis, [(i, i ^ mask) for i in range(lax.axis_size(axis))])


def transpose_block(units, order, block, out):
    flipped = block[...].T
    rows = flipped.shape[0] // units
    for unit in range(units):
        place = pl.multiple_of(order[pl.num_programs(0) + unit] * rows, rows)
        out[pl.ds(place, rows), :] = flipped[unit * rows : (unit + 1) * rows]


def pack(activations, blocks, units, width):
    tokens = activations.shape[0]
    count = len(blocks)
    rows = width // len(units)
    if width % LANES or rows % 32:
        flipped = activations.T
        return jnp.concatenate(
            [
                lax.dynamic_slice_in_dim(flipped, block * width + unit * rows, rows, 0)
                for block in blocks
                for unit in units
            ]
        )
    return pl.pallas_call(
        functools.partial(transpose_block, len(units)),
        grid_spec=pltpu.PrefetchScalarGridSpec(
            num_scalar_prefetch=1,
            grid=(count,),
            in_specs=[pl.BlockSpec((tokens, width), lambda j, order: (0, order[j]))],
            out_specs=pl.BlockSpec((width, tokens), lambda j, order: (j, 0)),
        ),
        out_shape=jax.ShapeDtypeStruct((count * width, tokens), activations.dtype),
        compiler_params=pltpu.CompilerParams(vmem_limit_bytes=VMEM),
        cost_estimate=pl.CostEstimate(
            flops=0, bytes_accessed=4 * count * width * tokens, transcendentals=0
        ),
    )(jnp.stack(list(blocks) + list(units)).astype(jnp.int32), activations)


def runs_of(units):
    runs = []
    for unit in units:
        if runs and runs[-1][1] == unit:
            runs[-1][1] = unit + 1
        else:
            runs.append([unit, unit + 1])
    return runs


def multiply(wanted, rows, blocks, *refs):
    count = len(wanted)
    sources = refs[:4]
    outs = refs[4 : 4 + count]
    near, far, near_grad, far_grad, sems = refs[4 + count :]
    per_block = near.shape[0] // blocks
    copies = {}
    for at, (source, target) in enumerate(((sources[2], near_grad), (sources[3], far_grad))):
        copies["grad", at] = pltpu.make_async_copy(source, target, sems.at[at])
    for block in range(blocks):
        span = pl.ds(block * per_block, per_block)
        for at, (source, target) in enumerate(((sources[0], near), (sources[1], far))):
            copies[block, at] = pltpu.make_async_copy(
                source.at[span], target.at[span], sems.at[2 + 2 * block + at]
            )
    for copy in copies.values():
        copy.start()
    for at in range(2):
        copies["grad", at].wait()
    units_block = per_block // rows
    for block in range(blocks):
        for at in range(2):
            copies[block, at].wait()
        for (units, first, last, _), out in zip(wanted, outs):
            here = [unit for unit in units if unit // units_block == block]
            for low, high in runs_of(here):
                span = slice(low * rows, high * rows)
                place = units.index(low) * rows
                product = dot32(near[span, :], near_grad[:, first:last])
                product += dot32(far[span, :], far_grad[:, first:last])
                out[place : place + (high - low) * rows, :] = product.astype(out.dtype)


def products(lefts, grads, wanted, rows, blocks):
    total, tokens = lefts[0].shape
    columns = grads[0].shape[1]
    if rows % 32 or any((first | last) % LANES for _, first, last, _ in wanted):
        return [
            jnp.concatenate(
                [
                    sum(
                        dot32(left[low * rows : high * rows], grad[:, first:last])
                        for left, grad in zip(lefts, grads)
                    )
                    for low, high in runs_of(units)
                ]
            ).astype(kind)
            for units, first, last, kind in wanted
        ]
    shapes = [
        jax.ShapeDtypeStruct((len(units) * rows, last - first), kind)
        for units, first, last, kind in wanted
    ]
    work = sum(shape.size for shape in shapes)
    return pl.pallas_call(
        functools.partial(multiply, wanted, rows, blocks),
        out_shape=shapes,
        in_specs=[pl.BlockSpec(memory_space=pl.ANY)] * 4,
        out_specs=[pl.BlockSpec(memory_space=pltpu.VMEM)] * len(shapes),
        scratch_shapes=[pltpu.VMEM((total, tokens), lefts[0].dtype)] * 2
        + [pltpu.VMEM((tokens, columns), grads[0].dtype)] * 2
        + [pltpu.SemaphoreType.DMA((2 + 2 * blocks,))],
        compiler_params=pltpu.CompilerParams(vmem_limit_bytes=VMEM),
        cost_estimate=pl.CostEstimate(
            flops=4 * work * tokens,
            bytes_accessed=4 * tokens * (total + columns) + 4 * work,
            transcendentals=0,
        ),
    )(*lefts, *grads)


def pick_rows(place, *refs):
    slabs, out, held = refs[:SLAB], refs[SLAB], refs[SLAB + 1]
    held[...] = jnp.zeros_like(held)
    for k in range(SLAB):
        inside = place[pl.program_id(0) * SLAB + k]

        @pl.when(inside >= 0)
        def _():
            rows = slabs[k][...].astype(jnp.float32)
            at = lax.broadcasted_iota(jnp.int32, rows.shape, 0)
            chosen = jnp.where(at == lax.rem(inside, SLAB), rows, 0.0)
            held[k : k + 1, :] = jnp.sum(chosen, axis=0, keepdims=True)

    out[...] = held[...].astype(out.dtype)


def lookup(embed_table, token_ids, start):
    here, width = embed_table.shape
    count = token_ids.shape[0]
    inside = token_ids - start
    place = jnp.where((inside >= 0) & (inside < here), inside, -1)

    def slab_of(k):
        return lambda i, place: (jnp.maximum(place[i * SLAB + k], 0) // SLAB, 0)

    return pl.pallas_call(
        pick_rows,
        grid_spec=pltpu.PrefetchScalarGridSpec(
            num_scalar_prefetch=1,
            grid=(count // SLAB,),
            in_specs=[pl.BlockSpec((SLAB, width), slab_of(k)) for k in range(SLAB)],
            out_specs=pl.BlockSpec((SLAB, width), lambda i, place: (i, 0)),
            scratch_shapes=[pltpu.VMEM((SLAB, width), jnp.float32)],
        ),
        out_shape=jax.ShapeDtypeStruct((count, width), embed_table.dtype),
        compiler_params=pltpu.CompilerParams(vmem_limit_bytes=32 << 20),
        cost_estimate=pl.CostEstimate(
            flops=0, bytes_accessed=2 * count * SLAB * width, transcendentals=0
        ),
    )(place.astype(jnp.int32), *([embed_table] * SLAB))


def dot32(left, right):
    return jnp.dot(left, right, preferred_element_type=jnp.float32)


def per_device(
    activations,
    grad_out,
    master_w,
    embed_table,
    token_ids,
    queries,
    cache_keys,
    cache_values,
    new_key,
    first_value,
    residual_mix,
    lengths,
):
    count_fsdp = lax.axis_size("fsdp")
    count_tp = lax.axis_size("tp")
    devices_all = count_fsdp * count_tp
    width = activations.shape[1]
    tokens_total = activations.shape[0] * devices_all
    coef = 1.0 / math.sqrt(tokens_total * width)
    f = lax.axis_index("fsdp")
    t = lax.axis_index("tp")
    core = f & 1
    upper = f >> 1
    upper_bits = count_fsdp.bit_length() - 2
    uppers = 1 << upper_bits

    block = width // count_fsdp
    rows = master_w.shape[0]
    columns = master_w.shape[1]
    arranged = [r ^ (r >> 1) for r in range(uppers)][::-1]
    units_tp = [t ^ unit for unit in range(count_tp)]
    grads = [grad_out, exchange(grad_out, "fsdp", 1)]
    outgoing = pack(
        activations, [((r ^ upper) << 1) | (1 - core) for r in arranged], units_tp, block
    )
    incoming = exchange(outgoing, "fsdp", 1)
    staying = pack(activations, [((r ^ upper) << 1) | core for r in arranged], units_tp, block)
    lefts = [staying, incoming]

    places = [(r, unit) for r in arranged for unit in range(count_tp)]
    steps_upper = [("fsdp", bit) for bit in range(upper_bits)]
    steps_tp = [("tp", bit) for bit in range(count_tp.bit_length() - 1)]
    wide = columns * 3 // 8
    orders = [
        (0, wide, steps_upper + steps_tp),
        (wide, 2 * wide, steps_upper[::-1] + steps_tp),
        (2 * wide, columns, steps_tp[:1] + steps_upper + steps_tp[1:]),
    ]

    def has(place, step):
        return (place[step[0] == "tp"] >> step[1]) & 1

    def flip(place, step):
        mask = 1 << step[1]
        return (place[0], place[1] ^ mask) if step[0] == "tp" else (place[0] ^ mask, place[1])

    def split(held, step):
        return [p for p in held if has(p, step)], [p for p in held if not has(p, step)]

    wanted_sent, wanted_kept, kept = [], [], []
    for first, last, steps in orders:
        go, stay = split(places, steps[0])
        kept.append(stay)
        wanted_sent.append(([places.index(p) for p in go], first, last, jnp.bfloat16))
        wanted_kept.append(([places.index(p) for p in stay], first, last, jnp.float32))
    sending = products(lefts, grads, wanted_sent, rows, uppers)

    def take(value, held, chosen):
        runs = runs_of([held.index(p) for p in chosen])
        return jnp.concatenate([value[low * rows : high * rows] for low, high in runs])

    def send(value, step):
        mask = 1 << step[1]
        return exchange(value, step[0], 2 * mask if step[0] == "fsdp" else mask)

    first_got = [send(value, order[2][0]) for value, order in zip(sending, orders)]
    values = products(lefts, grads, wanted_kept, rows, uppers)
    finished = []
    for value, got, held, (first, last, steps) in zip(values, first_got, kept, orders):
        for at, step in enumerate(steps):
            if at:
                go, held = split(held, step)
                got = send(take(value, whole, go).astype(jnp.bfloat16), step)
                value = take(value, whole, held)
            else:
                go = split(places, step)[0]
            whole = held
            value = value + take(got, [flip(p, step) for p in go], held).astype(jnp.float32)
        finished.append(value)
    w_next = jnp.concatenate(
        [master_w[:, o[0] : o[1]] - coef * value for o, value in zip(orders, finished)], axis=1
    )

    flat = f * count_tp + t
    embedded = lax.psum(
        lookup(embed_table, token_ids, flat * embed_table.shape[0]), ("fsdp", "tp")
    )

    through = lax.dot_general(
        embedded, activations, (((1,), (1,)), ((), ())), preferred_element_type=jnp.float32
    )
    high = through.astype(jnp.bfloat16)
    low = (through - high.astype(jnp.float32)).astype(jnp.bfloat16)
    own_columns = lax.dynamic_slice_in_dim(embedded, flat * rows, rows, 1).astype(jnp.float32)
    share_own = jnp.dot(
        own_columns,
        master_w,
        preferred_element_type=jnp.float32,
        precision=lax.Precision.HIGHEST,
    ) - coef * (dot32(high, grad_out) + dot32(low, grad_out))
    rows_f = token_ids.shape[0] // count_fsdp
    col_width = columns // count_tp
    own_value = lax.psum_scatter(
        share_own.reshape(count_fsdp, rows_f, count_tp, col_width)
        .transpose(0, 2, 1, 3)
        .reshape(devices_all * rows_f, col_width),
        ("fsdp", "tp"),
        scatter_dimension=0,
        tiled=True,
    )

    share = jnp.repeat(residual_mix, HD)[None, :]
    new_value = (share * own_value + (1.0 - share) * first_value.astype(jnp.float32)).astype(
        jnp.bfloat16
    )
    rows = queries.shape[0]
    heads_kv = residual_mix.shape[0]
    group = HEADS // KV
    context = cache_keys.shape[1]
    scale = 1.0 / math.sqrt(HD)
    query_b = queries.reshape(rows, heads_kv, group, HD)
    keys_b = cache_keys.reshape(rows, context, heads_kv, HD)
    vals_b = cache_values.reshape(rows, context, heads_kv, HD)
    newk_b = new_key.reshape(rows, heads_kv, HD)
    newv_b = new_value.reshape(rows, heads_kv, HD)
    scores = (
        jnp.einsum("rkgd,rckd->rkgc", query_b, keys_b, preferred_element_type=jnp.float32) * scale
    )
    fresh = jnp.einsum("rkgd,rkd->rkg", query_b, newk_b, preferred_element_type=jnp.float32) * scale
    valid = jnp.arange(context, dtype=jnp.int32)[None, :] < lengths[:, None]
    scores = jnp.where(valid[:, None, None, :], scores, -1e30)
    peak = jnp.maximum(jnp.max(scores, axis=-1), fresh)
    expo = jnp.exp(scores - peak[..., None])
    expo_new = jnp.exp(fresh - peak)
    total = jnp.sum(expo, axis=-1) + expo_new
    probs = (expo / total[..., None]).astype(jnp.bfloat16)
    probs_new = (expo_new / total).astype(jnp.bfloat16)
    mixed = jnp.einsum("rkgc,rckd->rkgd", probs, vals_b, preferred_element_type=jnp.float32)
    mixed = (
        mixed + probs_new.astype(jnp.float32)[..., None] * newv_b.astype(jnp.float32)[:, :, None, :]
    )
    attended = mixed.reshape(rows, group * heads_kv * HD).astype(jnp.bfloat16)
    return (w_next, new_value, attended)


def solution(mesh):
    return jax.shard_map(
        per_device,
        mesh=mesh,
        in_specs=(
            P(("fsdp", "tp"), None),
            P(("fsdp", "tp"), None),
            P(("fsdp", "tp"), None),
            P(("fsdp", "tp"), None),
            P(),
            P("fsdp", "tp"),
            P("fsdp", None, "tp"),
            P("fsdp", None, "tp"),
            P("fsdp", "tp"),
            P("fsdp", "tp"),
            P("tp"),
            P("fsdp"),
        ),
        out_specs=(P(("fsdp", "tp"), None), P("fsdp", "tp"), P("fsdp", "tp")),
        check_vma=False,
    )
```

time: 214 us -> 369 us (1.72)
  waiting for transfers between devices: 39.9 us -> 288 us
  matrix products: 79.1 us -> 12.4 us
  starting transfers between devices: 64.9 us -> 13.8 us
  Pallas kernels: 12.2 us -> 32.1 us
  between operations: 1.81 us -> 14.4 us
  local copies, waits for them, and re-layouts: 8.5 us -> 2.47 us
    psum x0 -> x1, waiting for transfers between devices: none -> 131 us  [per_device(): lax.psum(lookup(embed_table, token_ids, flat * embed_table.shape[0]), ('f...]
    reduce_scatter x0 -> x1, waiting for transfers between devices: none -> 119 us  [per_device(): lax.psum_scatter(share_own.reshape(count_fsdp, rows_f, count_tp, col_widt...]
    dot_general x38 -> x2, matrix products: 70.8 us -> 3.12 us  [dot32(): return jnp.dot(left, right, preferred_element_type=jnp.float32)]
    ppermute x48 -> x14, starting transfers between devices: 64.9 us -> 13.6 us  [exchange(): lax.ppermute(value, axis, [(i, i ^ mask) for i in range(lax.axis_size(axi...]
    pallas_call x2 -> x4, Pallas kernels: 5.15 us -> 25.2 us  [the longest x2 15 us: products(): pl.pallas_call(functools.partial(multiply, wanted, rows, blocks), out_sha...]
    unnamed x72 -> x21, local copies, waits for them, and re-layouts: 6.73 us -> 0.69 us
    ppermute x48 -> x14, waiting for transfers between devices: 39.9 us -> 38.5 us  [exchange(): lax.ppermute(value, axis, [(i, i ^ mask) for i in range(lax.axis_size(axi...]
  transfers between devices with their start and end apart: 48 -> 16, of which waited for: 22 -> 10; matrix products, arithmetic and copies ran while one was open for 40% -> 5% of each run, Pallas kernels for 4% -> 7%
where the time goes in v2:
time: 369 us; the launch traced here: 368 us
  waiting for transfers between devices  288 us (78%)
  Pallas kernels  32.1 us (9%)
  between operations  14.4 us (4%)
  starting transfers between devices  13.8 us (4%)
  matrix products  12.4 us (3%)
  other arithmetic  5.23 us (1%)
    psum x1, waiting for transfers between devices, per_device(): lax.psum(lookup(embed_table, token_ids, flat * embed_table.shape[0]), ('f...  131 us
    reduce_scatter x1, waiting for transfers between devices, per_device(): lax.psum_scatter(share_own.reshape(count_fsdp, rows_f, count_tp, col_widt...  119 us
    ppermute x14, waiting for transfers between devices, exchange(): lax.ppermute(value, axis, [(i, i ^ mask) for i in range(lax.axis_size(axi...  38.5 us
    pallas_call x2, Pallas kernels, products(): pl.pallas_call(functools.partial(multiply, wanted, rows, blocks), out_sha...  15 us
    ppermute x14, starting transfers between devices, exchange(): lax.ppermute(value, axis, [(i, i ^ mask) for i in range(lax.axis_size(axi...  13.6 us
    pallas_call x2, Pallas kernels, pack(): pl.pallas_call(functools.partial(transpose_block, len(units)), grid_spec=...  10.3 us
  transfers between devices with their start and end apart: 16, of which 10 were waited for; matrix products, arithmetic and copies ran while one was open for 5% of the time, Pallas kernels for 7%

profile of v2, /device:TPU:0, one launch (start us, length us, event | category | flops | bytes accessed | tf_op | source)
XLA Modules:
  0.0 368.5 jit_solution(7033567699637406483)
XLA Ops:
  7.2 0.6 stack.59.order
  7.9 5.2 %shard_map.140 = bf16[2560,512]{1,0:T(8,128)(2,1)} custom-call(s32[8]{0:T(128)} %stack.59.order, bf16[512,5120]{1,0:T(8,128)(2,1)} %block.3), custom_call_target="tpu_custom_call" | custom-call | bytes 5242880 | tf_op jit(solution)/shard_map/pallas_call | solution.py:44
  13.0 0.5 collective-permute-start
  13.6 6.9 %shard_map.143 = bf16[64,5120]{1,0:T(8,128)(2,1)} custom-call(s32[64]{0:T(128)S(1)} %and_select_fusion.place, bf16[4748,5120]{1,0:T(8,128)(2,1)} %refs_15_.1, bf16[4748,5120]{1,0:T(8,128)(2,1)} %refs_15_.1, bf16[4748,5120]{1,0:T(8,128)(2,1)} %refs_15_.1, bf16[4748,5120]{1,0:T(8,128)(2,1)} %refs_15_.1, bf16[4748,5120]{1,0:T(8,128)(2,1)} %refs_15_.1, ...), custom_call_target="tpu_custom_call" | custom-call | bytes 10485760 | tf_op jit(solution)/shard_map/pallas_call | solution.py:166
  20.5 0.2 reduce-scatter.2.cloned.1.call-start
  20.7 0.1 iota_compare_fusion
  20.9 0.1 fusion.35
  21.0 0.7 fusion.50
  21.9 130.8 %all-reduce.2.cloned.1.call-done = bf16[64,5120]{1,0:T(8,128)(2,1)} async-done(((bf16[64,5120]{1,0:T(8,128)(2,1)}), bf16[64,5120]{1,0:T(8,128)(2,1)}) %all-reduce.2.cloned.1.call-update) | async-done | bytes 655376 | tf_op jit(solution)/shard_map/psum | solution.py:282
  152.7 4.4 %fusion.51 = f32[64,512]{1,0:T(8,128)S(1)} fusion(bf16[64,5120]{1,0:T(8,128)(2,1)} %all-reduce.2.cloned.1.call-done, bf16[512,5120]{1,0:T(8,128)(2,1)} %block.3), kind=kOutput, calls=%fused_computation.78 | convolution fusion | flops 335544320 | bytes 6029312 | tf_op jit(solution)/shard_map/dot_general | solution.py:286
  157.1 1.6 fusion.32
  158.7 1.5 fusion.12
  160.2 1.9 convolution_subtract_fusion
  162.2 0.2 fusion.26
  162.4 0.6 stack.54.order
  163.0 5.1 %shard_map.139.refs_0_ = bf16[2560,512]{1,0:T(8,128)(2,1)} custom-call(s32[8]{0:T(128)} %stack.54.order, bf16[512,5120]{1,0:T(8,128)(2,1)} %block.3), custom_call_target="tpu_custom_call" | custom-call | bytes 5242880 | tf_op jit(solution)/shard_map/pallas_call | solution.py:44
  168.2 7.2 %shard_map.142 = (bf16[1280,384]{1,0:T(8,128)(2,1)}, bf16[1280,384]{1,0:T(8,128)(2,1)}, bf16[1280,256]{1,0:T(8,128)(2,1)}) custom-call(bf16[2560,512]{1,0:T(8,128)(2,1)} %shard_map.139.refs_0_, bf16[2560,512]{1,0:T(8,128)(2,1)} %collective-permute-done.refs_1_, bf16[512,1024]{1,0:T(8,128)(2,1)} %refs_2_.4, bf16[512,1024]{1,0:T(8,128)(2,1)} %collective-permute-done.1.refs_3_), custom_call_target="tpu_custom_call" | custom-call | flops 2684354560 | bytes 12582912 | tf_op jit(solution)/shard_map/pallas_call | solution.py:124
  175.4 1.5 collective-permute-start.10
  176.9 118.8 %reduce-scatter.2.cloned.1.call-done = f32[8,256]{1,0:T(8,128)} async-done(((f32[256,256]{1,0:T(8,128)}), f32[8,256]{1,0:T(8,128)}) %reduce-scatter.2.cloned.1.call-update) | async-done | bytes 8208 | tf_op jit(solution)/shard_map/reduce_scatter | solution.py:300
  295.6 1.3 bitcast_convert_fusion
  296.9 2.0 fusion.19
  299.0 0.6 copy.53
  299.6 0.1 collective-permute-start.6
  299.7 7.7 %shard_map.141 = (f32[1280,384]{1,0:T(8,128)}, f32[1280,384]{1,0:T(8,128)}, f32[1280,256]{1,0:T(8,128)}) custom-call(bf16[2560,512]{1,0:T(8,128)(2,1)} %shard_map.139.refs_0_, bf16[2560,512]{1,0:T(8,128)(2,1)} %collective-permute-done.refs_1_, bf16[512,1024]{1,0:T(8,128)(2,1)} %refs_2_.4, bf16[512,1024]{1,0:T(8,128)(2,1)} %collective-permute-done.1.refs_3_), custom_call_target="tpu_custom_call" | custom-call | flops 2684354560 | bytes 12582912 | tf_op jit(solution)/shard_map/pallas_call | solution.py:124
  307.5 1.6 convert_add_fusion.2
  309.1 2.1 collective-permute-start.11
  311.3 7.4 %collective-permute-done.6 = bf16[1280,384]{1,0:T(8,128)(2,1)S(1)} collective-permute-done((bf16[1280,384]{1,0:T(8,128)(2,1)}, bf16[1280,384]{1,0:T(8,128)(2,1)S(1)}, u32[]{:S(2)}, u32[]{:S(2)}) %collective-permute-start.6) | collective-permute-done | bytes 983072 | tf_op jit(solution)/shard_map/ppermute | solution.py:20
  318.7 0.1 fusion.47
  318.8 0.2 convert_add_fusion
  319.1 0.1 collective-permute-start.7
  319.2 12.0 %collective-permute-done.11 = bf16[640,256]{1,0:T(8,128)(2,1)S(1)} collective-permute-done((bf16[640,256]{1,0:T(8,128)(2,1)S(1)}, bf16[640,256]{1,0:T(8,128)(2,1)S(1)}, u32[]{:S(2)}, u32[]{:S(2)}) %collective-permute-start.11) | collective-permute-done | bytes 327712 | tf_op jit(solution)/shard_map/ppermute | solution.py:20
  331.2 1.6 collective-permute-start.12
  332.9 0.2 convert_add_fusion.1
  333.2 0.5 collective-permute-start.3
  333.7 3.0 collective-permute-done.12
  336.7 1.0 collective-permute-start.13
  337.7 0.1 fusion.43
  337.9 0.1 collective-permute-start.8
  338.0 4.0 %collective-permute-done.3 = bf16[640,384]{1,0:T(8,128)(2,1)S(1)} collective-permute-done((bf16[640,384]{1,0:T(8,128)(2,1)S(1)}, bf16[640,384]{1,0:T(8,128)(2,1)S(1)}, u32[]{:S(2)}, u32[]{:S(2)}) %collective-permute-start.3) | collective-permute-done | bytes 491552 | tf_op jit(solution)/shard_map/ppermute | solution.py:20
  342.1 0.1 fusion.42
  342.4 4.8 %collective-permute-done.8 = bf16[320,384]{1,0:T(8,128)(2,1)S(1)} collective-permute-done((bf16[320,384]{1,0:T(8,128)(2,1)S(1)}, bf16[320,384]{1,0:T(8,128)(2,1)S(1)}, u32[]{:S(2)}, u32[]{:S(2)}) %collective-permute-start.8) | collective-permute-done | bytes 245792 | tf_op jit(solution)/shard_map/ppermute | solution.py:20
  347.2 1.7 collective-permute-start.9
  348.9 2.2 collective-permute-done.4
  351.2 4.3 %collective-permute-start.5 = (bf16[160,384]{1,0:T(8,128)(2,1)S(1)}, bf16[160,384]{1,0:T(8,128)(2,1)S(1)}, u32[]{:S(2)}, u32[]{:S(2)}) collective-permute-start(bf16[160,384]{1,0:T(8,128)(2,1)S(1)} %slice.181), channel_id=1, source_target_pairs={{0,2},{1,3},{2,0},{3,1},{4,6},{5,7},{6,4},{7,5},{8,10},{9,11},{10,... | collective-permute-start | bytes 368648 | tf_op jit(solution)/shard_map/ppermute | solution.py:20
  355.5 3.3 collective-permute-done.9
  358.8 1.8 collective-permute-done.5
  360.6 0.1 fusion.25
  360.7 0.9 pad_maximum_fusion
  (57 shorter events, 1.1 us)
Async XLA Ops:
  7.2 13.9 %copy-start = (bf16[8,512,256]{2,1,0:T(8,128)(2,1)S(1)}, bf16[8,512,256]{2,1,0:T(8,128)(2,1)}, u32[]{:S(2)}) copy-start(bf16[8,512,256]{2,1,0:T(8,128)(2,1)} %param.18) | copy-start | bytes 6291460
  7.2 145.5 %all-reduce.2.cloned.1.call-start = ((), (), s32[]{:S(2)}) async-start(), calls=%async_computation.1 | async-start | bytes 1310720 | tf_op jit(solution)/shard_map/psum | solution.py:282
  7.9 5.7 %copy-start.8 = (s32[64]{0:T(128)S(1)}, s32[64]{0:T(128)}, u32[]{:S(2)}) copy-start(s32[64]{0:T(128)} %param.16) | copy-start | bytes 772
  13.0 155.1 %collective-permute-start = (bf16[2560,512]{1,0:T(8,128)(2,1)}, bf16[2560,512]{1,0:T(8,128)(2,1)}, u32[]{:S(2)}, u32[]{:S(2)}) collective-permute-start(bf16[2560,512]{1,0:T(8,128)(2,1)} %shard_map.140), channel_id=1, source_target_pairs={{0,4},{4,0},{8,12},{12,8},{16,20},{20,16},{24,28},{28,24},{1,5},{5... | collective-permute-start | bytes 7864328 | tf_op jit(solution)/shard_map/ppermute | solution.py:20
  13.5 154.6 %collective-permute-start.1 = (bf16[512,1024]{1,0:T(8,128)(2,1)}, bf16[512,1024]{1,0:T(8,128)(2,1)}, u32[]{:S(2)}, u32[]{:S(2)}) collective-permute-start(bf16[512,1024]{1,0:T(8,128)(2,1)} %refs_2_.4), channel_id=1, source_target_pairs={{0,4},{4,0},{8,12},{12,8},{16,20},{20,16},{24,28},{28,24},{1,5},{5... | collective-permute-start | bytes 3145736 | tf_op jit(solution)/shard_map/ppermute | solution.py:20
  13.6 7.2 %copy-start.6 = (s32[8]{0:T(128)S(1)}, s32[8]{0:T(128)}, u32[]{:S(2)}) copy-start(s32[8]{0:T(128)} %param.23) | copy-start | bytes 100
  13.6 7.3 %copy-start.9 = (f32[2]{0:T(128)S(1)}, f32[2]{0:T(128)}, u32[]{:S(2)}) copy-start(f32[2]{0:T(128)} %param.22) | copy-start | bytes 28
  13.6 7.3 %copy-start.4 = (bf16[8,2048]{1,0:T(8,128)(2,1)S(1)}, bf16[8,2048]{1,0:T(8,128)(2,1)}, u32[]{:S(2)}) copy-start(bf16[8,2048]{1,0:T(8,128)(2,1)} %param.17) | copy-start | bytes 98308
  13.6 7.3 %copy-start.7 = (bf16[8,256]{1,0:T(8,128)(2,1)S(1)}, bf16[8,256]{1,0:T(8,128)(2,1)}, u32[]{:S(2)}) copy-start(bf16[8,256]{1,0:T(8,128)(2,1)} %param.20) | copy-start | bytes 12292
  20.5 275.1 %reduce-scatter.2.cloned.1.call-start = ((), (), s32[]{:S(2)}) async-start(), calls=%async_computation.2 | async-start | bytes 270336 | tf_op jit(solution)/shard_map/reduce_scatter | solution.py:300
  157.1 3.1 copy-start.1
  168.1 127.5 %copy-start.5 = (bf16[8,256]{1,0:T(8,128)(2,1)S(1)}, bf16[8,256]{1,0:T(8,128)(2,1)}, u32[]{:S(2)}) copy-start(bf16[8,256]{1,0:T(8,128)(2,1)} %param.21) | copy-start | bytes 12292
  175.4 132.1 %collective-permute-start.10 = (bf16[1280,256]{1,0:T(8,128)(2,1)}, bf16[1280,256]{1,0:T(8,128)(2,1)}, u32[]{:S(2)}, u32[]{:S(2)}) collective-permute-start(bf16[1280,256]{1,0:T(8,128)(2,1)} %get-tuple-element.14), channel_id=1, source_target_pairs={{0,1},{1,0},{2,3},{3,2},{4,5},{5,4},{6,7},{7,6},{8,9},{9,8},{10,11... | collective-permute-start | bytes 1966088 | tf_op jit(solution)/shard_map/ppermute | solution.py:20
  299.6 19.1 %collective-permute-start.6 = (bf16[1280,384]{1,0:T(8,128)(2,1)}, bf16[1280,384]{1,0:T(8,128)(2,1)S(1)}, u32[]{:S(2)}, u32[]{:S(2)}) collective-permute-start(bf16[1280,384]{1,0:T(8,128)(2,1)} %get-tuple-element.12), channel_id=1, source_target_pairs={{0,16},{4,20},{8,24},{12,28},{16,0},{20,4},{24,8},{28,12},{1,17},{... | collective-permute-start | bytes 2949128 | tf_op jit(solution)/shard_map/ppermute | solution.py:20
  299.7 33.2 %collective-permute-start.2 = (bf16[1280,384]{1,0:T(8,128)(2,1)}, bf16[1280,384]{1,0:T(8,128)(2,1)S(1)}, u32[]{:S(2)}, u32[]{:S(2)}) collective-permute-start(bf16[1280,384]{1,0:T(8,128)(2,1)} %get-tuple-element.10), channel_id=1, source_target_pairs={{0,8},{4,12},{8,0},{12,4},{16,24},{20,28},{24,16},{28,20},{1,9},{5... | collective-permute-start | bytes 2949128 | tf_op jit(solution)/shard_map/ppermute | solution.py:20
  309.1 9.7 %copy-start.3 = (f32[1280,384]{1,0:T(8,128)S(1)}, f32[1280,384]{1,0:T(8,128)}, u32[]{:S(2)}) copy-start(f32[1280,384]{1,0:T(8,128)} %get-tuple-element.11) | copy-start | bytes 5898244
  309.1 22.0 %collective-permute-start.11 = (bf16[640,256]{1,0:T(8,128)(2,1)S(1)}, bf16[640,256]{1,0:T(8,128)(2,1)S(1)}, u32[]{:S(2)}, u32[]{:S(2)}) collective-permute-start(bf16[640,256]{1,0:T(8,128)(2,1)S(1)} %slice.178), channel_id=1, source_target_pairs={{0,8},{4,12},{8,0},{12,4},{16,24},{20,28},{24,16},{28,20},{1,9},{5... | collective-permute-start | bytes 983048 | tf_op jit(solution)/shard_map/ppermute | solution.py:20
  319.0 13.9 %copy-start.2 = (f32[1280,384]{1,0:T(8,128)S(1)}, f32[1280,384]{1,0:T(8,128)}, u32[]{:S(2)}) copy-start(f32[1280,384]{1,0:T(8,128)} %get-tuple-element.9) | copy-start | bytes 5898244
  319.1 18.6 %collective-permute-start.7 = (bf16[640,384]{1,0:T(8,128)(2,1)S(1)}, bf16[640,384]{1,0:T(8,128)(2,1)S(1)}, u32[]{:S(2)}, u32[]{:S(2)}) collective-permute-start(bf16[640,384]{1,0:T(8,128)(2,1)S(1)} %slice.176), channel_id=1, source_target_pairs={{0,8},{4,12},{8,0},{12,4},{16,24},{20,28},{24,16},{28,20},{1,9},{5... | collective-permute-start | bytes 1474568 | tf_op jit(solution)/shard_map/ppermute | solution.py:20
  331.2 5.4 %collective-permute-start.12 = (bf16[320,256]{1,0:T(8,128)(2,1)S(1)}, bf16[320,256]{1,0:T(8,128)(2,1)S(1)}, u32[]{:S(2)}, u32[]{:S(2)}) collective-permute-start(bf16[320,256]{1,0:T(8,128)(2,1)S(1)} %slice.179), channel_id=1, source_target_pairs={{0,16},{4,20},{8,24},{12,28},{16,0},{20,4},{24,8},{28,12},{1,17},{... | collective-permute-start | bytes 491528 | tf_op jit(solution)/shard_map/ppermute | solution.py:20
  333.2 8.9 %collective-permute-start.3 = (bf16[640,384]{1,0:T(8,128)(2,1)S(1)}, bf16[640,384]{1,0:T(8,128)(2,1)S(1)}, u32[]{:S(2)}, u32[]{:S(2)}) collective-permute-start(bf16[640,384]{1,0:T(8,128)(2,1)S(1)} %slice.177), channel_id=1, source_target_pairs={{0,16},{4,20},{8,24},{12,28},{16,0},{20,4},{24,8},{28,12},{1,17},{... | collective-permute-start | bytes 1474568 | tf_op jit(solution)/shard_map/ppermute | solution.py:20
  336.7 18.8 %collective-permute-start.13 = (bf16[160,256]{1,0:T(8,128)(2,1)S(1)}, bf16[160,256]{1,0:T(8,128)(2,1)S(1)}, u32[]{:S(2)}, u32[]{:S(2)}) collective-permute-start(bf16[160,256]{1,0:T(8,128)(2,1)S(1)} %slice.182), channel_id=1, source_target_pairs={{0,2},{1,3},{2,0},{3,1},{4,6},{5,7},{6,4},{7,5},{8,10},{9,11},{10,... | collective-permute-start | bytes 245768 | tf_op jit(solution)/shard_map/ppermute | solution.py:20
  337.9 9.2 %collective-permute-start.8 = (bf16[320,384]{1,0:T(8,128)(2,1)S(1)}, bf16[320,384]{1,0:T(8,128)(2,1)S(1)}, u32[]{:S(2)}, u32[]{:S(2)}) collective-permute-start(bf16[320,384]{1,0:T(8,128)(2,1)S(1)} %pad_maximum_fusion.2), channel_id=1, source_target_pairs={{0,1},{1,0},{2,3},{3,2},{4,5},{5,4},{6,7},{7,6},{8,9},{9,8},{10,11... | collective-permute-start | bytes 737288 | tf_op jit(solution)/shard_map/ppermute | solution.py:20
  342.3 8.8 %collective-permute-start.4 = (bf16[320,384]{1,0:T(8,128)(2,1)S(1)}, bf16[320,384]{1,0:T(8,128)(2,1)S(1)}, u32[]{:S(2)}, u32[]{:S(2)}) collective-permute-start(bf16[320,384]{1,0:T(8,128)(2,1)S(1)} %pad_maximum_fusion.1), channel_id=1, source_target_pairs={{0,1},{1,0},{2,3},{3,2},{4,5},{5,4},{6,7},{7,6},{8,9},{9,8},{10,11... | collective-permute-start | bytes 737288 | tf_op jit(solution)/shard_map/ppermute | solution.py:20
  347.2 11.6 %collective-permute-start.9 = (bf16[160,384]{1,0:T(8,128)(2,1)S(1)}, bf16[160,384]{1,0:T(8,128)(2,1)S(1)}, u32[]{:S(2)}, u32[]{:S(2)}) collective-permute-start(bf16[160,384]{1,0:T(8,128)(2,1)S(1)} %slice.180), channel_id=1, source_target_pairs={{0,2},{1,3},{2,0},{3,1},{4,6},{5,7},{6,4},{7,5},{8,10},{9,11},{10,... | collective-permute-start | bytes 368648 | tf_op jit(solution)/shard_map/ppermute | solution.py:20
  351.2 9.5 %collective-permute-start.5 = (bf16[160,384]{1,0:T(8,128)(2,1)S(1)}, bf16[160,384]{1,0:T(8,128)(2,1)S(1)}, u32[]{:S(2)}, u32[]{:S(2)}) collective-permute-start(bf16[160,384]{1,0:T(8,128)(2,1)S(1)} %slice.181), channel_id=1, source_target_pairs={{0,2},{1,3},{2,0},{3,1},{4,6},{5,7},{6,4},{7,5},{8,10},{9,11},{10,... | collective-permute-start | bytes 368648 | tf_op jit(solution)/shard_map/ppermute | solution.py:20
Sparse Core Ops, SparseCore 0:
  20.6 132.0 all-reduce.1
  162.3 133.2 reduce-scatter.1

commit v3 on v2

--- a/solution.py
+++ b/solution.py
@@ -21,11 +21,18 @@
 
 
 def transpose_block(units, order, block, out):
-    flipped = block[...].T
-    rows = flipped.shape[0] // units
-    for unit in range(units):
-        place = pl.multiple_of(order[pl.num_programs(0) + unit] * rows, rows)
-        out[pl.ds(place, rows), :] = flipped[unit * rows : (unit + 1) * rows]
+    width = block.shape[1]
+    rows = width // units
+    for low in range(0, width, LANES):
+        flipped = block[:, low : low + LANES].T
+        edge = low
+        while edge < low + LANES:
+            unit = edge // rows
+            end = min(low + LANES, (unit + 1) * rows)
+            place = order[pl.num_programs(0) + unit] * rows + (edge - unit * rows)
+            place = pl.multiple_of(place, 32)
+            out[pl.ds(place, end - edge), :] = flipped[edge - low : end - low]
+            edge = end
 
 
 def pack(activations, blocks, units, width):
@@ -67,16 +74,23 @@
     return runs
 
 
-def multiply(wanted, rows, blocks, *refs):
+def multiply(wanted, rows, blocks, base, *refs):
     count = len(wanted)
     sources = refs[:4]
     outs = refs[4 : 4 + count]
     near, far, near_grad, far_grad, sems = refs[4 + count :]
     per_block = near.shape[0] // blocks
+    units_block = per_block // rows
+    needed = [
+        block
+        for block in range(blocks)
+        if any(unit // units_block == block for item in wanted for unit in item[0])
+    ]
+    columns = pl.ds(base, near_grad.shape[1])
     copies = {}
     for at, (source, target) in enumerate(((sources[2], near_grad), (sources[3], far_grad))):
-        copies["grad", at] = pltpu.make_async_copy(source, target, sems.at[at])
-    for block in range(blocks):
+        copies["grad", at] = pltpu.make_async_copy(source.at[:, columns], target, sems.at[at])
+    for block in needed:
         span = pl.ds(block * per_block, per_block)
         for at, (source, target) in enumerate(((sources[0], near), (sources[1], far))):
             copies[block, at] = pltpu.make_async_copy(
@@ -86,8 +100,7 @@
         copy.start()
     for at in range(2):
         copies["grad", at].wait()
-    units_block = per_block // rows
-    for block in range(blocks):
+    for block in needed:
         for at in range(2):
             copies[block, at].wait()
         for (units, first, last, _), out in zip(wanted, outs):
@@ -95,14 +108,16 @@
             for low, high in runs_of(here):
                 span = slice(low * rows, high * rows)
                 place = units.index(low) * rows
-                product = dot32(near[span, :], near_grad[:, first:last])
-                product += dot32(far[span, :], far_grad[:, first:last])
+                cut = slice(first - base, last - base)
+                product = dot32(near[span, :], near_grad[:, cut])
+                product += dot32(far[span, :], far_grad[:, cut])
                 out[place : place + (high - low) * rows, :] = product.astype(out.dtype)
 
 
 def products(lefts, grads, wanted, rows, blocks):
     total, tokens = lefts[0].shape
-    columns = grads[0].shape[1]
+    base = min(first for _, first, _, _ in wanted)
+    columns = max(last for _, _, last, _ in wanted) - base
     if rows % 32 or any((first | last) % LANES for _, first, last, _ in wanted):
         return [
             jnp.concatenate(
@@ -122,7 +137,7 @@
     ]
     work = sum(shape.size for shape in shapes)
     return pl.pallas_call(
-        functools.partial(multiply, wanted, rows, blocks),
+        functools.partial(multiply, wanted, rows, blocks, base),
         out_shape=shapes,
         in_specs=[pl.BlockSpec(memory_space=pl.ANY)] * 4,
         out_specs=[pl.BlockSpec(memory_space=pltpu.VMEM)] * len(shapes),
@@ -178,6 +193,60 @@
             flops=0, bytes_accessed=2 * count * SLAB * width, transcendentals=0
         ),
     )(place.astype(jnp.int32), *([embed_table] * SLAB))
+
+
+def spread(blocks, units, folds, order, found, out, flipped):
+    width = flipped.shape[0]
+    rows = width // units
+    lines = rows // folds
+    for block in range(blocks):
+        start = pl.multiple_of(order[block] * width, LANES)
+        flipped[...] = found[:, pl.ds(start, width)].astype(jnp.float32).T
+        for unit in range(units):
+            from_row = order[blocks + unit] * rows
+            pieces = [
+                flipped[pl.ds(pl.multiple_of(from_row + fold * lines, 8), lines), :]
+                for fold in range(folds)
+            ]
+            place = (block * units + unit) * lines
+            out[place : place + lines, :] = jnp.concatenate(pieces, axis=1)
+
+
+def arrange(found, blocks, units, width, lanes):
+    tokens = found.shape[0]
+    rows = width // len(units)
+    folds = lanes // tokens
+    lines = rows // folds
+    if width % LANES or lines % 8:
+        flipped = found.T
+        parts = [
+            lax.dynamic_slice_in_dim(flipped, block * width + unit * rows, rows, 0)
+            for block in blocks
+            for unit in units
+        ]
+        return jnp.concatenate(
+            [
+                jnp.concatenate(
+                    [part[fold * lines : (fold + 1) * lines] for fold in range(folds)], axis=1
+                )
+                for part in parts
+            ]
+        )
+    shape = jax.ShapeDtypeStruct((len(blocks) * len(units) * lines, lanes), jnp.float32)
+    return pl.pallas_call(
+        functools.partial(spread, len(blocks), len(units), folds),
+        in_specs=[
+            pl.BlockSpec(memory_space=pltpu.SMEM),
+            pl.BlockSpec(memory_space=pltpu.VMEM),
+        ],
+        out_specs=pl.BlockSpec(memory_space=pltpu.VMEM),
+        out_shape=shape,
+        scratch_shapes=[pltpu.VMEM((width, tokens), jnp.float32)],
+        compiler_params=pltpu.CompilerParams(vmem_limit_bytes=32 << 20),
+        cost_estimate=pl.CostEstimate(
+            flops=0, bytes_accessed=2 * found.size + 4 * shape.size, transcendentals=0
+        ),
+    )(jnp.stack(list(blocks) + list(units)).astype(jnp.int32), found).astype(found.dtype)
 
 
 def dot32(left, right):
@@ -224,15 +293,28 @@
     staying = pack(activations, [((r ^ upper) << 1) | core for r in arranged], units_tp, block)
     lefts = [staying, incoming]
 
+    tokens_new = token_ids.shape[0]
+    flat = f * count_tp + t
+    quarter = columns // 4
+    eighth = columns // 8
+    folds = quarter // tokens_new
+    found = lookup(embed_table, token_ids, flat * embed_table.shape[0])
+    theirs = arrange(found, [((r ^ upper) << 1) | (1 - core) for r in arranged], units_tp, block, quarter)
+    ours = arrange(found, [((r ^ upper) << 1) | core for r in arranged], units_tp, block, quarter)
+    asked = ours + exchange(theirs, "fsdp", 1)
+    lines = rows // folds
+
     places = [(r, unit) for r in arranged for unit in range(count_tp)]
     steps_upper = [("fsdp", bit) for bit in range(upper_bits)]
     steps_tp = [("tp", bit) for bit in range(count_tp.bit_length() - 1)]
-    wide = columns * 3 // 8
-    orders = [
-        (0, wide, steps_upper + steps_tp),
-        (wide, 2 * wide, steps_upper[::-1] + steps_tp),
-        (2 * wide, columns, steps_tp[:1] + steps_upper + steps_tp[1:]),
-    ]
+    one, two, three = (
+        steps_upper + steps_tp,
+        steps_upper[::-1] + steps_tp,
+        steps_tp + steps_upper,
+    )
+    edges = [0, quarter, 2 * quarter, 3 * quarter, 3 * quarter + eighth, columns]
+    spans = list(zip(edges[:-1], edges[1:]))
+    orders = [one, two, three, one, two]
 
     def has(place, step):
         return (place[step[0] == "tp"] >> step[1]) & 1
@@ -244,66 +326,94 @@
     def split(held, step):
         return [p for p in held if has(p, step)], [p for p in held if not has(p, step)]
 
-    wanted_sent, wanted_kept, kept = [], [], []
-    for first, last, steps in orders:
-        go, stay = split(places, steps[0])
-        kept.append(stay)
-        wanted_sent.append(([places.index(p) for p in go], first, last, jnp.bfloat16))
-        wanted_kept.append(([places.index(p) for p in stay], first, last, jnp.float32))
-    sending = products(lefts, grads, wanted_sent, rows, uppers)
-
-    def take(value, held, chosen):
+    def take(value, held, chosen, size):
         runs = runs_of([held.index(p) for p in chosen])
-        return jnp.concatenate([value[low * rows : high * rows] for low, high in runs])
+        return jnp.concatenate([value[low * size : high * size] for low, high in runs])
 
     def send(value, step):
         mask = 1 << step[1]
         return exchange(value, step[0], 2 * mask if step[0] == "fsdp" else mask)
 
-    first_got = [send(value, order[2][0]) for value, order in zip(sending, orders)]
-    values = products(lefts, grads, wanted_kept, rows, uppers)
-    finished = []
-    for value, got, held, (first, last, steps) in zip(values, first_got, kept, orders):
-        for at, step in enumerate(steps):
-            if at:
-                go, held = split(held, step)
-                got = send(take(value, whole, go).astype(jnp.bfloat16), step)
-                value = take(value, whole, held)
-            else:
-                go = split(places, step)[0]
-            whole = held
-            value = value + take(got, [flip(p, step) for p in go], held).astype(jnp.float32)
-        finished.append(value)
+    def compute(which, sent):
+        wanted = []
+        for index in which:
+            chosen = split(places, orders[index][0])[0 if sent else 1]
+            units = [places.index(p) for p in chosen]
+            kind = jnp.bfloat16 if sent else jnp.float32
+            wanted.append((units, *spans[index], kind))
+        return dict(zip(which, products(lefts, grads, wanted, rows, uppers)))
+
+    going = compute([0, 1], True)
+    going |= compute([2, 3, 4], True)
+    go, stay = split(places, three[0])
+    going[2] = jnp.concatenate([going[2], take(asked, places, go, lines)])
+    got = {index: send(value, orders[index][0]) for index, value in going.items()}
+    values = {index: [value] for index, value in compute(list(range(5)), False).items()}
+    values[2].append(take(asked, places, stay, lines).astype(jnp.float32))
+    sizes = {index: [rows] for index in range(5)}
+    sizes[2].append(lines)
+    held = {index: places for index in range(5)}
+    token = going[4]
+
+    def receive(index, step):
+        gone, kept = split(held[index], step)
+        landed = [flip(p, step) for p in gone]
+        start = 0
+        added = []
+        for value, size in zip(values[index], sizes[index]):
+            piece = got[index][start : start + len(gone) * size]
+            start += len(gone) * size
+            added.append(value + take(piece, landed, kept, size).astype(jnp.float32))
+        values[index], held[index] = added, kept
+
+    for at in range(len(one)):
+        for group in ((0, 1), (2,), (3, 4)) if at == 0 else ((0, 1), (3, 4), (2,)):
+            tied = lax.optimization_barrier([got[index] for index in group] + [token])
+            for index, arrived in zip(group, tied):
+                got[index] = arrived
+                receive(index, orders[index][at])
+            if at + 1 == len(one):
+                continue
+            outgoing = []
+            for index in group:
+                gone, kept = split(held[index], orders[index][at + 1])
+                pieces = [
+                    take(value, held[index], gone, size).astype(jnp.bfloat16)
+                    for value, size in zip(values[index], sizes[index])
+                ]
+                values[index] = [
+                    take(value, held[index], kept, size)
+                    for value, size in zip(values[index], sizes[index])
+                ]
+                outgoing.append(jnp.concatenate(pieces))
+            outgoing = lax.optimization_barrier(outgoing)
+            token = outgoing[-1]
+            for index, value in zip(group, outgoing):
+                got[index] = send(value, orders[index][at + 1])
     w_next = jnp.concatenate(
-        [master_w[:, o[0] : o[1]] - coef * value for o, value in zip(orders, finished)], axis=1
-    )
-
-    flat = f * count_tp + t
-    embedded = lax.psum(
-        lookup(embed_table, token_ids, flat * embed_table.shape[0]), ("fsdp", "tp")
-    )
-
-    through = lax.dot_general(
-        embedded, activations, (((1,), (1,)), ((), ())), preferred_element_type=jnp.float32
-    )
-    high = through.astype(jnp.bfloat16)
-    low = (through - high.astype(jnp.float32)).astype(jnp.bfloat16)
-    own_columns = lax.dynamic_slice_in_dim(embedded, flat * rows, rows, 1).astype(jnp.float32)
-    share_own = jnp.dot(
-        own_columns,
-        master_w,
+        [master_w[:, low:high] - coef * values[at][0] for at, (low, high) in enumerate(spans)],
+        axis=1,
+    )
+
+    flat_rows = values[2][1].astype(jnp.bfloat16)
+    columns_own = jnp.concatenate(
+        [flat_rows[:, fold * tokens_new : (fold + 1) * tokens_new] for fold in range(folds)]
+    )
+    share_own = lax.dot_general(
+        columns_own,
+        w_next.astype(jnp.bfloat16),
+        (((0,), (0,)), ((), ())),
         preferred_element_type=jnp.float32,
-        precision=lax.Precision.HIGHEST,
-    ) - coef * (dot32(high, grad_out) + dot32(low, grad_out))
-    rows_f = token_ids.shape[0] // count_fsdp
+    )
+    rows_f = tokens_new // count_fsdp
     col_width = columns // count_tp
-    own_value = lax.psum_scatter(
+    blocks_own = (
         share_own.reshape(count_fsdp, rows_f, count_tp, col_width)
         .transpose(0, 2, 1, 3)
-        .reshape(devices_all * rows_f, col_width),
-        ("fsdp", "tp"),
-        scatter_dimension=0,
-        tiled=True,
+        .reshape(devices_all, rows_f, col_width)
+    )
+    own_value = jnp.sum(
+        lax.all_to_all(blocks_own, ("fsdp", "tp"), split_axis=0, concat_axis=0), axis=0
     )
 
     share = jnp.repeat(residual_mix, HD)[None, :]

time: 369 us -> 116 us (0.31)
  waiting for transfers between devices: 288 us -> 30.4 us
  starting transfers between devices: 13.8 us -> 31.3 us
  between operations: 14.4 us -> 1.44 us
  matrix products: 12.4 us -> 3.82 us
  Pallas kernels: 32.1 us -> 38.1 us
    psum x1 -> x0, waiting for transfers between devices: 131 us -> none  [per_device(): lax.psum(lookup(embed_table, token_ids, flat * embed_table.shape[0]), ('f...]
    reduce_scatter x1 -> x0, waiting for transfers between devices: 119 us -> none  [per_device(): lax.psum_scatter(share_own.reshape(count_fsdp, rows_f, count_tp, col_widt...]
    ppermute x14 -> x23, waiting for transfers between devices: 38.5 us -> 20.5 us  [exchange(): lax.ppermute(value, axis, [(i, i ^ mask) for i in range(lax.axis_size(axi...]
    ppermute x14 -> x23, starting transfers between devices: 13.6 us -> 28.6 us  [exchange(): lax.ppermute(value, axis, [(i, i ^ mask) for i in range(lax.axis_size(axi...]
    all_to_all x0 -> x1, waiting for transfers between devices: none -> 9.9 us  [per_device(): lax.all_to_all(blocks_own, ('fsdp', 'tp'), split_axis=0, concat_axis=0)]
    dot_general x4 -> x1, matrix products: 9.45 us -> 0.92 us  [per_device(): lax.dot_general(columns_own, w_next.astype(jnp.bfloat16), (((0,), (0,)),...]
    pallas_call x2 -> x5, Pallas kernels: 15 us -> 21 us  [the longest x3 19 us: products(): pl.pallas_call(functools.partial(multiply, wanted, rows, blocks, base), o...]
  transfers between devices with their start and end apart: 16 -> 24, of which waited for: 10 -> 11; matrix products, arithmetic and copies ran while one was open for 5% -> 6% of each run, Pallas kernels for 7% -> 24%
where the time goes in v3:
time: 116 us; the launch traced here: 115 us
  Pallas kernels  38.1 us (33%)
  starting transfers between devices  31.3 us (27%)
  waiting for transfers between devices  30.4 us (26%)
  local copies, waits for them, and re-layouts  5.82 us (5%)
  other arithmetic  4.57 us (4%)
  matrix products  3.82 us (3%)
  between operations  1.44 us (1%)
    ppermute x23, starting transfers between devices, exchange(): lax.ppermute(value, axis, [(i, i ^ mask) for i in range(lax.axis_size(axi...  28.6 us
    ppermute x23, waiting for transfers between devices, exchange(): lax.ppermute(value, axis, [(i, i ^ mask) for i in range(lax.axis_size(axi...  20.5 us
    pallas_call x3, Pallas kernels, products(): pl.pallas_call(functools.partial(multiply, wanted, rows, blocks, base), o...  19 us
    pallas_call x2, Pallas kernels, pack(): pl.pallas_call(functools.partial(transpose_block, len(units)), grid_spec=...  10.4 us
    all_to_all x1, waiting for transfers between devices, per_device(): lax.all_to_all(blocks_own, ('fsdp', 'tp'), split_axis=0, concat_axis=0)  9.9 us
    pallas_call x1, Pallas kernels, lookup(): pl.pallas_call(pick_rows, grid_spec=pltpu.PrefetchScalarGridSpec(num_scal...  6.68 us
    unnamed x46, local copies, waits for them, and re-layouts  3.99 us
    all_to_all x1, starting transfers between devices, per_device(): lax.all_to_all(blocks_own, ('fsdp', 'tp'), split_axis=0, concat_axis=0)  2.73 us
  transfers between devices with their start and end apart: 24, of which 11 were waited for; matrix products, arithmetic and copies ran while one was open for 6% of the time, Pallas kernels for 24%

profile of v3, /device:TPU:0, one launch (start us, length us, event | category | flops | bytes accessed | tf_op | source)
XLA Modules:
  0.0 115.5 jit_solution(2732624537245816976)
XLA Ops:
  0.7 0.6 stack.77.order
  1.3 5.2 %shard_map.140 = bf16[2560,512]{1,0:T(8,128)(2,1)} custom-call(s32[8]{0:T(128)} %stack.77.order, bf16[512,5120]{1,0:T(8,128)(2,1)} %block.3), custom_call_target="tpu_custom_call" | custom-call | bytes 5242880 | tf_op jit(solution)/shard_map/pallas_call | solution.py:51
  6.9 6.7 %shard_map.144.found = bf16[64,5120]{1,0:T(8,128)(2,1)S(1)} custom-call(s32[64]{0:T(128)S(1)} %and_select_fusion.place, bf16[4748,5120]{1,0:T(8,128)(2,1)} %refs_15_.1, bf16[4748,5120]{1,0:T(8,128)(2,1)} %refs_15_.1, bf16[4748,5120]{1,0:T(8,128)(2,1)} %refs_15_.1, bf16[4748,5120]{1,0:T(8,128)(2,1)} %refs_15_.1, bf16[4748,5120]{1,0:T(8,128)(2,1)} %refs_15_.1, ...), custom_call_target="tpu_custom_call" | custom-call | bytes 10485760 | tf_op jit(solution)/shard_map/pallas_call | solution.py:181
  13.7 1.0 shard_map.146
  14.7 0.8 convert_element_type.139
  15.9 0.7 fusion.77
  16.8 0.6 stack.72.order
  17.4 5.2 %shard_map.139.refs_0_ = bf16[2560,512]{1,0:T(8,128)(2,1)} custom-call(s32[8]{0:T(128)} %stack.72.order, bf16[512,5120]{1,0:T(8,128)(2,1)} %block.3), custom_call_target="tpu_custom_call" | custom-call | bytes 5242880 | tf_op jit(solution)/shard_map/pallas_call | solution.py:51
  22.6 1.0 shard_map.145
  23.7 5.0 %shard_map.142 = (bf16[1280,256]{1,0:T(8,128)(2,1)}, bf16[1280,256]{1,0:T(8,128)(2,1)}) custom-call(bf16[2560,512]{1,0:T(8,128)(2,1)} %shard_map.139.refs_0_, bf16[2560,512]{1,0:T(8,128)(2,1)} %collective-permute-done.refs_1_, bf16[512,1024]{1,0:T(8,128)(2,1)} %refs_2_.6, bf16[512,1024]{1,0:T(8,128)(2,1)} %collective-permute-done.1.refs_3_), custom_call_target="tpu_custom_call" | custom-call | flops 1342177280 | bytes 8912896 | tf_op jit(solution)/shard_map/pallas_call | solution.py:139
  28.8 2.8 %collective-permute-start.2 = (bf16[1280,256]{1,0:T(8,128)(2,1)}, bf16[1280,256]{1,0:T(8,128)(2,1)S(1)}, u32[]{:S(2)}, u32[]{:S(2)}) collective-permute-start(bf16[1280,256]{1,0:T(8,128)(2,1)} %get-tuple-element.46), channel_id=1, source_target_pairs={{0,8},{4,12},{8,0},{12,4},{16,24},{20,28},{24,16},{28,20},{1,9},{5... | collective-permute-start | bytes 1966088 | tf_op jit(solution)/shard_map/ppermute | solution.py:20
  31.6 1.8 %collective-permute-start.3 = (bf16[1280,256]{1,0:T(8,128)(2,1)}, bf16[1280,256]{1,0:T(8,128)(2,1)S(1)}, u32[]{:S(2)}, u32[]{:S(2)}) collective-permute-start(bf16[1280,256]{1,0:T(8,128)(2,1)} %get-tuple-element.47), channel_id=1, source_target_pairs={{0,16},{4,20},{8,24},{12,28},{16,0},{20,4},{24,8},{28,12},{1,17},{... | collective-permute-start | bytes 1966088 | tf_op jit(solution)/shard_map/ppermute | solution.py:20
  33.4 5.9 %shard_map.143 = (bf16[1280,256]{1,0:T(8,128)(2,1)}, bf16[1280,128]{1,0:T(8,128)(2,1)}, bf16[1280,128]{1,0:T(8,128)(2,1)}) custom-call(bf16[2560,512]{1,0:T(8,128)(2,1)} %shard_map.139.refs_0_, bf16[2560,512]{1,0:T(8,128)(2,1)} %collective-permute-done.refs_1_, bf16[512,1024]{1,0:T(8,128)(2,1)} %refs_2_.6, bf16[512,1024]{1,0:T(8,128)(2,1)} %collective-permute-done.1.refs_3_), custom_call_target="tpu_custom_call" | custom-call | flops 1342177280 | bytes 8912896 | tf_op jit(solution)/shard_map/pallas_call | solution.py:139
  39.2 0.6 collective-permute-start.6
  39.9 1.1 constant_dynamic-update-slice_fusion.8
  41.1 1.8 %collective-permute-start.9 = (bf16[1600,256]{1,0:T(8,128)(2,1)S(1)}, bf16[1600,256]{1,0:T(8,128)(2,1)S(1)}, u32[]{:S(2)}, u32[]{:S(2)}) collective-permute-start(bf16[1600,256]{1,0:T(8,128)(2,1)S(1)} %get-tuple-element.128), channel_id=1, source_target_pairs={{0,1},{1,0},{2,3},{3,2},{4,5},{5,4},{6,7},{7,6},{8,9},{9,8},{10,11... | collective-permute-start | bytes 2457608 | tf_op jit(solution)/shard_map/ppermute | solution.py:20
  42.9 8.1 %shard_map.141 = (f32[1280,256]{1,0:T(8,128)}, f32[1280,256]{1,0:T(8,128)}, f32[1280,256]{1,0:T(8,128)}, f32[1280,128]{1,0:T(8,128)}, f32[1280,128]{1,0:T(8,128)}) custom-call(bf16[2560,512]{1,0:T(8,128)(2,1)} %shard_map.139.refs_0_, bf16[2560,512]{1,0:T(8,128)(2,1)} %collective-permute-done.refs_1_, bf16[512,1024]{1,0:T(8,128)(2,1)} %refs_2_.6, ...), custom_call_target="tpu_custom_call" | custom-call | flops 2684354560 | bytes 12582912 | tf_op jit(solution)/shard_map/pallas_call | solution.py:139
  51.1 1.2 %copy-done.4 = f32[1280,256]{1,0:T(8,128)S(1)} copy-done((f32[1280,256]{1,0:T(8,128)S(1)}, f32[1280,256]{1,0:T(8,128)}, u32[]{:S(2)}) %copy-start.4) | copy-done | bytes 1310744
  52.3 1.6 %convert_add_fusion.1 = (f32[1280,256]{1,0:T(8,128)S(1)}, f32[1280,256]{1,0:T(8,128)S(1)}) fusion(f32[1280,256]{1,0:T(8,128)} %get-tuple-element.50, bf16[640,256]{1,0:T(8,128)(2,1)S(1)} %get-tuple-element.112, bf16[640,256]{1,0:T(8,128)(2,1)S(1)} %get-tuple-element.111, f32[1280,256]{1,0:T(8,128)S(1)} %copy-done.4, ...), kind=kLoop, calls=%fused_computation.7 | loop fusion | flops 2293760 | bytes 6553600 | tf_op jit(solution)/shard_map/add | solution.py:366
  54.0 1.7 %collective-permute-start.4 = (bf16[640,256]{1,0:T(8,128)(2,1)S(1)}, bf16[640,256]{1,0:T(8,128)(2,1)S(1)}, u32[]{:S(2)}, u32[]{:S(2)}) collective-permute-start(bf16[640,256]{1,0:T(8,128)(2,1)S(1)} %slice.580), channel_id=1, source_target_pairs={{0,16},{4,20},{8,24},{12,28},{16,0},{20,4},{24,8},{28,12},{1,17},{... | collective-permute-start | bytes 983048 | tf_op jit(solution)/shard_map/ppermute | solution.py:20
  55.7 1.6 %collective-permute-start.5 = (bf16[640,256]{1,0:T(8,128)(2,1)S(1)}, bf16[640,256]{1,0:T(8,128)(2,1)S(1)}, u32[]{:S(2)}, u32[]{:S(2)}) collective-permute-start(bf16[640,256]{1,0:T(8,128)(2,1)S(1)} %slice.579), channel_id=1, source_target_pairs={{0,8},{4,12},{8,0},{12,4},{16,24},{20,28},{24,16},{28,20},{1,9},{5... | collective-permute-start | bytes 983048 | tf_op jit(solution)/shard_map/ppermute | solution.py:20
  57.4 3.6 %collective-permute-done.9 = bf16[1600,256]{1,0:T(8,128)(2,1)S(1)} collective-permute-done((bf16[1600,256]{1,0:T(8,128)(2,1)S(1)}, bf16[1600,256]{1,0:T(8,128)(2,1)S(1)}, u32[]{:S(2)}, u32[]{:S(2)}) %collective-permute-start.9) | collective-permute-done | bytes 819232 | tf_op jit(solution)/shard_map/ppermute | solution.py:20
  61.4 2.7 %collective-permute-start.12 = (bf16[800,256]{1,0:T(8,128)(2,1)S(1)}, bf16[800,256]{1,0:T(8,128)(2,1)S(1)}, u32[]{:S(2)}, u32[]{:S(2)}) collective-permute-start(bf16[800,256]{1,0:T(8,128)(2,1)S(1)} %constant_dynamic-update-slice_fusion.17), channel_id=1, source_target_pairs={{0,2},{1,3},{2,0},{3,1},{4,6},{5,7},{6,4},{7,5},{8,10},{9,11},{10,... | collective-permute-start | bytes 1228808 | tf_op jit(solution)/shard_map/ppermute | solution.py:20
  64.3 1.6 %collective-permute-start.13 = (bf16[640,128]{1,0:T(8,128)(2,1)S(1)}, bf16[640,128]{1,0:T(8,128)(2,1)S(1)}, u32[]{:S(2)}, u32[]{:S(2)}) collective-permute-start(bf16[640,128]{1,0:T(8,128)(2,1)S(1)} %slice.583), channel_id=1, source_target_pairs={{0,16},{4,20},{8,24},{12,28},{16,0},{20,4},{24,8},{28,12},{1,17},{... | collective-permute-start | bytes 491528 | tf_op jit(solution)/shard_map/ppermute | solution.py:20
  65.9 1.7 %collective-permute-start.14 = (bf16[640,128]{1,0:T(8,128)(2,1)S(1)}, bf16[640,128]{1,0:T(8,128)(2,1)S(1)}, u32[]{:S(2)}, u32[]{:S(2)}) collective-permute-start(bf16[640,128]{1,0:T(8,128)(2,1)S(1)} %slice.582), channel_id=1, source_target_pairs={{0,8},{4,12},{8,0},{12,4},{16,24},{20,28},{24,16},{28,20},{1,9},{5... | collective-permute-start | bytes 491528 | tf_op jit(solution)/shard_map/ppermute | solution.py:20
  67.9 1.4 %collective-permute-start.10 = (bf16[320,256]{1,0:T(8,128)(2,1)S(1)}, bf16[320,256]{1,0:T(8,128)(2,1)S(1)}, u32[]{:S(2)}, u32[]{:S(2)}) collective-permute-start(bf16[320,256]{1,0:T(8,128)(2,1)S(1)} %pad_maximum_fusion.1), channel_id=1, source_target_pairs={{0,1},{1,0},{2,3},{3,2},{4,5},{5,4},{6,7},{7,6},{8,9},{9,8},{10,11... | collective-permute-start | bytes 491528 | tf_op jit(solution)/shard_map/ppermute | solution.py:20
  69.3 0.7 collective-permute-start.11
  70.1 1.2 %collective-permute-done.14 = bf16[640,128]{1,0:T(8,128)(2,1)S(1)} collective-permute-done((bf16[640,128]{1,0:T(8,128)(2,1)S(1)}, bf16[640,128]{1,0:T(8,128)(2,1)S(1)}, u32[]{:S(2)}, u32[]{:S(2)}) %collective-permute-start.14) | collective-permute-done | bytes 163872 | tf_op jit(solution)/shard_map/ppermute | solution.py:20
  71.4 1.6 %collective-permute-start.18 = (bf16[320,128]{1,0:T(8,128)(2,1)S(1)}, bf16[320,128]{1,0:T(8,128)(2,1)S(1)}, u32[]{:S(2)}, u32[]{:S(2)}) collective-permute-start(bf16[320,128]{1,0:T(8,128)(2,1)S(1)} %pad_maximum_fusion.4), channel_id=1, source_target_pairs={{0,1},{1,0},{2,3},{3,2},{4,5},{5,4},{6,7},{7,6},{8,9},{9,8},{10,11... | collective-permute-start | bytes 245768 | tf_op jit(solution)/shard_map/ppermute | solution.py:20
  73.0 0.5 collective-permute-start.19
  73.6 7.8 %collective-permute-done.12 = bf16[800,256]{1,0:T(8,128)(2,1)S(1)} collective-permute-done((bf16[800,256]{1,0:T(8,128)(2,1)S(1)}, bf16[800,256]{1,0:T(8,128)(2,1)S(1)}, u32[]{:S(2)}, u32[]{:S(2)}) %collective-permute-start.12) | collective-permute-done | bytes 409632 | tf_op jit(solution)/shard_map/ppermute | solution.py:20
  81.5 1.3 %collective-permute-start.17 = (bf16[400,256]{1,0:T(8,128)(2,1)S(1)}, bf16[400,256]{1,0:T(8,128)(2,1)S(1)}, u32[]{:S(2)}, u32[]{:S(2)}) collective-permute-start(bf16[400,256]{1,0:T(8,128)(2,1)S(1)} %pad_maximum_fusion), channel_id=1, source_target_pairs={{0,8},{4,12},{8,0},{12,4},{16,24},{20,28},{24,16},{28,20},{1,9},{5... | collective-permute-start | bytes 614408 | tf_op jit(solution)/shard_map/ppermute | solution.py:20
  82.9 2.1 %collective-permute-done.11 = bf16[320,256]{1,0:T(8,128)(2,1)S(1)} collective-permute-done((bf16[320,256]{1,0:T(8,128)(2,1)S(1)}, bf16[320,256]{1,0:T(8,128)(2,1)S(1)}, u32[]{:S(2)}, u32[]{:S(2)}) %collective-permute-start.11) | collective-permute-done | bytes 163872 | tf_op jit(solution)/shard_map/ppermute | solution.py:20
  85.1 0.8 collective-permute-start.15
  85.9 2.2 %collective-permute-start.16 = (bf16[160,256]{1,0:T(8,128)(2,1)S(1)}, bf16[160,256]{1,0:T(8,128)(2,1)S(1)}, u32[]{:S(2)}, u32[]{:S(2)}) collective-permute-start(bf16[160,256]{1,0:T(8,128)(2,1)S(1)} %slice.585), channel_id=1, source_target_pairs={{0,2},{1,3},{2,0},{3,1},{4,6},{5,7},{6,4},{7,5},{8,10},{9,11},{10,... | collective-permute-start | bytes 245768 | tf_op jit(solution)/shard_map/ppermute | solution.py:20
  88.1 1.3 %collective-permute-done.19 = bf16[320,128]{1,0:T(8,128)(2,1)S(1)} collective-permute-done((bf16[320,128]{1,0:T(8,128)(2,1)S(1)}, bf16[320,128]{1,0:T(8,128)(2,1)S(1)}, u32[]{:S(2)}, u32[]{:S(2)}) %collective-permute-start.19) | collective-permute-done | bytes 81952 | tf_op jit(solution)/shard_map/ppermute | solution.py:20
  89.5 2.9 %collective-permute-start.22 = (bf16[160,128]{1,0:T(8,128)(2,1)S(1)}, bf16[160,128]{1,0:T(8,128)(2,1)S(1)}, u32[]{:S(2)}, u32[]{:S(2)}) collective-permute-start(bf16[160,128]{1,0:T(8,128)(2,1)S(1)} %slice.587), channel_id=1, source_target_pairs={{0,2},{1,3},{2,0},{3,1},{4,6},{5,7},{6,4},{7,5},{8,10},{9,11},{10,... | collective-permute-start | bytes 122888 | tf_op jit(solution)/shard_map/ppermute | solution.py:20
  92.6 1.6 %collective-permute-done.15 = bf16[160,256]{1,0:T(8,128)(2,1)S(1)} collective-permute-done((bf16[160,256]{1,0:T(8,128)(2,1)S(1)}, bf16[160,256]{1,0:T(8,128)(2,1)S(1)}, u32[]{:S(2)}, u32[]{:S(2)}) %collective-permute-start.15) | collective-permute-done | bytes 81952 | tf_op jit(solution)/shard_map/ppermute | solution.py:20
  94.2 0.9 collective-permute-done.16
  95.2 0.8 collective-permute-done.21
  96.4 0.9 collective-permute-done.20
  97.5 0.8 copy-done.5
  98.3 0.9 fusion.21
  99.2 2.7 %all-to-all-start = ((f32[32,8,256]{2,1,0:T(8,128)}), f32[32,8,256]{2,1,0:T(8,128)S(1)}, u32[]{:S(2)}, u32[]{:S(2)}) async-start(f32[32,8,256]{2,1,0:T(8,128)} %bitcast.15), calls=%async_computation | async-start | bytes 524288 | tf_op jit(solution)/shard_map/all_to_all | solution.py:416
  102.2 9.9 %all-to-all-done = f32[32,8,256]{2,1,0:T(8,128)S(1)} async-done(((f32[32,8,256]{2,1,0:T(8,128)}), f32[32,8,256]{2,1,0:T(8,128)S(1)}, u32[]{:S(2)}, u32[]{:S(2)}) %all-to-all-start) | async-done | bytes 262176 | tf_op jit(solution)/shard_map/all_to_all | solution.py:416
  112.2 0.6 bitcast_convert_fusion
  112.8 2.0 %fusion.18 = bf16[1,8,16,128]{3,2,1,0:T(8,128)(2,1)S(1)} fusion(f32[8,2,8,512]{3,2,1,0:T(8,128)S(1)} %get-tuple-element.156, f32[8,2,8]{2,1,0:T(2,128)S(1)} %get-tuple-element.150, f32[8,2,8]{2,1,0:T(2,128)S(1)} %multiply_maximum_fusion, f32[8,2,128]{2,1,0:T(2,128)S(1)} %copy.18, f32[8,2,8]{2,1,0:T(2,128)S(1)} %get-tuple-element.149, ...), kind=kOutput, calls=%fused_computation.13 | convolution fusion | flops 17022976 | bytes 2401792 | tf_op jit(solution)/shard_map/rkgc,rckd->rkgd/dot_general | solution.py:445
  114.8 0.6 copy.53
  (130 shorter events, 3.9 us)
Async XLA Ops:
  0.6 15.3 %copy-start = (bf16[8,512,256]{2,1,0:T(8,128)(2,1)S(1)}, bf16[8,512,256]{2,1,0:T(8,128)(2,1)}, u32[]{:S(2)}) copy-start(bf16[8,512,256]{2,1,0:T(8,128)(2,1)} %param.18) | copy-start | bytes 6291460
  1.3 5.7 %copy-start.13 = (s32[64]{0:T(128)S(1)}, s32[64]{0:T(128)}, u32[]{:S(2)}) copy-start(s32[64]{0:T(128)} %param.16) | copy-start | bytes 772
  6.4 17.3 %collective-permute-start = (bf16[2560,512]{1,0:T(8,128)(2,1)}, bf16[2560,512]{1,0:T(8,128)(2,1)}, u32[]{:S(2)}, u32[]{:S(2)}) collective-permute-start(bf16[2560,512]{1,0:T(8,128)(2,1)} %shard_map.140), channel_id=1, source_target_pairs={{0,4},{4,0},{8,12},{12,8},{16,20},{20,16},{24,28},{28,24},{1,5},{5... | collective-permute-start | bytes 7864328 | tf_op jit(solution)/shard_map/ppermute | solution.py:20
  6.9 16.8 %collective-permute-start.1 = (bf16[512,1024]{1,0:T(8,128)(2,1)}, bf16[512,1024]{1,0:T(8,128)(2,1)}, u32[]{:S(2)}, u32[]{:S(2)}) collective-permute-start(bf16[512,1024]{1,0:T(8,128)(2,1)} %refs_2_.6), channel_id=1, source_target_pairs={{0,4},{4,0},{8,12},{12,8},{16,20},{20,16},{24,28},{28,24},{1,5},{5... | collective-permute-start | bytes 3145736 | tf_op jit(solution)/shard_map/ppermute | solution.py:20
  6.9 6.7 %copy-start.1 = (s32[8]{0:T(128)S(1)}, s32[8]{0:T(128)}, u32[]{:S(2)}) copy-start(s32[8]{0:T(128)} %stack.77.order) | copy-start | bytes 100
  13.6 2.1 %copy-start.9 = (bf16[8,2048]{1,0:T(8,128)(2,1)S(1)}, bf16[8,2048]{1,0:T(8,128)(2,1)}, u32[]{:S(2)}) copy-start(bf16[8,2048]{1,0:T(8,128)(2,1)} %param.17) | copy-start | bytes 98308
  13.6 2.1 %copy-start.12 = (bf16[8,256]{1,0:T(8,128)(2,1)S(1)}, bf16[8,256]{1,0:T(8,128)(2,1)}, u32[]{:S(2)}) copy-start(bf16[8,256]{1,0:T(8,128)(2,1)} %param.20) | copy-start | bytes 12292
  13.7 2.2 %copy-start.11 = (s32[8]{0:T(128)S(1)}, s32[8]{0:T(128)}, u32[]{:S(2)}) copy-start(s32[8]{0:T(128)} %param.23) | copy-start | bytes 100
  15.4 1.2 %copy-start.14 = (f32[2]{0:T(128)S(1)}, f32[2]{0:T(128)}, u32[]{:S(2)}) copy-start(f32[2]{0:T(128)} %param.22) | copy-start | bytes 28
  15.4 8.2 %collective-permute-start.8 = (bf16[640,256]{1,0:T(8,128)(2,1)}, bf16[640,256]{1,0:T(8,128)(2,1)S(1)}, u32[]{:S(2)}, u32[]{:S(2)}) collective-permute-start(bf16[640,256]{1,0:T(8,128)(2,1)} %convert_element_type.139), channel_id=1, source_target_pairs={{0,4},{4,0},{8,12},{12,8},{16,20},{20,16},{24,28},{28,24},{1,5},{5... | collective-permute-start | bytes 983048 | tf_op jit(solution)/shard_map/ppermute | solution.py:20
  17.4 5.2 %copy-start.2 = (s32[8]{0:T(128)S(1)}, s32[8]{0:T(128)}, u32[]{:S(2)}) copy-start(s32[8]{0:T(128)} %stack.72.order) | copy-start | bytes 100
  28.8 22.2 %collective-permute-start.2 = (bf16[1280,256]{1,0:T(8,128)(2,1)}, bf16[1280,256]{1,0:T(8,128)(2,1)S(1)}, u32[]{:S(2)}, u32[]{:S(2)}) collective-permute-start(bf16[1280,256]{1,0:T(8,128)(2,1)} %get-tuple-element.46), channel_id=1, source_target_pairs={{0,8},{4,12},{8,0},{12,4},{16,24},{20,28},{24,16},{28,20},{1,9},{5... | collective-permute-start | bytes 1966088 | tf_op jit(solution)/shard_map/ppermute | solution.py:20
  31.6 19.4 %collective-permute-start.3 = (bf16[1280,256]{1,0:T(8,128)(2,1)}, bf16[1280,256]{1,0:T(8,128)(2,1)S(1)}, u32[]{:S(2)}, u32[]{:S(2)}) collective-permute-start(bf16[1280,256]{1,0:T(8,128)(2,1)} %get-tuple-element.47), channel_id=1, source_target_pairs={{0,16},{4,20},{8,24},{12,28},{16,0},{20,4},{24,8},{28,12},{1,17},{... | collective-permute-start | bytes 1966088 | tf_op jit(solution)/shard_map/ppermute | solution.py:20
  39.2 24.8 %collective-permute-start.6 = (bf16[1280,128]{1,0:T(8,128)(2,1)}, bf16[1280,128]{1,0:T(8,128)(2,1)S(1)}, u32[]{:S(2)}, u32[]{:S(2)}) collective-permute-start(bf16[1280,128]{1,0:T(8,128)(2,1)} %get-tuple-element.55), channel_id=1, source_target_pairs={{0,8},{4,12},{8,0},{12,4},{16,24},{20,28},{24,16},{28,20},{1,9},{5... | collective-permute-start | bytes 983048 | tf_op jit(solution)/shard_map/ppermute | solution.py:20
  39.9 24.2 %collective-permute-start.7 = (bf16[1280,128]{1,0:T(8,128)(2,1)}, bf16[1280,128]{1,0:T(8,128)(2,1)S(1)}, u32[]{:S(2)}, u32[]{:S(2)}) collective-permute-start(bf16[1280,128]{1,0:T(8,128)(2,1)} %get-tuple-element.48), channel_id=1, source_target_pairs={{0,16},{4,20},{8,24},{12,28},{16,0},{20,4},{24,8},{28,12},{1,17},{... | collective-permute-start | bytes 983048 | tf_op jit(solution)/shard_map/ppermute | solution.py:20
  41.1 19.8 %collective-permute-start.9 = (bf16[1600,256]{1,0:T(8,128)(2,1)S(1)}, bf16[1600,256]{1,0:T(8,128)(2,1)S(1)}, u32[]{:S(2)}, u32[]{:S(2)}) collective-permute-start(bf16[1600,256]{1,0:T(8,128)(2,1)S(1)} %get-tuple-element.128), channel_id=1, source_target_pairs={{0,1},{1,0},{2,3},{3,2},{4,5},{5,4},{6,7},{7,6},{8,9},{9,8},{10,11... | collective-permute-start | bytes 2457608 | tf_op jit(solution)/shard_map/ppermute | solution.py:20
  51.0 1.3 %copy-start.4 = (f32[1280,256]{1,0:T(8,128)S(1)}, f32[1280,256]{1,0:T(8,128)}, u32[]{:S(2)}) copy-start(f32[1280,256]{1,0:T(8,128)} %get-tuple-element.45) | copy-start | bytes 3932164
  53.9 7.1 %copy-start.3 = (f32[1280,256]{1,0:T(8,128)S(1)}, f32[1280,256]{1,0:T(8,128)}, u32[]{:S(2)}) copy-start(f32[1280,256]{1,0:T(8,128)} %get-tuple-element.56) | copy-start | bytes 3932164
  54.0 13.6 %collective-permute-start.4 = (bf16[640,256]{1,0:T(8,128)(2,1)S(1)}, bf16[640,256]{1,0:T(8,128)(2,1)S(1)}, u32[]{:S(2)}, u32[]{:S(2)}) collective-permute-start(bf16[640,256]{1,0:T(8,128)(2,1)S(1)} %slice.580), channel_id=1, source_target_pairs={{0,16},{4,20},{8,24},{12,28},{16,0},{20,4},{24,8},{28,12},{1,17},{... | collective-permute-start | bytes 983048 | tf_op jit(solution)/shard_map/ppermute | solution.py:20
  55.7 11.9 %collective-permute-start.5 = (bf16[640,256]{1,0:T(8,128)(2,1)S(1)}, bf16[640,256]{1,0:T(8,128)(2,1)S(1)}, u32[]{:S(2)}, u32[]{:S(2)}) collective-permute-start(bf16[640,256]{1,0:T(8,128)(2,1)S(1)} %slice.579), channel_id=1, source_target_pairs={{0,8},{4,12},{8,0},{12,4},{16,24},{20,28},{24,16},{28,20},{1,9},{5... | collective-permute-start | bytes 983048 | tf_op jit(solution)/shard_map/ppermute | solution.py:20
  61.2 2.9 %copy-start.7 = (f32[1280,128]{1,0:T(8,128)S(1)}, f32[1280,128]{1,0:T(8,128)}, u32[]{:S(2)}) copy-start(f32[1280,128]{1,0:T(8,128)} %get-tuple-element.54) | copy-start | bytes 1966084
  61.3 2.9 %copy-start.6 = (f32[1280,128]{1,0:T(8,128)S(1)}, f32[1280,128]{1,0:T(8,128)}, u32[]{:S(2)}) copy-start(f32[1280,128]{1,0:T(8,128)} %get-tuple-element.60) | copy-start | bytes 1966084
  61.4 19.9 %collective-permute-start.12 = (bf16[800,256]{1,0:T(8,128)(2,1)S(1)}, bf16[800,256]{1,0:T(8,128)(2,1)S(1)}, u32[]{:S(2)}, u32[]{:S(2)}) collective-permute-start(bf16[800,256]{1,0:T(8,128)(2,1)S(1)} %constant_dynamic-update-slice_fusion.17), channel_id=1, source_target_pairs={{0,2},{1,3},{2,0},{3,1},{4,6},{5,7},{6,4},{7,5},{8,10},{9,11},{10,... | collective-permute-start | bytes 1228808 | tf_op jit(solution)/shard_map/ppermute | solution.py:20
  64.3 5.7 %collective-permute-start.13 = (bf16[640,128]{1,0:T(8,128)(2,1)S(1)}, bf16[640,128]{1,0:T(8,128)(2,1)S(1)}, u32[]{:S(2)}, u32[]{:S(2)}) collective-permute-start(bf16[640,128]{1,0:T(8,128)(2,1)S(1)} %slice.583), channel_id=1, source_target_pairs={{0,16},{4,20},{8,24},{12,28},{16,0},{20,4},{24,8},{28,12},{1,17},{... | collective-permute-start | bytes 491528 | tf_op jit(solution)/shard_map/ppermute | solution.py:20
  65.9 5.3 %collective-permute-start.14 = (bf16[640,128]{1,0:T(8,128)(2,1)S(1)}, bf16[640,128]{1,0:T(8,128)(2,1)S(1)}, u32[]{:S(2)}, u32[]{:S(2)}) collective-permute-start(bf16[640,128]{1,0:T(8,128)(2,1)S(1)} %slice.582), channel_id=1, source_target_pairs={{0,8},{4,12},{8,0},{12,4},{16,24},{20,28},{24,16},{28,20},{1,9},{5... | collective-permute-start | bytes 491528 | tf_op jit(solution)/shard_map/ppermute | solution.py:20
  67.9 14.9 %collective-permute-start.10 = (bf16[320,256]{1,0:T(8,128)(2,1)S(1)}, bf16[320,256]{1,0:T(8,128)(2,1)S(1)}, u32[]{:S(2)}, u32[]{:S(2)}) collective-permute-start(bf16[320,256]{1,0:T(8,128)(2,1)S(1)} %pad_maximum_fusion.1), channel_id=1, source_target_pairs={{0,1},{1,0},{2,3},{3,2},{4,5},{5,4},{6,7},{7,6},{8,9},{9,8},{10,11... | collective-permute-start | bytes 491528 | tf_op jit(solution)/shard_map/ppermute | solution.py:20
  69.3 15.6 %collective-permute-start.11 = (bf16[320,256]{1,0:T(8,128)(2,1)S(1)}, bf16[320,256]{1,0:T(8,128)(2,1)S(1)}, u32[]{:S(2)}, u32[]{:S(2)}) collective-permute-start(bf16[320,256]{1,0:T(8,128)(2,1)S(1)} %pad_maximum_fusion.2), channel_id=1, source_target_pairs={{0,1},{1,0},{2,3},{3,2},{4,5},{5,4},{6,7},{7,6},{8,9},{9,8},{10,11... | collective-permute-start | bytes 491528 | tf_op jit(solution)/shard_map/ppermute | solution.py:20
  71.4 16.6 %collective-permute-start.18 = (bf16[320,128]{1,0:T(8,128)(2,1)S(1)}, bf16[320,128]{1,0:T(8,128)(2,1)S(1)}, u32[]{:S(2)}, u32[]{:S(2)}) collective-permute-start(bf16[320,128]{1,0:T(8,128)(2,1)S(1)} %pad_maximum_fusion.4), channel_id=1, source_target_pairs={{0,1},{1,0},{2,3},{3,2},{4,5},{5,4},{6,7},{7,6},{8,9},{9,8},{10,11... | collective-permute-start | bytes 245768 | tf_op jit(solution)/shard_map/ppermute | solution.py:20
  73.0 16.3 %collective-permute-start.19 = (bf16[320,128]{1,0:T(8,128)(2,1)S(1)}, bf16[320,128]{1,0:T(8,128)(2,1)S(1)}, u32[]{:S(2)}, u32[]{:S(2)}) collective-permute-start(bf16[320,128]{1,0:T(8,128)(2,1)S(1)} %pad_maximum_fusion.5), channel_id=1, source_target_pairs={{0,1},{1,0},{2,3},{3,2},{4,5},{5,4},{6,7},{7,6},{8,9},{9,8},{10,11... | collective-permute-start | bytes 245768 | tf_op jit(solution)/shard_map/ppermute | solution.py:20
  81.5 10.9 %collective-permute-start.17 = (bf16[400,256]{1,0:T(8,128)(2,1)S(1)}, bf16[400,256]{1,0:T(8,128)(2,1)S(1)}, u32[]{:S(2)}, u32[]{:S(2)}) collective-permute-start(bf16[400,256]{1,0:T(8,128)(2,1)S(1)} %pad_maximum_fusion), channel_id=1, source_target_pairs={{0,8},{4,12},{8,0},{12,4},{16,24},{20,28},{24,16},{28,20},{1,9},{5... | collective-permute-start | bytes 614408 | tf_op jit(solution)/shard_map/ppermute | solution.py:20
  85.1 10.0 %copy-start.8 = (f32[160,1024]{1,0:T(8,128)S(1)}, f32[160,1024]{1,0:T(8,128)}, u32[]{:S(2)}) copy-start(f32[160,1024]{1,0:T(8,128)} %param.14) | copy-start | bytes 1966084
  85.1 9.1 %collective-permute-start.15 = (bf16[160,256]{1,0:T(8,128)(2,1)S(1)}, bf16[160,256]{1,0:T(8,128)(2,1)S(1)}, u32[]{:S(2)}, u32[]{:S(2)}) collective-permute-start(bf16[160,256]{1,0:T(8,128)(2,1)S(1)} %slice.586), channel_id=1, source_target_pairs={{0,2},{1,3},{2,0},{3,1},{4,6},{5,7},{6,4},{7,5},{8,10},{9,11},{10,... | collective-permute-start | bytes 245768 | tf_op jit(solution)/shard_map/ppermute | solution.py:20
  85.9 9.2 %collective-permute-start.16 = (bf16[160,256]{1,0:T(8,128)(2,1)S(1)}, bf16[160,256]{1,0:T(8,128)(2,1)S(1)}, u32[]{:S(2)}, u32[]{:S(2)}) collective-permute-start(bf16[160,256]{1,0:T(8,128)(2,1)S(1)} %slice.585), channel_id=1, source_target_pairs={{0,2},{1,3},{2,0},{3,1},{4,6},{5,7},{6,4},{7,5},{8,10},{9,11},{10,... | collective-permute-start | bytes 245768 | tf_op jit(solution)/shard_map/ppermute | solution.py:20
  89.4 6.5 %collective-permute-start.21 = (bf16[160,128]{1,0:T(8,128)(2,1)S(1)}, bf16[160,128]{1,0:T(8,128)(2,1)S(1)}, u32[]{:S(2)}, u32[]{:S(2)}) collective-permute-start(bf16[160,128]{1,0:T(8,128)(2,1)S(1)} %slice.588), channel_id=1, source_target_pairs={{0,2},{1,3},{2,0},{3,1},{4,6},{5,7},{6,4},{7,5},{8,10},{9,11},{10,... | collective-permute-start | bytes 122888 | tf_op jit(solution)/shard_map/ppermute | solution.py:20
  89.5 6.9 %collective-permute-start.22 = (bf16[160,128]{1,0:T(8,128)(2,1)S(1)}, bf16[160,128]{1,0:T(8,128)(2,1)S(1)}, u32[]{:S(2)}, u32[]{:S(2)}) collective-permute-start(bf16[160,128]{1,0:T(8,128)(2,1)S(1)} %slice.587), channel_id=1, source_target_pairs={{0,2},{1,3},{2,0},{3,1},{4,6},{5,7},{6,4},{7,5},{8,10},{9,11},{10,... | collective-permute-start | bytes 122888 | tf_op jit(solution)/shard_map/ppermute | solution.py:20
  92.5 4.7 %collective-permute-start.20 = (bf16[200,256]{1,0:T(8,128)(2,1)S(1)}, bf16[200,256]{1,0:T(8,128)(2,1)S(1)}, u32[]{:S(2)}, u32[]{:S(2)}) collective-permute-start(bf16[200,256]{1,0:T(8,128)(2,1)S(1)} %pad_maximum_fusion.3), channel_id=1, source_target_pairs={{0,16},{4,20},{8,24},{12,28},{16,0},{20,4},{24,8},{28,12},{1,17},{... | collective-permute-start | bytes 307208 | tf_op jit(solution)/shard_map/ppermute | solution.py:20
  97.4 14.8 %copy-start.10 = (bf16[8,256]{1,0:T(8,128)(2,1)S(1)}, bf16[8,256]{1,0:T(8,128)(2,1)}, u32[]{:S(2)}) copy-start(bf16[8,256]{1,0:T(8,128)(2,1)} %param.21) | copy-start | bytes 12292
  97.4 0.8 copy-start.5
  99.2 12.9 %all-to-all-start = ((f32[32,8,256]{2,1,0:T(8,128)}), f32[32,8,256]{2,1,0:T(8,128)S(1)}, u32[]{:S(2)}, u32[]{:S(2)}) async-start(f32[32,8,256]{2,1,0:T(8,128)} %bitcast.15), calls=%async_computation | async-start | bytes 524288 | tf_op jit(solution)/shard_map/all_to_all | solution.py:416

commit v4 on v3

v4 whole, which is shorter than its diff:
```python
import functools
import math

import jax
import jax.numpy as jnp
from jax import lax
from jax.experimental import pallas as pl
from jax.experimental.pallas import tpu as pltpu
from jax.sharding import PartitionSpec as P

HEADS = 64
KV = 8
HD = 128
LANES = 128
SLAB = 16
VMEM = 56 << 20


def exchange(value, axis, mask):
    return lax.ppermute(value, axis, [(i, i ^ mask) for i in range(lax.axis_size(axis))])


def own_place():
    f = lax.axis_index("fsdp")
    return f & 1, f >> 1, lax.axis_index("tp")


def transpose_blocks(arranged, mine, units, source, out, wide, tall, arrived, left):
    core, upper, t = own_place()
    width = wide.shape[2]
    rows = width // units
    side = core if mine else 1 - core
    taken, given = [], []
    for j, r in enumerate(arranged):
        start = pl.multiple_of((((r ^ upper) << 1) | side) * width, LANES)
        copy = pltpu.make_async_copy(source.at[:, pl.ds(start, width)], wide.at[j], arrived.at[j])
        copy.start()
        taken.append(copy)
    for j in range(len(arranged)):
        taken[j].wait()
        for low in range(0, width, LANES):
            tall[j, low : low + LANES, :] = wide[j, :, low : low + LANES].T
        for unit in range(units):
            place = pl.multiple_of(j * width + (unit ^ t) * rows, 32)
            copy = pltpu.make_async_copy(
                tall.at[j, pl.ds(unit * rows, rows)],
                out.at[pl.ds(place, rows)],
                left.at[j * units + unit],
            )
            copy.start()
            given.append(copy)
    for copy in given:
        copy.wait()


def pack(activations, arranged, mine, units, width):
    tokens = activations.shape[0]
    count = len(arranged)
    rows = width // units
    if width % LANES or rows % 32:
        core, upper, t = own_place()
        side = core if mine else 1 - core
        flipped = activations.T
        return jnp.concatenate(
            [
                lax.dynamic_slice_in_dim(
                    flipped, (((r ^ upper) << 1) | side) * width + (unit ^ t) * rows, rows, 0
                )
                for r in arranged
                for unit in range(units)
            ]
        )
    kind = activations.dtype
    return pl.pallas_call(
        functools.partial(transpose_blocks, arranged, mine, units),
        in_specs=[pl.BlockSpec(memory_space=pl.ANY)],
        out_specs=pl.BlockSpec(memory_space=pl.ANY),
        out_shape=jax.ShapeDtypeStruct((count * width, tokens), kind),
        scratch_shapes=[
            pltpu.VMEM((count, tokens, width), kind),
            pltpu.VMEM((count, width, tokens), kind),
            pltpu.SemaphoreType.DMA((count,)),
            pltpu.SemaphoreType.DMA((count * units,)),
        ],
        compiler_params=pltpu.CompilerParams(vmem_limit_bytes=VMEM),
        cost_estimate=pl.CostEstimate(
            flops=0, bytes_accessed=4 * count * width * tokens, transcendentals=0
        ),
    )(activations)


def runs_of(units):
    runs = []
    for unit in units:
        if runs and runs[-1][1] == unit:
            runs[-1][1] = unit + 1
        else:
            runs.append([unit, unit + 1])
    return runs


def multiply(wanted, rows, blocks, base, *refs):
    count = len(wanted)
    sources = refs[:4]
    outs = refs[4 : 4 + count]
    left, right, sems = refs[4 + count :]
    tokens = left.shape[1] // 2
    per_block = left.shape[0] // blocks
    units_block = per_block // rows
    needed = [
        block
        for block in range(blocks)
        if any(unit // units_block == block for item in wanted for unit in item[0])
    ]
    columns = pl.ds(base, right.shape[1])
    halves = [pl.ds(0, tokens), pl.ds(tokens, tokens)]
    grads, lefts = [], {}
    for at, half in enumerate(halves):
        grads.append(
            pltpu.make_async_copy(sources[2 + at].at[:, columns], right.at[half], sems.at[at])
        )
        grads[at].start()
    for block in needed:
        span = pl.ds(block * per_block, per_block)
        for at, half in enumerate(halves):
            lefts[block, at] = pltpu.make_async_copy(
                sources[at].at[span], left.at[span, half], sems.at[2 + 2 * block + at]
            )
            lefts[block, at].start()
    for copy in grads:
        copy.wait()
    for block in needed:
        for at in range(2):
            lefts[block, at].wait()
        for (units, first, last, _), out in zip(wanted, outs):
            here = [unit for unit in units if unit // units_block == block]
            for low, high in runs_of(here):
                place = units.index(low) * rows
                product = dot32(
                    left[low * rows : high * rows, :], right[:, first - base : last - base]
                )
                out[place : place + (high - low) * rows, :] = product.astype(out.dtype)


def products(lefts, grads, wanted, rows, blocks):
    total, tokens = lefts[0].shape
    base = min(first for _, first, _, _ in wanted)
    columns = max(last for _, _, last, _ in wanted) - base
    if rows % 32 or any((first | last) % LANES for _, first, last, _ in wanted):
        return [
            jnp.concatenate(
                [
                    sum(
                        dot32(left[low * rows : high * rows], grad[:, first:last])
                        for left, grad in zip(lefts, grads)
                    )
                    for low, high in runs_of(units)
                ]
            ).astype(kind)
            for units, first, last, kind in wanted
        ]
    shapes = [
        jax.ShapeDtypeStruct((len(units) * rows, last - first), kind)
        for units, first, last, kind in wanted
    ]
    return pl.pallas_call(
        functools.partial(multiply, wanted, rows, blocks, base),
        out_shape=shapes,
        in_specs=[pl.BlockSpec(memory_space=pl.ANY)] * 4,
        out_specs=[pl.BlockSpec(memory_space=pltpu.VMEM)] * len(shapes),
        scratch_shapes=[
            pltpu.VMEM((total, 2 * tokens), lefts[0].dtype),
            pltpu.VMEM((2 * tokens, columns), grads[0].dtype),
            pltpu.SemaphoreType.DMA((2 + 2 * blocks,)),
        ],
        compiler_params=pltpu.CompilerParams(vmem_limit_bytes=VMEM // 2),
        cost_estimate=pl.CostEstimate(flops=1, bytes_accessed=1, transcendentals=0),
    )(*lefts, *grads)


def pick_rows(arranged, units, place, table, tail, *refs):
    outs, (slabs, found, flipped, sems) = refs[:2], refs[2:]
    here = table.shape[0]
    whole = here // SLAB * SLAB
    tokens, width_all = found.shape
    width = flipped.shape[0]
    rows = width // units
    lanes = outs[0].shape[1]
    folds = lanes // tokens
    lines = rows // folds

    def slab_copy(source, k):
        return pltpu.make_async_copy(source, slabs.at[k], sems.at[k])

    for k in range(tokens):
        inside = place[k]

        @pl.when((inside >= 0) & (inside < whole))
        def _():
            start = pl.multiple_of(lax.div(inside, SLAB) * SLAB, SLAB)
            slab_copy(table.at[pl.ds(start, SLAB)], k).start()

        @pl.when(inside >= whole)
        def _():
            slab_copy(tail, k).start()

    found[...] = jnp.zeros_like(found)
    for k in range(tokens):
        inside = place[k]

        @pl.when(inside >= 0)
        def _():
            slab_copy(tail, k).wait()
            line = jnp.where(inside < whole, lax.rem(inside, SLAB), inside - (here - SLAB))
            held = slabs[k].astype(jnp.float32)
            at = lax.broadcasted_iota(jnp.int32, held.shape, 0)
            found[k : k + 1, :] = jnp.sum(
                jnp.where(at == line, held, 0.0), axis=0, keepdims=True
            )

    core, upper, t = own_place()
    for side, out in zip((1 - core, core), outs):
        for j, r in enumerate(arranged):
            start = pl.multiple_of((((r ^ upper) << 1) | side) * width, LANES)
            flipped[...] = found[:, pl.ds(start, width)].T
            for unit in range(units):
                from_row = (unit ^ t) * rows
                pieces = [
                    flipped[pl.ds(pl.multiple_of(from_row + fold * lines, 8), lines), :]
                    for fold in range(folds)
                ]
                put = (j * units + unit) * lines
                out[put : put + lines, :] = jnp.concatenate(pieces, axis=1).astype(out.dtype)


def fold_unit(part, lanes):
    rows, tokens = part.shape
    if tokens >= lanes:
        return jnp.concatenate([part[:, at : at + lanes] for at in range(0, tokens, lanes)])
    lines = rows * tokens // lanes
    return jnp.concatenate([part[at : at + lines] for at in range(0, rows, lines)], axis=1)


def unfold_unit(folded, rows):
    lines, lanes = folded.shape
    tokens = lines * lanes // rows
    if tokens >= lanes:
        return jnp.concatenate([folded[at : at + rows] for at in range(0, lines, rows)], axis=1)
    return jnp.concatenate([folded[:, at : at + tokens] for at in range(0, lanes, tokens)])


def lookup(embed_table, token_ids, arranged, units, width, lanes):
    here, width_all = embed_table.shape
    tokens = token_ids.shape[0]
    rows = width // units
    core, upper, t = own_place()
    inside = token_ids - (lax.axis_index("fsdp") * units + t) * here
    place = jnp.where((inside >= 0) & (inside < here), inside, -1).astype(jnp.int32)
    kind = embed_table.dtype
    if width % LANES or lanes % tokens or (rows * tokens // lanes) % 16:
        found = jnp.where(
            (place >= 0)[:, None], embed_table[jnp.maximum(place, 0)], jnp.zeros((), kind)
        )
        flipped = found.T
        return [
            jnp.concatenate(
                [
                    fold_unit(
                        lax.dynamic_slice_in_dim(
                            flipped,
                            (((r ^ upper) << 1) | side) * width + (unit ^ t) * rows,
                            rows,
                            0,
                        ),
                        lanes,
                    )
                    for r in arranged
                    for unit in range(units)
                ]
            )
            for side in (1 - core, core)
        ]
    shape = jax.ShapeDtypeStruct((len(arranged) * width * tokens // lanes, lanes), kind)
    return pl.pallas_call(
        functools.partial(pick_rows, arranged, units),
        in_specs=[
            pl.BlockSpec(memory_space=pltpu.SMEM),
            pl.BlockSpec(memory_space=pl.ANY),
            pl.BlockSpec(memory_space=pl.ANY),
        ],
        out_specs=[pl.BlockSpec(memory_space=pltpu.VMEM)] * 2,
        out_shape=[shape, shape],
        scratch_shapes=[
            pltpu.VMEM((tokens, SLAB, width_all), kind),
            pltpu.VMEM((tokens, width_all), jnp.float32),
            pltpu.VMEM((width, tokens), jnp.float32),
            pltpu.SemaphoreType.DMA((tokens,)),
        ],
        compiler_params=pltpu.CompilerParams(vmem_limit_bytes=VMEM // 2),
        cost_estimate=pl.CostEstimate(flops=1, bytes_accessed=1, transcendentals=0),
    )(place, embed_table, embed_table[here - SLAB :])


def dot32(left, right):
    return jnp.dot(left, right, preferred_element_type=jnp.float32)


def per_device(
    activations,
    grad_out,
    master_w,
    embed_table,
    token_ids,
    queries,
    cache_keys,
    cache_values,
    new_key,
    first_value,
    residual_mix,
    lengths,
):
    count_fsdp = lax.axis_size("fsdp")
    count_tp = lax.axis_size("tp")
    devices_all = count_fsdp * count_tp
    width = activations.shape[1]
    tokens_total = activations.shape[0] * devices_all
    coef = 1.0 / math.sqrt(tokens_total * width)
    upper_bits = count_fsdp.bit_length() - 2
    uppers = 1 << upper_bits

    block = width // count_fsdp
    rows = master_w.shape[0]
    columns = master_w.shape[1]
    arranged = [r ^ (r >> 1) for r in range(uppers)][::-1]
    grads = [grad_out, exchange(grad_out, "fsdp", 1)]
    incoming = exchange(pack(activations, arranged, False, count_tp, block), "fsdp", 1)
    staying = pack(activations, arranged, True, count_tp, block)
    lefts = [staying, incoming]
    tokens_new = token_ids.shape[0]
    quarter = columns // 4
    eighth = columns // 8
    lines = rows * tokens_new // eighth

    places = [(r, unit) for r in arranged for unit in range(count_tp)]
    steps_upper = [("fsdp", bit) for bit in range(upper_bits)]
    steps_tp = [("tp", bit) for bit in range(count_tp.bit_length() - 1)]
    one, two, three = (
        steps_upper + steps_tp,
        steps_upper[::-1] + steps_tp,
        steps_tp + steps_upper,
    )
    edges = [0, quarter, 2 * quarter, 3 * quarter, 3 * quarter + eighth, columns]
    spans = list(zip(edges[:-1], edges[1:]))
    orders = [one, two, three, one, two]

    def has(place, step):
        return (place[step[0] == "tp"] >> step[1]) & 1

    def flip(place, step):
        mask = 1 << step[1]
        return (place[0], place[1] ^ mask) if step[0] == "tp" else (place[0] ^ mask, place[1])

    def split(held, step):
        return [p for p in held if has(p, step)], [p for p in held if not has(p, step)]

    def take(value, held, chosen, size):
        runs = runs_of([held.index(p) for p in chosen])
        return jnp.concatenate([value[low * size : high * size] for low, high in runs])

    def send(value, step):
        mask = 1 << step[1]
        return exchange(value, step[0], 2 * mask if step[0] == "fsdp" else mask)

    def compute(which, sent, factors):
        wanted = []
        for index in which:
            chosen = split(places, orders[index][0])[0 if sent else 1]
            units = [places.index(p) for p in chosen]
            kind = jnp.bfloat16 if sent else jnp.float32
            wanted.append((units, *spans[index], kind))
        return dict(zip(which, products(factors, grads, wanted, rows, uppers)))

    going = compute([2, 0, 1], True, lefts)
    got = {index: send(value, orders[index][0]) for index, value in going.items()}
    going |= compute([3, 4], True, lefts)
    got[3] = send(going[3], orders[3][0])

    theirs, ours = lookup(embed_table, token_ids, arranged, count_tp, block, eighth)
    asked = ours + exchange(theirs, "fsdp", 1)
    go, stay = split(places, orders[4][0])
    values = compute([0, 1, 2], False, lefts)
    token = jnp.concatenate([going[4], take(asked, places, go, lines)])
    got[4] = send(token, orders[4][0])
    values |= compute([3, 4], False, lefts)
    values = {index: [value] for index, value in values.items()}
    values[4].append(take(asked, places, stay, lines).astype(jnp.float32))
    sizes = {index: [rows] for index in range(5)}
    sizes[4].append(lines)
    held = {index: places for index in range(5)}

    def receive(index, step):
        gone, kept = split(held[index], step)
        landed = [flip(p, step) for p in gone]
        start = 0
        added = []
        for value, size in zip(values[index], sizes[index]):
            piece = got[index][start : start + len(gone) * size]
            start += len(gone) * size
            added.append(value + take(piece, landed, kept, size).astype(jnp.float32))
        values[index], held[index] = added, kept

    for at in range(len(one)):
        for group in ((0, 1), (2,), (3, 4)):
            tied = lax.optimization_barrier([got[index] for index in group] + [token])
            for index, arrived in zip(group, tied):
                got[index] = arrived
                receive(index, orders[index][at])
            if at + 1 == len(one):
                continue
            outgoing = []
            for index in group:
                gone, kept = split(held[index], orders[index][at + 1])
                pieces = [
                    take(value, held[index], gone, size).astype(jnp.bfloat16)
                    for value, size in zip(values[index], sizes[index])
                ]
                values[index] = [
                    take(value, held[index], kept, size)
                    for value, size in zip(values[index], sizes[index])
                ]
                outgoing.append(jnp.concatenate(pieces))
            outgoing = lax.optimization_barrier(outgoing)
            token = outgoing[-1]
            for index, value in zip(group, outgoing):
                got[index] = send(value, orders[index][at + 1])
    w_next = jnp.concatenate(
        [master_w[:, low:high] - coef * values[at][0] for at, (low, high) in enumerate(spans)],
        axis=1,
    )

    columns_own = unfold_unit(values[4][1].astype(jnp.bfloat16), rows)
    share_own = lax.dot_general(
        columns_own,
        w_next.astype(jnp.bfloat16),
        (((0,), (0,)), ((), ())),
        preferred_element_type=jnp.float32,
    )
    rows_f = tokens_new // count_fsdp
    col_width = columns // count_tp
    blocks_own = (
        share_own.reshape(count_fsdp, rows_f, count_tp, col_width)
        .transpose(0, 2, 1, 3)
        .reshape(devices_all, rows_f, col_width)
    )
    own_value = jnp.sum(
        lax.all_to_all(blocks_own, ("fsdp", "tp"), split_axis=0, concat_axis=0), axis=0
    )

    share = jnp.repeat(residual_mix, HD)[None, :]
    new_value = (share * own_value + (1.0 - share) * first_value.astype(jnp.float32)).astype(
        jnp.bfloat16
    )
    rows = queries.shape[0]
    heads_kv = residual_mix.shape[0]
    group = HEADS // KV
    context = cache_keys.shape[1]
    scale = 1.0 / math.sqrt(HD)
    query_b = queries.reshape(rows, heads_kv, group, HD)
    keys_b = cache_keys.reshape(rows, context, heads_kv, HD)
    vals_b = cache_values.reshape(rows, context, heads_kv, HD)
    newk_b = new_key.reshape(rows, heads_kv, HD)
    newv_b = new_value.reshape(rows, heads_kv, HD)
    scores = (
        jnp.einsum("rkgd,rckd->rkgc", query_b, keys_b, preferred_element_type=jnp.float32) * scale
    )
    fresh = jnp.einsum("rkgd,rkd->rkg", query_b, newk_b, preferred_element_type=jnp.float32) * scale
    valid = jnp.arange(context, dtype=jnp.int32)[None, :] < lengths[:, None]
    scores = jnp.where(valid[:, None, None, :], scores, -1e30)
    peak = jnp.maximum(jnp.max(scores, axis=-1), fresh)
    expo = jnp.exp(scores - peak[..., None])
    expo_new = jnp.exp(fresh - peak)
    total = jnp.sum(expo, axis=-1) + expo_new
    probs = (expo / total[..., None]).astype(jnp.bfloat16)
    probs_new = (expo_new / total).astype(jnp.bfloat16)
    mixed = lax.optimization_barrier(
        jnp.einsum("rkgc,rckd->rkgd", probs, vals_b, preferred_element_type=jnp.float32)
    )
    mixed = (
        mixed + probs_new.astype(jnp.float32)[..., None] * newv_b.astype(jnp.float32)[:, :, None, :]
    )
    attended = mixed.reshape(rows, group * heads_kv * HD).astype(jnp.bfloat16)
    return (w_next, new_value, attended)


def solution(mesh):
    return jax.shard_map(
        per_device,
        mesh=mesh,
        in_specs=(
            P(("fsdp", "tp"), None),
            P(("fsdp", "tp"), None),
            P(("fsdp", "tp"), None),
            P(("fsdp", "tp"), None),
            P(),
            P("fsdp", "tp"),
            P("fsdp", None, "tp"),
            P("fsdp", None, "tp"),
            P("fsdp", "tp"),
            P("fsdp", "tp"),
            P("tp"),
            P("fsdp"),
        ),
        out_specs=(P(("fsdp", "tp"), None), P("fsdp", "tp"), P("fsdp", "tp")),
        check_vma=False,
    )
```

time: 116 us -> 111 us (0.957)
  Pallas kernels: 38.1 us -> 27.7 us
  waiting for transfers between devices: 30.4 us -> 40.6 us
  other arithmetic: 4.57 us -> 2.67 us
  local copies, waits for them, and re-layouts: 5.82 us -> 4.08 us
    ppermute x23, waiting for transfers between devices: 20.5 us -> 32.8 us  [exchange(): lax.ppermute(value, axis, [(i, i ^ mask) for i in range(lax.axis_size(axi...]
    pallas_call x5 -> x3, Pallas kernels: 19.1 us -> 10.2 us  [the longest x2 6.31 us: pack(): pl.pallas_call(functools.partial(transpose_blocks, arranged, mine, units)...]
    ppermute x23, starting transfers between devices: 28.6 us -> 26.2 us  [exchange(): lax.ppermute(value, axis, [(i, i ^ mask) for i in range(lax.axis_size(axi...]
    all_to_all x1, waiting for transfers between devices: 9.9 us -> 7.84 us  [per_device(): lax.all_to_all(blocks_own, ('fsdp', 'tp'), split_axis=0, concat_axis=0)]
    all_to_all x1, starting transfers between devices: 2.73 us -> 4.43 us  [per_device(): lax.all_to_all(blocks_own, ('fsdp', 'tp'), split_axis=0, concat_axis=0)]
    pallas_call x3 -> x4, Pallas kernels: 19 us -> 17.4 us  [products(): pl.pallas_call(functools.partial(multiply, wanted, rows, blocks, base), o...]
    unnamed x46 -> x25, local copies, waits for them, and re-layouts: 3.99 us -> 2.44 us
    add x12 -> x11, other arithmetic: 2.01 us -> 0.7 us  [receive(): added.append(value + take(piece, landed, kept, size).astype(jnp.float32))]
  transfers between devices with their start and end apart: 24 -> 24, of which waited for: 11 -> 11; matrix products, arithmetic and copies ran while one was open for 6% -> 6% of each run, Pallas kernels for 24% -> 22%
where the time goes in v4:
time: 111 us
  waiting for transfers between devices  40.6 us (37%)
  starting transfers between devices  30.6 us (28%)
  Pallas kernels  27.7 us (25%)
  local copies, waits for them, and re-layouts  4.08 us (4%)
  matrix products  3.99 us (4%)
  other arithmetic  2.67 us (2%)
  between operations  1.28 us (1%)
    ppermute x23, waiting for transfers between devices, exchange(): lax.ppermute(value, axis, [(i, i ^ mask) for i in range(lax.axis_size(axi...  32.8 us
    ppermute x23, starting transfers between devices, exchange(): lax.ppermute(value, axis, [(i, i ^ mask) for i in range(lax.axis_size(axi...  26.2 us
    pallas_call x4, Pallas kernels, products(): pl.pallas_call(functools.partial(multiply, wanted, rows, blocks, base), o...  17.4 us
    all_to_all x1, waiting for transfers between devices, per_device(): lax.all_to_all(blocks_own, ('fsdp', 'tp'), split_axis=0, concat_axis=0)  7.84 us
    pallas_call x2, Pallas kernels, pack(): pl.pallas_call(functools.partial(transpose_blocks, arranged, mine, units)...  6.31 us
    all_to_all x1, starting transfers between devices, per_device(): lax.all_to_all(blocks_own, ('fsdp', 'tp'), split_axis=0, concat_axis=0)  4.43 us
    pallas_call x1, Pallas kernels, lookup(): pl.pallas_call(functools.partial(pick_rows, arranged, units), in_specs=[p...  3.92 us
    unnamed x25, local copies, waits for them, and re-layouts  2.44 us
  transfers between devices with their start and end apart: 24, of which 11 were waited for; matrix products, arithmetic and copies ran while one was open for 6% of the time, Pallas kernels for 22%

profile of v4, /device:TPU:0, one launch (start us, length us, event | category | flops | bytes accessed | tf_op | source)
XLA Modules:
  0.0 110.8 jit_solution(17279678570776575948)
XLA Ops:
  0.7 3.2 %shard_map.140 = bf16[2560,512]{1,0:T(8,128)(2,1)} custom-call(bf16[512,5120]{1,0:T(8,128)(2,1)} %source.3), custom_call_target="tpu_custom_call" | custom-call | bytes 5242880 | tf_op jit(solution)/shard_map/pallas_call | solution.py:74
  3.9 0.5 collective-permute-start
  4.5 1.0 slice.258.tail
  5.5 3.9 %shard_map.144 = (bf16[1280,128]{1,0:T(8,128)(2,1)S(1)}, bf16[1280,128]{1,0:T(8,128)(2,1)S(1)}) custom-call(s32[64]{0:T(128)S(1)} %and_select_fusion.place, bf16[4748,5120]{1,0:T(8,128)(2,1)} %table.1, bf16[16,5120]{1,0:T(8,128)(2,1)S(1)} %slice.258.tail), custom_call_target="tpu_custom_call" | custom-call | flops 1 | bytes 1 | tf_op jit(solution)/shard_map/pallas_call | solution.py:284
  9.4 0.5 collective-permute-start.4
  10.0 3.1 %shard_map.139.refs_0_ = bf16[2560,512]{1,0:T(8,128)(2,1)} custom-call(bf16[512,5120]{1,0:T(8,128)(2,1)} %source.3), custom_call_target="tpu_custom_call" | custom-call | bytes 5242880 | tf_op jit(solution)/shard_map/pallas_call | solution.py:74
  13.2 0.7 fusion.67
  13.9 1.7 %copy-done.2 = bf16[2560,512]{1,0:T(8,128)(2,1)S(1)} copy-done((bf16[2560,512]{1,0:T(8,128)(2,1)S(1)}, bf16[2560,512]{1,0:T(8,128)(2,1)}, u32[]{:S(2)}) %copy-start.2) | copy-done | bytes 2621464
  15.7 4.9 %shard_map.142 = (bf16[1280,256]{1,0:T(8,128)(2,1)S(1)}, bf16[1280,256]{1,0:T(8,128)(2,1)S(1)}, bf16[1280,256]{1,0:T(8,128)(2,1)S(1)}) custom-call(bf16[2560,512]{1,0:T(8,128)(2,1)S(1)} %copy-done.2, bf16[2560,512]{1,0:T(8,128)(2,1)} %collective-permute-done.refs_1_, bf16[512,1024]{1,0:T(8,128)(2,1)S(1)} %copy-done.3, ...), custom_call_target="tpu_custom_call" | custom-call | flops 1 | bytes 1 | tf_op jit(solution)/shard_map/pallas_call | solution.py:166
  20.6 2.6 %collective-permute-start.2 = (bf16[1280,256]{1,0:T(8,128)(2,1)S(1)}, bf16[1280,256]{1,0:T(8,128)(2,1)S(1)}, u32[]{:S(2)}, u32[]{:S(2)}) collective-permute-start(bf16[1280,256]{1,0:T(8,128)(2,1)S(1)} %get-tuple-element.48), channel_id=1, source_target_pairs={{0,8},{4,12},{8,0},{12,4},{16,24},{20,28},{24,16},{28,20},{1,9},{5... | collective-permute-start | bytes 1966088 | tf_op jit(solution)/shard_map/ppermute | solution.py:20
  23.2 1.4 %collective-permute-start.3 = (bf16[1280,256]{1,0:T(8,128)(2,1)S(1)}, bf16[1280,256]{1,0:T(8,128)(2,1)S(1)}, u32[]{:S(2)}, u32[]{:S(2)}) collective-permute-start(bf16[1280,256]{1,0:T(8,128)(2,1)S(1)} %get-tuple-element.49), channel_id=1, source_target_pairs={{0,16},{4,20},{8,24},{12,28},{16,0},{20,4},{24,8},{28,12},{1,17},{... | collective-permute-start | bytes 1966088 | tf_op jit(solution)/shard_map/ppermute | solution.py:20
  24.8 0.2 fusion.14
  25.1 3.8 %shard_map.143 = (bf16[1280,128]{1,0:T(8,128)(2,1)S(1)}, bf16[1280,128]{1,0:T(8,128)(2,1)S(1)}) custom-call(bf16[2560,512]{1,0:T(8,128)(2,1)S(1)} %copy-done.2, bf16[2560,512]{1,0:T(8,128)(2,1)} %collective-permute-done.refs_1_, bf16[512,1024]{1,0:T(8,128)(2,1)S(1)} %copy-done.3, bf16[512,1024]{1,0:T(8,128)(2,1)} %collective-permute-done.1.refs_3_), custom_call_target="tpu_custom_call" | custom-call | flops 1 | bytes 1 | tf_op jit(solution)/shard_map/pallas_call | solution.py:166
  28.9 0.7 collective-permute-start.7
  29.8 2.1 %collective-permute-start.9 = (bf16[1280,256]{1,0:T(8,128)(2,1)S(1)}, bf16[1280,256]{1,0:T(8,128)(2,1)S(1)}, u32[]{:S(2)}, u32[]{:S(2)}) collective-permute-start(bf16[1280,256]{1,0:T(8,128)(2,1)S(1)} %get-tuple-element.61), channel_id=1, source_target_pairs={{0,1},{1,0},{2,3},{3,2},{4,5},{5,4},{6,7},{7,6},{8,9},{9,8},{10,11... | collective-permute-start | bytes 1966088 | tf_op jit(solution)/shard_map/ppermute | solution.py:20
  31.9 3.8 %shard_map.145 = (f32[1280,128]{1,0:T(8,128)S(1)}, f32[1280,128]{1,0:T(8,128)S(1)}) custom-call(bf16[2560,512]{1,0:T(8,128)(2,1)S(1)} %copy-done.2, bf16[2560,512]{1,0:T(8,128)(2,1)} %collective-permute-done.refs_1_, bf16[512,1024]{1,0:T(8,128)(2,1)S(1)} %copy-done.3, bf16[512,1024]{1,0:T(8,128)(2,1)} %collective-permute-done.1.refs_3_), custom_call_target="tpu_custom_call" | custom-call | flops 1 | bytes 1 | tf_op jit(solution)/shard_map/pallas_call | solution.py:166
  35.7 4.9 %shard_map.141 = (f32[1280,256]{1,0:T(8,128)S(1)}, f32[1280,256]{1,0:T(8,128)S(1)}, f32[1280,256]{1,0:T(8,128)S(1)}) custom-call(bf16[2560,512]{1,0:T(8,128)(2,1)S(1)} %copy-done.2, bf16[2560,512]{1,0:T(8,128)(2,1)} %collective-permute-done.refs_1_, bf16[512,1024]{1,0:T(8,128)(2,1)S(1)} %copy-done.3, bf16[512,1024]{1,0:T(8,128)(2,1)} %collective-permute-done.1.refs_3_), custom_call_target="tpu_custom_call" | custom-call | flops 1 | bytes 1 | tf_op jit(solution)/shard_map/pallas_call | solution.py:166
  40.8 0.3 convert_add_fusion.1
  41.2 1.3 %collective-permute-start.6 = (bf16[640,256]{1,0:T(8,128)(2,1)S(1)}, bf16[640,256]{1,0:T(8,128)(2,1)S(1)}, u32[]{:S(2)}, u32[]{:S(2)}) collective-permute-start(bf16[640,256]{1,0:T(8,128)(2,1)S(1)} %slice.456), channel_id=1, source_target_pairs={{0,8},{4,12},{8,0},{12,4},{16,24},{20,28},{24,16},{28,20},{1,9},{5... | collective-permute-start | bytes 983048 | tf_op jit(solution)/shard_map/ppermute | solution.py:20
  42.5 3.6 %collective-permute-done.9 = bf16[1280,256]{1,0:T(8,128)(2,1)S(1)} collective-permute-done((bf16[1280,256]{1,0:T(8,128)(2,1)S(1)}, bf16[1280,256]{1,0:T(8,128)(2,1)S(1)}, u32[]{:S(2)}, u32[]{:S(2)}) %collective-permute-start.9) | collective-permute-done | bytes 655392 | tf_op jit(solution)/shard_map/ppermute | solution.py:20
  46.3 4.2 %collective-permute-done.8 = bf16[1920,128]{1,0:T(8,128)(2,1)S(1)} collective-permute-done((bf16[1920,128]{1,0:T(8,128)(2,1)S(1)}, bf16[1920,128]{1,0:T(8,128)(2,1)S(1)}, u32[]{:S(2)}, u32[]{:S(2)}) %collective-permute-start.8) | collective-permute-done | bytes 491552 | tf_op jit(solution)/shard_map/ppermute | solution.py:20
  50.6 2.6 %collective-permute-start.14 = (bf16[640,256]{1,0:T(8,128)(2,1)S(1)}, bf16[640,256]{1,0:T(8,128)(2,1)S(1)}, u32[]{:S(2)}, u32[]{:S(2)}) collective-permute-start(bf16[640,256]{1,0:T(8,128)(2,1)S(1)} %pad_maximum_fusion.1), channel_id=1, source_target_pairs={{0,2},{1,3},{2,0},{3,1},{4,6},{5,7},{6,4},{7,5},{8,10},{9,11},{10,... | collective-permute-start | bytes 983048 | tf_op jit(solution)/shard_map/ppermute | solution.py:20
  53.2 1.4 %collective-permute-start.5 = (bf16[640,256]{1,0:T(8,128)(2,1)S(1)}, bf16[640,256]{1,0:T(8,128)(2,1)S(1)}, u32[]{:S(2)}, u32[]{:S(2)}) collective-permute-start(bf16[640,256]{1,0:T(8,128)(2,1)S(1)} %slice.457), channel_id=1, source_target_pairs={{0,16},{4,20},{8,24},{12,28},{16,0},{20,4},{24,8},{28,12},{1,17},{... | collective-permute-start | bytes 983048 | tf_op jit(solution)/shard_map/ppermute | solution.py:20
  54.9 0.7 collective-permute-start.12
  55.6 0.4 collective-permute-start.13
  56.0 7.7 %collective-permute-done.5 = bf16[640,256]{1,0:T(8,128)(2,1)S(1)} collective-permute-done((bf16[640,256]{1,0:T(8,128)(2,1)S(1)}, bf16[640,256]{1,0:T(8,128)(2,1)S(1)}, u32[]{:S(2)}, u32[]{:S(2)}) %collective-permute-start.5) | collective-permute-done | bytes 327712 | tf_op jit(solution)/shard_map/ppermute | solution.py:20
  64.0 1.3 %collective-permute-start.11 = (bf16[320,256]{1,0:T(8,128)(2,1)S(1)}, bf16[320,256]{1,0:T(8,128)(2,1)S(1)}, u32[]{:S(2)}, u32[]{:S(2)}) collective-permute-start(bf16[320,256]{1,0:T(8,128)(2,1)S(1)} %pad_maximum_fusion.4), channel_id=1, source_target_pairs={{0,1},{1,0},{2,3},{3,2},{4,5},{5,4},{6,7},{7,6},{8,9},{9,8},{10,11... | collective-permute-start | bytes 491528 | tf_op jit(solution)/shard_map/ppermute | solution.py:20
  65.2 2.4 %collective-permute-done.14 = bf16[640,256]{1,0:T(8,128)(2,1)S(1)} collective-permute-done((bf16[640,256]{1,0:T(8,128)(2,1)S(1)}, bf16[640,256]{1,0:T(8,128)(2,1)S(1)}, u32[]{:S(2)}, u32[]{:S(2)}) %collective-permute-start.14) | collective-permute-done | bytes 327712 | tf_op jit(solution)/shard_map/ppermute | solution.py:20
  67.9 0.7 collective-permute-start.19
  68.7 0.2 collective-permute-start.10
  69.0 1.9 %collective-permute-start.17 = (bf16[320,128]{1,0:T(8,128)(2,1)S(1)}, bf16[320,128]{1,0:T(8,128)(2,1)S(1)}, u32[]{:S(2)}, u32[]{:S(2)}) collective-permute-start(bf16[320,128]{1,0:T(8,128)(2,1)S(1)} %pad_maximum_fusion.6), channel_id=1, source_target_pairs={{0,1},{1,0},{2,3},{3,2},{4,5},{5,4},{6,7},{7,6},{8,9},{9,8},{10,11... | collective-permute-start | bytes 245768 | tf_op jit(solution)/shard_map/ppermute | solution.py:20
  70.9 0.2 collective-permute-start.18
  71.2 4.6 %collective-permute-done.10 = bf16[320,256]{1,0:T(8,128)(2,1)S(1)} collective-permute-done((bf16[320,256]{1,0:T(8,128)(2,1)S(1)}, bf16[320,256]{1,0:T(8,128)(2,1)S(1)}, u32[]{:S(2)}, u32[]{:S(2)}) %collective-permute-start.10) | collective-permute-done | bytes 163872 | tf_op jit(solution)/shard_map/ppermute | solution.py:20
  76.0 1.6 %collective-permute-done.17 = bf16[320,128]{1,0:T(8,128)(2,1)S(1)} collective-permute-done((bf16[320,128]{1,0:T(8,128)(2,1)S(1)}, bf16[320,128]{1,0:T(8,128)(2,1)S(1)}, u32[]{:S(2)}, u32[]{:S(2)}) %collective-permute-start.17) | collective-permute-done | bytes 81952 | tf_op jit(solution)/shard_map/ppermute | solution.py:20
  77.5 1.4 %collective-permute-done.18 = bf16[480,128]{1,0:T(8,128)(2,1)S(1)} collective-permute-done((bf16[480,128]{1,0:T(8,128)(2,1)S(1)}, bf16[480,128]{1,0:T(8,128)(2,1)S(1)}, u32[]{:S(2)}, u32[]{:S(2)}) %collective-permute-start.18) | collective-permute-done | bytes 122912 | tf_op jit(solution)/shard_map/ppermute | solution.py:20
  79.1 1.8 %collective-permute-start.21 = (bf16[160,128]{1,0:T(8,128)(2,1)S(1)}, bf16[160,128]{1,0:T(8,128)(2,1)S(1)}, u32[]{:S(2)}, u32[]{:S(2)}) collective-permute-start(bf16[160,128]{1,0:T(8,128)(2,1)S(1)} %slice.466), channel_id=1, source_target_pairs={{0,2},{1,3},{2,0},{3,1},{4,6},{5,7},{6,4},{7,5},{8,10},{9,11},{10,... | collective-permute-start | bytes 122888 | tf_op jit(solution)/shard_map/ppermute | solution.py:20
  80.9 1.2 %collective-permute-start.22 = (bf16[240,128]{1,0:T(8,128)(2,1)S(1)}, bf16[240,128]{1,0:T(8,128)(2,1)S(1)}, u32[]{:S(2)}, u32[]{:S(2)}) collective-permute-start(bf16[240,128]{1,0:T(8,128)(2,1)S(1)} %pad_maximum_fusion.7), channel_id=1, source_target_pairs={{0,2},{1,3},{2,0},{3,1},{4,6},{5,7},{6,4},{7,5},{8,10},{9,11},{10,... | collective-permute-start | bytes 184328 | tf_op jit(solution)/shard_map/ppermute | solution.py:20
  82.1 1.8 %collective-permute-start.16 = (bf16[160,256]{1,0:T(8,128)(2,1)S(1)}, bf16[160,256]{1,0:T(8,128)(2,1)S(1)}, u32[]{:S(2)}, u32[]{:S(2)}) collective-permute-start(bf16[160,256]{1,0:T(8,128)(2,1)S(1)} %slice.462), channel_id=1, source_target_pairs={{0,2},{1,3},{2,0},{3,1},{4,6},{5,7},{6,4},{7,5},{8,10},{9,11},{10,... | collective-permute-start | bytes 245768 | tf_op jit(solution)/shard_map/ppermute | solution.py:20
  83.9 1.7 %collective-permute-start.20 = (bf16[160,256]{1,0:T(8,128)(2,1)S(1)}, bf16[160,256]{1,0:T(8,128)(2,1)S(1)}, u32[]{:S(2)}, u32[]{:S(2)}) collective-permute-start(bf16[160,256]{1,0:T(8,128)(2,1)S(1)} %slice.461), channel_id=1, source_target_pairs={{0,16},{4,20},{8,24},{12,28},{16,0},{20,4},{24,8},{28,12},{1,17},{... | collective-permute-start | bytes 245768 | tf_op jit(solution)/shard_map/ppermute | solution.py:20
  85.5 0.9 collective-permute-start.15
  86.5 3.6 %collective-permute-done.22 = bf16[240,128]{1,0:T(8,128)(2,1)S(1)} collective-permute-done((bf16[240,128]{1,0:T(8,128)(2,1)S(1)}, bf16[240,128]{1,0:T(8,128)(2,1)S(1)}, u32[]{:S(2)}, u32[]{:S(2)}) %collective-permute-start.22) | collective-permute-done | bytes 61472 | tf_op jit(solution)/shard_map/ppermute | solution.py:20
  90.2 3.5 %collective-permute-done.15 = bf16[160,256]{1,0:T(8,128)(2,1)S(1)} collective-permute-done((bf16[160,256]{1,0:T(8,128)(2,1)S(1)}, bf16[160,256]{1,0:T(8,128)(2,1)S(1)}, u32[]{:S(2)}, u32[]{:S(2)}) %collective-permute-start.15) | collective-permute-done | bytes 81952 | tf_op jit(solution)/shard_map/ppermute | solution.py:20
  93.9 0.9 fusion.12
  94.8 4.4 %all-to-all-start = ((f32[32,8,256]{2,1,0:T(8,128)}), f32[32,8,256]{2,1,0:T(8,128)S(1)}, u32[]{:S(2)}, u32[]{:S(2)}) async-start(f32[32,8,256]{2,1,0:T(8,128)} %bitcast.3), calls=%async_computation | async-start | bytes 524288 | tf_op jit(solution)/shard_map/all_to_all | solution.py:456
  99.3 2.2 %fusion = f32[8,2,8,128]{3,2,1,0:T(8,128)S(1)} fusion(f32[8,2,8,512]{3,2,1,0:T(8,128)S(1)} %get-tuple-element.146, f32[8,2,8]{2,1,0:T(2,128)S(1)} %get-tuple-element.142, f32[8,2,8]{2,1,0:T(2,128)S(1)} %multiply_maximum_fusion, bf16[8,512,256]{2,1,0:T(8,128)(2,1)} %param.19), kind=kOutput, calls=%fused_computation | convolution fusion | flops 16973824 | bytes 2425856 | tf_op jit(solution)/shard_map/rkgc,rckd->rkgd/dot_general | solution.py:486
  101.6 7.8 %all-to-all-done = f32[32,8,256]{2,1,0:T(8,128)S(1)} async-done(((f32[32,8,256]{2,1,0:T(8,128)}), f32[32,8,256]{2,1,0:T(8,128)S(1)}, u32[]{:S(2)}, u32[]{:S(2)}) %all-to-all-start) | async-done | bytes 262176 | tf_op jit(solution)/shard_map/all_to_all | solution.py:456
  109.5 0.6 bitcast_convert_fusion
  110.2 0.6 copy.47
  (110 shorter events, 2.8 us)
Async XLA Ops:
  0.6 12.6 %copy-start = (bf16[8,512,256]{2,1,0:T(8,128)(2,1)S(1)}, bf16[8,512,256]{2,1,0:T(8,128)(2,1)}, u32[]{:S(2)}) copy-start(bf16[8,512,256]{2,1,0:T(8,128)(2,1)} %param.18) | copy-start | bytes 6291460
  0.6 3.8 %copy-start.3 = (bf16[512,1024]{1,0:T(8,128)(2,1)S(1)}, bf16[512,1024]{1,0:T(8,128)(2,1)}, u32[]{:S(2)}) copy-start(bf16[512,1024]{1,0:T(8,128)(2,1)} %refs_2_.7) | copy-start | bytes 3145732
  0.7 3.8 %copy-start.10 = (s32[64]{0:T(128)S(1)}, s32[64]{0:T(128)}, u32[]{:S(2)}) copy-start(s32[64]{0:T(128)} %param.16) | copy-start | bytes 772
  3.9 10.1 %collective-permute-start = (bf16[2560,512]{1,0:T(8,128)(2,1)}, bf16[2560,512]{1,0:T(8,128)(2,1)}, u32[]{:S(2)}, u32[]{:S(2)}) collective-permute-start(bf16[2560,512]{1,0:T(8,128)(2,1)} %shard_map.140), channel_id=1, source_target_pairs={{0,4},{4,0},{8,12},{12,8},{16,20},{20,16},{24,28},{28,24},{1,5},{5... | collective-permute-start | bytes 7864328 | tf_op jit(solution)/shard_map/ppermute | solution.py:20
  4.4 9.5 %collective-permute-start.1 = (bf16[512,1024]{1,0:T(8,128)(2,1)S(1)}, bf16[512,1024]{1,0:T(8,128)(2,1)}, u32[]{:S(2)}, u32[]{:S(2)}) collective-permute-start(bf16[512,1024]{1,0:T(8,128)(2,1)S(1)} %copy-done.3), channel_id=1, source_target_pairs={{0,4},{4,0},{8,12},{12,8},{16,20},{20,16},{24,28},{28,24},{1,5},{5... | collective-permute-start | bytes 3145736 | tf_op jit(solution)/shard_map/ppermute | solution.py:20
  9.4 3.7 %copy-start.8 = (s32[8]{0:T(128)S(1)}, s32[8]{0:T(128)}, u32[]{:S(2)}) copy-start(s32[8]{0:T(128)} %param.23) | copy-start | bytes 100
  9.4 3.8 %copy-start.6 = (bf16[8,2048]{1,0:T(8,128)(2,1)S(1)}, bf16[8,2048]{1,0:T(8,128)(2,1)}, u32[]{:S(2)}) copy-start(bf16[8,2048]{1,0:T(8,128)(2,1)} %param.17) | copy-start | bytes 98308
  9.4 15.5 %collective-permute-start.4 = (bf16[1280,128]{1,0:T(8,128)(2,1)S(1)}, bf16[1280,128]{1,0:T(8,128)(2,1)S(1)}, u32[]{:S(2)}, u32[]{:S(2)}) collective-permute-start(bf16[1280,128]{1,0:T(8,128)(2,1)S(1)} %get-tuple-element.52), channel_id=1, source_target_pairs={{0,4},{4,0},{8,12},{12,8},{16,20},{20,16},{24,28},{28,24},{1,5},{5... | collective-permute-start | bytes 983048 | tf_op jit(solution)/shard_map/ppermute | solution.py:20
  13.2 11.4 %copy-start.9 = (bf16[8,256]{1,0:T(8,128)(2,1)S(1)}, bf16[8,256]{1,0:T(8,128)(2,1)}, u32[]{:S(2)}) copy-start(bf16[8,256]{1,0:T(8,128)(2,1)} %param.20) | copy-start | bytes 12292
  13.9 1.8 %copy-start.2 = (bf16[2560,512]{1,0:T(8,128)(2,1)S(1)}, bf16[2560,512]{1,0:T(8,128)(2,1)}, u32[]{:S(2)}) copy-start(bf16[2560,512]{1,0:T(8,128)(2,1)} %shard_map.139.refs_0_) | copy-start | bytes 7864324
  20.6 20.0 %collective-permute-start.2 = (bf16[1280,256]{1,0:T(8,128)(2,1)S(1)}, bf16[1280,256]{1,0:T(8,128)(2,1)S(1)}, u32[]{:S(2)}, u32[]{:S(2)}) collective-permute-start(bf16[1280,256]{1,0:T(8,128)(2,1)S(1)} %get-tuple-element.48), channel_id=1, source_target_pairs={{0,8},{4,12},{8,0},{12,4},{16,24},{20,28},{24,16},{28,20},{1,9},{5... | collective-permute-start | bytes 1966088 | tf_op jit(solution)/shard_map/ppermute | solution.py:20
  23.2 17.6 %collective-permute-start.3 = (bf16[1280,256]{1,0:T(8,128)(2,1)S(1)}, bf16[1280,256]{1,0:T(8,128)(2,1)S(1)}, u32[]{:S(2)}, u32[]{:S(2)}) collective-permute-start(bf16[1280,256]{1,0:T(8,128)(2,1)S(1)} %get-tuple-element.49), channel_id=1, source_target_pairs={{0,16},{4,20},{8,24},{12,28},{16,0},{20,4},{24,8},{28,12},{1,17},{... | collective-permute-start | bytes 1966088 | tf_op jit(solution)/shard_map/ppermute | solution.py:20
  28.9 17.4 %collective-permute-start.7 = (bf16[1280,128]{1,0:T(8,128)(2,1)S(1)}, bf16[1280,128]{1,0:T(8,128)(2,1)S(1)}, u32[]{:S(2)}, u32[]{:S(2)}) collective-permute-start(bf16[1280,128]{1,0:T(8,128)(2,1)S(1)} %get-tuple-element.59), channel_id=1, source_target_pairs={{0,8},{4,12},{8,0},{12,4},{16,24},{20,28},{24,16},{28,20},{1,9},{5... | collective-permute-start | bytes 983048 | tf_op jit(solution)/shard_map/ppermute | solution.py:20
  29.7 20.9 %collective-permute-start.8 = (bf16[1920,128]{1,0:T(8,128)(2,1)S(1)}, bf16[1920,128]{1,0:T(8,128)(2,1)S(1)}, u32[]{:S(2)}, u32[]{:S(2)}) collective-permute-start(bf16[1920,128]{1,0:T(8,128)(2,1)S(1)} %pad_maximum_fusion), channel_id=1, source_target_pairs={{0,16},{4,20},{8,24},{12,28},{16,0},{20,4},{24,8},{28,12},{1,17},{... | collective-permute-start | bytes 1474568 | tf_op jit(solution)/shard_map/ppermute | solution.py:20
  29.8 16.3 %collective-permute-start.9 = (bf16[1280,256]{1,0:T(8,128)(2,1)S(1)}, bf16[1280,256]{1,0:T(8,128)(2,1)S(1)}, u32[]{:S(2)}, u32[]{:S(2)}) collective-permute-start(bf16[1280,256]{1,0:T(8,128)(2,1)S(1)} %get-tuple-element.61), channel_id=1, source_target_pairs={{0,1},{1,0},{2,3},{3,2},{4,5},{5,4},{6,7},{7,6},{8,9},{9,8},{10,11... | collective-permute-start | bytes 1966088 | tf_op jit(solution)/shard_map/ppermute | solution.py:20
  41.2 22.5 %collective-permute-start.6 = (bf16[640,256]{1,0:T(8,128)(2,1)S(1)}, bf16[640,256]{1,0:T(8,128)(2,1)S(1)}, u32[]{:S(2)}, u32[]{:S(2)}) collective-permute-start(bf16[640,256]{1,0:T(8,128)(2,1)S(1)} %slice.456), channel_id=1, source_target_pairs={{0,8},{4,12},{8,0},{12,4},{16,24},{20,28},{24,16},{28,20},{1,9},{5... | collective-permute-start | bytes 983048 | tf_op jit(solution)/shard_map/ppermute | solution.py:20
  50.6 17.1 %collective-permute-start.14 = (bf16[640,256]{1,0:T(8,128)(2,1)S(1)}, bf16[640,256]{1,0:T(8,128)(2,1)S(1)}, u32[]{:S(2)}, u32[]{:S(2)}) collective-permute-start(bf16[640,256]{1,0:T(8,128)(2,1)S(1)} %pad_maximum_fusion.1), channel_id=1, source_target_pairs={{0,2},{1,3},{2,0},{3,1},{4,6},{5,7},{6,4},{7,5},{8,10},{9,11},{10,... | collective-permute-start | bytes 983048 | tf_op jit(solution)/shard_map/ppermute | solution.py:20
  53.2 10.5 %collective-permute-start.5 = (bf16[640,256]{1,0:T(8,128)(2,1)S(1)}, bf16[640,256]{1,0:T(8,128)(2,1)S(1)}, u32[]{:S(2)}, u32[]{:S(2)}) collective-permute-start(bf16[640,256]{1,0:T(8,128)(2,1)S(1)} %slice.457), channel_id=1, source_target_pairs={{0,16},{4,20},{8,24},{12,28},{16,0},{20,4},{24,8},{28,12},{1,17},{... | collective-permute-start | bytes 983048 | tf_op jit(solution)/shard_map/ppermute | solution.py:20
  54.9 12.9 %collective-permute-start.12 = (bf16[640,128]{1,0:T(8,128)(2,1)S(1)}, bf16[640,128]{1,0:T(8,128)(2,1)S(1)}, u32[]{:S(2)}, u32[]{:S(2)}) collective-permute-start(bf16[640,128]{1,0:T(8,128)(2,1)S(1)} %slice.460), channel_id=1, source_target_pairs={{0,16},{4,20},{8,24},{12,28},{16,0},{20,4},{24,8},{28,12},{1,17},{... | collective-permute-start | bytes 491528 | tf_op jit(solution)/shard_map/ppermute | solution.py:20
  55.6 12.2 %collective-permute-start.13 = (bf16[960,128]{1,0:T(8,128)(2,1)S(1)}, bf16[960,128]{1,0:T(8,128)(2,1)S(1)}, u32[]{:S(2)}, u32[]{:S(2)}) collective-permute-start(bf16[960,128]{1,0:T(8,128)(2,1)S(1)} %pad_maximum_fusion.2), channel_id=1, source_target_pairs={{0,8},{4,12},{8,0},{12,4},{16,24},{20,28},{24,16},{28,20},{1,9},{5... | collective-permute-start | bytes 737288 | tf_op jit(solution)/shard_map/ppermute | solution.py:20
  64.0 11.8 %collective-permute-start.11 = (bf16[320,256]{1,0:T(8,128)(2,1)S(1)}, bf16[320,256]{1,0:T(8,128)(2,1)S(1)}, u32[]{:S(2)}, u32[]{:S(2)}) collective-permute-start(bf16[320,256]{1,0:T(8,128)(2,1)S(1)} %pad_maximum_fusion.4), channel_id=1, source_target_pairs={{0,1},{1,0},{2,3},{3,2},{4,5},{5,4},{6,7},{7,6},{8,9},{9,8},{10,11... | collective-permute-start | bytes 491528 | tf_op jit(solution)/shard_map/ppermute | solution.py:20
  67.9 8.0 %collective-permute-start.19 = (bf16[320,256]{1,0:T(8,128)(2,1)S(1)}, bf16[320,256]{1,0:T(8,128)(2,1)S(1)}, u32[]{:S(2)}, u32[]{:S(2)}) collective-permute-start(bf16[320,256]{1,0:T(8,128)(2,1)S(1)} %slice.458), channel_id=1, source_target_pairs={{0,8},{4,12},{8,0},{12,4},{16,24},{20,28},{24,16},{28,20},{1,9},{5... | collective-permute-start | bytes 491528 | tf_op jit(solution)/shard_map/ppermute | solution.py:20
  68.7 7.1 %collective-permute-start.10 = (bf16[320,256]{1,0:T(8,128)(2,1)S(1)}, bf16[320,256]{1,0:T(8,128)(2,1)S(1)}, u32[]{:S(2)}, u32[]{:S(2)}) collective-permute-start(bf16[320,256]{1,0:T(8,128)(2,1)S(1)} %pad_maximum_fusion.3), channel_id=1, source_target_pairs={{0,1},{1,0},{2,3},{3,2},{4,5},{5,4},{6,7},{7,6},{8,9},{9,8},{10,11... | collective-permute-start | bytes 491528 | tf_op jit(solution)/shard_map/ppermute | solution.py:20
  69.0 8.5 %collective-permute-start.17 = (bf16[320,128]{1,0:T(8,128)(2,1)S(1)}, bf16[320,128]{1,0:T(8,128)(2,1)S(1)}, u32[]{:S(2)}, u32[]{:S(2)}) collective-permute-start(bf16[320,128]{1,0:T(8,128)(2,1)S(1)} %pad_maximum_fusion.6), channel_id=1, source_target_pairs={{0,1},{1,0},{2,3},{3,2},{4,5},{5,4},{6,7},{7,6},{8,9},{9,8},{10,11... | collective-permute-start | bytes 245768 | tf_op jit(solution)/shard_map/ppermute | solution.py:20
  70.9 8.0 %collective-permute-start.18 = (bf16[480,128]{1,0:T(8,128)(2,1)S(1)}, bf16[480,128]{1,0:T(8,128)(2,1)S(1)}, u32[]{:S(2)}, u32[]{:S(2)}) collective-permute-start(bf16[480,128]{1,0:T(8,128)(2,1)S(1)} %pad_maximum_fusion.5), channel_id=1, source_target_pairs={{0,1},{1,0},{2,3},{3,2},{4,5},{5,4},{6,7},{7,6},{8,9},{9,8},{10,11... | collective-permute-start | bytes 368648 | tf_op jit(solution)/shard_map/ppermute | solution.py:20
  75.9 17.8 %copy-start.5 = (f32[160,1024]{1,0:T(8,128)S(1)}, f32[160,1024]{1,0:T(8,128)}, u32[]{:S(2)}) copy-start(f32[160,1024]{1,0:T(8,128)} %param.14) | copy-start | bytes 1966084
  79.1 7.4 %collective-permute-start.21 = (bf16[160,128]{1,0:T(8,128)(2,1)S(1)}, bf16[160,128]{1,0:T(8,128)(2,1)S(1)}, u32[]{:S(2)}, u32[]{:S(2)}) collective-permute-start(bf16[160,128]{1,0:T(8,128)(2,1)S(1)} %slice.466), channel_id=1, source_target_pairs={{0,2},{1,3},{2,0},{3,1},{4,6},{5,7},{6,4},{7,5},{8,10},{9,11},{10,... | collective-permute-start | bytes 122888 | tf_op jit(solution)/shard_map/ppermute | solution.py:20
  80.9 9.3 %collective-permute-start.22 = (bf16[240,128]{1,0:T(8,128)(2,1)S(1)}, bf16[240,128]{1,0:T(8,128)(2,1)S(1)}, u32[]{:S(2)}, u32[]{:S(2)}) collective-permute-start(bf16[240,128]{1,0:T(8,128)(2,1)S(1)} %pad_maximum_fusion.7), channel_id=1, source_target_pairs={{0,2},{1,3},{2,0},{3,1},{4,6},{5,7},{6,4},{7,5},{8,10},{9,11},{10,... | collective-permute-start | bytes 184328 | tf_op jit(solution)/shard_map/ppermute | solution.py:20
  82.1 11.6 %collective-permute-start.16 = (bf16[160,256]{1,0:T(8,128)(2,1)S(1)}, bf16[160,256]{1,0:T(8,128)(2,1)S(1)}, u32[]{:S(2)}, u32[]{:S(2)}) collective-permute-start(bf16[160,256]{1,0:T(8,128)(2,1)S(1)} %slice.462), channel_id=1, source_target_pairs={{0,2},{1,3},{2,0},{3,1},{4,6},{5,7},{6,4},{7,5},{8,10},{9,11},{10,... | collective-permute-start | bytes 245768 | tf_op jit(solution)/shard_map/ppermute | solution.py:20
  83.9 9.8 %collective-permute-start.20 = (bf16[160,256]{1,0:T(8,128)(2,1)S(1)}, bf16[160,256]{1,0:T(8,128)(2,1)S(1)}, u32[]{:S(2)}, u32[]{:S(2)}) collective-permute-start(bf16[160,256]{1,0:T(8,128)(2,1)S(1)} %slice.461), channel_id=1, source_target_pairs={{0,16},{4,20},{8,24},{12,28},{16,0},{20,4},{24,8},{28,12},{1,17},{... | collective-permute-start | bytes 245768 | tf_op jit(solution)/shard_map/ppermute | solution.py:20
  85.5 8.1 %collective-permute-start.15 = (bf16[160,256]{1,0:T(8,128)(2,1)S(1)}, bf16[160,256]{1,0:T(8,128)(2,1)S(1)}, u32[]{:S(2)}, u32[]{:S(2)}) collective-permute-start(bf16[160,256]{1,0:T(8,128)(2,1)S(1)} %slice.463), channel_id=1, source_target_pairs={{0,2},{1,3},{2,0},{3,1},{4,6},{5,7},{6,4},{7,5},{8,10},{9,11},{10,... | collective-permute-start | bytes 245768 | tf_op jit(solution)/shard_map/ppermute | solution.py:20
  93.9 7.6 %copy-start.4 = (f32[160,1024]{1,0:T(8,128)}, f32[160,1024]{1,0:T(8,128)S(1)}, u32[]{:S(2)}) copy-start(f32[160,1024]{1,0:T(8,128)S(1)} %fusion.28) | copy-start | bytes 1966084
  94.8 14.6 %all-to-all-start = ((f32[32,8,256]{2,1,0:T(8,128)}), f32[32,8,256]{2,1,0:T(8,128)S(1)}, u32[]{:S(2)}, u32[]{:S(2)}) async-start(f32[32,8,256]{2,1,0:T(8,128)} %bitcast.3), calls=%async_computation | async-start | bytes 524288 | tf_op jit(solution)/shard_map/all_to_all | solution.py:456
  99.3 11.6 %copy-start.1 = (bf16[8,512,256]{2,1,0:T(8,128)(2,1)S(1)}, bf16[8,512,256]{2,1,0:T(8,128)(2,1)}, u32[]{:S(2)}) copy-start(bf16[8,512,256]{2,1,0:T(8,128)(2,1)} %param.18) | copy-start | bytes 6291460
  99.3 2.2 %copy-start.11 = (f32[2]{0:T(128)S(1)}, f32[2]{0:T(128)}, u32[]{:S(2)}) copy-start(f32[2]{0:T(128)} %param.22) | copy-start | bytes 28
  99.3 10.2 %copy-start.7 = (bf16[8,256]{1,0:T(8,128)(2,1)S(1)}, bf16[8,256]{1,0:T(8,128)(2,1)}, u32[]{:S(2)}) copy-start(bf16[8,256]{1,0:T(8,128)(2,1)} %param.21) | copy-start | bytes 12292

commit v5 on v4

--- a/solution.py
+++ b/solution.py
@@ -73,8 +73,8 @@
     kind = activations.dtype
     return pl.pallas_call(
         functools.partial(transpose_blocks, arranged, mine, units),
-        in_specs=[pl.BlockSpec(memory_space=pl.ANY)],
-        out_specs=pl.BlockSpec(memory_space=pl.ANY),
+        in_specs=[pl.BlockSpec(memory_space=pltpu.HBM)],
+        out_specs=pl.BlockSpec(memory_space=pltpu.HBM),
         out_shape=jax.ShapeDtypeStruct((count * width, tokens), kind),
         scratch_shapes=[
             pltpu.VMEM((count, tokens, width), kind),
@@ -166,7 +166,7 @@
     return pl.pallas_call(
         functools.partial(multiply, wanted, rows, blocks, base),
         out_shape=shapes,
-        in_specs=[pl.BlockSpec(memory_space=pl.ANY)] * 4,
+        in_specs=[pl.BlockSpec(memory_space=pltpu.HBM)] * 4,
         out_specs=[pl.BlockSpec(memory_space=pltpu.VMEM)] * len(shapes),
         scratch_shapes=[
             pltpu.VMEM((total, 2 * tokens), lefts[0].dtype),
@@ -180,8 +180,7 @@
 
 def pick_rows(arranged, units, place, table, tail, *refs):
     outs, (slabs, found, flipped, sems) = refs[:2], refs[2:]
-    here = table.shape[0]
-    whole = here // SLAB * SLAB
+    whole = (table.shape[0] - 1) // SLAB * SLAB
     tokens, width_all = found.shape
     width = flipped.shape[0]
     rows = width // units
@@ -189,34 +188,32 @@
     folds = lanes // tokens
     lines = rows // folds
 
-    def slab_copy(source, k):
-        return pltpu.make_async_copy(source, slabs.at[k], sems.at[k])
+    def slab_copy(k):
+        start = pl.multiple_of(lax.div(place[k], SLAB) * SLAB, SLAB)
+        return pltpu.make_async_copy(table.at[pl.ds(start, SLAB)], slabs.at[k], sems.at[k])
+
+    def add_row(k, held):
+        at = lax.broadcasted_iota(jnp.int32, held.shape, 0)
+        chosen = jnp.where(at == lax.rem(place[k], SLAB), held.astype(jnp.float32), 0.0)
+        found[k : k + 1, :] = jnp.sum(chosen, axis=0, keepdims=True)
 
     for k in range(tokens):
-        inside = place[k]
-
-        @pl.when((inside >= 0) & (inside < whole))
+
+        @pl.when((place[k] >= 0) & (place[k] < whole))
         def _():
-            start = pl.multiple_of(lax.div(inside, SLAB) * SLAB, SLAB)
-            slab_copy(table.at[pl.ds(start, SLAB)], k).start()
-
-        @pl.when(inside >= whole)
-        def _():
-            slab_copy(tail, k).start()
+            slab_copy(k).start()
 
     found[...] = jnp.zeros_like(found)
     for k in range(tokens):
-        inside = place[k]
-
-        @pl.when(inside >= 0)
+
+        @pl.when((place[k] >= 0) & (place[k] < whole))
         def _():
-            slab_copy(tail, k).wait()
-            line = jnp.where(inside < whole, lax.rem(inside, SLAB), inside - (here - SLAB))
-            held = slabs[k].astype(jnp.float32)
-            at = lax.broadcasted_iota(jnp.int32, held.shape, 0)
-            found[k : k + 1, :] = jnp.sum(
-                jnp.where(at == line, held, 0.0), axis=0, keepdims=True
-            )
+            slab_copy(k).wait()
+            add_row(k, slabs[k])
+
+        @pl.when(place[k] >= whole)
+        def _():
+            add_row(k, tail[...])
 
     core, upper, t = own_place()
     for side, out in zip((1 - core, core), outs):
@@ -231,6 +228,61 @@
                 ]
                 put = (j * units + unit) * lines
                 out[put : put + lines, :] = jnp.concatenate(pieces, axis=1).astype(out.dtype)
+
+
+def add_and_split(plans, *refs):
+    refs = list(refs)
+    takes = [[refs.pop(0) for _ in plan] + [refs.pop(0)] for plan in plans]
+    gives = [[refs.pop(0) for _ in plan] + [refs.pop(0)] for plan in plans]
+    for plan, inputs, outputs in zip(plans, takes, gives):
+        got, sent = inputs[-1], outputs[-1]
+        start = put = 0
+        for (size, order, go, keep), value, kept in zip(plan, inputs, outputs):
+
+            def sum_of(low, high):
+                pieces = []
+                for at in range(low, high):
+                    place, lies = order[at]
+                    pieces.append(
+                        value[place * size : (place + 1) * size, :]
+                        + got[start + lies * size : start + (lies + 1) * size, :].astype(
+                            jnp.float32
+                        )
+                    )
+                return pieces
+
+            for at, piece in enumerate(sum_of(0, go)):
+                sent[put + at * size : put + (at + 1) * size, :] = piece.astype(sent.dtype)
+            for at, piece in enumerate(sum_of(go, go + keep)):
+                kept[at * size : (at + 1) * size, :] = piece
+            start += len(order) * size
+            put += go * size
+
+
+def combine(plans, values, got):
+    columns = [arrived.shape[1] for arrived in got]
+    outs = []
+    for plan, width in zip(plans, columns):
+        outs += [
+            jax.ShapeDtypeStruct((keep * size, width), jnp.float32) for size, _, _, keep in plan
+        ]
+        total = sum(size * go for size, _, go, _ in plan)
+        outs.append(jax.ShapeDtypeStruct((total, width), jnp.bfloat16))
+    arrays = [array for parts, arrived in zip(values, got) for array in parts + [arrived]]
+    results = pl.pallas_call(
+        functools.partial(add_and_split, plans),
+        in_specs=[pl.BlockSpec(memory_space=pltpu.VMEM)] * len(arrays),
+        out_specs=[pl.BlockSpec(memory_space=pltpu.VMEM)] * len(outs),
+        out_shape=outs,
+        compiler_params=pltpu.CompilerParams(vmem_limit_bytes=VMEM // 4),
+        cost_estimate=pl.CostEstimate(flops=1, bytes_accessed=1, transcendentals=0),
+    )(*arrays)
+    results = list(results)
+    kept, sent = [], []
+    for plan in plans:
+        kept.append([results.pop(0) for _ in plan])
+        sent.append(results.pop(0))
+    return kept, sent
 
 
 def fold_unit(part, lanes):
@@ -283,10 +335,11 @@
     shape = jax.ShapeDtypeStruct((len(arranged) * width * tokens // lanes, lanes), kind)
     return pl.pallas_call(
         functools.partial(pick_rows, arranged, units),
+        grid=(1,),
         in_specs=[
             pl.BlockSpec(memory_space=pltpu.SMEM),
-            pl.BlockSpec(memory_space=pl.ANY),
-            pl.BlockSpec(memory_space=pl.ANY),
+            pl.BlockSpec(memory_space=pltpu.HBM),
+            pl.BlockSpec((SLAB, width_all), lambda i: ((here - 1) // SLAB, 0)),
         ],
         out_specs=[pl.BlockSpec(memory_space=pltpu.VMEM)] * 2,
         out_shape=[shape, shape],
@@ -298,7 +351,7 @@
         ],
         compiler_params=pltpu.CompilerParams(vmem_limit_bytes=VMEM // 2),
         cost_estimate=pl.CostEstimate(flops=1, bytes_accessed=1, transcendentals=0),
-    )(place, embed_table, embed_table[here - SLAB :])
+    )(place, embed_table, embed_table)
 
 
 def dot32(left, right):
@@ -409,26 +462,51 @@
             added.append(value + take(piece, landed, kept, size).astype(jnp.float32))
         values[index], held[index] = added, kept
 
+    def forward(index, step, following):
+        gone, kept = split(held[index], step)
+        landed = [flip(p, step) for p in gone]
+        go, keep = split(kept, following)
+        plan = [
+            (size, [(held_now[index].index(p), landed.index(p)) for p in go + keep], len(go), len(keep))
+            for size in sizes[index]
+        ]
+        held[index], held_now[index] = kept, keep
+        return plan
+
+    held_now = {
+        index: split(places, orders[index][0])[1] for index in range(5)
+    }
+    plain = rows % 32 or any(size % 16 for size in sizes[4])
     for at in range(len(one)):
         for group in ((0, 1), (2,), (3, 4)):
             tied = lax.optimization_barrier([got[index] for index in group] + [token])
             for index, arrived in zip(group, tied):
                 got[index] = arrived
-                receive(index, orders[index][at])
             if at + 1 == len(one):
+                for index in group:
+                    receive(index, orders[index][at])
                 continue
-            outgoing = []
-            for index in group:
-                gone, kept = split(held[index], orders[index][at + 1])
-                pieces = [
-                    take(value, held[index], gone, size).astype(jnp.bfloat16)
-                    for value, size in zip(values[index], sizes[index])
-                ]
-                values[index] = [
-                    take(value, held[index], kept, size)
-                    for value, size in zip(values[index], sizes[index])
-                ]
-                outgoing.append(jnp.concatenate(pieces))
+            if plain:
+                outgoing = []
+                for index in group:
+                    receive(index, orders[index][at])
+                    gone, kept = split(held[index], orders[index][at + 1])
+                    pieces = [
+                        take(value, held[index], gone, size).astype(jnp.bfloat16)
+                        for value, size in zip(values[index], sizes[index])
+                    ]
+                    values[index] = [
+                        take(value, held[index], kept, size)
+                        for value, size in zip(values[index], sizes[index])
+                    ]
+                    outgoing.append(jnp.concatenate(pieces))
+            else:
+                plans = [forward(i, orders[i][at], orders[i][at + 1]) for i in group]
+                kept, outgoing = combine(
+                    plans, [values[i] for i in group], [got[i] for i in group]
+                )
+                for index, value in zip(group, kept):
+                    values[index] = value
             outgoing = lax.optimization_barrier(outgoing)
             token = outgoing[-1]
             for index, value in zip(group, outgoing):

time: 111 us -> 101 us (0.910)
  waiting for transfers between devices: 40.6 us -> 31.6 us
  local copies, waits for them, and re-layouts: 4.08 us -> 2.57 us
  other arithmetic: 2.67 us -> 1.43 us
    ppermute x23, waiting for transfers between devices: 32.8 us -> 23.6 us  [exchange(): lax.ppermute(value, axis, [(i, i ^ mask) for i in range(lax.axis_size(axi...]
    ppermute x23, starting transfers between devices: 26.2 us -> 28.1 us  [exchange(): lax.ppermute(value, axis, [(i, i ^ mask) for i in range(lax.axis_size(axi...]
    slice x30 -> x0, local copies, waits for them, and re-layouts: 1.49 us -> none  [the longest x1 0.99 us: lookup(): embed_table[here - SLAB:]]
    pallas_call x1 -> x10, Pallas kernels: 3.92 us -> 5.06 us  [the longest x1 4.17 us: lookup(): pl.pallas_call(functools.partial(pick_rows, arranged, units), grid=(1,),...]
    unnamed x25 -> x23, local copies, waits for them, and re-layouts: 2.44 us -> 2.41 us
  transfers between devices with their start and end apart: 24 -> 24, of which waited for: 11 -> 12; matrix products, arithmetic and copies ran while one was open for 6% -> 4% of each run, Pallas kernels for 22% -> 20%
where the time goes in v5:
time: 101 us
  waiting for transfers between devices  31.6 us (31%)
  starting transfers between devices  31.5 us (31%)
  Pallas kernels  28.7 us (28%)
  matrix products  3.87 us (4%)
  local copies, waits for them, and re-layouts  2.57 us (3%)
  other arithmetic  1.43 us (1%)
    ppermute x23, starting transfers between devices, exchange(): lax.ppermute(value, axis, [(i, i ^ mask) for i in range(lax.axis_size(axi...  28.1 us
    ppermute x23, waiting for transfers between devices, exchange(): lax.ppermute(value, axis, [(i, i ^ mask) for i in range(lax.axis_size(axi...  23.6 us
    pallas_call x4, Pallas kernels, products(): pl.pallas_call(functools.partial(multiply, wanted, rows, blocks, base), o...  17.4 us
    all_to_all x1, waiting for transfers between devices, per_device(): lax.all_to_all(blocks_own, ('fsdp', 'tp'), split_axis=0, concat_axis=0)  8.01 us
    pallas_call x2, Pallas kernels, pack(): pl.pallas_call(functools.partial(transpose_blocks, arranged, mine, units)...  6.27 us
    pallas_call x1, Pallas kernels, lookup(): pl.pallas_call(functools.partial(pick_rows, arranged, units), grid=(1,),...  4.17 us
    all_to_all x1, starting transfers between devices, per_device(): lax.all_to_all(blocks_own, ('fsdp', 'tp'), split_axis=0, concat_axis=0)  3.4 us
    unnamed x23, local copies, waits for them, and re-layouts  2.41 us
  transfers between devices with their start and end apart: 24, of which 12 were waited for; matrix products, arithmetic and copies ran while one was open for 4% of the time, Pallas kernels for 20%

profile of v5, /device:TPU:0, one launch (start us, length us, event | category | flops | bytes accessed | tf_op | source)
XLA Modules:
  0.0 100.7 jit_solution(6621293073913040663)
XLA Ops:
  0.7 3.2 %shard_map.140 = bf16[2560,512]{1,0:T(8,128)(2,1)} custom-call(bf16[512,5120]{1,0:T(8,128)(2,1)} %source.3), custom_call_target="tpu_custom_call" | custom-call | bytes 5242880 | tf_op jit(solution)/shard_map/pallas_call | solution.py:74
  3.9 0.5 collective-permute-start
  4.5 4.2 %shard_map.144 = (bf16[1280,128]{1,0:T(8,128)(2,1)S(1)}, bf16[1280,128]{1,0:T(8,128)(2,1)S(1)}) custom-call(s32[64]{0:T(128)S(1)} %and_select_fusion.place, bf16[4748,5120]{1,0:T(8,128)(2,1)} %tail.1, bf16[4748,5120]{1,0:T(8,128)(2,1)} %tail.1), custom_call_target="tpu_custom_call" | custom-call | flops 1 | bytes 1 | tf_op jit(solution)/shard_map/pallas_call | solution.py:336
  8.7 1.2 %collective-permute-start.4 = (bf16[1280,128]{1,0:T(8,128)(2,1)S(1)}, bf16[1280,128]{1,0:T(8,128)(2,1)S(1)}, u32[]{:S(2)}, u32[]{:S(2)}) collective-permute-start(bf16[1280,128]{1,0:T(8,128)(2,1)S(1)} %get-tuple-element.85), channel_id=1, source_target_pairs={{0,4},{4,0},{8,12},{12,8},{16,20},{20,16},{24,28},{28,24},{1,5},{5... | collective-permute-start | bytes 983048 | tf_op jit(solution)/shard_map/ppermute | solution.py:20
  9.9 3.0 %shard_map.139.refs_0_ = bf16[2560,512]{1,0:T(8,128)(2,1)} custom-call(bf16[512,5120]{1,0:T(8,128)(2,1)} %source.3), custom_call_target="tpu_custom_call" | custom-call | bytes 5242880 | tf_op jit(solution)/shard_map/pallas_call | solution.py:74
  13.1 1.7 %copy-done.1 = bf16[2560,512]{1,0:T(8,128)(2,1)S(1)} copy-done((bf16[2560,512]{1,0:T(8,128)(2,1)S(1)}, bf16[2560,512]{1,0:T(8,128)(2,1)}, u32[]{:S(2)}) %copy-start.1) | copy-done | bytes 2621464
  14.8 4.9 %shard_map.142 = (bf16[1280,256]{1,0:T(8,128)(2,1)S(1)}, bf16[1280,256]{1,0:T(8,128)(2,1)S(1)}, bf16[1280,256]{1,0:T(8,128)(2,1)S(1)}) custom-call(bf16[2560,512]{1,0:T(8,128)(2,1)S(1)} %copy-done.1, bf16[2560,512]{1,0:T(8,128)(2,1)} %collective-permute-done.refs_1_, bf16[512,1024]{1,0:T(8,128)(2,1)S(1)} %copy-done.2, ...), custom_call_target="tpu_custom_call" | custom-call | flops 1 | bytes 1 | tf_op jit(solution)/shard_map/pallas_call | solution.py:166
  19.7 2.5 %collective-permute-start.2 = (bf16[1280,256]{1,0:T(8,128)(2,1)S(1)}, bf16[1280,256]{1,0:T(8,128)(2,1)S(1)}, u32[]{:S(2)}, u32[]{:S(2)}) collective-permute-start(bf16[1280,256]{1,0:T(8,128)(2,1)S(1)} %get-tuple-element.81), channel_id=1, source_target_pairs={{0,8},{4,12},{8,0},{12,4},{16,24},{20,28},{24,16},{28,20},{1,9},{5... | collective-permute-start | bytes 1966088 | tf_op jit(solution)/shard_map/ppermute | solution.py:20
  22.1 1.7 %collective-permute-start.3 = (bf16[1280,256]{1,0:T(8,128)(2,1)S(1)}, bf16[1280,256]{1,0:T(8,128)(2,1)S(1)}, u32[]{:S(2)}, u32[]{:S(2)}) collective-permute-start(bf16[1280,256]{1,0:T(8,128)(2,1)S(1)} %get-tuple-element.82), channel_id=1, source_target_pairs={{0,16},{4,20},{8,24},{12,28},{16,0},{20,4},{24,8},{28,12},{1,17},{... | collective-permute-start | bytes 1966088 | tf_op jit(solution)/shard_map/ppermute | solution.py:20
  23.8 1.7 %collective-permute-start.9 = (bf16[1280,256]{1,0:T(8,128)(2,1)S(1)}, bf16[1280,256]{1,0:T(8,128)(2,1)S(1)}, u32[]{:S(2)}, u32[]{:S(2)}) collective-permute-start(bf16[1280,256]{1,0:T(8,128)(2,1)S(1)} %get-tuple-element.97), channel_id=1, source_target_pairs={{0,1},{1,0},{2,3},{3,2},{4,5},{5,4},{6,7},{7,6},{8,9},{9,8},{10,11... | collective-permute-start | bytes 1966088 | tf_op jit(solution)/shard_map/ppermute | solution.py:20
  25.5 3.8 %shard_map.143 = (bf16[1280,128]{1,0:T(8,128)(2,1)S(1)}, bf16[1280,128]{1,0:T(8,128)(2,1)S(1)}) custom-call(bf16[2560,512]{1,0:T(8,128)(2,1)S(1)} %copy-done.1, bf16[2560,512]{1,0:T(8,128)(2,1)} %collective-permute-done.refs_1_, bf16[512,1024]{1,0:T(8,128)(2,1)S(1)} %copy-done.2, bf16[512,1024]{1,0:T(8,128)(2,1)} %collective-permute-done.1.refs_3_), custom_call_target="tpu_custom_call" | custom-call | flops 1 | bytes 1 | tf_op jit(solution)/shard_map/pallas_call | solution.py:166
  29.4 0.2 collective-permute-start.7
  29.6 1.0 collective-permute-start.8
  30.6 4.9 %shard_map.141 = (f32[1280,256]{1,0:T(8,128)S(1)}, f32[1280,256]{1,0:T(8,128)S(1)}, f32[1280,256]{1,0:T(8,128)S(1)}) custom-call(bf16[2560,512]{1,0:T(8,128)(2,1)S(1)} %copy-done.1, bf16[2560,512]{1,0:T(8,128)(2,1)} %collective-permute-done.refs_1_, bf16[512,1024]{1,0:T(8,128)(2,1)S(1)} %copy-done.2, bf16[512,1024]{1,0:T(8,128)(2,1)} %collective-permute-done.1.refs_3_), custom_call_target="tpu_custom_call" | custom-call | flops 1 | bytes 1 | tf_op jit(solution)/shard_map/pallas_call | solution.py:166
  35.5 2.2 %collective-permute-done.2.refs_1_ = bf16[1280,256]{1,0:T(8,128)(2,1)S(1)} collective-permute-done((bf16[1280,256]{1,0:T(8,128)(2,1)S(1)}, bf16[1280,256]{1,0:T(8,128)(2,1)S(1)}, u32[]{:S(2)}, u32[]{:S(2)}) %collective-permute-start.2) | collective-permute-done | bytes 655392 | tf_op jit(solution)/shard_map/ppermute | solution.py:20
  37.7 2.0 %collective-permute-done.3.refs_3_ = bf16[1280,256]{1,0:T(8,128)(2,1)S(1)} collective-permute-done((bf16[1280,256]{1,0:T(8,128)(2,1)S(1)}, bf16[1280,256]{1,0:T(8,128)(2,1)S(1)}, u32[]{:S(2)}, u32[]{:S(2)}) %collective-permute-start.3) | collective-permute-done | bytes 655392 | tf_op jit(solution)/shard_map/ppermute | solution.py:20
  39.7 0.3 shard_map.145
  40.0 1.8 %collective-permute-start.5 = (bf16[640,256]{1,0:T(8,128)(2,1)S(1)}, bf16[640,256]{1,0:T(8,128)(2,1)S(1)}, u32[]{:S(2)}, u32[]{:S(2)}) collective-permute-start(bf16[640,256]{1,0:T(8,128)(2,1)S(1)} %get-tuple-element.92), channel_id=1, source_target_pairs={{0,16},{4,20},{8,24},{12,28},{16,0},{20,4},{24,8},{28,12},{1,17},{... | collective-permute-start | bytes 983048 | tf_op jit(solution)/shard_map/ppermute | solution.py:20
  41.8 0.4 collective-permute-start.6
  42.3 2.9 %collective-permute-start.14 = (bf16[640,256]{1,0:T(8,128)(2,1)S(1)}, bf16[640,256]{1,0:T(8,128)(2,1)S(1)}, u32[]{:S(2)}, u32[]{:S(2)}) collective-permute-start(bf16[640,256]{1,0:T(8,128)(2,1)S(1)} %get-tuple-element.99), channel_id=1, source_target_pairs={{0,2},{1,3},{2,0},{3,1},{4,6},{5,7},{6,4},{7,5},{8,10},{9,11},{10,... | collective-permute-start | bytes 983048 | tf_op jit(solution)/shard_map/ppermute | solution.py:20
  45.2 0.7 fusion.29
  45.9 3.8 %shard_map.146 = (f32[1280,128]{1,0:T(8,128)S(1)}, f32[1280,128]{1,0:T(8,128)S(1)}) custom-call(bf16[2560,512]{1,0:T(8,128)(2,1)S(1)} %copy-done.1, bf16[2560,512]{1,0:T(8,128)(2,1)} %collective-permute-done.refs_1_, bf16[512,1024]{1,0:T(8,128)(2,1)S(1)} %copy-done.2, bf16[512,1024]{1,0:T(8,128)(2,1)} %collective-permute-done.1.refs_3_), custom_call_target="tpu_custom_call" | custom-call | flops 1 | bytes 1 | tf_op jit(solution)/shard_map/pallas_call | solution.py:166
  49.8 0.5 collective-permute-done.8.refs_4_
  50.4 1.0 %collective-permute-start.13 = (bf16[960,128]{1,0:T(8,128)(2,1)S(1)}, bf16[960,128]{1,0:T(8,128)(2,1)S(1)}, u32[]{:S(2)}, u32[]{:S(2)}) collective-permute-start(bf16[960,128]{1,0:T(8,128)(2,1)S(1)} %get-tuple-element.105), channel_id=1, source_target_pairs={{0,8},{4,12},{8,0},{12,4},{16,24},{20,28},{24,16},{28,20},{1,9},{5... | collective-permute-start | bytes 737288 | tf_op jit(solution)/shard_map/ppermute | solution.py:20
  51.4 0.1 fusion.21
  51.5 1.2 %collective-permute-start.12 = (bf16[640,128]{1,0:T(8,128)(2,1)S(1)}, bf16[640,128]{1,0:T(8,128)(2,1)S(1)}, u32[]{:S(2)}, u32[]{:S(2)}) collective-permute-start(bf16[640,128]{1,0:T(8,128)(2,1)S(1)} %get-tuple-element.115), channel_id=1, source_target_pairs={{0,16},{4,20},{8,24},{12,28},{16,0},{20,4},{24,8},{28,12},{1,17},{... | collective-permute-start | bytes 491528 | tf_op jit(solution)/shard_map/ppermute | solution.py:20
  52.7 4.5 %collective-permute-done.5.refs_1_ = bf16[640,256]{1,0:T(8,128)(2,1)S(1)} collective-permute-done((bf16[640,256]{1,0:T(8,128)(2,1)S(1)}, bf16[640,256]{1,0:T(8,128)(2,1)S(1)}, u32[]{:S(2)}, u32[]{:S(2)}) %collective-permute-start.5) | collective-permute-done | bytes 327712 | tf_op jit(solution)/shard_map/ppermute | solution.py:20
  57.4 1.6 %collective-permute-start.10 = (bf16[320,256]{1,0:T(8,128)(2,1)S(1)}, bf16[320,256]{1,0:T(8,128)(2,1)S(1)}, u32[]{:S(2)}, u32[]{:S(2)}) collective-permute-start(bf16[320,256]{1,0:T(8,128)(2,1)S(1)} %get-tuple-element.112), channel_id=1, source_target_pairs={{0,1},{1,0},{2,3},{3,2},{4,5},{5,4},{6,7},{7,6},{8,9},{9,8},{10,11... | collective-permute-start | bytes 491528 | tf_op jit(solution)/shard_map/ppermute | solution.py:20
  59.0 0.5 collective-permute-start.11
  59.6 0.4 collective-permute-start.19
  60.1 2.0 %collective-permute-start.17 = (bf16[320,128]{1,0:T(8,128)(2,1)S(1)}, bf16[320,128]{1,0:T(8,128)(2,1)S(1)}, u32[]{:S(2)}, u32[]{:S(2)}) collective-permute-start(bf16[320,128]{1,0:T(8,128)(2,1)S(1)} %get-tuple-element.135), channel_id=1, source_target_pairs={{0,1},{1,0},{2,3},{3,2},{4,5},{5,4},{6,7},{7,6},{8,9},{9,8},{10,11... | collective-permute-start | bytes 245768 | tf_op jit(solution)/shard_map/ppermute | solution.py:20
  62.2 0.2 fusion.14
  62.4 2.2 %collective-permute-done.10.refs_1_ = bf16[320,256]{1,0:T(8,128)(2,1)S(1)} collective-permute-done((bf16[320,256]{1,0:T(8,128)(2,1)S(1)}, bf16[320,256]{1,0:T(8,128)(2,1)S(1)}, u32[]{:S(2)}, u32[]{:S(2)}) %collective-permute-start.10) | collective-permute-done | bytes 163872 | tf_op jit(solution)/shard_map/ppermute | solution.py:20
  64.6 3.3 %collective-permute-done.11.refs_3_ = bf16[320,256]{1,0:T(8,128)(2,1)S(1)} collective-permute-done((bf16[320,256]{1,0:T(8,128)(2,1)S(1)}, bf16[320,256]{1,0:T(8,128)(2,1)S(1)}, u32[]{:S(2)}, u32[]{:S(2)}) %collective-permute-start.11) | collective-permute-done | bytes 163872 | tf_op jit(solution)/shard_map/ppermute | solution.py:20
  68.0 0.8 collective-permute-done.17.refs_1_
  68.8 1.3 %collective-permute-done.18.refs_4_ = bf16[480,128]{1,0:T(8,128)(2,1)S(1)} collective-permute-done((bf16[480,128]{1,0:T(8,128)(2,1)S(1)}, bf16[480,128]{1,0:T(8,128)(2,1)S(1)}, u32[]{:S(2)}, u32[]{:S(2)}) %collective-permute-start.18) | collective-permute-done | bytes 122912 | tf_op jit(solution)/shard_map/ppermute | solution.py:20
  70.2 2.9 %collective-permute-start.21 = (bf16[160,128]{1,0:T(8,128)(2,1)S(1)}, bf16[160,128]{1,0:T(8,128)(2,1)S(1)}, u32[]{:S(2)}, u32[]{:S(2)}) collective-permute-start(bf16[160,128]{1,0:T(8,128)(2,1)S(1)} %get-tuple-element.152), channel_id=1, source_target_pairs={{0,2},{1,3},{2,0},{3,1},{4,6},{5,7},{6,4},{7,5},{8,10},{9,11},{10,... | collective-permute-start | bytes 122888 | tf_op jit(solution)/shard_map/ppermute | solution.py:20
  73.2 2.9 %collective-permute-start.16 = (bf16[160,256]{1,0:T(8,128)(2,1)S(1)}, bf16[160,256]{1,0:T(8,128)(2,1)S(1)}, u32[]{:S(2)}, u32[]{:S(2)}) collective-permute-start(bf16[160,256]{1,0:T(8,128)(2,1)S(1)} %get-tuple-element.133), channel_id=1, source_target_pairs={{0,2},{1,3},{2,0},{3,1},{4,6},{5,7},{6,4},{7,5},{8,10},{9,11},{10,... | collective-permute-start | bytes 245768 | tf_op jit(solution)/shard_map/ppermute | solution.py:20
  76.1 1.3 %collective-permute-start.20 = (bf16[160,256]{1,0:T(8,128)(2,1)S(1)}, bf16[160,256]{1,0:T(8,128)(2,1)S(1)}, u32[]{:S(2)}, u32[]{:S(2)}) collective-permute-start(bf16[160,256]{1,0:T(8,128)(2,1)S(1)} %get-tuple-element.138), channel_id=1, source_target_pairs={{0,16},{4,20},{8,24},{12,28},{16,0},{20,4},{24,8},{28,12},{1,17},{... | collective-permute-start | bytes 245768 | tf_op jit(solution)/shard_map/ppermute | solution.py:20
  77.5 0.3 collective-permute-start.15
  77.8 3.6 %collective-permute-done.22 = bf16[240,128]{1,0:T(8,128)(2,1)S(1)} collective-permute-done((bf16[240,128]{1,0:T(8,128)(2,1)S(1)}, bf16[240,128]{1,0:T(8,128)(2,1)S(1)}, u32[]{:S(2)}, u32[]{:S(2)}) %collective-permute-start.22) | collective-permute-done | bytes 61472 | tf_op jit(solution)/shard_map/ppermute | solution.py:20
  81.4 3.1 %collective-permute-done.15 = bf16[160,256]{1,0:T(8,128)(2,1)S(1)} collective-permute-done((bf16[160,256]{1,0:T(8,128)(2,1)S(1)}, bf16[160,256]{1,0:T(8,128)(2,1)S(1)}, u32[]{:S(2)}, u32[]{:S(2)}) %collective-permute-start.15) | collective-permute-done | bytes 81952 | tf_op jit(solution)/shard_map/ppermute | solution.py:20
  84.7 1.0 fusion.12
  85.7 3.4 %all-to-all-start = ((f32[32,8,256]{2,1,0:T(8,128)}), f32[32,8,256]{2,1,0:T(8,128)S(1)}, u32[]{:S(2)}, u32[]{:S(2)}) async-start(f32[32,8,256]{2,1,0:T(8,128)} %bitcast.3), calls=%async_computation | async-start | bytes 524288 | tf_op jit(solution)/shard_map/all_to_all | solution.py:534
  89.1 2.0 %fusion = f32[8,2,8,128]{3,2,1,0:T(8,128)S(1)} fusion(f32[8,2,8,512]{3,2,1,0:T(8,128)S(1)} %get-tuple-element.166, f32[8,2,8]{2,1,0:T(2,128)S(1)} %get-tuple-element.162, f32[8,2,8]{2,1,0:T(2,128)S(1)} %multiply_maximum_fusion, bf16[8,512,256]{2,1,0:T(8,128)(2,1)} %param.19), kind=kOutput, calls=%fused_computation | convolution fusion | flops 16973824 | bytes 2425856 | tf_op jit(solution)/shard_map/rkgc,rckd->rkgd/dot_general | solution.py:564
  91.3 8.0 %all-to-all-done = f32[32,8,256]{2,1,0:T(8,128)S(1)} async-done(((f32[32,8,256]{2,1,0:T(8,128)}), f32[32,8,256]{2,1,0:T(8,128)S(1)}, u32[]{:S(2)}, u32[]{:S(2)}) %all-to-all-start) | async-done | bytes 262176 | tf_op jit(solution)/shard_map/all_to_all | solution.py:534
  99.4 0.6 bitcast_convert_fusion
  100.1 0.6 copy.47
  (64 shorter events, 1.9 us)
Async XLA Ops:
  0.6 44.6 %copy-start = (bf16[8,512,256]{2,1,0:T(8,128)(2,1)S(1)}, bf16[8,512,256]{2,1,0:T(8,128)(2,1)}, u32[]{:S(2)}) copy-start(bf16[8,512,256]{2,1,0:T(8,128)(2,1)} %param.18) | copy-start | bytes 6291460
  0.6 3.8 %copy-start.2 = (bf16[512,1024]{1,0:T(8,128)(2,1)S(1)}, bf16[512,1024]{1,0:T(8,128)(2,1)}, u32[]{:S(2)}) copy-start(bf16[512,1024]{1,0:T(8,128)(2,1)} %refs_2_.7) | copy-start | bytes 3145732
  0.7 3.8 %copy-start.9 = (s32[64]{0:T(128)S(1)}, s32[64]{0:T(128)}, u32[]{:S(2)}) copy-start(s32[64]{0:T(128)} %param.16) | copy-start | bytes 772
  3.9 9.2 %collective-permute-start = (bf16[2560,512]{1,0:T(8,128)(2,1)}, bf16[2560,512]{1,0:T(8,128)(2,1)}, u32[]{:S(2)}, u32[]{:S(2)}) collective-permute-start(bf16[2560,512]{1,0:T(8,128)(2,1)} %shard_map.140), channel_id=1, source_target_pairs={{0,4},{4,0},{8,12},{12,8},{16,20},{20,16},{24,28},{28,24},{1,5},{5... | collective-permute-start | bytes 7864328 | tf_op jit(solution)/shard_map/ppermute | solution.py:20
  4.4 8.6 %collective-permute-start.1 = (bf16[512,1024]{1,0:T(8,128)(2,1)S(1)}, bf16[512,1024]{1,0:T(8,128)(2,1)}, u32[]{:S(2)}, u32[]{:S(2)}) collective-permute-start(bf16[512,1024]{1,0:T(8,128)(2,1)S(1)} %copy-done.2), channel_id=1, source_target_pairs={{0,4},{4,0},{8,12},{12,8},{16,20},{20,16},{24,28},{28,24},{1,5},{5... | collective-permute-start | bytes 3145736 | tf_op jit(solution)/shard_map/ppermute | solution.py:20
  8.7 4.2 %collective-permute-start.4 = (bf16[1280,128]{1,0:T(8,128)(2,1)S(1)}, bf16[1280,128]{1,0:T(8,128)(2,1)S(1)}, u32[]{:S(2)}, u32[]{:S(2)}) collective-permute-start(bf16[1280,128]{1,0:T(8,128)(2,1)S(1)} %get-tuple-element.85), channel_id=1, source_target_pairs={{0,4},{4,0},{8,12},{12,8},{16,20},{20,16},{24,28},{28,24},{1,5},{5... | collective-permute-start | bytes 983048 | tf_op jit(solution)/shard_map/ppermute | solution.py:20
  13.1 1.7 %copy-start.1 = (bf16[2560,512]{1,0:T(8,128)(2,1)S(1)}, bf16[2560,512]{1,0:T(8,128)(2,1)}, u32[]{:S(2)}) copy-start(bf16[2560,512]{1,0:T(8,128)(2,1)} %shard_map.139.refs_0_) | copy-start | bytes 7864324
  19.7 18.0 %collective-permute-start.2 = (bf16[1280,256]{1,0:T(8,128)(2,1)S(1)}, bf16[1280,256]{1,0:T(8,128)(2,1)S(1)}, u32[]{:S(2)}, u32[]{:S(2)}) collective-permute-start(bf16[1280,256]{1,0:T(8,128)(2,1)S(1)} %get-tuple-element.81), channel_id=1, source_target_pairs={{0,8},{4,12},{8,0},{12,4},{16,24},{20,28},{24,16},{28,20},{1,9},{5... | collective-permute-start | bytes 1966088 | tf_op jit(solution)/shard_map/ppermute | solution.py:20
  22.1 17.6 %collective-permute-start.3 = (bf16[1280,256]{1,0:T(8,128)(2,1)S(1)}, bf16[1280,256]{1,0:T(8,128)(2,1)S(1)}, u32[]{:S(2)}, u32[]{:S(2)}) collective-permute-start(bf16[1280,256]{1,0:T(8,128)(2,1)S(1)} %get-tuple-element.82), channel_id=1, source_target_pairs={{0,16},{4,20},{8,24},{12,28},{16,0},{20,4},{24,8},{28,12},{1,17},{... | collective-permute-start | bytes 1966088 | tf_op jit(solution)/shard_map/ppermute | solution.py:20
  23.8 18.4 %collective-permute-start.9 = (bf16[1280,256]{1,0:T(8,128)(2,1)S(1)}, bf16[1280,256]{1,0:T(8,128)(2,1)S(1)}, u32[]{:S(2)}, u32[]{:S(2)}) collective-permute-start(bf16[1280,256]{1,0:T(8,128)(2,1)S(1)} %get-tuple-element.97), channel_id=1, source_target_pairs={{0,1},{1,0},{2,3},{3,2},{4,5},{5,4},{6,7},{7,6},{8,9},{9,8},{10,11... | collective-permute-start | bytes 1966088 | tf_op jit(solution)/shard_map/ppermute | solution.py:20
  25.5 5.0 %copy-start.7 = (s32[8]{0:T(128)S(1)}, s32[8]{0:T(128)}, u32[]{:S(2)}) copy-start(s32[8]{0:T(128)} %param.23) | copy-start | bytes 100
  29.4 20.4 %collective-permute-start.7 = (bf16[1280,128]{1,0:T(8,128)(2,1)S(1)}, bf16[1280,128]{1,0:T(8,128)(2,1)S(1)}, u32[]{:S(2)}, u32[]{:S(2)}) collective-permute-start(bf16[1280,128]{1,0:T(8,128)(2,1)S(1)} %get-tuple-element.95), channel_id=1, source_target_pairs={{0,8},{4,12},{8,0},{12,4},{16,24},{20,28},{24,16},{28,20},{1,9},{5... | collective-permute-start | bytes 983048 | tf_op jit(solution)/shard_map/ppermute | solution.py:20
  29.6 20.7 %collective-permute-start.8 = (bf16[1920,128]{1,0:T(8,128)(2,1)S(1)}, bf16[1920,128]{1,0:T(8,128)(2,1)S(1)}, u32[]{:S(2)}, u32[]{:S(2)}) collective-permute-start(bf16[1920,128]{1,0:T(8,128)(2,1)S(1)} %pad_maximum_fusion), channel_id=1, source_target_pairs={{0,16},{4,20},{8,24},{12,28},{16,0},{20,4},{24,8},{28,12},{1,17},{... | collective-permute-start | bytes 1474568 | tf_op jit(solution)/shard_map/ppermute | solution.py:20
  39.7 5.5 %copy-start.5 = (bf16[8,2048]{1,0:T(8,128)(2,1)S(1)}, bf16[8,2048]{1,0:T(8,128)(2,1)}, u32[]{:S(2)}) copy-start(bf16[8,2048]{1,0:T(8,128)(2,1)} %param.17) | copy-start | bytes 98308
  40.0 17.3 %collective-permute-start.5 = (bf16[640,256]{1,0:T(8,128)(2,1)S(1)}, bf16[640,256]{1,0:T(8,128)(2,1)S(1)}, u32[]{:S(2)}, u32[]{:S(2)}) collective-permute-start(bf16[640,256]{1,0:T(8,128)(2,1)S(1)} %get-tuple-element.92), channel_id=1, source_target_pairs={{0,16},{4,20},{8,24},{12,28},{16,0},{20,4},{24,8},{28,12},{1,17},{... | collective-permute-start | bytes 983048 | tf_op jit(solution)/shard_map/ppermute | solution.py:20
  41.8 15.5 %collective-permute-start.6 = (bf16[640,256]{1,0:T(8,128)(2,1)S(1)}, bf16[640,256]{1,0:T(8,128)(2,1)S(1)}, u32[]{:S(2)}, u32[]{:S(2)}) collective-permute-start(bf16[640,256]{1,0:T(8,128)(2,1)S(1)} %get-tuple-element.93), channel_id=1, source_target_pairs={{0,8},{4,12},{8,0},{12,4},{16,24},{20,28},{24,16},{28,20},{1,9},{5... | collective-permute-start | bytes 983048 | tf_op jit(solution)/shard_map/ppermute | solution.py:20
  42.3 17.2 %collective-permute-start.14 = (bf16[640,256]{1,0:T(8,128)(2,1)S(1)}, bf16[640,256]{1,0:T(8,128)(2,1)S(1)}, u32[]{:S(2)}, u32[]{:S(2)}) collective-permute-start(bf16[640,256]{1,0:T(8,128)(2,1)S(1)} %get-tuple-element.99), channel_id=1, source_target_pairs={{0,2},{1,3},{2,0},{3,1},{4,6},{5,7},{6,4},{7,5},{8,10},{9,11},{10,... | collective-permute-start | bytes 983048 | tf_op jit(solution)/shard_map/ppermute | solution.py:20
  49.8 1.6 %copy-start.8 = (bf16[8,256]{1,0:T(8,128)(2,1)S(1)}, bf16[8,256]{1,0:T(8,128)(2,1)}, u32[]{:S(2)}) copy-start(bf16[8,256]{1,0:T(8,128)(2,1)} %param.20) | copy-start | bytes 12292
  50.4 9.7 %collective-permute-start.13 = (bf16[960,128]{1,0:T(8,128)(2,1)S(1)}, bf16[960,128]{1,0:T(8,128)(2,1)S(1)}, u32[]{:S(2)}, u32[]{:S(2)}) collective-permute-start(bf16[960,128]{1,0:T(8,128)(2,1)S(1)} %get-tuple-element.105), channel_id=1, source_target_pairs={{0,8},{4,12},{8,0},{12,4},{16,24},{20,28},{24,16},{28,20},{1,9},{5... | collective-permute-start | bytes 737288 | tf_op jit(solution)/shard_map/ppermute | solution.py:20
  51.5 8.5 %collective-permute-start.12 = (bf16[640,128]{1,0:T(8,128)(2,1)S(1)}, bf16[640,128]{1,0:T(8,128)(2,1)S(1)}, u32[]{:S(2)}, u32[]{:S(2)}) collective-permute-start(bf16[640,128]{1,0:T(8,128)(2,1)S(1)} %get-tuple-element.115), channel_id=1, source_target_pairs={{0,16},{4,20},{8,24},{12,28},{16,0},{20,4},{24,8},{28,12},{1,17},{... | collective-permute-start | bytes 491528 | tf_op jit(solution)/shard_map/ppermute | solution.py:20
  57.4 7.2 %collective-permute-start.10 = (bf16[320,256]{1,0:T(8,128)(2,1)S(1)}, bf16[320,256]{1,0:T(8,128)(2,1)S(1)}, u32[]{:S(2)}, u32[]{:S(2)}) collective-permute-start(bf16[320,256]{1,0:T(8,128)(2,1)S(1)} %get-tuple-element.112), channel_id=1, source_target_pairs={{0,1},{1,0},{2,3},{3,2},{4,5},{5,4},{6,7},{7,6},{8,9},{9,8},{10,11... | collective-permute-start | bytes 491528 | tf_op jit(solution)/shard_map/ppermute | solution.py:20
  59.0 9.0 %collective-permute-start.11 = (bf16[320,256]{1,0:T(8,128)(2,1)S(1)}, bf16[320,256]{1,0:T(8,128)(2,1)S(1)}, u32[]{:S(2)}, u32[]{:S(2)}) collective-permute-start(bf16[320,256]{1,0:T(8,128)(2,1)S(1)} %get-tuple-element.113), channel_id=1, source_target_pairs={{0,1},{1,0},{2,3},{3,2},{4,5},{5,4},{6,7},{7,6},{8,9},{9,8},{10,11... | collective-permute-start | bytes 491528 | tf_op jit(solution)/shard_map/ppermute | solution.py:20
  59.5 25.0 %copy-start.4 = (f32[160,1024]{1,0:T(8,128)S(1)}, f32[160,1024]{1,0:T(8,128)}, u32[]{:S(2)}) copy-start(f32[160,1024]{1,0:T(8,128)} %param.14) | copy-start | bytes 1966084
  59.6 8.4 %collective-permute-start.19 = (bf16[320,256]{1,0:T(8,128)(2,1)S(1)}, bf16[320,256]{1,0:T(8,128)(2,1)S(1)}, u32[]{:S(2)}, u32[]{:S(2)}) collective-permute-start(bf16[320,256]{1,0:T(8,128)(2,1)S(1)} %get-tuple-element.118), channel_id=1, source_target_pairs={{0,8},{4,12},{8,0},{12,4},{16,24},{20,28},{24,16},{28,20},{1,9},{5... | collective-permute-start | bytes 491528 | tf_op jit(solution)/shard_map/ppermute | solution.py:20
  60.1 8.7 %collective-permute-start.17 = (bf16[320,128]{1,0:T(8,128)(2,1)S(1)}, bf16[320,128]{1,0:T(8,128)(2,1)S(1)}, u32[]{:S(2)}, u32[]{:S(2)}) collective-permute-start(bf16[320,128]{1,0:T(8,128)(2,1)S(1)} %get-tuple-element.135), channel_id=1, source_target_pairs={{0,1},{1,0},{2,3},{3,2},{4,5},{5,4},{6,7},{7,6},{8,9},{9,8},{10,11... | collective-permute-start | bytes 245768 | tf_op jit(solution)/shard_map/ppermute | solution.py:20
  62.1 8.0 %collective-permute-start.18 = (bf16[480,128]{1,0:T(8,128)(2,1)S(1)}, bf16[480,128]{1,0:T(8,128)(2,1)S(1)}, u32[]{:S(2)}, u32[]{:S(2)}) collective-permute-start(bf16[480,128]{1,0:T(8,128)(2,1)S(1)} %get-tuple-element.125), channel_id=1, source_target_pairs={{0,1},{1,0},{2,3},{3,2},{4,5},{5,4},{6,7},{7,6},{8,9},{9,8},{10,11... | collective-permute-start | bytes 368648 | tf_op jit(solution)/shard_map/ppermute | solution.py:20
  70.2 7.6 %collective-permute-start.21 = (bf16[160,128]{1,0:T(8,128)(2,1)S(1)}, bf16[160,128]{1,0:T(8,128)(2,1)S(1)}, u32[]{:S(2)}, u32[]{:S(2)}) collective-permute-start(bf16[160,128]{1,0:T(8,128)(2,1)S(1)} %get-tuple-element.152), channel_id=1, source_target_pairs={{0,2},{1,3},{2,0},{3,1},{4,6},{5,7},{6,4},{7,5},{8,10},{9,11},{10,... | collective-permute-start | bytes 122888 | tf_op jit(solution)/shard_map/ppermute | solution.py:20
  73.1 8.3 %collective-permute-start.22 = (bf16[240,128]{1,0:T(8,128)(2,1)S(1)}, bf16[240,128]{1,0:T(8,128)(2,1)S(1)}, u32[]{:S(2)}, u32[]{:S(2)}) collective-permute-start(bf16[240,128]{1,0:T(8,128)(2,1)S(1)} %get-tuple-element.145), channel_id=1, source_target_pairs={{0,2},{1,3},{2,0},{3,1},{4,6},{5,7},{6,4},{7,5},{8,10},{9,11},{10,... | collective-permute-start | bytes 184328 | tf_op jit(solution)/shard_map/ppermute | solution.py:20
  73.2 11.3 %collective-permute-start.16 = (bf16[160,256]{1,0:T(8,128)(2,1)S(1)}, bf16[160,256]{1,0:T(8,128)(2,1)S(1)}, u32[]{:S(2)}, u32[]{:S(2)}) collective-permute-start(bf16[160,256]{1,0:T(8,128)(2,1)S(1)} %get-tuple-element.133), channel_id=1, source_target_pairs={{0,2},{1,3},{2,0},{3,1},{4,6},{5,7},{6,4},{7,5},{8,10},{9,11},{10,... | collective-permute-start | bytes 245768 | tf_op jit(solution)/shard_map/ppermute | solution.py:20
  76.1 8.4 %collective-permute-start.20 = (bf16[160,256]{1,0:T(8,128)(2,1)S(1)}, bf16[160,256]{1,0:T(8,128)(2,1)S(1)}, u32[]{:S(2)}, u32[]{:S(2)}) collective-permute-start(bf16[160,256]{1,0:T(8,128)(2,1)S(1)} %get-tuple-element.138), channel_id=1, source_target_pairs={{0,16},{4,20},{8,24},{12,28},{16,0},{20,4},{24,8},{28,12},{1,17},{... | collective-permute-start | bytes 245768 | tf_op jit(solution)/shard_map/ppermute | solution.py:20
  77.5 7.1 %collective-permute-start.15 = (bf16[160,256]{1,0:T(8,128)(2,1)S(1)}, bf16[160,256]{1,0:T(8,128)(2,1)S(1)}, u32[]{:S(2)}, u32[]{:S(2)}) collective-permute-start(bf16[160,256]{1,0:T(8,128)(2,1)S(1)} %get-tuple-element.132), channel_id=1, source_target_pairs={{0,2},{1,3},{2,0},{3,1},{4,6},{5,7},{6,4},{7,5},{8,10},{9,11},{10,... | collective-permute-start | bytes 245768 | tf_op jit(solution)/shard_map/ppermute | solution.py:20
  84.7 6.4 %copy-start.3 = (f32[160,1024]{1,0:T(8,128)}, f32[160,1024]{1,0:T(8,128)S(1)}, u32[]{:S(2)}) copy-start(f32[160,1024]{1,0:T(8,128)S(1)} %subtract_dynamic-update-slice_fusion.3) | copy-start | bytes 1966084
  85.7 5.4 %copy-start.10 = (f32[2]{0:T(128)S(1)}, f32[2]{0:T(128)}, u32[]{:S(2)}) copy-start(f32[2]{0:T(128)} %param.22) | copy-start | bytes 28
  85.7 13.6 %copy-start.6 = (bf16[8,256]{1,0:T(8,128)(2,1)S(1)}, bf16[8,256]{1,0:T(8,128)(2,1)}, u32[]{:S(2)}) copy-start(bf16[8,256]{1,0:T(8,128)(2,1)} %param.21) | copy-start | bytes 12292
  85.7 13.6 %all-to-all-start = ((f32[32,8,256]{2,1,0:T(8,128)}), f32[32,8,256]{2,1,0:T(8,128)S(1)}, u32[]{:S(2)}, u32[]{:S(2)}) async-start(f32[32,8,256]{2,1,0:T(8,128)} %bitcast.3), calls=%async_computation | async-start | bytes 524288 | tf_op jit(solution)/shard_map/all_to_all | solution.py:534

commit v6 on v5

--- a/solution.py
+++ b/solution.py
@@ -99,11 +99,12 @@
     return runs
 
 
-def multiply(wanted, rows, blocks, base, *refs):
+def multiply(wanted, rows, blocks, base, staged, *refs):
     count = len(wanted)
     sources = refs[:4]
     outs = refs[4 : 4 + count]
-    left, right, sems = refs[4 + count :]
+    left, right, sems = refs[4 + count : 7 + count]
+    stages, given = refs[7 + count : -1] if staged else outs, []
     tokens = left.shape[1] // 2
     per_block = left.shape[0] // blocks
     units_block = per_block // rows
@@ -132,17 +133,26 @@
     for block in needed:
         for at in range(2):
             lefts[block, at].wait()
-        for (units, first, last, _), out in zip(wanted, outs):
+        for at, (units, first, last, _) in enumerate(wanted):
             here = [unit for unit in units if unit // units_block == block]
             for low, high in runs_of(here):
                 place = units.index(low) * rows
                 product = dot32(
                     left[low * rows : high * rows, :], right[:, first - base : last - base]
                 )
-                out[place : place + (high - low) * rows, :] = product.astype(out.dtype)
-
-
-def products(lefts, grads, wanted, rows, blocks):
+                stages[at][place : place + (high - low) * rows, :] = product.astype(outs[at].dtype)
+            if staged and here:
+                span = pl.ds(units.index(here[0]) * rows, len(here) * rows)
+                copy = pltpu.make_async_copy(
+                    stages[at].at[span], outs[at].at[span], refs[-1].at[block, at]
+                )
+                copy.start()
+                given.append(copy)
+    for copy in given:
+        copy.wait()
+
+
+def products(lefts, grads, wanted, rows, blocks, staged):
     total, tokens = lefts[0].shape
     base = min(first for _, first, _, _ in wanted)
     columns = max(last for _, _, last, _ in wanted) - base
@@ -163,17 +173,22 @@
         jax.ShapeDtypeStruct((len(units) * rows, last - first), kind)
         for units, first, last, kind in wanted
     ]
+    staging = []
+    if staged:
+        staging = [pltpu.VMEM(shape.shape, shape.dtype) for shape in shapes]
+        staging.append(pltpu.SemaphoreType.DMA((blocks, len(shapes))))
     return pl.pallas_call(
-        functools.partial(multiply, wanted, rows, blocks, base),
+        functools.partial(multiply, wanted, rows, blocks, base, staged),
         out_shape=shapes,
         in_specs=[pl.BlockSpec(memory_space=pltpu.HBM)] * 4,
-        out_specs=[pl.BlockSpec(memory_space=pltpu.VMEM)] * len(shapes),
+        out_specs=[pl.BlockSpec(memory_space=pltpu.HBM if staged else pltpu.VMEM)] * len(shapes),
         scratch_shapes=[
             pltpu.VMEM((total, 2 * tokens), lefts[0].dtype),
             pltpu.VMEM((2 * tokens, columns), grads[0].dtype),
             pltpu.SemaphoreType.DMA((2 + 2 * blocks,)),
-        ],
-        compiler_params=pltpu.CompilerParams(vmem_limit_bytes=VMEM // 2),
+        ]
+        + staging,
+        compiler_params=pltpu.CompilerParams(vmem_limit_bytes=62 << 20 if staged else VMEM // 2),
         cost_estimate=pl.CostEstimate(flops=1, bytes_accessed=1, transcendentals=0),
     )(*lefts, *grads)
 
@@ -206,14 +221,16 @@
     found[...] = jnp.zeros_like(found)
     for k in range(tokens):
 
-        @pl.when((place[k] >= 0) & (place[k] < whole))
+        @pl.when(place[k] >= 0)
         def _():
-            slab_copy(k).wait()
-            add_row(k, slabs[k])
-
-        @pl.when(place[k] >= whole)
-        def _():
-            add_row(k, tail[...])
+            @pl.when(place[k] < whole)
+            def _():
+                slab_copy(k).wait()
+                add_row(k, slabs[k])
+
+            @pl.when(place[k] >= whole)
+            def _():
+                add_row(k, tail[...])
 
     core, upper, t = own_place()
     for side, out in zip((1 - core, core), outs):
@@ -230,13 +247,18 @@
                 out[put : put + lines, :] = jnp.concatenate(pieces, axis=1).astype(out.dtype)
 
 
-def add_and_split(plans, *refs):
+def add_and_split(plans, arrays, merged, *refs):
     refs = list(refs)
-    takes = [[refs.pop(0) for _ in plan] + [refs.pop(0)] for plan in plans]
-    gives = [[refs.pop(0) for _ in plan] + [refs.pop(0)] for plan in plans]
-    for plan, inputs, outputs in zip(plans, takes, gives):
-        got, sent = inputs[-1], outputs[-1]
-        start = put = 0
+    takes = [[refs.pop(0) for _ in plan] for plan in plans]
+    inbox = [refs.pop(0) for _ in range(arrays)]
+    gives = [[refs.pop(0) for _ in plan] for plan in plans]
+    start = put = 0
+    for at_plan, (plan, inputs, outputs) in enumerate(zip(plans, takes, gives)):
+        got, sent = inbox[min(at_plan, arrays - 1)], refs[0 if merged else at_plan]
+        if arrays > 1:
+            start = 0
+        if not merged:
+            put = 0
         for (size, order, go, keep), value, kept in zip(plan, inputs, outputs):
 
             def sum_of(low, high):
@@ -259,18 +281,22 @@
             put += go * size
 
 
-def combine(plans, values, got):
-    columns = [arrived.shape[1] for arrived in got]
-    outs = []
-    for plan, width in zip(plans, columns):
-        outs += [
-            jax.ShapeDtypeStruct((keep * size, width), jnp.float32) for size, _, _, keep in plan
-        ]
-        total = sum(size * go for size, _, go, _ in plan)
-        outs.append(jax.ShapeDtypeStruct((total, width), jnp.bfloat16))
-    arrays = [array for parts, arrived in zip(values, got) for array in parts + [arrived]]
+def combine(plans, values, got, merged):
+    columns = [parts[0].shape[1] for parts in values]
+    totals = [sum(size * go for size, _, go, _ in plan) for plan in plans]
+    outs = [
+        jax.ShapeDtypeStruct((keep * size, width), jnp.float32)
+        for plan, width in zip(plans, columns)
+        for size, _, _, keep in plan
+    ]
+    if merged:
+        outs.append(jax.ShapeDtypeStruct((sum(totals), columns[0]), jnp.bfloat16))
+    else:
+        for total, width in zip(totals, columns):
+            outs.append(jax.ShapeDtypeStruct((total, width), jnp.bfloat16))
+    arrays = [array for parts in values for array in parts] + list(got)
     results = pl.pallas_call(
-        functools.partial(add_and_split, plans),
+        functools.partial(add_and_split, plans, len(got), merged),
         in_specs=[pl.BlockSpec(memory_space=pltpu.VMEM)] * len(arrays),
         out_specs=[pl.BlockSpec(memory_space=pltpu.VMEM)] * len(outs),
         out_shape=outs,
@@ -278,11 +304,8 @@
         cost_estimate=pl.CostEstimate(flops=1, bytes_accessed=1, transcendentals=0),
     )(*arrays)
     results = list(results)
-    kept, sent = [], []
-    for plan in plans:
-        kept.append([results.pop(0) for _ in plan])
-        sent.append(results.pop(0))
-    return kept, sent
+    kept = [[results.pop(0) for _ in plan] for plan in plans]
+    return kept, results, totals
 
 
 def fold_unit(part, lanes):
@@ -400,7 +423,7 @@
     one, two, three = (
         steps_upper + steps_tp,
         steps_upper[::-1] + steps_tp,
-        steps_tp + steps_upper,
+        steps_tp[:1] + steps_upper + steps_tp[1:],
     )
     edges = [0, quarter, 2 * quarter, 3 * quarter, 3 * quarter + eighth, columns]
     spans = list(zip(edges[:-1], edges[1:]))
@@ -424,27 +447,27 @@
         mask = 1 << step[1]
         return exchange(value, step[0], 2 * mask if step[0] == "fsdp" else mask)
 
-    def compute(which, sent, factors):
+    def compute(which, sent):
         wanted = []
         for index in which:
             chosen = split(places, orders[index][0])[0 if sent else 1]
             units = [places.index(p) for p in chosen]
             kind = jnp.bfloat16 if sent else jnp.float32
             wanted.append((units, *spans[index], kind))
-        return dict(zip(which, products(factors, grads, wanted, rows, uppers)))
-
-    going = compute([2, 0, 1], True, lefts)
+        return dict(zip(which, products(lefts, grads, wanted, rows, uppers, sent)))
+
+    going = compute([2, 0, 1], True)
     got = {index: send(value, orders[index][0]) for index, value in going.items()}
-    going |= compute([3, 4], True, lefts)
+    going |= compute([3, 4], True)
     got[3] = send(going[3], orders[3][0])
 
     theirs, ours = lookup(embed_table, token_ids, arranged, count_tp, block, eighth)
     asked = ours + exchange(theirs, "fsdp", 1)
     go, stay = split(places, orders[4][0])
-    values = compute([0, 1, 2], False, lefts)
+    values = compute([0, 1, 2], False)
     token = jnp.concatenate([going[4], take(asked, places, go, lines)])
     got[4] = send(token, orders[4][0])
-    values |= compute([3, 4], False, lefts)
+    values |= compute([3, 4], False)
     values = {index: [value] for index, value in values.items()}
     values[4].append(take(asked, places, stay, lines).astype(jnp.float32))
     sizes = {index: [rows] for index in range(5)}
@@ -477,19 +500,27 @@
         index: split(places, orders[index][0])[1] for index in range(5)
     }
     plain = rows % 32 or any(size % 16 for size in sizes[4])
+    groups = ((0, 1), (2,), (3, 4))
+    inbox = {group: [got[index] for index in group] for group in groups}
+    totals = {}
     for at in range(len(one)):
-        for group in ((0, 1), (2,), (3, 4)):
-            tied = lax.optimization_barrier([got[index] for index in group] + [token])
-            for index, arrived in zip(group, tied):
-                got[index] = arrived
-            if at + 1 == len(one):
-                for index in group:
+        for group in groups:
+            *inbox[group], token = lax.optimization_barrier(inbox[group] + [token])
+            last = at + 1 == len(one)
+            if plain or last:
+                if len(inbox[group]) < len(group):
+                    whole = inbox[group][0]
+                    cuts = [sum(totals[group][:place]) for place in range(len(group) + 1)]
+                    inbox[group] = [whole[low:high] for low, high in zip(cuts[:-1], cuts[1:])]
+                for index, arrived in zip(group, inbox[group]):
+                    got[index] = arrived
                     receive(index, orders[index][at])
+            if last:
+                token = values[group[-1]][0]
                 continue
             if plain:
                 outgoing = []
                 for index in group:
-                    receive(index, orders[index][at])
                     gone, kept = split(held[index], orders[index][at + 1])
                     pieces = [
                         take(value, held[index], gone, size).astype(jnp.bfloat16)
@@ -502,15 +533,16 @@
                     outgoing.append(jnp.concatenate(pieces))
             else:
                 plans = [forward(i, orders[i][at], orders[i][at + 1]) for i in group]
-                kept, outgoing = combine(
-                    plans, [values[i] for i in group], [got[i] for i in group]
+                merged = len({orders[i][at + 1] for i in group}) == 1
+                kept, outgoing, totals[group] = combine(
+                    plans, [values[i] for i in group], inbox[group], merged
                 )
-                for index, value in zip(group, kept):
-                    values[index] = value
+                values |= dict(zip(group, kept))
             outgoing = lax.optimization_barrier(outgoing)
             token = outgoing[-1]
-            for index, value in zip(group, outgoing):
-                got[index] = send(value, orders[index][at + 1])
+            inbox[group] = [
+                send(value, orders[index][at + 1]) for index, value in zip(group, outgoing)
+            ]
     w_next = jnp.concatenate(
         [master_w[:, low:high] - coef * values[at][0] for at, (low, high) in enumerate(spans)],
         axis=1,
@@ -526,13 +558,13 @@
     rows_f = tokens_new // count_fsdp
     col_width = columns // count_tp
     blocks_own = (
-        share_own.reshape(count_fsdp, rows_f, count_tp, col_width)
+        share_own.astype(jnp.bfloat16)
+        .reshape(count_fsdp, rows_f, count_tp, col_width)
         .transpose(0, 2, 1, 3)
         .reshape(devices_all, rows_f, col_width)
     )
-    own_value = jnp.sum(
-        lax.all_to_all(blocks_own, ("fsdp", "tp"), split_axis=0, concat_axis=0), axis=0
-    )
+    parts_own = lax.all_to_all(blocks_own, ("fsdp", "tp"), split_axis=0, concat_axis=0)
+    own_value = jnp.sum(parts_own.astype(jnp.float32), axis=0)
 
     share = jnp.repeat(residual_mix, HD)[None, :]
     new_value = (share * own_value + (1.0 - share) * first_value.astype(jnp.float32)).astype(

time: 101 us -> 99.2 us (0.982)
  waiting for transfers between devices: 31.6 us -> 26.1 us
  Pallas kernels: 28.7 us -> 32.5 us
  starting transfers between devices: 31.5 us -> 29.4 us
  other arithmetic: 1.43 us -> 2.53 us
    ppermute x23 -> x19, waiting for transfers between devices: 23.6 us -> 17.9 us  [exchange(): lax.ppermute(value, axis, [(i, i ^ mask) for i in range(lax.axis_size(axi...]
    pallas_call x13, Pallas kernels: 18.3 us -> 21.7 us  [the longest x4 19.5 us: products(): pl.pallas_call(functools.partial(multiply, wanted, rows, blocks, base, st...]
    ppermute x23 -> x19, starting transfers between devices: 28.1 us -> 25.2 us  [exchange(): lax.ppermute(value, axis, [(i, i ^ mask) for i in range(lax.axis_size(axi...]
    dot_general x1, matrix products: 2.02 us -> 0.43 us  [per_device(): jnp.einsum('rkgc,rckd->rkgd', probs, vals_b, preferred_element_type=jnp.f...]
    dot_general x1, matrix products: 0.73 us -> 2.32 us  [per_device(): jnp.einsum('rkgd,rckd->rkgc', query_b, keys_b, preferred_element_type=jnp...]
    concatenate x1, other arithmetic: 0.03 us -> 1.16 us  [per_device(): token = jnp.concatenate([going[4], take(asked, places, go, lines)])]
    unnamed x23 -> x31, local copies, waits for them, and re-layouts: 2.41 us -> 2.98 us
  transfers between devices with their start and end apart: 24 -> 20, of which waited for: 12 -> 9; matrix products, arithmetic and copies ran while one was open for 4% -> 5% of each run, Pallas kernels for 20% -> 24%
where the time goes in v6:
time: 99.2 us; the launch traced here: 98.6 us
  Pallas kernels  32.5 us (33%)
  starting transfers between devices  29.4 us (30%)
  waiting for transfers between devices  26.1 us (26%)
  matrix products  3.8 us (4%)
  local copies, waits for them, and re-layouts  3.14 us (3%)
  other arithmetic  2.53 us (3%)
    ppermute x19, starting transfers between devices, exchange(): lax.ppermute(value, axis, [(i, i ^ mask) for i in range(lax.axis_size(axi...  25.2 us
    pallas_call x4, Pallas kernels, products(): pl.pallas_call(functools.partial(multiply, wanted, rows, blocks, base, st...  19.5 us
    ppermute x19, waiting for transfers between devices, exchange(): lax.ppermute(value, axis, [(i, i ^ mask) for i in range(lax.axis_size(axi...  17.9 us
    all_to_all x1, waiting for transfers between devices, per_device(): lax.all_to_all(blocks_own, ('fsdp', 'tp'), split_axis=0, concat_axis=0)  8.25 us
    pallas_call x2, Pallas kernels, pack(): pl.pallas_call(functools.partial(transpose_blocks, arranged, mine, units)...  6.22 us
    pallas_call x1, Pallas kernels, lookup(): pl.pallas_call(functools.partial(pick_rows, arranged, units), grid=(1,),...  4.66 us
    all_to_all x1, starting transfers between devices, per_device(): lax.all_to_all(blocks_own, ('fsdp', 'tp'), split_axis=0, concat_axis=0)  4.26 us
    unnamed x31, local copies, waits for them, and re-layouts  2.98 us
  transfers between devices with their start and end apart: 20, of which 9 were waited for; matrix products, arithmetic and copies ran while one was open for 5% of the time, Pallas kernels for 24%

profile of v6, /device:TPU:0, one launch (start us, length us, event | category | flops | bytes accessed | tf_op | source)
XLA Modules:
  0.0 98.6 jit_solution(12875523123545939696)
XLA Ops:
  0.7 3.1 %shard_map.140 = bf16[2560,512]{1,0:T(8,128)(2,1)} custom-call(bf16[512,5120]{1,0:T(8,128)(2,1)} %source.3), custom_call_target="tpu_custom_call" | custom-call | bytes 5242880 | tf_op jit(solution)/shard_map/pallas_call | solution.py:74
  3.8 0.5 collective-permute-start
  4.4 4.7 %shard_map.144 = (bf16[1280,128]{1,0:T(8,128)(2,1)S(1)}, bf16[1280,128]{1,0:T(8,128)(2,1)S(1)}) custom-call(s32[64]{0:T(128)S(1)} %and_select_fusion.place, bf16[4748,5120]{1,0:T(8,128)(2,1)} %tail.1, bf16[4748,5120]{1,0:T(8,128)(2,1)} %tail.1), custom_call_target="tpu_custom_call" | custom-call | flops 1 | bytes 1 | tf_op jit(solution)/shard_map/pallas_call | solution.py:359
  9.2 3.1 %shard_map.139.refs_0_ = bf16[2560,512]{1,0:T(8,128)(2,1)} custom-call(bf16[512,5120]{1,0:T(8,128)(2,1)} %source.3), custom_call_target="tpu_custom_call" | custom-call | bytes 5242880 | tf_op jit(solution)/shard_map/pallas_call | solution.py:74
  12.5 1.1 %copy-done.4 = bf16[512,1024]{1,0:T(8,128)(2,1)} copy-done((bf16[512,1024]{1,0:T(8,128)(2,1)}, bf16[512,1024]{1,0:T(8,128)(2,1)S(1)}, u32[]{:S(2)}) %copy-start.4) | copy-done | bytes 1048600
  13.5 6.0 %shard_map.142 = (bf16[1280,256]{1,0:T(8,128)(2,1)}, bf16[1280,256]{1,0:T(8,128)(2,1)}, bf16[1280,256]{1,0:T(8,128)(2,1)}) custom-call(bf16[2560,512]{1,0:T(8,128)(2,1)} %shard_map.139.refs_0_, bf16[2560,512]{1,0:T(8,128)(2,1)} %collective-permute-done.refs_1_, bf16[512,1024]{1,0:T(8,128)(2,1)} %refs_2_.7, bf16[512,1024]{1,0:T(8,128)(2,1)} %copy-done.4), custom_call_target="tpu_custom_call" | custom-call | flops 1 | bytes 1 | tf_op jit(solution)/shard_map/pallas_call | solution.py:180
  19.5 2.8 %collective-permute-start.2 = (bf16[1280,256]{1,0:T(8,128)(2,1)}, bf16[1280,256]{1,0:T(8,128)(2,1)}, u32[]{:S(2)}, u32[]{:S(2)}) collective-permute-start(bf16[1280,256]{1,0:T(8,128)(2,1)} %get-tuple-element.66), channel_id=1, source_target_pairs={{0,8},{4,12},{8,0},{12,4},{16,24},{20,28},{24,16},{28,20},{1,9},{5... | collective-permute-start | bytes 1966088 | tf_op jit(solution)/shard_map/ppermute | solution.py:20
  22.3 1.4 %collective-permute-start.3 = (bf16[1280,256]{1,0:T(8,128)(2,1)}, bf16[1280,256]{1,0:T(8,128)(2,1)}, u32[]{:S(2)}, u32[]{:S(2)}) collective-permute-start(bf16[1280,256]{1,0:T(8,128)(2,1)} %get-tuple-element.67), channel_id=1, source_target_pairs={{0,16},{4,20},{8,24},{12,28},{16,0},{20,4},{24,8},{28,12},{1,17},{... | collective-permute-start | bytes 1966088 | tf_op jit(solution)/shard_map/ppermute | solution.py:20
  23.7 4.9 %shard_map.143 = (bf16[1280,128]{1,0:T(8,128)(2,1)}, bf16[1280,128]{1,0:T(8,128)(2,1)}) custom-call(bf16[2560,512]{1,0:T(8,128)(2,1)} %shard_map.139.refs_0_, bf16[2560,512]{1,0:T(8,128)(2,1)} %collective-permute-done.refs_1_, bf16[512,1024]{1,0:T(8,128)(2,1)} %refs_2_.7, bf16[512,1024]{1,0:T(8,128)(2,1)} %copy-done.4), custom_call_target="tpu_custom_call" | custom-call | flops 1 | bytes 1 | tf_op jit(solution)/shard_map/pallas_call | solution.py:180
  28.6 1.2 %pad_maximum_fusion = bf16[1920,128]{1,0:T(8,128)(2,1)S(1)} fusion(bf16[640,128]{1,0:T(8,128)(2,1)S(1)} %get-tuple-element.132, bf16[1280,128]{1,0:T(8,128)(2,1)} %get-tuple-element.68), kind=kLoop, calls=%fused_computation.9 | loop fusion | flops 983040 | bytes 983040 | tf_op jit(solution)/shard_map/concatenate | solution.py:468
  29.8 0.7 collective-permute-start.8
  30.5 1.7 %collective-permute-start.9 = (bf16[1280,256]{1,0:T(8,128)(2,1)}, bf16[1280,256]{1,0:T(8,128)(2,1)S(1)}, u32[]{:S(2)}, u32[]{:S(2)}) collective-permute-start(bf16[1280,256]{1,0:T(8,128)(2,1)} %get-tuple-element.83), channel_id=1, source_target_pairs={{0,1},{1,0},{2,3},{3,2},{4,5},{5,4},{6,7},{7,6},{8,9},{9,8},{10,11... | collective-permute-start | bytes 1966088 | tf_op jit(solution)/shard_map/ppermute | solution.py:20
  32.2 2.3 %fusion.28 = (f32[8,2,8]{2,1,0:T(2,128)S(1)}, f32[8,2,8,512]{3,2,1,0:T(8,128)S(1)}) fusion(bf16[8,2,8,128]{3,0,2,1:T(8,128)(2,1)S(1)} %bitcast.44, pred[8,512]{1,0:T(8,128)(4,1)S(1)} %iota_compare_fusion, bf16[8,512,256]{2,1,0:T(8,128)(2,1)} %param.18), kind=kOutput, calls=%fused_computation.49 | convolution fusion | flops 16973696 | bytes 2396672 | tf_op jit(solution)/shard_map/rkgd,rckd->rkgc/dot_general | solution.py:584
  34.5 0.5 collective-permute-start.7
  35.0 1.2 %copy-done.5 = bf16[512,1024]{1,0:T(8,128)(2,1)S(1)} copy-done((bf16[512,1024]{1,0:T(8,128)(2,1)S(1)}, bf16[512,1024]{1,0:T(8,128)(2,1)}, u32[]{:S(2)}) %copy-start.5) | copy-done | bytes 1048600
  36.2 4.8 %shard_map.141 = (f32[1280,256]{1,0:T(8,128)S(1)}, f32[1280,256]{1,0:T(8,128)S(1)}, f32[1280,256]{1,0:T(8,128)S(1)}) custom-call(bf16[2560,512]{1,0:T(8,128)(2,1)S(1)} %copy-done.1, bf16[2560,512]{1,0:T(8,128)(2,1)} %collective-permute-done.refs_1_, bf16[512,1024]{1,0:T(8,128)(2,1)S(1)} %copy-done.3, bf16[512,1024]{1,0:T(8,128)(2,1)S(1)} %copy-done.5), custom_call_target="tpu_custom_call" | custom-call | flops 1 | bytes 1 | tf_op jit(solution)/shard_map/pallas_call | solution.py:180
  41.0 1.6 %shard_map.145 = (f32[640,256]{1,0:T(8,128)S(1)}, f32[640,256]{1,0:T(8,128)S(1)}, bf16[640,256]{1,0:T(8,128)(2,1)S(1)}, bf16[640,256]{1,0:T(8,128)(2,1)S(1)}) custom-call(f32[1280,256]{1,0:T(8,128)S(1)} %get-tuple-element.64.refs_0_, f32[1280,256]{1,0:T(8,128)S(1)} %get-tuple-element.65.refs_1_, bf16[1280,256]{1,0:T(8,128)(2,1)} %collective-permute-done.2.refs_2_, ...), custom_call_target="tpu_custom_call" | custom-call | flops 1 | bytes 1 | tf_op jit(solution)/shard_map/pallas_call | solution.py:298
  42.6 1.6 %collective-permute-start.5 = (bf16[640,256]{1,0:T(8,128)(2,1)S(1)}, bf16[640,256]{1,0:T(8,128)(2,1)S(1)}, u32[]{:S(2)}, u32[]{:S(2)}) collective-permute-start(bf16[640,256]{1,0:T(8,128)(2,1)S(1)} %get-tuple-element.77), channel_id=1, source_target_pairs={{0,16},{4,20},{8,24},{12,28},{16,0},{20,4},{24,8},{28,12},{1,17},{... | collective-permute-start | bytes 983048 | tf_op jit(solution)/shard_map/ppermute | solution.py:20
  44.2 1.3 %collective-permute-start.6 = (bf16[640,256]{1,0:T(8,128)(2,1)S(1)}, bf16[640,256]{1,0:T(8,128)(2,1)S(1)}, u32[]{:S(2)}, u32[]{:S(2)}) collective-permute-start(bf16[640,256]{1,0:T(8,128)(2,1)S(1)} %get-tuple-element.78), channel_id=1, source_target_pairs={{0,8},{4,12},{8,0},{12,4},{16,24},{20,28},{24,16},{28,20},{1,9},{5... | collective-permute-start | bytes 983048 | tf_op jit(solution)/shard_map/ppermute | solution.py:20
  45.5 0.1 fusion.20
  45.7 3.8 %shard_map.146 = (f32[1280,128]{1,0:T(8,128)S(1)}, f32[1280,128]{1,0:T(8,128)S(1)}) custom-call(bf16[2560,512]{1,0:T(8,128)(2,1)S(1)} %copy-done.1, bf16[2560,512]{1,0:T(8,128)(2,1)} %collective-permute-done.refs_1_, bf16[512,1024]{1,0:T(8,128)(2,1)S(1)} %copy-done.3, bf16[512,1024]{1,0:T(8,128)(2,1)S(1)} %copy-done.5), custom_call_target="tpu_custom_call" | custom-call | flops 1 | bytes 1 | tf_op jit(solution)/shard_map/pallas_call | solution.py:180
  49.5 0.1 shard_map.147
  49.7 0.8 collective-permute-start.13
  50.4 0.2 collective-permute-done.8.refs_4_
  50.6 0.1 shard_map.148
  50.7 1.2 %collective-permute-start.12 = (bf16[960,128]{1,0:T(8,128)(2,1)S(1)}, bf16[960,128]{1,0:T(8,128)(2,1)S(1)}, u32[]{:S(2)}, u32[]{:S(2)}) collective-permute-start(bf16[960,128]{1,0:T(8,128)(2,1)S(1)} %get-tuple-element.90), channel_id=1, source_target_pairs={{0,8},{4,12},{8,0},{12,4},{16,24},{20,28},{24,16},{28,20},{1,9},{5... | collective-permute-start | bytes 737288 | tf_op jit(solution)/shard_map/ppermute | solution.py:20
  52.0 4.9 %collective-permute-done.5.refs_2_ = bf16[640,256]{1,0:T(8,128)(2,1)S(1)} collective-permute-done((bf16[640,256]{1,0:T(8,128)(2,1)S(1)}, bf16[640,256]{1,0:T(8,128)(2,1)S(1)}, u32[]{:S(2)}, u32[]{:S(2)}) %collective-permute-start.5) | collective-permute-done | bytes 327712 | tf_op jit(solution)/shard_map/ppermute | solution.py:20
  56.9 0.1 shard_map.149
  57.0 1.8 %collective-permute-start.10 = (bf16[640,256]{1,0:T(8,128)(2,1)S(1)}, bf16[640,256]{1,0:T(8,128)(2,1)S(1)}, u32[]{:S(2)}, u32[]{:S(2)}) collective-permute-start(bf16[640,256]{1,0:T(8,128)(2,1)S(1)} %get-tuple-element.95), channel_id=1, source_target_pairs={{0,1},{1,0},{2,3},{3,2},{4,5},{5,4},{6,7},{7,6},{8,9},{9,8},{10,11... | collective-permute-start | bytes 983048 | tf_op jit(solution)/shard_map/ppermute | solution.py:20
  58.8 0.2 fusion.13
  59.0 1.1 %collective-permute-start.11 = (bf16[640,128]{1,0:T(8,128)(2,1)S(1)}, bf16[640,128]{1,0:T(8,128)(2,1)S(1)}, u32[]{:S(2)}, u32[]{:S(2)}) collective-permute-start(bf16[640,128]{1,0:T(8,128)(2,1)S(1)} %get-tuple-element.99), channel_id=1, source_target_pairs={{0,16},{4,20},{8,24},{12,28},{16,0},{20,4},{24,8},{28,12},{1,17},{... | collective-permute-start | bytes 491528 | tf_op jit(solution)/shard_map/ppermute | solution.py:20
  60.1 0.6 collective-permute-done.13.refs_1_
  60.8 1.7 %collective-permute-start.16 = (bf16[320,256]{1,0:T(8,128)(2,1)S(1)}, bf16[320,256]{1,0:T(8,128)(2,1)S(1)}, u32[]{:S(2)}, u32[]{:S(2)}) collective-permute-start(bf16[320,256]{1,0:T(8,128)(2,1)S(1)} %get-tuple-element.102), channel_id=1, source_target_pairs={{0,16},{4,20},{8,24},{12,28},{16,0},{20,4},{24,8},{28,12},{1,17},{... | collective-permute-start | bytes 491528 | tf_op jit(solution)/shard_map/ppermute | solution.py:20
  62.5 3.5 %collective-permute-done.11.refs_3_ = bf16[640,128]{1,0:T(8,128)(2,1)S(1)} collective-permute-done((bf16[640,128]{1,0:T(8,128)(2,1)S(1)}, bf16[640,128]{1,0:T(8,128)(2,1)S(1)}, u32[]{:S(2)}, u32[]{:S(2)}) %collective-permute-start.11) | collective-permute-done | bytes 163872 | tf_op jit(solution)/shard_map/ppermute | solution.py:20
  66.1 0.4 collective-permute-start.15
  66.5 2.7 %collective-permute-start.14 = (bf16[320,256]{1,0:T(8,128)(2,1)S(1)}, bf16[320,256]{1,0:T(8,128)(2,1)S(1)}, u32[]{:S(2)}, u32[]{:S(2)}) collective-permute-start(bf16[320,256]{1,0:T(8,128)(2,1)S(1)} %get-tuple-element.108), channel_id=1, source_target_pairs={{0,2},{1,3},{2,0},{3,1},{4,6},{5,7},{6,4},{7,5},{8,10},{9,11},{10,... | collective-permute-start | bytes 491528 | tf_op jit(solution)/shard_map/ppermute | solution.py:20
  69.2 0.4 fusion
  69.7 0.8 collective-permute-start.17
  70.4 2.2 %collective-permute-done.15.refs_3_ = bf16[800,128]{1,0:T(8,128)(2,1)S(1)} collective-permute-done((bf16[800,128]{1,0:T(8,128)(2,1)S(1)}, bf16[800,128]{1,0:T(8,128)(2,1)S(1)}, u32[]{:S(2)}, u32[]{:S(2)}) %collective-permute-start.15) | collective-permute-done | bytes 204832 | tf_op jit(solution)/shard_map/ppermute | solution.py:20
  72.7 4.2 %collective-permute-start.18 = (bf16[400,128]{1,0:T(8,128)(2,1)S(1)}, bf16[400,128]{1,0:T(8,128)(2,1)S(1)}, u32[]{:S(2)}, u32[]{:S(2)}) collective-permute-start(bf16[400,128]{1,0:T(8,128)(2,1)S(1)} %get-tuple-element.116), channel_id=1, source_target_pairs={{0,2},{1,3},{2,0},{3,1},{4,6},{5,7},{6,4},{7,5},{8,10},{9,11},{10,... | collective-permute-start | bytes 307208 | tf_op jit(solution)/shard_map/ppermute | solution.py:20
  76.8 4.4 %collective-permute-done.14 = bf16[320,256]{1,0:T(8,128)(2,1)S(1)} collective-permute-done((bf16[320,256]{1,0:T(8,128)(2,1)S(1)}, bf16[320,256]{1,0:T(8,128)(2,1)S(1)}, u32[]{:S(2)}, u32[]{:S(2)}) %collective-permute-start.14) | collective-permute-done | bytes 163872 | tf_op jit(solution)/shard_map/ppermute | solution.py:20
  81.3 1.0 %collective-permute-done.17 = bf16[160,256]{1,0:T(8,128)(2,1)S(1)} collective-permute-done((bf16[160,256]{1,0:T(8,128)(2,1)S(1)}, bf16[160,256]{1,0:T(8,128)(2,1)S(1)}, u32[]{:S(2)}, u32[]{:S(2)}) %collective-permute-start.17) | collective-permute-done | bytes 81952 | tf_op jit(solution)/shard_map/ppermute | solution.py:20
  82.4 1.1 %collective-permute-done.18 = bf16[400,128]{1,0:T(8,128)(2,1)S(1)} collective-permute-done((bf16[400,128]{1,0:T(8,128)(2,1)S(1)}, bf16[400,128]{1,0:T(8,128)(2,1)S(1)}, u32[]{:S(2)}, u32[]{:S(2)}) %collective-permute-start.18) | collective-permute-done | bytes 102432 | tf_op jit(solution)/shard_map/ppermute | solution.py:20
  83.6 0.9 convolution_convert_fusion
  84.5 4.3 %all-to-all-start = ((bf16[32,8,256]{2,1,0:T(8,128)(2,1)}), bf16[32,8,256]{2,1,0:T(8,128)(2,1)S(1)}, u32[]{:S(2)}, u32[]{:S(2)}) async-start(bf16[32,8,256]{2,1,0:T(8,128)(2,1)} %bitcast.3), calls=%async_computation | async-start | bytes 262144 | tf_op jit(solution)/shard_map/all_to_all | solution.py:566
  88.9 8.3 %all-to-all-done = bf16[32,8,256]{2,1,0:T(8,128)(2,1)S(1)} async-done(((bf16[32,8,256]{2,1,0:T(8,128)(2,1)}), bf16[32,8,256]{2,1,0:T(8,128)(2,1)S(1)}, u32[]{:S(2)}, u32[]{:S(2)}) %all-to-all-start) | async-done | bytes 131104 | tf_op jit(solution)/shard_map/all_to_all | solution.py:566
  97.2 0.6 bitcast_convert_fusion
  97.9 0.6 copy.47
  (64 shorter events, 1.2 us)
Async XLA Ops:
  0.6 44.9 %copy-start = (bf16[8,256]{1,0:T(8,128)(2,1)S(1)}, bf16[8,256]{1,0:T(8,128)(2,1)}, u32[]{:S(2)}) copy-start(bf16[8,256]{1,0:T(8,128)(2,1)} %param.20) | copy-start | bytes 12292
  0.6 3.7 %copy-start.2 = (bf16[512,1024]{1,0:T(8,128)(2,1)S(1)}, bf16[512,1024]{1,0:T(8,128)(2,1)}, u32[]{:S(2)}) copy-start(bf16[512,1024]{1,0:T(8,128)(2,1)} %refs_2_.7) | copy-start | bytes 3145732
  0.7 3.8 %copy-start.13 = (s32[64]{0:T(128)S(1)}, s32[64]{0:T(128)}, u32[]{:S(2)}) copy-start(s32[64]{0:T(128)} %param.16) | copy-start | bytes 772
  3.8 9.7 %collective-permute-start = (bf16[2560,512]{1,0:T(8,128)(2,1)}, bf16[2560,512]{1,0:T(8,128)(2,1)}, u32[]{:S(2)}, u32[]{:S(2)}) collective-permute-start(bf16[2560,512]{1,0:T(8,128)(2,1)} %shard_map.140), channel_id=1, source_target_pairs={{0,4},{4,0},{8,12},{12,8},{16,20},{20,16},{24,28},{28,24},{1,5},{5... | collective-permute-start | bytes 7864328 | tf_op jit(solution)/shard_map/ppermute | solution.py:20
  4.3 8.1 %collective-permute-start.1 = (bf16[512,1024]{1,0:T(8,128)(2,1)S(1)}, bf16[512,1024]{1,0:T(8,128)(2,1)S(1)}, u32[]{:S(2)}, u32[]{:S(2)}) collective-permute-start(bf16[512,1024]{1,0:T(8,128)(2,1)S(1)} %copy-done.2), channel_id=1, source_target_pairs={{0,4},{4,0},{8,12},{12,8},{16,20},{20,16},{24,28},{28,24},{1,5},{5... | collective-permute-start | bytes 3145736 | tf_op jit(solution)/shard_map/ppermute | solution.py:20
  9.1 3.2 %copy-start.10 = (s32[8]{0:T(128)S(1)}, s32[8]{0:T(128)}, u32[]{:S(2)}) copy-start(s32[8]{0:T(128)} %param.23) | copy-start | bytes 100
  9.1 3.2 %collective-permute-start.4 = (bf16[1280,128]{1,0:T(8,128)(2,1)S(1)}, bf16[1280,128]{1,0:T(8,128)(2,1)S(1)}, u32[]{:S(2)}, u32[]{:S(2)}) collective-permute-start(bf16[1280,128]{1,0:T(8,128)(2,1)S(1)} %get-tuple-element.70), channel_id=1, source_target_pairs={{0,4},{4,0},{8,12},{12,8},{16,20},{20,16},{24,28},{28,24},{1,5},{5... | collective-permute-start | bytes 983048 | tf_op jit(solution)/shard_map/ppermute | solution.py:20
  12.5 1.1 %copy-start.4 = (bf16[512,1024]{1,0:T(8,128)(2,1)}, bf16[512,1024]{1,0:T(8,128)(2,1)S(1)}, u32[]{:S(2)}) copy-start(bf16[512,1024]{1,0:T(8,128)(2,1)S(1)} %collective-permute-done.1.refs_3_) | copy-start | bytes 3145732
  19.5 21.5 %collective-permute-start.2 = (bf16[1280,256]{1,0:T(8,128)(2,1)}, bf16[1280,256]{1,0:T(8,128)(2,1)}, u32[]{:S(2)}, u32[]{:S(2)}) collective-permute-start(bf16[1280,256]{1,0:T(8,128)(2,1)} %get-tuple-element.66), channel_id=1, source_target_pairs={{0,8},{4,12},{8,0},{12,4},{16,24},{20,28},{24,16},{28,20},{1,9},{5... | collective-permute-start | bytes 1966088 | tf_op jit(solution)/shard_map/ppermute | solution.py:20
  22.3 18.7 %collective-permute-start.3 = (bf16[1280,256]{1,0:T(8,128)(2,1)}, bf16[1280,256]{1,0:T(8,128)(2,1)}, u32[]{:S(2)}, u32[]{:S(2)}) collective-permute-start(bf16[1280,256]{1,0:T(8,128)(2,1)} %get-tuple-element.67), channel_id=1, source_target_pairs={{0,16},{4,20},{8,24},{12,28},{16,0},{20,4},{24,8},{28,12},{1,17},{... | collective-permute-start | bytes 1966088 | tf_op jit(solution)/shard_map/ppermute | solution.py:20
  23.7 8.5 %copy-start.8 = (bf16[8,2048]{1,0:T(8,128)(2,1)S(1)}, bf16[8,2048]{1,0:T(8,128)(2,1)}, u32[]{:S(2)}) copy-start(bf16[8,2048]{1,0:T(8,128)(2,1)} %param.17) | copy-start | bytes 98308
  23.7 11.3 %copy-start.3 = (bf16[512,1024]{1,0:T(8,128)(2,1)S(1)}, bf16[512,1024]{1,0:T(8,128)(2,1)}, u32[]{:S(2)}) copy-start(bf16[512,1024]{1,0:T(8,128)(2,1)} %refs_2_.7) | copy-start | bytes 3145732
  28.6 5.9 %copy-start.12 = (bf16[1280,128]{1,0:T(8,128)(2,1)S(1)}, bf16[1280,128]{1,0:T(8,128)(2,1)}, u32[]{:S(2)}) copy-start(bf16[1280,128]{1,0:T(8,128)(2,1)} %get-tuple-element.81) | copy-start | bytes 983044
  28.6 6.4 %copy-start.1 = (bf16[2560,512]{1,0:T(8,128)(2,1)S(1)}, bf16[2560,512]{1,0:T(8,128)(2,1)}, u32[]{:S(2)}) copy-start(bf16[2560,512]{1,0:T(8,128)(2,1)} %shard_map.139.refs_0_) | copy-start | bytes 7864324
  29.8 20.8 %collective-permute-start.8 = (bf16[1920,128]{1,0:T(8,128)(2,1)S(1)}, bf16[1920,128]{1,0:T(8,128)(2,1)S(1)}, u32[]{:S(2)}, u32[]{:S(2)}) collective-permute-start(bf16[1920,128]{1,0:T(8,128)(2,1)S(1)} %pad_maximum_fusion), channel_id=1, source_target_pairs={{0,16},{4,20},{8,24},{12,28},{16,0},{20,4},{24,8},{28,12},{1,17},{... | collective-permute-start | bytes 1474568 | tf_op jit(solution)/shard_map/ppermute | solution.py:20
  30.5 19.1 %collective-permute-start.9 = (bf16[1280,256]{1,0:T(8,128)(2,1)}, bf16[1280,256]{1,0:T(8,128)(2,1)S(1)}, u32[]{:S(2)}, u32[]{:S(2)}) collective-permute-start(bf16[1280,256]{1,0:T(8,128)(2,1)} %get-tuple-element.83), channel_id=1, source_target_pairs={{0,1},{1,0},{2,3},{3,2},{4,5},{5,4},{6,7},{7,6},{8,9},{9,8},{10,11... | collective-permute-start | bytes 1966088 | tf_op jit(solution)/shard_map/ppermute | solution.py:20
  34.5 15.9 %collective-permute-start.7 = (bf16[1280,128]{1,0:T(8,128)(2,1)S(1)}, bf16[1280,128]{1,0:T(8,128)(2,1)S(1)}, u32[]{:S(2)}, u32[]{:S(2)}) collective-permute-start(bf16[1280,128]{1,0:T(8,128)(2,1)S(1)} %copy-done.12), channel_id=1, source_target_pairs={{0,8},{4,12},{8,0},{12,4},{16,24},{20,28},{24,16},{28,20},{1,9},{5... | collective-permute-start | bytes 983048 | tf_op jit(solution)/shard_map/ppermute | solution.py:20
  35.0 1.2 %copy-start.5 = (bf16[512,1024]{1,0:T(8,128)(2,1)S(1)}, bf16[512,1024]{1,0:T(8,128)(2,1)}, u32[]{:S(2)}) copy-start(bf16[512,1024]{1,0:T(8,128)(2,1)} %copy-done.4) | copy-start | bytes 3145732
  42.6 14.3 %collective-permute-start.5 = (bf16[640,256]{1,0:T(8,128)(2,1)S(1)}, bf16[640,256]{1,0:T(8,128)(2,1)S(1)}, u32[]{:S(2)}, u32[]{:S(2)}) collective-permute-start(bf16[640,256]{1,0:T(8,128)(2,1)S(1)} %get-tuple-element.77), channel_id=1, source_target_pairs={{0,16},{4,20},{8,24},{12,28},{16,0},{20,4},{24,8},{28,12},{1,17},{... | collective-permute-start | bytes 983048 | tf_op jit(solution)/shard_map/ppermute | solution.py:20
  44.2 12.7 %collective-permute-start.6 = (bf16[640,256]{1,0:T(8,128)(2,1)S(1)}, bf16[640,256]{1,0:T(8,128)(2,1)S(1)}, u32[]{:S(2)}, u32[]{:S(2)}) collective-permute-start(bf16[640,256]{1,0:T(8,128)(2,1)S(1)} %get-tuple-element.78), channel_id=1, source_target_pairs={{0,8},{4,12},{8,0},{12,4},{16,24},{20,28},{24,16},{28,20},{1,9},{5... | collective-permute-start | bytes 983048 | tf_op jit(solution)/shard_map/ppermute | solution.py:20
  49.7 11.1 %collective-permute-start.13 = (bf16[640,256]{1,0:T(8,128)(2,1)S(1)}, bf16[640,256]{1,0:T(8,128)(2,1)S(1)}, u32[]{:S(2)}, u32[]{:S(2)}) collective-permute-start(bf16[640,256]{1,0:T(8,128)(2,1)S(1)} %get-tuple-element.85), channel_id=1, source_target_pairs={{0,8},{4,12},{8,0},{12,4},{16,24},{20,28},{24,16},{28,20},{1,9},{5... | collective-permute-start | bytes 983048 | tf_op jit(solution)/shard_map/ppermute | solution.py:20
  50.7 15.3 %collective-permute-start.12 = (bf16[960,128]{1,0:T(8,128)(2,1)S(1)}, bf16[960,128]{1,0:T(8,128)(2,1)S(1)}, u32[]{:S(2)}, u32[]{:S(2)}) collective-permute-start(bf16[960,128]{1,0:T(8,128)(2,1)S(1)} %get-tuple-element.90), channel_id=1, source_target_pairs={{0,8},{4,12},{8,0},{12,4},{16,24},{20,28},{24,16},{28,20},{1,9},{5... | collective-permute-start | bytes 737288 | tf_op jit(solution)/shard_map/ppermute | solution.py:20
  57.0 12.2 %copy-start.11 = (bf16[8,512,256]{2,1,0:T(8,128)(2,1)S(1)}, bf16[8,512,256]{2,1,0:T(8,128)(2,1)}, u32[]{:S(2)}) copy-start(bf16[8,512,256]{2,1,0:T(8,128)(2,1)} %param.19) | copy-start | bytes 6291460
  57.0 9.5 %collective-permute-start.10 = (bf16[640,256]{1,0:T(8,128)(2,1)S(1)}, bf16[640,256]{1,0:T(8,128)(2,1)S(1)}, u32[]{:S(2)}, u32[]{:S(2)}) collective-permute-start(bf16[640,256]{1,0:T(8,128)(2,1)S(1)} %get-tuple-element.95), channel_id=1, source_target_pairs={{0,1},{1,0},{2,3},{3,2},{4,5},{5,4},{6,7},{7,6},{8,9},{9,8},{10,11... | collective-permute-start | bytes 983048 | tf_op jit(solution)/shard_map/ppermute | solution.py:20
  59.0 7.0 %collective-permute-start.11 = (bf16[640,128]{1,0:T(8,128)(2,1)S(1)}, bf16[640,128]{1,0:T(8,128)(2,1)S(1)}, u32[]{:S(2)}, u32[]{:S(2)}) collective-permute-start(bf16[640,128]{1,0:T(8,128)(2,1)S(1)} %get-tuple-element.99), channel_id=1, source_target_pairs={{0,16},{4,20},{8,24},{12,28},{16,0},{20,4},{24,8},{28,12},{1,17},{... | collective-permute-start | bytes 491528 | tf_op jit(solution)/shard_map/ppermute | solution.py:20
  60.8 8.8 %collective-permute-start.16 = (bf16[320,256]{1,0:T(8,128)(2,1)S(1)}, bf16[320,256]{1,0:T(8,128)(2,1)S(1)}, u32[]{:S(2)}, u32[]{:S(2)}) collective-permute-start(bf16[320,256]{1,0:T(8,128)(2,1)S(1)} %get-tuple-element.102), channel_id=1, source_target_pairs={{0,16},{4,20},{8,24},{12,28},{16,0},{20,4},{24,8},{28,12},{1,17},{... | collective-permute-start | bytes 491528 | tf_op jit(solution)/shard_map/ppermute | solution.py:20
  66.1 6.5 %collective-permute-start.15 = (bf16[800,128]{1,0:T(8,128)(2,1)S(1)}, bf16[800,128]{1,0:T(8,128)(2,1)S(1)}, u32[]{:S(2)}, u32[]{:S(2)}) collective-permute-start(bf16[800,128]{1,0:T(8,128)(2,1)S(1)} %get-tuple-element.105), channel_id=1, source_target_pairs={{0,1},{1,0},{2,3},{3,2},{4,5},{5,4},{6,7},{7,6},{8,9},{9,8},{10,11... | collective-permute-start | bytes 614408 | tf_op jit(solution)/shard_map/ppermute | solution.py:20
  66.5 14.7 %collective-permute-start.14 = (bf16[320,256]{1,0:T(8,128)(2,1)S(1)}, bf16[320,256]{1,0:T(8,128)(2,1)S(1)}, u32[]{:S(2)}, u32[]{:S(2)}) collective-permute-start(bf16[320,256]{1,0:T(8,128)(2,1)S(1)} %get-tuple-element.108), channel_id=1, source_target_pairs={{0,2},{1,3},{2,0},{3,1},{4,6},{5,7},{6,4},{7,5},{8,10},{9,11},{10,... | collective-permute-start | bytes 491528 | tf_op jit(solution)/shard_map/ppermute | solution.py:20
  69.2 12.1 %copy-start.7 = (f32[160,1024]{1,0:T(8,128)S(1)}, f32[160,1024]{1,0:T(8,128)}, u32[]{:S(2)}) copy-start(f32[160,1024]{1,0:T(8,128)} %param.14) | copy-start | bytes 1966084
  69.7 19.1 %copy-start.14 = (f32[2]{0:T(128)S(1)}, f32[2]{0:T(128)}, u32[]{:S(2)}) copy-start(f32[2]{0:T(128)} %param.22) | copy-start | bytes 28
  69.7 12.7 %collective-permute-start.17 = (bf16[160,256]{1,0:T(8,128)(2,1)S(1)}, bf16[160,256]{1,0:T(8,128)(2,1)S(1)}, u32[]{:S(2)}, u32[]{:S(2)}) collective-permute-start(bf16[160,256]{1,0:T(8,128)(2,1)S(1)} %get-tuple-element.114), channel_id=1, source_target_pairs={{0,2},{1,3},{2,0},{3,1},{4,6},{5,7},{6,4},{7,5},{8,10},{9,11},{10,... | collective-permute-start | bytes 245768 | tf_op jit(solution)/shard_map/ppermute | solution.py:20
  72.6 24.6 %copy-start.9 = (bf16[8,256]{1,0:T(8,128)(2,1)S(1)}, bf16[8,256]{1,0:T(8,128)(2,1)}, u32[]{:S(2)}) copy-start(bf16[8,256]{1,0:T(8,128)(2,1)} %param.21) | copy-start | bytes 12292
  72.7 10.8 %collective-permute-start.18 = (bf16[400,128]{1,0:T(8,128)(2,1)S(1)}, bf16[400,128]{1,0:T(8,128)(2,1)S(1)}, u32[]{:S(2)}, u32[]{:S(2)}) collective-permute-start(bf16[400,128]{1,0:T(8,128)(2,1)S(1)} %get-tuple-element.116), channel_id=1, source_target_pairs={{0,2},{1,3},{2,0},{3,1},{4,6},{5,7},{6,4},{7,5},{8,10},{9,11},{10,... | collective-permute-start | bytes 307208 | tf_op jit(solution)/shard_map/ppermute | solution.py:20
  83.6 15.0 %copy-start.6 = (f32[160,1024]{1,0:T(8,128)}, f32[160,1024]{1,0:T(8,128)S(1)}, u32[]{:S(2)}) copy-start(f32[160,1024]{1,0:T(8,128)S(1)} %subtract_dynamic-update-slice_fusion.3) | copy-start | bytes 1966084
  84.5 12.7 %all-to-all-start = ((bf16[32,8,256]{2,1,0:T(8,128)(2,1)}), bf16[32,8,256]{2,1,0:T(8,128)(2,1)S(1)}, u32[]{:S(2)}, u32[]{:S(2)}) async-start(bf16[32,8,256]{2,1,0:T(8,128)(2,1)} %bitcast.3), calls=%async_computation | async-start | bytes 262144 | tf_op jit(solution)/shard_map/all_to_all | solution.py:566

commit v7 on v6

--- a/solution.py
+++ b/solution.py
@@ -99,9 +99,11 @@
     return runs
 
 
-def multiply(wanted, rows, blocks, base, staged, *refs):
+def multiply(wanted, rows, blocks, base, staged, tail, *refs):
     count = len(wanted)
     sources = refs[:4]
+    if tail:
+        appended, refs = refs[4], refs[:4] + refs[5:]
     outs = refs[4 : 4 + count]
     left, right, sems = refs[4 + count : 7 + count]
     stages, given = refs[7 + count : -1] if staged else outs, []
@@ -128,6 +130,15 @@
                 sources[at].at[span], left.at[span, half], sems.at[2 + 2 * block + at]
             )
             lefts[block, at].start()
+    if tail:
+        given.append(
+            pltpu.make_async_copy(
+                appended.at[pl.ds(tail, tail)],
+                outs[0].at[pl.ds(len(wanted[0][0]) * rows, tail)],
+                refs[-1].at[blocks, 0],
+            )
+        )
+        given[0].start()
     for copy in grads:
         copy.wait()
     for block in needed:
@@ -152,12 +163,12 @@
         copy.wait()
 
 
-def products(lefts, grads, wanted, rows, blocks, staged):
+def products(lefts, grads, wanted, rows, blocks, staged, appended=None):
     total, tokens = lefts[0].shape
     base = min(first for _, first, _, _ in wanted)
     columns = max(last for _, _, last, _ in wanted) - base
     if rows % 32 or any((first | last) % LANES for _, first, last, _ in wanted):
-        return [
+        results = [
             jnp.concatenate(
                 [
                     sum(
@@ -169,6 +180,10 @@
             ).astype(kind)
             for units, first, last, kind in wanted
         ]
+        if appended is not None:
+            results[0] = jnp.concatenate([results[0], appended[appended.shape[0] // 2 :]])
+        return results
+    tail = 0 if appended is None else appended.shape[0] // 2
     shapes = [
         jax.ShapeDtypeStruct((len(units) * rows, last - first), kind)
         for units, first, last, kind in wanted
@@ -176,11 +191,14 @@
     staging = []
     if staged:
         staging = [pltpu.VMEM(shape.shape, shape.dtype) for shape in shapes]
-        staging.append(pltpu.SemaphoreType.DMA((blocks, len(shapes))))
+        staging.append(pltpu.SemaphoreType.DMA((blocks + 1, len(shapes))))
+    if tail:
+        grown = (shapes[0].shape[0] + tail, shapes[0].shape[1])
+        shapes[0] = jax.ShapeDtypeStruct(grown, shapes[0].dtype)
     return pl.pallas_call(
-        functools.partial(multiply, wanted, rows, blocks, base, staged),
+        functools.partial(multiply, wanted, rows, blocks, base, staged, tail),
         out_shape=shapes,
-        in_specs=[pl.BlockSpec(memory_space=pltpu.HBM)] * 4,
+        in_specs=[pl.BlockSpec(memory_space=pltpu.HBM)] * (5 if tail else 4),
         out_specs=[pl.BlockSpec(memory_space=pltpu.HBM if staged else pltpu.VMEM)] * len(shapes),
         scratch_shapes=[
             pltpu.VMEM((total, 2 * tokens), lefts[0].dtype),
@@ -188,9 +206,9 @@
             pltpu.SemaphoreType.DMA((2 + 2 * blocks,)),
         ]
         + staging,
-        compiler_params=pltpu.CompilerParams(vmem_limit_bytes=62 << 20 if staged else VMEM // 2),
+        compiler_params=pltpu.CompilerParams(vmem_limit_bytes=127 << 19 if staged else VMEM // 2),
         cost_estimate=pl.CostEstimate(flops=1, bytes_accessed=1, transcendentals=0),
-    )(*lefts, *grads)
+    )(*lefts, *grads, *([appended] if tail else []))
 
 
 def pick_rows(arranged, units, place, table, tail, *refs):
@@ -200,6 +218,7 @@
     width = flipped.shape[0]
     rows = width // units
     lanes = outs[0].shape[1]
+    lanes = lanes // 2
     folds = lanes // tokens
     lines = rows // folds
 
@@ -243,8 +262,11 @@
                     flipped[pl.ds(pl.multiple_of(from_row + fold * lines, 8), lines), :]
                     for fold in range(folds)
                 ]
-                put = (j * units + unit) * lines
-                out[put : put + lines, :] = jnp.concatenate(pieces, axis=1).astype(out.dtype)
+                put = ((unit & 1) * len(arranged) + j) * lines
+                side_lanes = slice((unit >> 1) * lanes, ((unit >> 1) + 1) * lanes)
+                out[put : put + lines, side_lanes] = jnp.concatenate(pieces, axis=1).astype(
+                    out.dtype
+                )
 
 
 def add_and_split(plans, arrays, merged, *refs):
@@ -259,7 +281,7 @@
             start = 0
         if not merged:
             put = 0
-        for (size, order, go, keep), value, kept in zip(plan, inputs, outputs):
+        for (size, order, go, keep, have), value, kept in zip(plan, inputs, outputs):
 
             def sum_of(low, high):
                 pieces = []
@@ -277,17 +299,17 @@
                 sent[put + at * size : put + (at + 1) * size, :] = piece.astype(sent.dtype)
             for at, piece in enumerate(sum_of(go, go + keep)):
                 kept[at * size : (at + 1) * size, :] = piece
-            start += len(order) * size
+            start += have * size
             put += go * size
 
 
 def combine(plans, values, got, merged):
     columns = [parts[0].shape[1] for parts in values]
-    totals = [sum(size * go for size, _, go, _ in plan) for plan in plans]
+    totals = [sum(size * go for size, _, go, _, _ in plan) for plan in plans]
     outs = [
         jax.ShapeDtypeStruct((keep * size, width), jnp.float32)
         for plan, width in zip(plans, columns)
-        for size, _, _, keep in plan
+        for size, _, _, keep, _ in plan
     ]
     if merged:
         outs.append(jax.ShapeDtypeStruct((sum(totals), columns[0]), jnp.bfloat16))
@@ -308,6 +330,51 @@
     return kept, results, totals
 
 
+def own_share(coef, spans, plans, rows, tokens, blocks, *refs):
+    emb, master, out = refs[0], refs[1], refs[-1]
+    arrays = refs[2:-1]
+    lanes = emb.shape[1] // blocks
+    count_fsdp = tokens // out.shape[1]
+    col_width = out.shape[2]
+    folded = emb[...].astype(jnp.bfloat16)
+    lefts = [
+        jnp.concatenate(
+            [
+                folded[:, unit * lanes + at : unit * lanes + at + tokens]
+                for at in range(0, lanes, tokens)
+            ]
+        )
+        for unit in range(blocks)
+    ]
+
+    def both(left, right):
+        high = right.astype(jnp.bfloat16)
+        total = across(left, high)
+        if right.dtype == jnp.float32:
+            total += across(left, (right - high.astype(jnp.float32)).astype(jnp.bfloat16))
+        return total
+
+    pieces = []
+    for (first, last), plan in zip(spans, plans):
+        moved = jnp.zeros((tokens, last - first), jnp.float32)
+        for array, units in plan:
+            for at, unit in enumerate(units):
+                moved += both(lefts[unit], arrays[array][at * rows : (at + 1) * rows, :])
+        pieces.append(both(lefts[0], master[:, first:last]) - coef * moved)
+    share = jnp.concatenate(pieces, axis=1)
+    for f in range(count_fsdp):
+        for t in range(out.shape[0] // count_fsdp):
+            out[f * (out.shape[0] // count_fsdp) + t] = share[
+                f * out.shape[1] : (f + 1) * out.shape[1], t * col_width : (t + 1) * col_width
+            ]
+
+
+def across(left, right):
+    return lax.dot_general(
+        left, right, (((0,), (0,)), ((), ())), preferred_element_type=jnp.float32
+    )
+
+
 def fold_unit(part, lanes):
     rows, tokens = part.shape
     if tokens >= lanes:
@@ -337,25 +404,24 @@
             (place >= 0)[:, None], embed_table[jnp.maximum(place, 0)], jnp.zeros((), kind)
         )
         flipped = found.T
+
+        def folded(r, side, unit):
+            start = (((r ^ upper) << 1) | side) * width + (unit ^ t) * rows
+            return fold_unit(lax.dynamic_slice_in_dim(flipped, start, rows, 0), lanes)
+
         return [
             jnp.concatenate(
                 [
-                    fold_unit(
-                        lax.dynamic_slice_in_dim(
-                            flipped,
-                            (((r ^ upper) << 1) | side) * width + (unit ^ t) * rows,
-                            rows,
-                            0,
-                        ),
-                        lanes,
+                    jnp.concatenate(
+                        [folded(r, side, unit) for unit in range(low, units, 2)], axis=1
                     )
+                    for low in range(2)
                     for r in arranged
-                    for unit in range(units)
                 ]
             )
             for side in (1 - core, core)
         ]
-    shape = jax.ShapeDtypeStruct((len(arranged) * width * tokens // lanes, lanes), kind)
+    shape = jax.ShapeDtypeStruct((len(arranged) * width * tokens // lanes // 2, 2 * lanes), kind)
     return pl.pallas_call(
         functools.partial(pick_rows, arranged, units),
         grid=(1,),
@@ -447,90 +513,136 @@
         mask = 1 << step[1]
         return exchange(value, step[0], 2 * mask if step[0] == "fsdp" else mask)
 
-    def compute(which, sent):
+    def compute(which, sent, appended=None):
         wanted = []
         for index in which:
             chosen = split(places, orders[index][0])[0 if sent else 1]
             units = [places.index(p) for p in chosen]
             kind = jnp.bfloat16 if sent else jnp.float32
             wanted.append((units, *spans[index], kind))
-        return dict(zip(which, products(lefts, grads, wanted, rows, uppers, sent)))
-
-    going = compute([2, 0, 1], True)
-    got = {index: send(value, orders[index][0]) for index, value in going.items()}
-    going |= compute([3, 4], True)
-    got[3] = send(going[3], orders[3][0])
+        return dict(zip(which, products(lefts, grads, wanted, rows, uppers, sent, appended)))
 
     theirs, ours = lookup(embed_table, token_ids, arranged, count_tp, block, eighth)
     asked = ours + exchange(theirs, "fsdp", 1)
-    go, stay = split(places, orders[4][0])
+    pairs = [(r, low) for low in range(2) for r in arranged]
+    going = compute([0, 1], True)
+    got = {index: send(value, orders[index][0]) for index, value in going.items()}
+    going |= compute([2, 3, 4], True, asked)
+    got |= {index: send(going[index], orders[index][0]) for index in (3, 4, 2)}
+    token = going[4]
     values = compute([0, 1, 2], False)
-    token = jnp.concatenate([going[4], take(asked, places, go, lines)])
-    got[4] = send(token, orders[4][0])
     values |= compute([3, 4], False)
     values = {index: [value] for index, value in values.items()}
-    values[4].append(take(asked, places, stay, lines).astype(jnp.float32))
+    values[2].append(asked[: asked.shape[0] // 2].astype(jnp.float32))
     sizes = {index: [rows] for index in range(5)}
-    sizes[4].append(lines)
-    held = {index: places for index in range(5)}
-
-    def receive(index, step):
-        gone, kept = split(held[index], step)
-        landed = [flip(p, step) for p in gone]
+    sizes[2].append(lines)
+    held = {index: [split(places, orders[index][0])[1]] for index in range(5)}
+    held[2].append(split(pairs, orders[2][0])[1])
+    gone = {index: [split(places, orders[index][0])[0]] for index in range(5)}
+    gone[2].append(split(pairs, orders[2][0])[0])
+
+    def receive(index, step, arrived):
         start = 0
-        added = []
-        for value, size in zip(values[index], sizes[index]):
-            piece = got[index][start : start + len(gone) * size]
-            start += len(gone) * size
-            added.append(value + take(piece, landed, kept, size).astype(jnp.float32))
-        values[index], held[index] = added, kept
+        for part, (value, size) in enumerate(zip(values[index], sizes[index])):
+            landed = [flip(p, step) for p in gone[index][part]]
+            piece = arrived[start : start + len(landed) * size]
+            start += len(landed) * size
+            if part and step == last_tp:
+                piece = jnp.roll(piece, piece.shape[1] // 2, axis=1)
+            else:
+                piece = take(piece, landed, held[index][part], size)
+            values[index][part] = value + piece.astype(jnp.float32)
+
+    def onward(index, step):
+        return [
+            (places_now, places_now) if part and step == last_tp else split(places_now, step)
+            for part, places_now in enumerate(held[index])
+        ]
 
     def forward(index, step, following):
-        gone, kept = split(held[index], step)
-        landed = [flip(p, step) for p in gone]
-        go, keep = split(kept, following)
-        plan = [
-            (size, [(held_now[index].index(p), landed.index(p)) for p in go + keep], len(go), len(keep))
-            for size in sizes[index]
-        ]
-        held[index], held_now[index] = kept, keep
+        plan = []
+        for part, (go, keep) in enumerate(onward(index, following)):
+            landed = [flip(p, step) for p in gone[index][part]]
+            order = [(held[index][part].index(p), landed.index(p)) for p in go + keep]
+            plan.append((sizes[index][part], order, len(go), len(keep), len(landed)))
         return plan
 
-    held_now = {
-        index: split(places, orders[index][0])[1] for index in range(5)
-    }
-    plain = rows % 32 or any(size % 16 for size in sizes[4])
+    last_tp = steps_tp[-1]
+    rows_f = tokens_new // count_fsdp
+    col_width = columns // count_tp
+
+    def share_of(sums, emb):
+        if plain:
+            lefts_own = [
+                unfold_unit(emb[:, at * eighth : (at + 1) * eighth], rows) for at in range(2)
+            ]
+
+            def exact(left, right):
+                return lax.dot_general(
+                    left.astype(jnp.float32),
+                    right.astype(jnp.float32),
+                    (((0,), (0,)), ((), ())),
+                    precision=lax.Precision.HIGHEST,
+                )
+
+            pieces = []
+            for index, (first, last) in enumerate(spans):
+                moved = sum(exact(left, array) for left, array in zip(lefts_own, sums[index]))
+                pieces.append(exact(lefts_own[0], master_w[:, first:last]) - coef * moved)
+            out = jnp.concatenate(pieces, axis=1)
+            out = out.reshape(count_fsdp, rows_f, count_tp, col_width)
+            out = out.transpose(0, 2, 1, 3).reshape(devices_all, rows_f, col_width)
+            return out.astype(jnp.bfloat16)
+        arrays = [array for index in range(5) for array in sums[index]]
+        plans = [[(2 * index, [0]), (2 * index + 1, [1])] for index in range(5)]
+        return pl.pallas_call(
+            functools.partial(own_share, coef, spans, plans, rows, tokens_new, 2),
+            in_specs=[pl.BlockSpec(memory_space=pltpu.VMEM)] * (2 + len(arrays)),
+            out_specs=pl.BlockSpec(memory_space=pltpu.VMEM),
+            out_shape=jax.ShapeDtypeStruct((devices_all, rows_f, col_width), jnp.float32),
+            compiler_params=pltpu.CompilerParams(vmem_limit_bytes=VMEM // 4),
+            cost_estimate=pl.CostEstimate(flops=1, bytes_accessed=1, transcendentals=0),
+        )(emb, master_w, *arrays).astype(jnp.bfloat16)
+
+    plain = rows % 32 or lines % 16 or block % LANES or eighth % tokens_new
     groups = ((0, 1), (2,), (3, 4))
     inbox = {group: [got[index] for index in group] for group in groups}
     totals = {}
-    for at in range(len(one)):
-        for group in groups:
+    sums = {}
+    steps = len(one)
+    for at in range(steps):
+        last = at + 1 == steps
+        for group in ((2,), (0, 1), (3, 4)) if last else groups:
             *inbox[group], token = lax.optimization_barrier(inbox[group] + [token])
-            last = at + 1 == len(one)
             if plain or last:
                 if len(inbox[group]) < len(group):
                     whole = inbox[group][0]
                     cuts = [sum(totals[group][:place]) for place in range(len(group) + 1)]
                     inbox[group] = [whole[low:high] for low, high in zip(cuts[:-1], cuts[1:])]
                 for index, arrived in zip(group, inbox[group]):
-                    got[index] = arrived
-                    receive(index, orders[index][at])
+                    receive(index, orders[index][at], arrived)
             if last:
                 token = values[group[-1]][0]
+                if group == (2,):
+                    parts_own, token = lax.optimization_barrier(
+                        (share_of(sums, values[2][1]), token)
+                    )
+                    token = parts_own
+                    parts_own = lax.all_to_all(
+                        parts_own, ("fsdp", "tp"), split_axis=0, concat_axis=0
+                    )
                 continue
             if plain:
                 outgoing = []
                 for index in group:
-                    gone, kept = split(held[index], orders[index][at + 1])
-                    pieces = [
-                        take(value, held[index], gone, size).astype(jnp.bfloat16)
-                        for value, size in zip(values[index], sizes[index])
-                    ]
-                    values[index] = [
-                        take(value, held[index], kept, size)
-                        for value, size in zip(values[index], sizes[index])
-                    ]
-                    outgoing.append(jnp.concatenate(pieces))
+                    pieces = []
+                    for part, (go, keep) in enumerate(onward(index, orders[index][at + 1])):
+                        value, size = values[index][part], sizes[index][part]
+                        pieces.append(take(value, held[index][part], go, size))
+                        values[index][part] = take(value, held[index][part], keep, size)
+                    outgoing.append(jnp.concatenate(pieces).astype(jnp.bfloat16))
+                totals[group] = [value.shape[0] for value in outgoing]
+                merged = False
             else:
                 plans = [forward(i, orders[i][at], orders[i][at + 1]) for i in group]
                 merged = len({orders[i][at + 1] for i in group}) == 1
@@ -538,33 +650,28 @@
                     plans, [values[i] for i in group], inbox[group], merged
                 )
                 values |= dict(zip(group, kept))
+            for number, index in enumerate(group):
+                now = onward(index, orders[index][at + 1])
+                gone[index], held[index] = [list(parts) for parts in zip(*now)]
+                if at + 2 == steps:
+                    low = sum(totals[group][:number]) if merged else 0
+                    sent = outgoing[0 if merged else number]
+                    sums[index] = [values[index][0], sent[low : low + rows]]
             outgoing = lax.optimization_barrier(outgoing)
             token = outgoing[-1]
             inbox[group] = [
                 send(value, orders[index][at + 1]) for index, value in zip(group, outgoing)
             ]
+            if at == 1 and group == groups[0]:
+                queries, new_key, lengths, token = lax.optimization_barrier(
+                    (queries, new_key, lengths, token)
+                )
+    parts_own, _ = lax.optimization_barrier((parts_own, values[4][0]))
+    own_value = jnp.sum(parts_own.astype(jnp.float32), axis=0)
     w_next = jnp.concatenate(
         [master_w[:, low:high] - coef * values[at][0] for at, (low, high) in enumerate(spans)],
         axis=1,
     )
-
-    columns_own = unfold_unit(values[4][1].astype(jnp.bfloat16), rows)
-    share_own = lax.dot_general(
-        columns_own,
-        w_next.astype(jnp.bfloat16),
-        (((0,), (0,)), ((), ())),
-        preferred_element_type=jnp.float32,
-    )
-    rows_f = tokens_new // count_fsdp
-    col_width = columns // count_tp
-    blocks_own = (
-        share_own.astype(jnp.bfloat16)
-        .reshape(count_fsdp, rows_f, count_tp, col_width)
-        .transpose(0, 2, 1, 3)
-        .reshape(devices_all, rows_f, col_width)
-    )
-    parts_own = lax.all_to_all(blocks_own, ("fsdp", "tp"), split_axis=0, concat_axis=0)
-    own_value = jnp.sum(parts_own.astype(jnp.float32), axis=0)
 
     share = jnp.repeat(residual_mix, HD)[None, :]
     new_value = (share * own_value + (1.0 - share) * first_value.astype(jnp.float32)).astype(

time: 99.2 us -> 101 us (1.018)
  local copies, waits for them, and re-layouts: 3.14 us -> 6.04 us
  starting transfers between devices: 29.4 us -> 26.8 us
  matrix products: 3.8 us -> 1.31 us
  waiting for transfers between devices: 26.1 us -> 27.7 us
  other arithmetic: 2.53 us -> 3.79 us
    unnamed x31 -> x33, local copies, waits for them, and re-layouts: 2.98 us -> 5.94 us
    ppermute x19, starting transfers between devices: 25.2 us -> 23 us  [exchange(): lax.ppermute(value, axis, [(i, i ^ mask) for i in range(lax.axis_size(axi...]
    add x1, other arithmetic: 0.09 us -> 1.83 us  [per_device(): asked = ours + exchange(theirs, 'fsdp', 1)]
    ppermute x19, waiting for transfers between devices: 17.9 us -> 19.5 us  [exchange(): lax.ppermute(value, axis, [(i, i ^ mask) for i in range(lax.axis_size(axi...]
    dot_general x1, matrix products: 2.32 us -> 0.74 us  [per_device(): jnp.einsum('rkgd,rckd->rkgc', query_b, keys_b, preferred_element_type=jnp...]
    concatenate x1 -> x0, other arithmetic: 1.16 us -> none  [per_device(): token = jnp.concatenate([going[4], take(asked, places, go, lines)])]
  transfers between devices with their start and end apart: 20 -> 20, of which waited for: 9 -> 7; matrix products, arithmetic and copies ran while one was open for 5% -> 4% of each run, Pallas kernels for 24% -> 30%
where the time goes in v7:
time: 101 us; the launch traced here: 100 us
  Pallas kernels  33.3 us (33%)
  waiting for transfers between devices  27.7 us (27%)
  starting transfers between devices  26.8 us (27%)
  local copies, waits for them, and re-layouts  6.04 us (6%)
  other arithmetic  3.79 us (4%)
  matrix products  1.31 us (1%)
  between operations  1.01 us (1%)
    ppermute x19, starting transfers between devices, exchange(): lax.ppermute(value, axis, [(i, i ^ mask) for i in range(lax.axis_size(axi...  23 us
    pallas_call x4, Pallas kernels, products(): pl.pallas_call(functools.partial(multiply, wanted, rows, blocks, base, st...  20 us
    ppermute x19, waiting for transfers between devices, exchange(): lax.ppermute(value, axis, [(i, i ^ mask) for i in range(lax.axis_size(axi...  19.5 us
    all_to_all x1, waiting for transfers between devices, per_device(): lax.all_to_all(parts_own, ('fsdp', 'tp'), split_axis=0, concat_axis=0)  8.21 us
    pallas_call x2, Pallas kernels, pack(): pl.pallas_call(functools.partial(transpose_blocks, arranged, mine, units)...  6.22 us
    unnamed x33, local copies, waits for them, and re-layouts  5.94 us
    pallas_call x1, Pallas kernels, lookup(): pl.pallas_call(functools.partial(pick_rows, arranged, units), grid=(1,),...  4.33 us
    all_to_all x1, starting transfers between devices, per_device(): lax.all_to_all(parts_own, ('fsdp', 'tp'), split_axis=0, concat_axis=0)  3.84 us
  transfers between devices with their start and end apart: 20, of which 7 were waited for; matrix products, arithmetic and copies ran while one was open for 4% of the time, Pallas kernels for 30%

profile of v7, /device:TPU:0, one launch (start us, length us, event | category | flops | bytes accessed | tf_op | source)
XLA Modules:
  0.0 100.0 jit_solution(17033220437658061600)
XLA Ops:
  0.7 3.2 %shard_map.140 = bf16[2560,512]{1,0:T(8,128)(2,1)} custom-call(bf16[512,5120]{1,0:T(8,128)(2,1)} %source.3), custom_call_target="tpu_custom_call" | custom-call | bytes 5242880 | tf_op jit(solution)/shard_map/pallas_call | solution.py:74
  3.9 0.5 collective-permute-start
  4.5 4.3 %shard_map.143 = (bf16[640,256]{1,0:T(8,128)(2,1)}, bf16[640,256]{1,0:T(8,128)(2,1)S(1)}) custom-call(s32[64]{0:T(128)S(1)} %and_select_fusion.place, bf16[4748,5120]{1,0:T(8,128)(2,1)} %tail.1, bf16[4748,5120]{1,0:T(8,128)(2,1)} %tail.1), custom_call_target="tpu_custom_call" | custom-call | flops 1 | bytes 1 | tf_op jit(solution)/shard_map/pallas_call | solution.py:425
  8.8 1.0 %collective-permute-start.4 = (bf16[640,256]{1,0:T(8,128)(2,1)}, bf16[640,256]{1,0:T(8,128)(2,1)}, u32[]{:S(2)}, u32[]{:S(2)}) collective-permute-start(bf16[640,256]{1,0:T(8,128)(2,1)} %get-tuple-element.73), channel_id=1, source_target_pairs={{0,4},{4,0},{8,12},{12,8},{16,20},{20,16},{24,28},{28,24},{1,5},{5... | collective-permute-start | bytes 983048 | tf_op jit(solution)/shard_map/ppermute | solution.py:20
  9.9 3.0 %shard_map.139.refs_0_ = bf16[2560,512]{1,0:T(8,128)(2,1)} custom-call(bf16[512,5120]{1,0:T(8,128)(2,1)} %source.3), custom_call_target="tpu_custom_call" | custom-call | bytes 5242880 | tf_op jit(solution)/shard_map/pallas_call | solution.py:74
  12.9 1.1 %copy-done.4 = bf16[512,1024]{1,0:T(8,128)(2,1)} copy-done((bf16[512,1024]{1,0:T(8,128)(2,1)}, bf16[512,1024]{1,0:T(8,128)(2,1)S(1)}, u32[]{:S(2)}) %copy-start.4) | copy-done | bytes 1048600
  14.0 5.0 %shard_map.142 = (bf16[1280,256]{1,0:T(8,128)(2,1)}, bf16[1280,256]{1,0:T(8,128)(2,1)}) custom-call(bf16[2560,512]{1,0:T(8,128)(2,1)} %shard_map.139.refs_0_, bf16[2560,512]{1,0:T(8,128)(2,1)} %collective-permute-done.refs_1_, bf16[512,1024]{1,0:T(8,128)(2,1)} %refs_2_.7, bf16[512,1024]{1,0:T(8,128)(2,1)} %copy-done.4), custom_call_target="tpu_custom_call" | custom-call | flops 1 | bytes 1 | tf_op jit(solution)/shard_map/pallas_call | solution.py:198
  19.0 2.8 %collective-permute-start.2 = (bf16[1280,256]{1,0:T(8,128)(2,1)}, bf16[1280,256]{1,0:T(8,128)(2,1)}, u32[]{:S(2)}, u32[]{:S(2)}) collective-permute-start(bf16[1280,256]{1,0:T(8,128)(2,1)} %get-tuple-element.70), channel_id=1, source_target_pairs={{0,8},{4,12},{8,0},{12,4},{16,24},{20,28},{24,16},{28,20},{1,9},{5... | collective-permute-start | bytes 1966088 | tf_op jit(solution)/shard_map/ppermute | solution.py:20
  21.8 1.7 %collective-permute-start.3 = (bf16[1280,256]{1,0:T(8,128)(2,1)}, bf16[1280,256]{1,0:T(8,128)(2,1)}, u32[]{:S(2)}, u32[]{:S(2)}) collective-permute-start(bf16[1280,256]{1,0:T(8,128)(2,1)} %get-tuple-element.71), channel_id=1, source_target_pairs={{0,16},{4,20},{8,24},{12,28},{16,0},{20,4},{24,8},{28,12},{1,17},{... | collective-permute-start | bytes 1966088 | tf_op jit(solution)/shard_map/ppermute | solution.py:20
  23.5 1.8 %add.34.refs_4_ = bf16[640,256]{1,0:T(8,128)(2,1)} add(bf16[640,256]{1,0:T(8,128)(2,1)S(1)} %get-tuple-element.72, bf16[640,256]{1,0:T(8,128)(2,1)} %collective-permute-done.4) | non-fusion elementwise | flops 163840 | bytes 983040 | tf_op jit(solution)/shard_map/add | solution.py:526
  25.3 6.3 %shard_map.144 = (bf16[1600,256]{1,0:T(8,128)(2,1)}, bf16[1280,128]{1,0:T(8,128)(2,1)}, bf16[1280,128]{1,0:T(8,128)(2,1)}) custom-call(bf16[2560,512]{1,0:T(8,128)(2,1)} %shard_map.139.refs_0_, bf16[2560,512]{1,0:T(8,128)(2,1)} %collective-permute-done.refs_1_, bf16[512,1024]{1,0:T(8,128)(2,1)} %refs_2_.7, bf16[512,1024]{1,0:T(8,128)(2,1)} %copy-done.4, ...), custom_call_target="tpu_custom_call" | custom-call | flops 1 | bytes 1 | tf_op jit(solution)/shard_map/pallas_call | solution.py:198
  31.6 1.6 %collective-permute-start.9 = (bf16[1600,256]{1,0:T(8,128)(2,1)}, bf16[1600,256]{1,0:T(8,128)(2,1)S(1)}, u32[]{:S(2)}, u32[]{:S(2)}) collective-permute-start(bf16[1600,256]{1,0:T(8,128)(2,1)} %get-tuple-element.87), channel_id=1, source_target_pairs={{0,1},{1,0},{2,3},{3,2},{4,5},{5,4},{6,7},{7,6},{8,9},{9,8},{10,11... | collective-permute-start | bytes 2457608 | tf_op jit(solution)/shard_map/ppermute | solution.py:20
  33.3 0.4 collective-permute-start.7
  33.7 0.7 collective-permute-start.8
  34.4 1.7 %copy-done.1 = bf16[2560,512]{1,0:T(8,128)(2,1)S(1)} copy-done((bf16[2560,512]{1,0:T(8,128)(2,1)S(1)}, bf16[2560,512]{1,0:T(8,128)(2,1)}, u32[]{:S(2)}) %copy-start.1) | copy-done | bytes 2621464
  36.1 1.2 %copy-done.3 = bf16[512,1024]{1,0:T(8,128)(2,1)S(1)} copy-done((bf16[512,1024]{1,0:T(8,128)(2,1)S(1)}, bf16[512,1024]{1,0:T(8,128)(2,1)}, u32[]{:S(2)}) %copy-start.3) | copy-done | bytes 1048600
  37.4 1.2 %copy-done.5 = bf16[512,1024]{1,0:T(8,128)(2,1)S(1)} copy-done((bf16[512,1024]{1,0:T(8,128)(2,1)S(1)}, bf16[512,1024]{1,0:T(8,128)(2,1)}, u32[]{:S(2)}) %copy-start.5) | copy-done | bytes 1048600
  38.6 4.8 %shard_map.141 = (f32[1280,256]{1,0:T(8,128)S(1)}, f32[1280,256]{1,0:T(8,128)S(1)}, f32[1280,256]{1,0:T(8,128)S(1)}) custom-call(bf16[2560,512]{1,0:T(8,128)(2,1)S(1)} %copy-done.1, bf16[2560,512]{1,0:T(8,128)(2,1)} %collective-permute-done.refs_1_, bf16[512,1024]{1,0:T(8,128)(2,1)S(1)} %copy-done.3, bf16[512,1024]{1,0:T(8,128)(2,1)S(1)} %copy-done.5), custom_call_target="tpu_custom_call" | custom-call | flops 1 | bytes 1 | tf_op jit(solution)/shard_map/pallas_call | solution.py:198
  43.4 1.6 %shard_map.145 = (f32[640,256]{1,0:T(8,128)S(1)}, f32[640,256]{1,0:T(8,128)S(1)}, bf16[640,256]{1,0:T(8,128)(2,1)S(1)}, bf16[640,256]{1,0:T(8,128)(2,1)S(1)}) custom-call(f32[1280,256]{1,0:T(8,128)S(1)} %get-tuple-element.68.refs_0_, f32[1280,256]{1,0:T(8,128)S(1)} %get-tuple-element.69.refs_1_, bf16[1280,256]{1,0:T(8,128)(2,1)} %collective-permute-done.2.refs_2_, ...), custom_call_target="tpu_custom_call" | custom-call | flops 1 | bytes 1 | tf_op jit(solution)/shard_map/pallas_call | solution.py:320
  45.0 1.4 %collective-permute-start.5 = (bf16[640,256]{1,0:T(8,128)(2,1)S(1)}, bf16[640,256]{1,0:T(8,128)(2,1)S(1)}, u32[]{:S(2)}, u32[]{:S(2)}) collective-permute-start(bf16[640,256]{1,0:T(8,128)(2,1)S(1)} %get-tuple-element.81), channel_id=1, source_target_pairs={{0,16},{4,20},{8,24},{12,28},{16,0},{20,4},{24,8},{28,12},{1,17},{... | collective-permute-start | bytes 983048 | tf_op jit(solution)/shard_map/ppermute | solution.py:20
  46.4 1.6 %collective-permute-start.6 = (bf16[640,256]{1,0:T(8,128)(2,1)S(1)}, bf16[640,256]{1,0:T(8,128)(2,1)S(1)}, u32[]{:S(2)}, u32[]{:S(2)}) collective-permute-start(bf16[640,256]{1,0:T(8,128)(2,1)S(1)} %get-tuple-element.82), channel_id=1, source_target_pairs={{0,8},{4,12},{8,0},{12,4},{16,24},{20,28},{24,16},{28,20},{1,9},{5... | collective-permute-start | bytes 983048 | tf_op jit(solution)/shard_map/ppermute | solution.py:20
  48.2 3.8 %shard_map.146 = (f32[1280,128]{1,0:T(8,128)S(1)}, f32[1280,128]{1,0:T(8,128)S(1)}) custom-call(bf16[2560,512]{1,0:T(8,128)(2,1)S(1)} %copy-done.1, bf16[2560,512]{1,0:T(8,128)(2,1)} %collective-permute-done.refs_1_, bf16[512,1024]{1,0:T(8,128)(2,1)S(1)} %copy-done.3, bf16[512,1024]{1,0:T(8,128)(2,1)S(1)} %copy-done.5), custom_call_target="tpu_custom_call" | custom-call | flops 1 | bytes 1 | tf_op jit(solution)/shard_map/pallas_call | solution.py:198
  52.0 0.1 shard_map.147
  52.2 0.5 collective-permute-start.13
  52.8 0.8 collective-permute-start.11
  53.5 1.2 %collective-permute-start.12 = (bf16[640,128]{1,0:T(8,128)(2,1)S(1)}, bf16[640,128]{1,0:T(8,128)(2,1)S(1)}, u32[]{:S(2)}, u32[]{:S(2)}) collective-permute-start(bf16[640,128]{1,0:T(8,128)(2,1)S(1)} %get-tuple-element.94), channel_id=1, source_target_pairs={{0,8},{4,12},{8,0},{12,4},{16,24},{20,28},{24,16},{28,20},{1,9},{5... | collective-permute-start | bytes 491528 | tf_op jit(solution)/shard_map/ppermute | solution.py:20
  54.7 1.1 %collective-permute-done.6.refs_3_ = bf16[640,256]{1,0:T(8,128)(2,1)S(1)} collective-permute-done((bf16[640,256]{1,0:T(8,128)(2,1)S(1)}, bf16[640,256]{1,0:T(8,128)(2,1)S(1)}, u32[]{:S(2)}, u32[]{:S(2)}) %collective-permute-start.6) | collective-permute-done | bytes 327712 | tf_op jit(solution)/shard_map/ppermute | solution.py:20
  55.9 0.4 collective-permute-start.10
  56.4 0.1 fusion.16
  56.5 0.7 fusion.25
  57.3 0.2 fusion.12
  57.5 0.4 fusion
  58.0 6.7 %collective-permute-done.13.refs_2_ = bf16[800,256]{1,0:T(8,128)(2,1)S(1)} collective-permute-done((bf16[800,256]{1,0:T(8,128)(2,1)S(1)}, bf16[800,256]{1,0:T(8,128)(2,1)S(1)}, u32[]{:S(2)}, u32[]{:S(2)}) %collective-permute-start.13) | collective-permute-done | bytes 409632 | tf_op jit(solution)/shard_map/ppermute | solution.py:20
  64.8 1.1 %collective-permute-start.15 = (bf16[400,256]{1,0:T(8,128)(2,1)S(1)}, bf16[400,256]{1,0:T(8,128)(2,1)S(1)}, u32[]{:S(2)}, u32[]{:S(2)}) collective-permute-start(bf16[400,256]{1,0:T(8,128)(2,1)S(1)} %get-tuple-element.105), channel_id=1, source_target_pairs={{0,16},{4,20},{8,24},{12,28},{16,0},{20,4},{24,8},{28,12},{1,17},{... | collective-permute-start | bytes 614408 | tf_op jit(solution)/shard_map/ppermute | solution.py:20
  65.9 1.3 %collective-permute-done.12.refs_3_ = bf16[640,128]{1,0:T(8,128)(2,1)S(1)} collective-permute-done((bf16[640,128]{1,0:T(8,128)(2,1)S(1)}, bf16[640,128]{1,0:T(8,128)(2,1)S(1)}, u32[]{:S(2)}, u32[]{:S(2)}) %collective-permute-start.12) | collective-permute-done | bytes 163872 | tf_op jit(solution)/shard_map/ppermute | solution.py:20
  67.2 0.5 collective-permute-start.17
  67.8 2.6 %collective-permute-start.14 = (bf16[320,256]{1,0:T(8,128)(2,1)S(1)}, bf16[320,256]{1,0:T(8,128)(2,1)S(1)}, u32[]{:S(2)}, u32[]{:S(2)}) collective-permute-start(bf16[320,256]{1,0:T(8,128)(2,1)S(1)} %get-tuple-element.111), channel_id=1, source_target_pairs={{0,2},{1,3},{2,0},{3,1},{4,6},{5,7},{6,4},{7,5},{8,10},{9,11},{10,... | collective-permute-start | bytes 491528 | tf_op jit(solution)/shard_map/ppermute | solution.py:20
  70.4 0.2 collective-permute-done.15.refs_2_
  70.6 3.1 %collective-permute-start.16 = (bf16[240,256]{1,0:T(8,128)(2,1)S(1)}, bf16[240,256]{1,0:T(8,128)(2,1)S(1)}, u32[]{:S(2)}, u32[]{:S(2)}) collective-permute-start(bf16[240,256]{1,0:T(8,128)(2,1)S(1)} %get-tuple-element.116), channel_id=1, source_target_pairs={{0,2},{1,3},{2,0},{3,1},{4,6},{5,7},{6,4},{7,5},{8,10},{9,11},{10,... | collective-permute-start | bytes 368648 | tf_op jit(solution)/shard_map/ppermute | solution.py:20
  73.7 2.3 %collective-permute-done.17.refs_2_ = bf16[640,128]{1,0:T(8,128)(2,1)S(1)} collective-permute-done((bf16[640,128]{1,0:T(8,128)(2,1)S(1)}, bf16[640,128]{1,0:T(8,128)(2,1)S(1)}, u32[]{:S(2)}, u32[]{:S(2)}) %collective-permute-start.17) | collective-permute-done | bytes 163872 | tf_op jit(solution)/shard_map/ppermute | solution.py:20
  76.1 1.0 collective-permute-start.18
  77.0 8.0 %collective-permute-done.16 = bf16[240,256]{1,0:T(8,128)(2,1)S(1)} collective-permute-done((bf16[240,256]{1,0:T(8,128)(2,1)S(1)}, bf16[240,256]{1,0:T(8,128)(2,1)S(1)}, u32[]{:S(2)}, u32[]{:S(2)}) %collective-permute-start.16) | collective-permute-done | bytes 122912 | tf_op jit(solution)/shard_map/ppermute | solution.py:20
  85.1 0.6 shard_map.155
  85.7 0.7 convert_element_type.60
  86.4 3.8 %all-to-all-start = ((bf16[32,8,256]{2,1,0:T(8,128)(2,1)}), bf16[32,8,256]{2,1,0:T(8,128)(2,1)S(1)}, u32[]{:S(2)}, u32[]{:S(2)}) async-start(bf16[32,8,256]{2,1,0:T(8,128)(2,1)} %convert_element_type.60), calls=%async_computation | async-start | bytes 262144 | tf_op jit(solution)/shard_map/all_to_all | solution.py:631
  90.4 8.2 %all-to-all-done = bf16[32,8,256]{2,1,0:T(8,128)(2,1)S(1)} async-done(((bf16[32,8,256]{2,1,0:T(8,128)(2,1)}), bf16[32,8,256]{2,1,0:T(8,128)(2,1)S(1)}, u32[]{:S(2)}, u32[]{:S(2)}) %all-to-all-start) | async-done | bytes 131104 | tf_op jit(solution)/shard_map/all_to_all | solution.py:631
  98.7 0.6 bitcast_convert_fusion
  99.4 0.6 copy.47
  (70 shorter events, 1.2 us)
Async XLA Ops:
  0.6 55.8 %copy-start = (bf16[8,256]{1,0:T(8,128)(2,1)S(1)}, bf16[8,256]{1,0:T(8,128)(2,1)}, u32[]{:S(2)}) copy-start(bf16[8,256]{1,0:T(8,128)(2,1)} %param.20) | copy-start | bytes 12292
  0.6 3.7 %copy-start.2 = (bf16[512,1024]{1,0:T(8,128)(2,1)S(1)}, bf16[512,1024]{1,0:T(8,128)(2,1)}, u32[]{:S(2)}) copy-start(bf16[512,1024]{1,0:T(8,128)(2,1)} %refs_2_.7) | copy-start | bytes 3145732
  0.7 3.8 %copy-start.14 = (s32[64]{0:T(128)S(1)}, s32[64]{0:T(128)}, u32[]{:S(2)}) copy-start(s32[64]{0:T(128)} %param.16) | copy-start | bytes 772
  3.9 10.1 %collective-permute-start = (bf16[2560,512]{1,0:T(8,128)(2,1)}, bf16[2560,512]{1,0:T(8,128)(2,1)}, u32[]{:S(2)}, u32[]{:S(2)}) collective-permute-start(bf16[2560,512]{1,0:T(8,128)(2,1)} %shard_map.140), channel_id=1, source_target_pairs={{0,4},{4,0},{8,12},{12,8},{16,20},{20,16},{24,28},{28,24},{1,5},{5... | collective-permute-start | bytes 7864328 | tf_op jit(solution)/shard_map/ppermute | solution.py:20
  4.4 8.5 %collective-permute-start.1 = (bf16[512,1024]{1,0:T(8,128)(2,1)S(1)}, bf16[512,1024]{1,0:T(8,128)(2,1)S(1)}, u32[]{:S(2)}, u32[]{:S(2)}) collective-permute-start(bf16[512,1024]{1,0:T(8,128)(2,1)S(1)} %copy-done.2), channel_id=1, source_target_pairs={{0,4},{4,0},{8,12},{12,8},{16,20},{20,16},{24,28},{28,24},{1,5},{5... | collective-permute-start | bytes 3145736 | tf_op jit(solution)/shard_map/ppermute | solution.py:20
  8.8 14.7 %collective-permute-start.4 = (bf16[640,256]{1,0:T(8,128)(2,1)}, bf16[640,256]{1,0:T(8,128)(2,1)}, u32[]{:S(2)}, u32[]{:S(2)}) collective-permute-start(bf16[640,256]{1,0:T(8,128)(2,1)} %get-tuple-element.73), channel_id=1, source_target_pairs={{0,4},{4,0},{8,12},{12,8},{16,20},{20,16},{24,28},{28,24},{1,5},{5... | collective-permute-start | bytes 983048 | tf_op jit(solution)/shard_map/ppermute | solution.py:20
  12.9 1.1 %copy-start.4 = (bf16[512,1024]{1,0:T(8,128)(2,1)}, bf16[512,1024]{1,0:T(8,128)(2,1)S(1)}, u32[]{:S(2)}) copy-start(bf16[512,1024]{1,0:T(8,128)(2,1)S(1)} %collective-permute-done.1.refs_3_) | copy-start | bytes 3145732
  19.0 24.4 %collective-permute-start.2 = (bf16[1280,256]{1,0:T(8,128)(2,1)}, bf16[1280,256]{1,0:T(8,128)(2,1)}, u32[]{:S(2)}, u32[]{:S(2)}) collective-permute-start(bf16[1280,256]{1,0:T(8,128)(2,1)} %get-tuple-element.70), channel_id=1, source_target_pairs={{0,8},{4,12},{8,0},{12,4},{16,24},{20,28},{24,16},{28,20},{1,9},{5... | collective-permute-start | bytes 1966088 | tf_op jit(solution)/shard_map/ppermute | solution.py:20
  21.8 21.7 %collective-permute-start.3 = (bf16[1280,256]{1,0:T(8,128)(2,1)}, bf16[1280,256]{1,0:T(8,128)(2,1)}, u32[]{:S(2)}, u32[]{:S(2)}) collective-permute-start(bf16[1280,256]{1,0:T(8,128)(2,1)} %get-tuple-element.71), channel_id=1, source_target_pairs={{0,16},{4,20},{8,24},{12,28},{16,0},{20,4},{24,8},{28,12},{1,17},{... | collective-permute-start | bytes 1966088 | tf_op jit(solution)/shard_map/ppermute | solution.py:20
  25.3 7.9 %copy-start.15 = (f32[2]{0:T(128)S(1)}, f32[2]{0:T(128)}, u32[]{:S(2)}) copy-start(f32[2]{0:T(128)} %param.22) | copy-start | bytes 28
  31.6 20.4 %collective-permute-start.9 = (bf16[1600,256]{1,0:T(8,128)(2,1)}, bf16[1600,256]{1,0:T(8,128)(2,1)S(1)}, u32[]{:S(2)}, u32[]{:S(2)}) collective-permute-start(bf16[1600,256]{1,0:T(8,128)(2,1)} %get-tuple-element.87), channel_id=1, source_target_pairs={{0,1},{1,0},{2,3},{3,2},{4,5},{5,4},{6,7},{7,6},{8,9},{9,8},{10,11... | collective-permute-start | bytes 2457608 | tf_op jit(solution)/shard_map/ppermute | solution.py:20
  33.3 19.4 %collective-permute-start.7 = (bf16[1280,128]{1,0:T(8,128)(2,1)}, bf16[1280,128]{1,0:T(8,128)(2,1)S(1)}, u32[]{:S(2)}, u32[]{:S(2)}) collective-permute-start(bf16[1280,128]{1,0:T(8,128)(2,1)} %get-tuple-element.85), channel_id=1, source_target_pairs={{0,8},{4,12},{8,0},{12,4},{16,24},{20,28},{24,16},{28,20},{1,9},{5... | collective-permute-start | bytes 983048 | tf_op jit(solution)/shard_map/ppermute | solution.py:20
  33.7 19.0 %collective-permute-start.8 = (bf16[1280,128]{1,0:T(8,128)(2,1)}, bf16[1280,128]{1,0:T(8,128)(2,1)S(1)}, u32[]{:S(2)}, u32[]{:S(2)}) collective-permute-start(bf16[1280,128]{1,0:T(8,128)(2,1)} %get-tuple-element.74), channel_id=1, source_target_pairs={{0,16},{4,20},{8,24},{12,28},{16,0},{20,4},{24,8},{28,12},{1,17},{... | collective-permute-start | bytes 983048 | tf_op jit(solution)/shard_map/ppermute | solution.py:20
  34.4 1.7 %copy-start.1 = (bf16[2560,512]{1,0:T(8,128)(2,1)S(1)}, bf16[2560,512]{1,0:T(8,128)(2,1)}, u32[]{:S(2)}) copy-start(bf16[2560,512]{1,0:T(8,128)(2,1)} %shard_map.139.refs_0_) | copy-start | bytes 7864324
  36.1 1.2 %copy-start.3 = (bf16[512,1024]{1,0:T(8,128)(2,1)S(1)}, bf16[512,1024]{1,0:T(8,128)(2,1)}, u32[]{:S(2)}) copy-start(bf16[512,1024]{1,0:T(8,128)(2,1)} %refs_2_.7) | copy-start | bytes 3145732
  37.3 1.2 %copy-start.5 = (bf16[512,1024]{1,0:T(8,128)(2,1)S(1)}, bf16[512,1024]{1,0:T(8,128)(2,1)}, u32[]{:S(2)}) copy-start(bf16[512,1024]{1,0:T(8,128)(2,1)} %copy-done.4) | copy-start | bytes 3145732
  43.4 4.7 %copy-start.8 = (bf16[640,256]{1,0:T(8,128)(2,1)S(1)}, bf16[640,256]{1,0:T(8,128)(2,1)}, u32[]{:S(2)}) copy-start(bf16[640,256]{1,0:T(8,128)(2,1)} %add.34.refs_4_) | copy-start | bytes 983044
  45.0 9.7 %collective-permute-start.5 = (bf16[640,256]{1,0:T(8,128)(2,1)S(1)}, bf16[640,256]{1,0:T(8,128)(2,1)S(1)}, u32[]{:S(2)}, u32[]{:S(2)}) collective-permute-start(bf16[640,256]{1,0:T(8,128)(2,1)S(1)} %get-tuple-element.81), channel_id=1, source_target_pairs={{0,16},{4,20},{8,24},{12,28},{16,0},{20,4},{24,8},{28,12},{1,17},{... | collective-permute-start | bytes 983048 | tf_op jit(solution)/shard_map/ppermute | solution.py:20
  46.4 9.4 %collective-permute-start.6 = (bf16[640,256]{1,0:T(8,128)(2,1)S(1)}, bf16[640,256]{1,0:T(8,128)(2,1)S(1)}, u32[]{:S(2)}, u32[]{:S(2)}) collective-permute-start(bf16[640,256]{1,0:T(8,128)(2,1)S(1)} %get-tuple-element.82), channel_id=1, source_target_pairs={{0,8},{4,12},{8,0},{12,4},{16,24},{20,28},{24,16},{28,20},{1,9},{5... | collective-permute-start | bytes 983048 | tf_op jit(solution)/shard_map/ppermute | solution.py:20
  52.2 4.1 %copy-start.12 = (s32[8]{0:T(128)S(1)}, s32[8]{0:T(128)}, u32[]{:S(2)}) copy-start(s32[8]{0:T(128)} %param.23) | copy-start | bytes 100
  52.2 4.2 %copy-start.10 = (bf16[8,2048]{1,0:T(8,128)(2,1)S(1)}, bf16[8,2048]{1,0:T(8,128)(2,1)}, u32[]{:S(2)}) copy-start(bf16[8,2048]{1,0:T(8,128)(2,1)} %param.17) | copy-start | bytes 98308
  52.2 4.3 %copy-start.7 = (bf16[8,512,256]{2,1,0:T(8,128)(2,1)S(1)}, bf16[8,512,256]{2,1,0:T(8,128)(2,1)}, u32[]{:S(2)}) copy-start(bf16[8,512,256]{2,1,0:T(8,128)(2,1)} %param.18) | copy-start | bytes 6291460
  52.2 12.5 %collective-permute-start.13 = (bf16[800,256]{1,0:T(8,128)(2,1)S(1)}, bf16[800,256]{1,0:T(8,128)(2,1)S(1)}, u32[]{:S(2)}, u32[]{:S(2)}) collective-permute-start(bf16[800,256]{1,0:T(8,128)(2,1)S(1)} %get-tuple-element.89), channel_id=1, source_target_pairs={{0,8},{4,12},{8,0},{12,4},{16,24},{20,28},{24,16},{28,20},{1,9},{5... | collective-permute-start | bytes 1228808 | tf_op jit(solution)/shard_map/ppermute | solution.py:20
  52.8 13.1 %collective-permute-start.11 = (bf16[640,128]{1,0:T(8,128)(2,1)S(1)}, bf16[640,128]{1,0:T(8,128)(2,1)S(1)}, u32[]{:S(2)}, u32[]{:S(2)}) collective-permute-start(bf16[640,128]{1,0:T(8,128)(2,1)S(1)} %get-tuple-element.102), channel_id=1, source_target_pairs={{0,16},{4,20},{8,24},{12,28},{16,0},{20,4},{24,8},{28,12},{1,17},{... | collective-permute-start | bytes 491528 | tf_op jit(solution)/shard_map/ppermute | solution.py:20
  53.5 13.6 %collective-permute-start.12 = (bf16[640,128]{1,0:T(8,128)(2,1)S(1)}, bf16[640,128]{1,0:T(8,128)(2,1)S(1)}, u32[]{:S(2)}, u32[]{:S(2)}) collective-permute-start(bf16[640,128]{1,0:T(8,128)(2,1)S(1)} %get-tuple-element.94), channel_id=1, source_target_pairs={{0,8},{4,12},{8,0},{12,4},{16,24},{20,28},{24,16},{28,20},{1,9},{5... | collective-permute-start | bytes 491528 | tf_op jit(solution)/shard_map/ppermute | solution.py:20
  55.8 1.7 %copy-start.13 = (bf16[8,512,256]{2,1,0:T(8,128)(2,1)S(1)}, bf16[8,512,256]{2,1,0:T(8,128)(2,1)}, u32[]{:S(2)}) copy-start(bf16[8,512,256]{2,1,0:T(8,128)(2,1)} %param.19) | copy-start | bytes 6291460
  55.9 11.8 %collective-permute-start.10 = (bf16[640,256]{1,0:T(8,128)(2,1)S(1)}, bf16[640,256]{1,0:T(8,128)(2,1)S(1)}, u32[]{:S(2)}, u32[]{:S(2)}) collective-permute-start(bf16[640,256]{1,0:T(8,128)(2,1)S(1)} %get-tuple-element.99), channel_id=1, source_target_pairs={{0,1},{1,0},{2,3},{3,2},{4,5},{5,4},{6,7},{7,6},{8,9},{9,8},{10,11... | collective-permute-start | bytes 983048 | tf_op jit(solution)/shard_map/ppermute | solution.py:20
  64.7 20.3 %copy-start.6 = (f32[160,1024]{1,0:T(8,128)S(1)}, f32[160,1024]{1,0:T(8,128)}, u32[]{:S(2)}) copy-start(f32[160,1024]{1,0:T(8,128)} %refs_1_.1) | copy-start | bytes 1966084
  64.8 5.8 %collective-permute-start.15 = (bf16[400,256]{1,0:T(8,128)(2,1)S(1)}, bf16[400,256]{1,0:T(8,128)(2,1)S(1)}, u32[]{:S(2)}, u32[]{:S(2)}) collective-permute-start(bf16[400,256]{1,0:T(8,128)(2,1)S(1)} %get-tuple-element.105), channel_id=1, source_target_pairs={{0,16},{4,20},{8,24},{12,28},{16,0},{20,4},{24,8},{28,12},{1,17},{... | collective-permute-start | bytes 614408 | tf_op jit(solution)/shard_map/ppermute | solution.py:20
  67.2 8.9 %collective-permute-start.17 = (bf16[640,128]{1,0:T(8,128)(2,1)S(1)}, bf16[640,128]{1,0:T(8,128)(2,1)S(1)}, u32[]{:S(2)}, u32[]{:S(2)}) collective-permute-start(bf16[640,128]{1,0:T(8,128)(2,1)S(1)} %get-tuple-element.108), channel_id=1, source_target_pairs={{0,1},{1,0},{2,3},{3,2},{4,5},{5,4},{6,7},{7,6},{8,9},{9,8},{10,11... | collective-permute-start | bytes 491528 | tf_op jit(solution)/shard_map/ppermute | solution.py:20
  67.8 22.4 %collective-permute-start.14 = (bf16[320,256]{1,0:T(8,128)(2,1)S(1)}, bf16[320,256]{1,0:T(8,128)(2,1)S(1)}, u32[]{:S(2)}, u32[]{:S(2)}) collective-permute-start(bf16[320,256]{1,0:T(8,128)(2,1)S(1)} %get-tuple-element.111), channel_id=1, source_target_pairs={{0,2},{1,3},{2,0},{3,1},{4,6},{5,7},{6,4},{7,5},{8,10},{9,11},{10,... | collective-permute-start | bytes 491528 | tf_op jit(solution)/shard_map/ppermute | solution.py:20
  70.6 14.4 %collective-permute-start.16 = (bf16[240,256]{1,0:T(8,128)(2,1)S(1)}, bf16[240,256]{1,0:T(8,128)(2,1)S(1)}, u32[]{:S(2)}, u32[]{:S(2)}) collective-permute-start(bf16[240,256]{1,0:T(8,128)(2,1)S(1)} %get-tuple-element.116), channel_id=1, source_target_pairs={{0,2},{1,3},{2,0},{3,1},{4,6},{5,7},{6,4},{7,5},{8,10},{9,11},{10,... | collective-permute-start | bytes 368648 | tf_op jit(solution)/shard_map/ppermute | solution.py:20
  76.1 14.3 %collective-permute-start.18 = (bf16[320,128]{1,0:T(8,128)(2,1)S(1)}, bf16[320,128]{1,0:T(8,128)(2,1)S(1)}, u32[]{:S(2)}, u32[]{:S(2)}) collective-permute-start(bf16[320,128]{1,0:T(8,128)(2,1)S(1)} %get-tuple-element.120), channel_id=1, source_target_pairs={{0,2},{1,3},{2,0},{3,1},{4,6},{5,7},{6,4},{7,5},{8,10},{9,11},{10,... | collective-permute-start | bytes 245768 | tf_op jit(solution)/shard_map/ppermute | solution.py:20
  85.7 13.0 %copy-start.11 = (bf16[8,256]{1,0:T(8,128)(2,1)S(1)}, bf16[8,256]{1,0:T(8,128)(2,1)}, u32[]{:S(2)}) copy-start(bf16[8,256]{1,0:T(8,128)(2,1)} %param.21) | copy-start | bytes 12292
  86.4 12.3 %all-to-all-start = ((bf16[32,8,256]{2,1,0:T(8,128)(2,1)}), bf16[32,8,256]{2,1,0:T(8,128)(2,1)S(1)}, u32[]{:S(2)}, u32[]{:S(2)}) async-start(bf16[32,8,256]{2,1,0:T(8,128)(2,1)} %convert_element_type.60), calls=%async_computation | async-start | bytes 262144 | tf_op jit(solution)/shard_map/all_to_all | solution.py:631
  90.4 9.6 %copy-start.9 = (f32[160,1024]{1,0:T(8,128)}, f32[160,1024]{1,0:T(8,128)S(1)}, u32[]{:S(2)}) copy-start(f32[160,1024]{1,0:T(8,128)S(1)} %subtract_dynamic-update-slice_fusion.3) | copy-start | bytes 1966084

commit v8 on v7

--- a/solution.py
+++ b/solution.py
@@ -99,14 +99,14 @@
     return runs
 
 
-def multiply(wanted, rows, blocks, base, staged, tail, *refs):
+def multiply(wanted, rows, blocks, base, after, *refs):
     count = len(wanted)
     sources = refs[:4]
-    if tail:
-        appended, refs = refs[4], refs[:4] + refs[5:]
+    refs = refs[:4] + refs[4 + after :]
     outs = refs[4 : 4 + count]
-    left, right, sems = refs[4 + count : 7 + count]
-    stages, given = refs[7 + count : -1] if staged else outs, []
+    left, right, sems, given_sems = refs[4 + count : 8 + count]
+    spare, given = list(refs[8 + count :]), []
+    stages = [spare.pop(0) if item[3] == jnp.bfloat16 else out for item, out in zip(wanted, outs)]
     tokens = left.shape[1] // 2
     per_block = left.shape[0] // blocks
     units_block = per_block // rows
@@ -130,15 +130,6 @@
                 sources[at].at[span], left.at[span, half], sems.at[2 + 2 * block + at]
             )
             lefts[block, at].start()
-    if tail:
-        given.append(
-            pltpu.make_async_copy(
-                appended.at[pl.ds(tail, tail)],
-                outs[0].at[pl.ds(len(wanted[0][0]) * rows, tail)],
-                refs[-1].at[blocks, 0],
-            )
-        )
-        given[0].start()
     for copy in grads:
         copy.wait()
     for block in needed:
@@ -152,10 +143,10 @@
                     left[low * rows : high * rows, :], right[:, first - base : last - base]
                 )
                 stages[at][place : place + (high - low) * rows, :] = product.astype(outs[at].dtype)
-            if staged and here:
+            if here and stages[at] is not outs[at]:
                 span = pl.ds(units.index(here[0]) * rows, len(here) * rows)
                 copy = pltpu.make_async_copy(
-                    stages[at].at[span], outs[at].at[span], refs[-1].at[block, at]
+                    stages[at].at[span], outs[at].at[span], given_sems.at[block, at]
                 )
                 copy.start()
                 given.append(copy)
@@ -163,12 +154,12 @@
         copy.wait()
 
 
-def products(lefts, grads, wanted, rows, blocks, staged, appended=None):
+def products(lefts, grads, wanted, rows, blocks, after, limit):
     total, tokens = lefts[0].shape
     base = min(first for _, first, _, _ in wanted)
     columns = max(last for _, _, last, _ in wanted) - base
     if rows % 32 or any((first | last) % LANES for _, first, last, _ in wanted):
-        results = [
+        return [
             jnp.concatenate(
                 [
                     sum(
@@ -180,38 +171,33 @@
             ).astype(kind)
             for units, first, last, kind in wanted
         ]
-        if appended is not None:
-            results[0] = jnp.concatenate([results[0], appended[appended.shape[0] // 2 :]])
-        return results
-    tail = 0 if appended is None else appended.shape[0] // 2
     shapes = [
         jax.ShapeDtypeStruct((len(units) * rows, last - first), kind)
         for units, first, last, kind in wanted
     ]
-    staging = []
-    if staged:
-        staging = [pltpu.VMEM(shape.shape, shape.dtype) for shape in shapes]
-        staging.append(pltpu.SemaphoreType.DMA((blocks + 1, len(shapes))))
-    if tail:
-        grown = (shapes[0].shape[0] + tail, shapes[0].shape[1])
-        shapes[0] = jax.ShapeDtypeStruct(grown, shapes[0].dtype)
+    sent = [item[3] == jnp.bfloat16 for item in wanted]
+    staging = [pltpu.VMEM(shape.shape, shape.dtype) for shape, is_sent in zip(shapes, sent) if is_sent]
     return pl.pallas_call(
-        functools.partial(multiply, wanted, rows, blocks, base, staged, tail),
+        functools.partial(multiply, wanted, rows, blocks, base, len(after)),
         out_shape=shapes,
-        in_specs=[pl.BlockSpec(memory_space=pltpu.HBM)] * (5 if tail else 4),
-        out_specs=[pl.BlockSpec(memory_space=pltpu.HBM if staged else pltpu.VMEM)] * len(shapes),
+        in_specs=[pl.BlockSpec(memory_space=pltpu.HBM)] * 4
+        + [pl.BlockSpec(memory_space=pl.ANY)] * len(after),
+        out_specs=[
+            pl.BlockSpec(memory_space=pltpu.HBM if is_sent else pltpu.VMEM) for is_sent in sent
+        ],
         scratch_shapes=[
             pltpu.VMEM((total, 2 * tokens), lefts[0].dtype),
             pltpu.VMEM((2 * tokens, columns), grads[0].dtype),
             pltpu.SemaphoreType.DMA((2 + 2 * blocks,)),
+            pltpu.SemaphoreType.DMA((blocks, len(shapes))),
         ]
         + staging,
-        compiler_params=pltpu.CompilerParams(vmem_limit_bytes=127 << 19 if staged else VMEM // 2),
+        compiler_params=pltpu.CompilerParams(vmem_limit_bytes=limit),
         cost_estimate=pl.CostEstimate(flops=1, bytes_accessed=1, transcendentals=0),
-    )(*lefts, *grads, *([appended] if tail else []))
-
-
-def pick_rows(arranged, units, place, table, tail, *refs):
+    )(*lefts, *grads, *after)
+
+
+def pick_rows(arranged, units, place, table, tail, _, *refs):
     outs, (slabs, found, flipped, sems) = refs[:2], refs[2:]
     whole = (table.shape[0] - 1) // SLAB * SLAB
     tokens, width_all = found.shape
@@ -269,8 +255,8 @@
                 )
 
 
-def add_and_split(plans, arrays, merged, *refs):
-    refs = list(refs)
+def add_and_split(plans, arrays, merged, after, *refs):
+    refs = list(refs[after:])
     takes = [[refs.pop(0) for _ in plan] for plan in plans]
     inbox = [refs.pop(0) for _ in range(arrays)]
     gives = [[refs.pop(0) for _ in plan] for plan in plans]
@@ -303,7 +289,7 @@
             put += go * size
 
 
-def combine(plans, values, got, merged):
+def combine(plans, values, got, merged, after):
     columns = [parts[0].shape[1] for parts in values]
     totals = [sum(size * go for size, _, go, _, _ in plan) for plan in plans]
     outs = [
@@ -318,33 +304,36 @@
             outs.append(jax.ShapeDtypeStruct((total, width), jnp.bfloat16))
     arrays = [array for parts in values for array in parts] + list(got)
     results = pl.pallas_call(
-        functools.partial(add_and_split, plans, len(got), merged),
-        in_specs=[pl.BlockSpec(memory_space=pltpu.VMEM)] * len(arrays),
+        functools.partial(add_and_split, plans, len(got), merged, len(after)),
+        in_specs=[pl.BlockSpec(memory_space=pl.ANY)] * len(after)
+        + [pl.BlockSpec(memory_space=pltpu.VMEM)] * len(arrays),
         out_specs=[pl.BlockSpec(memory_space=pltpu.VMEM)] * len(outs),
         out_shape=outs,
         compiler_params=pltpu.CompilerParams(vmem_limit_bytes=VMEM // 4),
         cost_estimate=pl.CostEstimate(flops=1, bytes_accessed=1, transcendentals=0),
-    )(*arrays)
+    )(*after, *arrays)
     results = list(results)
     kept = [[results.pop(0) for _ in plan] for plan in plans]
     return kept, results, totals
 
 
-def own_share(coef, spans, plans, rows, tokens, blocks, *refs):
-    emb, master, out = refs[0], refs[1], refs[-1]
-    arrays = refs[2:-1]
-    lanes = emb.shape[1] // blocks
+def own_share(coef, spans, plans, rows, tokens, _, *refs):
+    emb, emb_got, master, out = refs[0], refs[1], refs[2], refs[-1]
+    arrays = refs[3:-1]
+    lines, lanes = emb.shape[0] // 2, emb.shape[1] // 2
     count_fsdp = tokens // out.shape[1]
     col_width = out.shape[2]
-    folded = emb[...].astype(jnp.bfloat16)
+    arrived = emb_got[...].astype(jnp.float32)
+    swapped = jnp.concatenate([arrived[:, lanes:], arrived[:, :lanes]], axis=1)
+    folded = (emb[...] + swapped).astype(jnp.bfloat16)
     lefts = [
         jnp.concatenate(
             [
-                folded[:, unit * lanes + at : unit * lanes + at + tokens]
-                for at in range(0, lanes, tokens)
+                folded[(unit & 1) * lines : ((unit & 1) + 1) * lines, at : at + tokens]
+                for at in range((unit >> 1) * lanes, ((unit >> 1) + 1) * lanes, tokens)
             ]
         )
-        for unit in range(blocks)
+        for unit in range(4)
     ]
 
     def both(left, right):
@@ -369,6 +358,10 @@
             ]
 
 
+def add_parts(_, parts, out):
+    out[...] = jnp.sum(parts[...].astype(jnp.float32), axis=0)
+
+
 def across(left, right):
     return lax.dot_general(
         left, right, (((0,), (0,)), ((), ())), preferred_element_type=jnp.float32
@@ -391,7 +384,7 @@
     return jnp.concatenate([folded[:, at : at + tokens] for at in range(0, lanes, tokens)])
 
 
-def lookup(embed_table, token_ids, arranged, units, width, lanes):
+def lookup(embed_table, token_ids, arranged, units, width, lanes, after):
     here, width_all = embed_table.shape
     tokens = token_ids.shape[0]
     rows = width // units
@@ -429,6 +422,7 @@
             pl.BlockSpec(memory_space=pltpu.SMEM),
             pl.BlockSpec(memory_space=pltpu.HBM),
             pl.BlockSpec((SLAB, width_all), lambda i: ((here - 1) // SLAB, 0)),
+            pl.BlockSpec(memory_space=pl.ANY),
         ],
         out_specs=[pl.BlockSpec(memory_space=pltpu.VMEM)] * 2,
         out_shape=[shape, shape],
@@ -440,7 +434,7 @@
         ],
         compiler_params=pltpu.CompilerParams(vmem_limit_bytes=VMEM // 2),
         cost_estimate=pl.CostEstimate(flops=1, bytes_accessed=1, transcendentals=0),
-    )(place, embed_table, embed_table)
+    )(place, embed_table, embed_table, after)
 
 
 def dot32(left, right):
@@ -475,7 +469,8 @@
     columns = master_w.shape[1]
     arranged = [r ^ (r >> 1) for r in range(uppers)][::-1]
     grads = [grad_out, exchange(grad_out, "fsdp", 1)]
-    incoming = exchange(pack(activations, arranged, False, count_tp, block), "fsdp", 1)
+    outward = pack(activations, arranged, False, count_tp, block)
+    incoming = exchange(outward, "fsdp", 1)
     staying = pack(activations, arranged, True, count_tp, block)
     lefts = [staying, incoming]
     tokens_new = token_ids.shape[0]
@@ -486,14 +481,11 @@
     places = [(r, unit) for r in arranged for unit in range(count_tp)]
     steps_upper = [("fsdp", bit) for bit in range(upper_bits)]
     steps_tp = [("tp", bit) for bit in range(count_tp.bit_length() - 1)]
-    one, two, three = (
-        steps_upper + steps_tp,
-        steps_upper[::-1] + steps_tp,
-        steps_tp[:1] + steps_upper + steps_tp[1:],
-    )
-    edges = [0, quarter, 2 * quarter, 3 * quarter, 3 * quarter + eighth, columns]
+    one, two = steps_upper + steps_tp, steps_upper[::-1] + steps_tp
+    edges = [0, quarter, 2 * quarter] + [2 * quarter + at * eighth for at in range(1, 5)]
     spans = list(zip(edges[:-1], edges[1:]))
-    orders = [one, two, three, one, two]
+    orders = [one, two] * 3
+    chunks = range(len(spans))
 
     def has(place, step):
         return (place[step[0] == "tp"] >> step[1]) & 1
@@ -513,69 +505,85 @@
         mask = 1 << step[1]
         return exchange(value, step[0], 2 * mask if step[0] == "fsdp" else mask)
 
-    def compute(which, sent, appended=None):
+    def compute(which, after, limit=127 << 19):
         wanted = []
-        for index in which:
+        for index, sent in which:
             chosen = split(places, orders[index][0])[0 if sent else 1]
             units = [places.index(p) for p in chosen]
             kind = jnp.bfloat16 if sent else jnp.float32
             wanted.append((units, *spans[index], kind))
-        return dict(zip(which, products(lefts, grads, wanted, rows, uppers, sent, appended)))
-
-    theirs, ours = lookup(embed_table, token_ids, arranged, count_tp, block, eighth)
-    asked = ours + exchange(theirs, "fsdp", 1)
-    pairs = [(r, low) for low in range(2) for r in arranged]
-    going = compute([0, 1], True)
-    got = {index: send(value, orders[index][0]) for index, value in going.items()}
-    going |= compute([2, 3, 4], True, asked)
-    got |= {index: send(going[index], orders[index][0]) for index in (3, 4, 2)}
-    token = going[4]
-    values = compute([0, 1, 2], False)
-    values |= compute([3, 4], False)
-    values = {index: [value] for index, value in values.items()}
-    values[2].append(asked[: asked.shape[0] // 2].astype(jnp.float32))
-    sizes = {index: [rows] for index in range(5)}
-    sizes[2].append(lines)
-    held = {index: [split(places, orders[index][0])[1]] for index in range(5)}
-    held[2].append(split(pairs, orders[2][0])[1])
-    gone = {index: [split(places, orders[index][0])[0]] for index in range(5)}
-    gone[2].append(split(pairs, orders[2][0])[0])
+        return products(lefts, grads, wanted, rows, uppers, after, limit)
+
+    theirs, ours = lookup(
+        embed_table, token_ids, arranged, count_tp, block, eighth, outward
+    )
+    emb = ours + exchange(theirs, "fsdp", 1)
+    emb_held = [(r, low) for low in range(2) for r in arranged]
+    emb_steps = steps_upper + steps_tp
+
+    def emb_split(step):
+        return (emb_held, emb_held) if step[0] == "tp" else split(emb_held, step)
+
+    def emb_forward(emb, got, step, following, after):
+        go, keep = emb_split(following)
+        landed = [flip(p, step) for p in emb_go]
+        if plain:
+            emb = emb + take(got, landed, emb_held, lines).astype(jnp.float32)
+            out = take(emb, emb_held, go, lines).astype(jnp.bfloat16)
+            return out, take(emb, emb_held, keep, lines), go, keep
+        order = [(emb_held.index(p), landed.index(p)) for p in go + keep]
+        plan = [(lines, order, len(go), len(keep), len(landed))]
+        kept, sent, _ = combine([plan], [[emb]], [got], False, [after])
+        return sent[0], kept[0][0], go, keep
+
+    plain = rows % 32 or lines % 16 or block % LANES or eighth % tokens_new
+    last_tp = steps_tp[-1]
+    emb_go, emb_keep = emb_split(emb_steps[0])
+    emb_out = take(emb, emb_held, emb_go, lines)
+    emb = take(emb, emb_held, emb_keep, lines).astype(jnp.float32)
+    emb_held = emb_keep
+    emb_got = send(emb_out, emb_steps[0])
+    lefts = [staying, incoming]
+    going = compute([(0, True), (1, True)], [emb_out])
+    inbox = [[send(value, orders[at][0]) for at, value in enumerate(going)], None, None]
+    emb_out, emb, emb_go, emb_held = emb_forward(
+        emb, emb_got, emb_steps[0], emb_steps[1], going[0]
+    )
+    emb_got = send(emb_out, emb_steps[1])
+    emb_at = 1
+    going = compute([(2, True), (3, True)], [going[0]])
+    inbox[1] = [send(value, orders[2 + at][0]) for at, value in enumerate(going)]
+    values = [[value] for value in compute([(at, False) for at in range(4)], [going[0]])]
+    token = values[0][0]
+    sizes = [[rows] for _ in chunks]
+    gone, held = [
+        [[split(places, orders[index][0])[side]] for index in chunks] for side in range(2)
+    ]
 
     def receive(index, step, arrived):
-        start = 0
-        for part, (value, size) in enumerate(zip(values[index], sizes[index])):
-            landed = [flip(p, step) for p in gone[index][part]]
-            piece = arrived[start : start + len(landed) * size]
-            start += len(landed) * size
-            if part and step == last_tp:
-                piece = jnp.roll(piece, piece.shape[1] // 2, axis=1)
-            else:
-                piece = take(piece, landed, held[index][part], size)
-            values[index][part] = value + piece.astype(jnp.float32)
-
-    def onward(index, step):
-        return [
-            (places_now, places_now) if part and step == last_tp else split(places_now, step)
-            for part, places_now in enumerate(held[index])
-        ]
+        landed = [flip(p, step) for p in gone[index][0]]
+        piece = take(arrived, landed, held[index][0], rows)
+        values[index][0] = values[index][0] + piece.astype(jnp.float32)
 
     def forward(index, step, following):
-        plan = []
-        for part, (go, keep) in enumerate(onward(index, following)):
-            landed = [flip(p, step) for p in gone[index][part]]
-            order = [(held[index][part].index(p), landed.index(p)) for p in go + keep]
-            plan.append((sizes[index][part], order, len(go), len(keep), len(landed)))
-        return plan
-
-    last_tp = steps_tp[-1]
+        go, keep = split(held[index][0], following)
+        landed = [flip(p, step) for p in gone[index][0]]
+        order = [(held[index][0].index(p), landed.index(p)) for p in go + keep]
+        return [(rows, order, len(go), len(keep), len(landed))]
+
     rows_f = tokens_new // count_fsdp
     col_width = columns // count_tp
 
-    def share_of(sums, emb):
+    def share_of(sums, emb, emb_got, after):
         if plain:
-            lefts_own = [
-                unfold_unit(emb[:, at * eighth : (at + 1) * eighth], rows) for at in range(2)
-            ]
+            emb = emb + jnp.roll(emb_got, emb_got.shape[1] // 2, axis=1).astype(jnp.float32)
+            lefts_own = {
+                (0, low + 2 * high): unfold_unit(
+                    emb[low * lines : (low + 1) * lines, high * eighth : (high + 1) * eighth], rows
+                )
+                for low in range(2)
+                for high in range(2)
+            }
 
             def exact(left, right):
                 return lax.dot_general(
@@ -587,87 +595,104 @@
 
             pieces = []
             for index, (first, last) in enumerate(spans):
-                moved = sum(exact(left, array) for left, array in zip(lefts_own, sums[index]))
-                pieces.append(exact(lefts_own[0], master_w[:, first:last]) - coef * moved)
+                moved = sum(
+                    exact(lefts_own[p], array[at * rows : (at + 1) * rows])
+                    for array, chosen in sums[index]
+                    for at, p in enumerate(chosen)
+                )
+                pieces.append(exact(lefts_own[0, 0], master_w[:, first:last]) - coef * moved)
             out = jnp.concatenate(pieces, axis=1)
             out = out.reshape(count_fsdp, rows_f, count_tp, col_width)
             out = out.transpose(0, 2, 1, 3).reshape(devices_all, rows_f, col_width)
             return out.astype(jnp.bfloat16)
-        arrays = [array for index in range(5) for array in sums[index]]
-        plans = [[(2 * index, [0]), (2 * index + 1, [1])] for index in range(5)]
+        arrays = [array for index in chunks for array, _ in sums[index]]
+        plans = [
+            [(2 * index + at, [p[1] for p in chosen]) for at, (_, chosen) in enumerate(sums[index])]
+            for index in chunks
+        ]
         return pl.pallas_call(
-            functools.partial(own_share, coef, spans, plans, rows, tokens_new, 2),
-            in_specs=[pl.BlockSpec(memory_space=pltpu.VMEM)] * (2 + len(arrays)),
+            functools.partial(own_share, coef, spans, plans, rows, tokens_new),
+            in_specs=[pl.BlockSpec(memory_space=pl.ANY)]
+            + [pl.BlockSpec(memory_space=pltpu.VMEM)] * (3 + len(arrays)),
             out_specs=pl.BlockSpec(memory_space=pltpu.VMEM),
             out_shape=jax.ShapeDtypeStruct((devices_all, rows_f, col_width), jnp.float32),
             compiler_params=pltpu.CompilerParams(vmem_limit_bytes=VMEM // 4),
             cost_estimate=pl.CostEstimate(flops=1, bytes_accessed=1, transcendentals=0),
-        )(emb, master_w, *arrays).astype(jnp.bfloat16)
-
-    plain = rows % 32 or lines % 16 or block % LANES or eighth % tokens_new
-    groups = ((0, 1), (2,), (3, 4))
-    inbox = {group: [got[index] for index in group] for group in groups}
-    totals = {}
+        )(after, emb, emb_got, master_w, *arrays).astype(jnp.bfloat16)
+
+    totals = [None] * 3
     sums = {}
     steps = len(one)
-    for at in range(steps):
+    events = [(pair, at) for at in range(steps) for pair in range(3)]
+    if steps == 4:
+        ranks = ((0, 2, 4, 9), (1, 5, 8, 11), (3, 6, 10, 12))
+        events.sort(key=lambda event: ranks[event[0]][event[1]])
+    parts_own, ended = None, []
+
+    for pair, at in events:
+        group = (2 * pair, 2 * pair + 1)
+        if emb_at + 1 < len(emb_steps) and pair < 2:
+            emb_out, emb, emb_go, emb_held = emb_forward(
+                emb, emb_got, emb_steps[emb_at], emb_steps[emb_at + 1], token
+            )
+            emb_at += 1
+            emb_got = send(emb_out, emb_steps[emb_at])
+            token = emb_out
         last = at + 1 == steps
-        for group in ((2,), (0, 1), (3, 4)) if last else groups:
-            *inbox[group], token = lax.optimization_barrier(inbox[group] + [token])
-            if plain or last:
-                if len(inbox[group]) < len(group):
-                    whole = inbox[group][0]
-                    cuts = [sum(totals[group][:place]) for place in range(len(group) + 1)]
-                    inbox[group] = [whole[low:high] for low, high in zip(cuts[:-1], cuts[1:])]
-                for index, arrived in zip(group, inbox[group]):
-                    receive(index, orders[index][at], arrived)
-            if last:
-                token = values[group[-1]][0]
-                if group == (2,):
-                    parts_own, token = lax.optimization_barrier(
-                        (share_of(sums, values[2][1]), token)
-                    )
-                    token = parts_own
-                    parts_own = lax.all_to_all(
-                        parts_own, ("fsdp", "tp"), split_axis=0, concat_axis=0
-                    )
-                continue
-            if plain:
-                outgoing = []
-                for index in group:
-                    pieces = []
-                    for part, (go, keep) in enumerate(onward(index, orders[index][at + 1])):
-                        value, size = values[index][part], sizes[index][part]
-                        pieces.append(take(value, held[index][part], go, size))
-                        values[index][part] = take(value, held[index][part], keep, size)
-                    outgoing.append(jnp.concatenate(pieces).astype(jnp.bfloat16))
-                totals[group] = [value.shape[0] for value in outgoing]
-                merged = False
-            else:
-                plans = [forward(i, orders[i][at], orders[i][at + 1]) for i in group]
-                merged = len({orders[i][at + 1] for i in group}) == 1
-                kept, outgoing, totals[group] = combine(
-                    plans, [values[i] for i in group], inbox[group], merged
-                )
-                values |= dict(zip(group, kept))
-            for number, index in enumerate(group):
-                now = onward(index, orders[index][at + 1])
-                gone[index], held[index] = [list(parts) for parts in zip(*now)]
-                if at + 2 == steps:
-                    low = sum(totals[group][:number]) if merged else 0
-                    sent = outgoing[0 if merged else number]
-                    sums[index] = [values[index][0], sent[low : low + rows]]
-            outgoing = lax.optimization_barrier(outgoing)
-            token = outgoing[-1]
-            inbox[group] = [
-                send(value, orders[index][at + 1]) for index, value in zip(group, outgoing)
-            ]
-            if at == 1 and group == groups[0]:
-                queries, new_key, lengths, token = lax.optimization_barrier(
-                    (queries, new_key, lengths, token)
-                )
-    parts_own, _ = lax.optimization_barrier((parts_own, values[4][0]))
-    own_value = jnp.sum(parts_own.astype(jnp.float32), axis=0)
+        if plain or last:
+            if len(inbox[pair]) < 2:
+                whole, cut = inbox[pair][0], totals[pair][0]
+                inbox[pair] = [whole[:cut], whole[cut:]]
+            for index, arrived in zip(group, inbox[pair]):
+                receive(index, orders[index][at], arrived)
+        if last:
+            ended.append(values[group[-1]][0])
+            continue
+        following = [orders[index][at + 1] for index in group]
+        if plain:
+            outgoing = []
+            for index, step in zip(group, following):
+                go, keep = split(held[index][0], step)
+                value = values[index][0]
+                values[index] = [take(value, held[index][0], keep, rows)]
+                outgoing.append(take(value, held[index][0], go, rows).astype(jnp.bfloat16))
+            totals[pair] = [value.shape[0] for value in outgoing]
+            merged = False
+        else:
+            plans = [forward(i, orders[i][at], orders[i][at + 1]) for i in group]
+            merged = following[0] == following[1]
+            kept, outgoing, totals[pair] = combine(
+                plans, [values[i] for i in group], inbox[pair], merged, [token] + ended
+            )
+            for index, value in zip(group, kept):
+                values[index] = value
+        for number, index in enumerate(group):
+            go, keep = split(held[index][0], following[number])
+            gone[index], held[index] = [go], [keep]
+            if at + 1 == upper_bits:
+                low = number * totals[pair][0] if merged else 0
+                sent = outgoing[0 if merged else number]
+                sums[index] = [(values[index][0], keep), (sent[low : low + totals[pair][number]], go)]
+        token = last_sent = outgoing[-1]
+        inbox[pair] = [send(value, step) for value, step in zip(outgoing, following)]
+        if inbox[2] is None:
+            going = compute(
+                [(4, True), (5, True), (4, False), (5, False)], [token], 44 << 20
+            )
+            inbox[2] = [send(value, orders[4 + at][0]) for at, value in enumerate(going[:2])]
+            values += [[value] for value in going[2:]]
+            token = going[0]
+        if len(sums) == len(spans) and emb_at + 1 == len(emb_steps) and parts_own is None:
+            parts_own = share_of(sums, emb, emb_got, token)
+            token = parts_own
+            parts_own = lax.all_to_all(parts_own, ("fsdp", "tp"), split_axis=0, concat_axis=0)
+    own_value = pl.pallas_call(
+        add_parts,
+        in_specs=[pl.BlockSpec(memory_space=pl.ANY), pl.BlockSpec(memory_space=pltpu.VMEM)],
+        out_specs=pl.BlockSpec(memory_space=pltpu.VMEM),
+        out_shape=jax.ShapeDtypeStruct(parts_own.shape[1:], jnp.float32),
+        compiler_params=pltpu.CompilerParams(vmem_limit_bytes=VMEM // 4),
+    )(last_sent, parts_own)
     w_next = jnp.concatenate(
         [master_w[:, low:high] - coef * values[at][0] for at, (low, high) in enumerate(spans)],
         axis=1,

time: 101 us -> 121 us (1.20)
  starting transfers between devices: 26.8 us -> 35.3 us
  Pallas kernels: 33.3 us -> 40.1 us
  other arithmetic: 3.79 us -> 8.04 us
  local copies, waits for them, and re-layouts: 6.04 us -> 7.57 us
  waiting for transfers between devices: 27.7 us -> 26.2 us
    ppermute x19 -> x25, starting transfers between devices: 23 us -> 31.7 us  [exchange(): lax.ppermute(value, axis, [(i, i ^ mask) for i in range(lax.axis_size(axi...]
    all_to_all x1, waiting for transfers between devices: 8.21 us -> 0.01 us  [per_device(): lax.all_to_all(parts_own, ('fsdp', 'tp'), split_axis=0, concat_axis=0)]
    ppermute x19 -> x25, waiting for transfers between devices: 19.5 us -> 26.2 us  [exchange(): lax.ppermute(value, axis, [(i, i ^ mask) for i in range(lax.axis_size(axi...]
    pallas_call x13 -> x17, Pallas kernels: 22.1 us -> 28.5 us  [the longest x4 24.5 us: products(): pl.pallas_call(functools.partial(multiply, wanted, rows, blocks, base, le...]
    unnamed x5 -> x6, other arithmetic: 0.19 us -> 3.43 us
    add x3 -> x1, other arithmetic: 1.85 us -> 0.09 us  [per_device(): emb = ours + exchange(theirs, 'fsdp', 1)]
    unnamed x33 -> x49, local copies, waits for them, and re-layouts: 5.94 us -> 7.43 us
  transfers between devices with their start and end apart: 20 -> 26, of which waited for: 7 -> 5; matrix products, arithmetic and copies ran while one was open for 4% -> 8% of each run, Pallas kernels for 30% -> 27%
where the time goes in v8:
time: 121 us; the launch traced here: 120 us
  Pallas kernels  40.1 us (33%)
  starting transfers between devices  35.3 us (29%)
  waiting for transfers between devices  26.2 us (22%)
  other arithmetic  8.04 us (7%)
  local copies, waits for them, and re-layouts  7.57 us (6%)
  matrix products  1.93 us (2%)
    ppermute x25, starting transfers between devices, exchange(): lax.ppermute(value, axis, [(i, i ^ mask) for i in range(lax.axis_size(axi...  31.7 us
    ppermute x25, waiting for transfers between devices, exchange(): lax.ppermute(value, axis, [(i, i ^ mask) for i in range(lax.axis_size(axi...  26.2 us
    pallas_call x4, Pallas kernels, products(): pl.pallas_call(functools.partial(multiply, wanted, rows, blocks, base, le...  24.5 us
    unnamed x49, local copies, waits for them, and re-layouts  7.43 us
    pallas_call x2, Pallas kernels, pack(): pl.pallas_call(functools.partial(transpose_blocks, arranged, mine, units)...  6.16 us
    pallas_call x1, Pallas kernels, lookup(): pl.pallas_call(functools.partial(pick_rows, arranged, units), grid=(1,),...  4.54 us
    pallas_call x12, Pallas kernels, combine(): pl.pallas_call(functools.partial(add_and_split, plans, len(got), merged,...  3.95 us
    all_to_all x1, starting transfers between devices, per_device(): lax.all_to_all(parts_own, ('fsdp', 'tp'), split_axis=0, concat_axis=0)  3.59 us
  transfers between devices with their start and end apart: 26, of which 5 were waited for; matrix products, arithmetic and copies ran while one was open for 8% of the time, Pallas kernels for 27%

profile of v8, /device:TPU:0, one launch (start us, length us, event | category | flops | bytes accessed | tf_op | source)
XLA Modules:
  0.0 120.2 jit_solution(1115685655571248656)
XLA Ops:
  0.7 3.1 %shard_map.140._ = bf16[2560,512]{1,0:T(8,128)(2,1)} custom-call(bf16[512,5120]{1,0:T(8,128)(2,1)} %source.3), custom_call_target="tpu_custom_call" | custom-call | bytes 5242880 | tf_op jit(solution)/shard_map/pallas_call | solution.py:74
  4.3 1.7 %copy-done.6 = bf16[2560,512]{1,0:T(8,128)(2,1)S(1)} copy-done((bf16[2560,512]{1,0:T(8,128)(2,1)S(1)}, bf16[2560,512]{1,0:T(8,128)(2,1)}, u32[]{:S(2)}) %copy-start.6) | copy-done | bytes 2621464
  6.1 4.5 %shard_map.141 = (bf16[640,256]{1,0:T(8,128)(2,1)S(1)}, bf16[640,256]{1,0:T(8,128)(2,1)S(1)}) custom-call(s32[64]{0:T(128)S(1)} %and_select_fusion.place, bf16[4748,5120]{1,0:T(8,128)(2,1)} %tail.1, bf16[4748,5120]{1,0:T(8,128)(2,1)} %tail.1, bf16[2560,512]{1,0:T(8,128)(2,1)S(1)} %copy-done.6), custom_call_target="tpu_custom_call" | custom-call | flops 1 | bytes 1 | tf_op jit(solution)/shard_map/pallas_call | solution.py:418
  11.3 1.4 %fusion.27 = (f32[8,2,8]{2,1,0:T(2,128)S(1)}, f32[8,2,8,512]{3,2,1,0:T(8,128)}) fusion(bf16[8,2,8,128]{3,0,2,1:T(8,128)(2,1)S(1)} %bitcast.39, pred[8,512]{1,0:T(8,128)(4,1)S(1)} %iota_compare_fusion, bf16[8,512,256]{2,1,0:T(8,128)(2,1)S(1)} %copy-done.15), kind=kOutput, calls=%fused_computation.45 | convolution fusion | flops 16973696 | bytes 2396672 | tf_op jit(solution)/shard_map/rkgd,rckd->rkgc/dot_general | solution.py:716
  12.8 3.0 %shard_map.139.refs_0_ = bf16[2560,512]{1,0:T(8,128)(2,1)} custom-call(bf16[512,5120]{1,0:T(8,128)(2,1)} %source.3), custom_call_target="tpu_custom_call" | custom-call | bytes 5242880 | tf_op jit(solution)/shard_map/pallas_call | solution.py:74
  16.0 0.7 pad_maximum_fusion.refs_4_
  16.6 1.0 copy-done.4
  17.6 5.0 %shard_map.142 = (bf16[1280,256]{1,0:T(8,128)(2,1)}, bf16[1280,256]{1,0:T(8,128)(2,1)}) custom-call(bf16[2560,512]{1,0:T(8,128)(2,1)} %shard_map.139.refs_0_, bf16[2560,512]{1,0:T(8,128)(2,1)} %collective-permute-done.refs_1_, bf16[512,1024]{1,0:T(8,128)(2,1)} %refs_2_.8, bf16[512,1024]{1,0:T(8,128)(2,1)} %copy-done.4, bf16[320,256]{1,0:T(8,128)(2,1)} %pad_maximum_fusion.refs_4_), custom_call_target="tpu_custom_call" | custom-call | flops 1 | bytes 1 | tf_op jit(solution)/shard_map/pallas_call | solution.py:180
  22.6 2.8 %collective-permute-start.5 = (bf16[1280,256]{1,0:T(8,128)(2,1)}, bf16[1280,256]{1,0:T(8,128)(2,1)}, u32[]{:S(2)}, u32[]{:S(2)}) collective-permute-start(bf16[1280,256]{1,0:T(8,128)(2,1)} %get-tuple-element.55.refs_4_.refs_0_), channel_id=1, source_target_pairs={{0,8},{4,12},{8,0},{12,4},{16,24},{20,28},{24,16},{28,20},{1,9},{5... | collective-permute-start | bytes 1966088 | tf_op jit(solution)/shard_map/ppermute | solution.py:20
  25.4 1.6 %collective-permute-start.6 = (bf16[1280,256]{1,0:T(8,128)(2,1)}, bf16[1280,256]{1,0:T(8,128)(2,1)}, u32[]{:S(2)}, u32[]{:S(2)}) collective-permute-start(bf16[1280,256]{1,0:T(8,128)(2,1)} %get-tuple-element.62), channel_id=1, source_target_pairs={{0,16},{4,20},{8,24},{12,28},{16,0},{20,4},{24,8},{28,12},{1,17},{... | collective-permute-start | bytes 1966088 | tf_op jit(solution)/shard_map/ppermute | solution.py:20
  27.0 1.1 fusion.12
  28.7 15.7 %collective-permute-done.3.refs_2_ = bf16[320,256]{1,0:T(8,128)(2,1)S(1)} collective-permute-done((bf16[320,256]{1,0:T(8,128)(2,1)}, bf16[320,256]{1,0:T(8,128)(2,1)S(1)}, u32[]{:S(2)}, u32[]{:S(2)}) %collective-permute-start.3) | collective-permute-done | bytes 163872 | tf_op jit(solution)/shard_map/ppermute | solution.py:20
  44.4 1.1 copy-done.9
  45.5 0.7 shard_map.145
  46.2 0.7 copy-done.13
  46.8 1.6 %collective-permute-start.4 = (bf16[160,256]{1,0:T(8,128)(2,1)}, bf16[160,256]{1,0:T(8,128)(2,1)S(1)}, u32[]{:S(2)}, u32[]{:S(2)}) collective-permute-start(bf16[160,256]{1,0:T(8,128)(2,1)} %get-tuple-element.59), channel_id=1, source_target_pairs={{0,16},{4,20},{8,24},{12,28},{16,0},{20,4},{24,8},{28,12},{1,17},{... | collective-permute-start | bytes 245768 | tf_op jit(solution)/shard_map/ppermute | solution.py:20
  48.4 4.8 %shard_map.143 = (bf16[1280,128]{1,0:T(8,128)(2,1)}, bf16[1280,128]{1,0:T(8,128)(2,1)}) custom-call(bf16[2560,512]{1,0:T(8,128)(2,1)} %shard_map.139.refs_0_, bf16[2560,512]{1,0:T(8,128)(2,1)} %collective-permute-done.refs_1_, bf16[512,1024]{1,0:T(8,128)(2,1)} %refs_2_.8, bf16[512,1024]{1,0:T(8,128)(2,1)} %copy-done.4, ...), custom_call_target="tpu_custom_call" | custom-call | flops 1 | bytes 1 | tf_op jit(solution)/shard_map/pallas_call | solution.py:180
  53.2 1.8 %collective-permute-start.8 = (bf16[1280,128]{1,0:T(8,128)(2,1)}, bf16[1280,128]{1,0:T(8,128)(2,1)S(1)}, u32[]{:S(2)}, u32[]{:S(2)}) collective-permute-start(bf16[1280,128]{1,0:T(8,128)(2,1)} %get-tuple-element.56.refs_4_), channel_id=1, source_target_pairs={{0,8},{4,12},{8,0},{12,4},{16,24},{20,28},{24,16},{28,20},{1,9},{5... | collective-permute-start | bytes 983048 | tf_op jit(solution)/shard_map/ppermute | solution.py:20
  56.1 6.5 %shard_map.144 = (f32[1280,256]{1,0:T(8,128)}, f32[1280,256]{1,0:T(8,128)}, f32[1280,128]{1,0:T(8,128)}, f32[1280,128]{1,0:T(8,128)}) custom-call(bf16[2560,512]{1,0:T(8,128)(2,1)} %shard_map.139.refs_0_, bf16[2560,512]{1,0:T(8,128)(2,1)} %collective-permute-done.refs_1_, bf16[512,1024]{1,0:T(8,128)(2,1)} %refs_2_.8, bf16[512,1024]{1,0:T(8,128)(2,1)} %copy-done.4, ...), custom_call_target="tpu_custom_call" | custom-call | flops 1 | bytes 1 | tf_op jit(solution)/shard_map/pallas_call | solution.py:180
  62.6 1.3 %copy-done.7 = f32[1280,256]{1,0:T(8,128)S(1)} copy-done((f32[1280,256]{1,0:T(8,128)S(1)}, f32[1280,256]{1,0:T(8,128)}, u32[]{:S(2)}) %copy-start.7) | copy-done | bytes 1310744
  63.9 0.9 copy-done.14
  64.8 1.3 %collective-permute-start.7 = (bf16[160,256]{1,0:T(8,128)(2,1)S(1)}, bf16[160,256]{1,0:T(8,128)(2,1)S(1)}, u32[]{:S(2)}, u32[]{:S(2)}) collective-permute-start(bf16[160,256]{1,0:T(8,128)(2,1)S(1)} %get-tuple-element.60.refs_0_), channel_id=1, source_target_pairs={{0,1},{1,0},{2,3},{3,2},{4,5},{5,4},{6,7},{7,6},{8,9},{9,8},{10,11... | collective-permute-start | bytes 245768 | tf_op jit(solution)/shard_map/ppermute | solution.py:20
  66.2 1.7 %shard_map.147 = (f32[640,256]{1,0:T(8,128)S(1)}, f32[640,256]{1,0:T(8,128)S(1)}, bf16[640,256]{1,0:T(8,128)(2,1)S(1)}, bf16[640,256]{1,0:T(8,128)(2,1)S(1)}) custom-call(bf16[160,256]{1,0:T(8,128)(2,1)S(1)} %get-tuple-element.60.refs_0_, f32[1280,256]{1,0:T(8,128)S(1)} %copy-done.7, f32[1280,256]{1,0:T(8,128)S(1)} %copy-done.10, ...), custom_call_target="tpu_custom_call" | custom-call | flops 1 | bytes 1 | tf_op jit(solution)/shard_map/pallas_call | solution.py:306
  67.9 1.6 %collective-permute-start.10 = (bf16[640,256]{1,0:T(8,128)(2,1)S(1)}, bf16[640,256]{1,0:T(8,128)(2,1)S(1)}, u32[]{:S(2)}, u32[]{:S(2)}) collective-permute-start(bf16[640,256]{1,0:T(8,128)(2,1)S(1)} %get-tuple-element.73), channel_id=1, source_target_pairs={{0,16},{4,20},{8,24},{12,28},{16,0},{20,4},{24,8},{28,12},{1,17},{... | collective-permute-start | bytes 983048 | tf_op jit(solution)/shard_map/ppermute | solution.py:20
  70.3 8.3 %shard_map.148 = (bf16[1280,128]{1,0:T(8,128)(2,1)S(1)}, bf16[1280,128]{1,0:T(8,128)(2,1)S(1)}, f32[1280,128]{1,0:T(8,128)S(1)}, f32[1280,128]{1,0:T(8,128)S(1)}) custom-call(bf16[2560,512]{1,0:T(8,128)(2,1)S(1)} %copy-done.1, bf16[2560,512]{1,0:T(8,128)(2,1)} %collective-permute-done.refs_1_, bf16[512,1024]{1,0:T(8,128)(2,1)S(1)} %copy-done.3, ...), custom_call_target="tpu_custom_call" | custom-call | flops 1 | bytes 1 | tf_op jit(solution)/shard_map/pallas_call | solution.py:180
  78.7 1.8 %collective-permute-start.12 = (bf16[1280,128]{1,0:T(8,128)(2,1)S(1)}, bf16[1280,128]{1,0:T(8,128)(2,1)S(1)}, u32[]{:S(2)}, u32[]{:S(2)}) collective-permute-start(bf16[1280,128]{1,0:T(8,128)(2,1)S(1)} %get-tuple-element.64.refs_0_), channel_id=1, source_target_pairs={{0,8},{4,12},{8,0},{12,4},{16,24},{20,28},{24,16},{28,20},{1,9},{5... | collective-permute-start | bytes 983048 | tf_op jit(solution)/shard_map/ppermute | solution.py:20
  81.0 1.1 shard_map.150
  82.3 1.2 %collective-permute-start.14 = (bf16[640,256]{1,0:T(8,128)(2,1)S(1)}, bf16[640,256]{1,0:T(8,128)(2,1)S(1)}, u32[]{:S(2)}, u32[]{:S(2)}) collective-permute-start(bf16[640,256]{1,0:T(8,128)(2,1)S(1)} %get-tuple-element.74.refs_0_), channel_id=1, source_target_pairs={{0,1},{1,0},{2,3},{3,2},{4,5},{5,4},{6,7},{7,6},{8,9},{9,8},{10,11... | collective-permute-start | bytes 983048 | tf_op jit(solution)/shard_map/ppermute | solution.py:20
  83.6 0.7 collective-permute-start.17
  84.3 3.0 %collective-permute-start.20 = (bf16[160,256]{1,0:T(8,128)(2,1)S(1)}, bf16[160,256]{1,0:T(8,128)(2,1)S(1)}, u32[]{:S(2)}, u32[]{:S(2)}) collective-permute-start(bf16[160,256]{1,0:T(8,128)(2,1)S(1)} %get-tuple-element.66.refs_0_), channel_id=1, source_target_pairs={{0,2},{1,3},{2,0},{3,1},{4,6},{5,7},{6,4},{7,5},{8,10},{9,11},{10,... | collective-permute-start | bytes 245768 | tf_op jit(solution)/shard_map/ppermute | solution.py:20
  87.3 1.0 collective-permute-done.12.refs_3_
  88.3 1.5 %collective-permute-start.16 = (bf16[640,128]{1,0:T(8,128)(2,1)S(1)}, bf16[640,128]{1,0:T(8,128)(2,1)S(1)}, u32[]{:S(2)}, u32[]{:S(2)}) collective-permute-start(bf16[640,128]{1,0:T(8,128)(2,1)S(1)} %get-tuple-element.86), channel_id=1, source_target_pairs={{0,16},{4,20},{8,24},{12,28},{16,0},{20,4},{24,8},{28,12},{1,17},{... | collective-permute-start | bytes 491528 | tf_op jit(solution)/shard_map/ppermute | solution.py:20
  90.6 0.8 collective-permute-done.14.refs_3_
  91.4 1.4 %collective-permute-start.19 = (bf16[640,128]{1,0:T(8,128)(2,1)S(1)}, bf16[640,128]{1,0:T(8,128)(2,1)S(1)}, u32[]{:S(2)}, u32[]{:S(2)}) collective-permute-start(bf16[640,128]{1,0:T(8,128)(2,1)S(1)} %get-tuple-element.78.refs_0_), channel_id=1, source_target_pairs={{0,8},{4,12},{8,0},{12,4},{16,24},{20,28},{24,16},{28,20},{1,9},{5... | collective-permute-start | bytes 491528 | tf_op jit(solution)/shard_map/ppermute | solution.py:20
  92.8 0.8 collective-permute-done.16.refs_3_
  93.6 2.7 %collective-permute-start.15 = (bf16[320,256]{1,0:T(8,128)(2,1)S(1)}, bf16[320,256]{1,0:T(8,128)(2,1)S(1)}, u32[]{:S(2)}, u32[]{:S(2)}) collective-permute-start(bf16[320,256]{1,0:T(8,128)(2,1)S(1)} %get-tuple-element.82.refs_0_), channel_id=1, source_target_pairs={{0,2},{1,3},{2,0},{3,1},{4,6},{5,7},{6,4},{7,5},{8,10},{9,11},{10,... | collective-permute-start | bytes 491528 | tf_op jit(solution)/shard_map/ppermute | solution.py:20
  96.4 1.5 %collective-permute-start.21 = (bf16[640,128]{1,0:T(8,128)(2,1)S(1)}, bf16[640,128]{1,0:T(8,128)(2,1)S(1)}, u32[]{:S(2)}, u32[]{:S(2)}) collective-permute-start(bf16[640,128]{1,0:T(8,128)(2,1)S(1)} %get-tuple-element.87.refs_0_), channel_id=1, source_target_pairs={{0,1},{1,0},{2,3},{3,2},{4,5},{5,4},{6,7},{7,6},{8,9},{9,8},{10,11... | collective-permute-start | bytes 491528 | tf_op jit(solution)/shard_map/ppermute | solution.py:20
  98.7 0.9 shard_map.156
  99.7 0.7 convert_element_type.58.refs_0_
  100.3 3.6 %all-to-all-start = ((bf16[32,8,256]{2,1,0:T(8,128)(2,1)}), bf16[32,8,256]{2,1,0:T(8,128)(2,1)S(1)}, u32[]{:S(2)}, u32[]{:S(2)}) async-start(bf16[32,8,256]{2,1,0:T(8,128)(2,1)} %convert_element_type.58.refs_0_), calls=%async_computation | async-start | bytes 262144 | tf_op jit(solution)/shard_map/all_to_all | solution.py:688
  104.0 2.7 %collective-permute-start.22 = (bf16[320,128]{1,0:T(8,128)(2,1)S(1)}, bf16[320,128]{1,0:T(8,128)(2,1)S(1)}, u32[]{:S(2)}, u32[]{:S(2)}) collective-permute-start(bf16[320,128]{1,0:T(8,128)(2,1)S(1)} %get-tuple-element.98.refs_0_), channel_id=1, source_target_pairs={{0,2},{1,3},{2,0},{3,1},{4,6},{5,7},{6,4},{7,5},{8,10},{9,11},{10,... | collective-permute-start | bytes 245768 | tf_op jit(solution)/shard_map/ppermute | solution.py:20
  106.7 0.7 subtract_dynamic-update-slice_fusion.1
  107.4 0.7 subtract_dynamic-update-slice_fusion
  108.5 7.8 %collective-permute-done.22 = bf16[320,128]{1,0:T(8,128)(2,1)S(1)} collective-permute-done((bf16[320,128]{1,0:T(8,128)(2,1)S(1)}, bf16[320,128]{1,0:T(8,128)(2,1)S(1)}, u32[]{:S(2)}, u32[]{:S(2)}) %collective-permute-start.22) | collective-permute-done | bytes 81952 | tf_op jit(solution)/shard_map/ppermute | solution.py:20
  116.3 0.7 subtract_dynamic-update-slice_fusion.5
  116.9 0.7 subtract_dynamic-update-slice_fusion.4
  117.6 0.7 subtract_dynamic-update-slice_fusion.3
  118.2 0.7 subtract_dynamic-update-slice_fusion.2
  (102 shorter events, 8.0 us)
Async XLA Ops:
  0.6 12.0 %copy-start = (bf16[8,256]{1,0:T(8,128)(2,1)S(1)}, bf16[8,256]{1,0:T(8,128)(2,1)}, u32[]{:S(2)}) copy-start(bf16[8,256]{1,0:T(8,128)(2,1)} %param.20) | copy-start | bytes 12292
  0.6 3.7 %copy-start.22 = (s32[64]{0:T(128)S(1)}, s32[64]{0:T(128)}, u32[]{:S(2)}) copy-start(s32[64]{0:T(128)} %param.16) | copy-start | bytes 772
  3.8 13.9 %collective-permute-start = (bf16[2560,512]{1,0:T(8,128)(2,1)}, bf16[2560,512]{1,0:T(8,128)(2,1)}, u32[]{:S(2)}, u32[]{:S(2)}) collective-permute-start(bf16[2560,512]{1,0:T(8,128)(2,1)} %shard_map.140._), channel_id=1, source_target_pairs={{0,4},{4,0},{8,12},{12,8},{16,20},{20,16},{24,28},{28,24},{1,5},{5... | collective-permute-start | bytes 7864328 | tf_op jit(solution)/shard_map/ppermute | solution.py:20
  4.3 1.7 %copy-start.6 = (bf16[2560,512]{1,0:T(8,128)(2,1)S(1)}, bf16[2560,512]{1,0:T(8,128)(2,1)}, u32[]{:S(2)}) copy-start(bf16[2560,512]{1,0:T(8,128)(2,1)} %shard_map.140._) | copy-start | bytes 7864324
  6.1 4.6 %copy-start.2 = (bf16[512,1024]{1,0:T(8,128)(2,1)S(1)}, bf16[512,1024]{1,0:T(8,128)(2,1)}, u32[]{:S(2)}) copy-start(bf16[512,1024]{1,0:T(8,128)(2,1)} %refs_2_.8) | copy-start | bytes 3145732
  6.1 5.1 %copy-start.20 = (s32[8]{0:T(128)S(1)}, s32[8]{0:T(128)}, u32[]{:S(2)}) copy-start(s32[8]{0:T(128)} %param.23) | copy-start | bytes 100
  6.1 5.2 %copy-start.15 = (bf16[8,512,256]{2,1,0:T(8,128)(2,1)S(1)}, bf16[8,512,256]{2,1,0:T(8,128)(2,1)}, u32[]{:S(2)}) copy-start(bf16[8,512,256]{2,1,0:T(8,128)(2,1)} %param.18) | copy-start | bytes 6291460
  6.1 5.2 %copy-start.17 = (bf16[8,2048]{1,0:T(8,128)(2,1)S(1)}, bf16[8,2048]{1,0:T(8,128)(2,1)}, u32[]{:S(2)}) copy-start(bf16[8,2048]{1,0:T(8,128)(2,1)} %param.17) | copy-start | bytes 98308
  10.6 5.2 %collective-permute-start.2 = (bf16[640,256]{1,0:T(8,128)(2,1)S(1)}, bf16[640,256]{1,0:T(8,128)(2,1)S(1)}, u32[]{:S(2)}, u32[]{:S(2)}) collective-permute-start(bf16[640,256]{1,0:T(8,128)(2,1)S(1)} %get-tuple-element.54), channel_id=1, source_target_pairs={{0,4},{4,0},{8,12},{12,8},{16,20},{20,16},{24,28},{28,24},{1,5},{5... | collective-permute-start | bytes 983048 | tf_op jit(solution)/shard_map/ppermute | solution.py:20
  10.7 5.9 %collective-permute-start.1 = (bf16[512,1024]{1,0:T(8,128)(2,1)S(1)}, bf16[512,1024]{1,0:T(8,128)(2,1)S(1)}, u32[]{:S(2)}, u32[]{:S(2)}) collective-permute-start(bf16[512,1024]{1,0:T(8,128)(2,1)S(1)} %copy-done.2), channel_id=1, source_target_pairs={{0,4},{4,0},{8,12},{12,8},{16,20},{20,16},{24,28},{28,24},{1,5},{5... | collective-permute-start | bytes 3145736 | tf_op jit(solution)/shard_map/ppermute | solution.py:20
  16.6 1.0 copy-start.4
  22.6 43.5 %collective-permute-start.5 = (bf16[1280,256]{1,0:T(8,128)(2,1)}, bf16[1280,256]{1,0:T(8,128)(2,1)}, u32[]{:S(2)}, u32[]{:S(2)}) collective-permute-start(bf16[1280,256]{1,0:T(8,128)(2,1)} %get-tuple-element.55.refs_4_.refs_0_), channel_id=1, source_target_pairs={{0,8},{4,12},{8,0},{12,4},{16,24},{20,28},{24,16},{28,20},{1,9},{5... | collective-permute-start | bytes 1966088 | tf_op jit(solution)/shard_map/ppermute | solution.py:20
  25.4 40.7 %collective-permute-start.6 = (bf16[1280,256]{1,0:T(8,128)(2,1)}, bf16[1280,256]{1,0:T(8,128)(2,1)}, u32[]{:S(2)}, u32[]{:S(2)}) collective-permute-start(bf16[1280,256]{1,0:T(8,128)(2,1)} %get-tuple-element.62), channel_id=1, source_target_pairs={{0,16},{4,20},{8,24},{12,28},{16,0},{20,4},{24,8},{28,12},{1,17},{... | collective-permute-start | bytes 1966088 | tf_op jit(solution)/shard_map/ppermute | solution.py:20
  28.1 16.3 %collective-permute-start.3 = (bf16[320,256]{1,0:T(8,128)(2,1)}, bf16[320,256]{1,0:T(8,128)(2,1)S(1)}, u32[]{:S(2)}, u32[]{:S(2)}) collective-permute-start(bf16[320,256]{1,0:T(8,128)(2,1)} %pad_maximum_fusion.refs_4_), channel_id=1, source_target_pairs={{0,8},{4,12},{8,0},{12,4},{16,24},{20,28},{24,16},{28,20},{1,9},{5... | collective-permute-start | bytes 491528 | tf_op jit(solution)/shard_map/ppermute | solution.py:20
  44.4 1.1 copy-start.9
  46.8 15.7 %collective-permute-start.4 = (bf16[160,256]{1,0:T(8,128)(2,1)}, bf16[160,256]{1,0:T(8,128)(2,1)S(1)}, u32[]{:S(2)}, u32[]{:S(2)}) collective-permute-start(bf16[160,256]{1,0:T(8,128)(2,1)} %get-tuple-element.59), channel_id=1, source_target_pairs={{0,16},{4,20},{8,24},{12,28},{16,0},{20,4},{24,8},{28,12},{1,17},{... | collective-permute-start | bytes 245768 | tf_op jit(solution)/shard_map/ppermute | solution.py:20
  53.2 27.2 %collective-permute-start.8 = (bf16[1280,128]{1,0:T(8,128)(2,1)}, bf16[1280,128]{1,0:T(8,128)(2,1)S(1)}, u32[]{:S(2)}, u32[]{:S(2)}) collective-permute-start(bf16[1280,128]{1,0:T(8,128)(2,1)} %get-tuple-element.56.refs_4_), channel_id=1, source_target_pairs={{0,8},{4,12},{8,0},{12,4},{16,24},{20,28},{24,16},{28,20},{1,9},{5... | collective-permute-start | bytes 983048 | tf_op jit(solution)/shard_map/ppermute | solution.py:20
  55.6 25.4 %collective-permute-start.9 = (bf16[1280,128]{1,0:T(8,128)(2,1)}, bf16[1280,128]{1,0:T(8,128)(2,1)}, u32[]{:S(2)}, u32[]{:S(2)}) collective-permute-start(bf16[1280,128]{1,0:T(8,128)(2,1)} %get-tuple-element.69), channel_id=1, source_target_pairs={{0,16},{4,20},{8,24},{12,28},{16,0},{20,4},{24,8},{28,12},{1,17},{... | collective-permute-start | bytes 983048 | tf_op jit(solution)/shard_map/ppermute | solution.py:20
  62.6 1.3 %copy-start.7 = (f32[1280,256]{1,0:T(8,128)S(1)}, f32[1280,256]{1,0:T(8,128)}, u32[]{:S(2)}) copy-start(f32[1280,256]{1,0:T(8,128)} %get-tuple-element.57.refs_0_.refs_1_) | copy-start | bytes 3932164
  64.8 1.3 %copy-start.10 = (f32[1280,256]{1,0:T(8,128)S(1)}, f32[1280,256]{1,0:T(8,128)}, u32[]{:S(2)}) copy-start(f32[1280,256]{1,0:T(8,128)} %get-tuple-element.61.refs_2_) | copy-start | bytes 3932164
  64.8 5.0 %copy-start.16 = (f32[8,2,8,512]{3,2,1,0:T(8,128)S(1)}, f32[8,2,8,512]{3,2,1,0:T(8,128)}, u32[]{:S(2)}) copy-start(f32[8,2,8,512]{3,2,1,0:T(8,128)} %get-tuple-element.121) | copy-start | bytes 786436
  64.8 5.0 %copy-start.18 = (f32[8,2,8]{2,1,0:T(2,128)S(1)}, f32[8,2,8]{2,1,0:T(2,128)}, u32[]{:S(2)}) copy-start(f32[8,2,8]{2,1,0:T(2,128)} %get-tuple-element.119) | copy-start | bytes 1540
  64.8 5.0 %copy-start.21 = (bf16[8,512,256]{2,1,0:T(8,128)(2,1)S(1)}, bf16[8,512,256]{2,1,0:T(8,128)(2,1)}, u32[]{:S(2)}) copy-start(bf16[8,512,256]{2,1,0:T(8,128)(2,1)} %param.19) | copy-start | bytes 6291460
  64.8 13.8 %collective-permute-start.7 = (bf16[160,256]{1,0:T(8,128)(2,1)S(1)}, bf16[160,256]{1,0:T(8,128)(2,1)S(1)}, u32[]{:S(2)}, u32[]{:S(2)}) collective-permute-start(bf16[160,256]{1,0:T(8,128)(2,1)S(1)} %get-tuple-element.60.refs_0_), channel_id=1, source_target_pairs={{0,1},{1,0},{2,3},{3,2},{4,5},{5,4},{6,7},{7,6},{8,9},{9,8},{10,11... | collective-permute-start | bytes 245768 | tf_op jit(solution)/shard_map/ppermute | solution.py:20
  66.1 4.2 %copy-start.3 = (bf16[512,1024]{1,0:T(8,128)(2,1)S(1)}, bf16[512,1024]{1,0:T(8,128)(2,1)}, u32[]{:S(2)}) copy-start(bf16[512,1024]{1,0:T(8,128)(2,1)} %refs_2_.8) | copy-start | bytes 3145732
  66.1 4.1 %copy-start.5 = (bf16[512,1024]{1,0:T(8,128)(2,1)S(1)}, bf16[512,1024]{1,0:T(8,128)(2,1)}, u32[]{:S(2)}) copy-start(bf16[512,1024]{1,0:T(8,128)(2,1)} %copy-done.4) | copy-start | bytes 3145732
  67.9 2.4 %copy-start.1 = (bf16[2560,512]{1,0:T(8,128)(2,1)S(1)}, bf16[2560,512]{1,0:T(8,128)(2,1)}, u32[]{:S(2)}) copy-start(bf16[2560,512]{1,0:T(8,128)(2,1)} %shard_map.139.refs_0_) | copy-start | bytes 7864324
  67.9 14.2 %collective-permute-start.10 = (bf16[640,256]{1,0:T(8,128)(2,1)S(1)}, bf16[640,256]{1,0:T(8,128)(2,1)S(1)}, u32[]{:S(2)}, u32[]{:S(2)}) collective-permute-start(bf16[640,256]{1,0:T(8,128)(2,1)S(1)} %get-tuple-element.73), channel_id=1, source_target_pairs={{0,16},{4,20},{8,24},{12,28},{16,0},{20,4},{24,8},{28,12},{1,17},{... | collective-permute-start | bytes 983048 | tf_op jit(solution)/shard_map/ppermute | solution.py:20
  69.5 12.6 %collective-permute-start.11 = (bf16[640,256]{1,0:T(8,128)(2,1)S(1)}, bf16[640,256]{1,0:T(8,128)(2,1)S(1)}, u32[]{:S(2)}, u32[]{:S(2)}) collective-permute-start(bf16[640,256]{1,0:T(8,128)(2,1)S(1)} %get-tuple-element.63.refs_4_), channel_id=1, source_target_pairs={{0,8},{4,12},{8,0},{12,4},{16,24},{20,28},{24,16},{28,20},{1,9},{5... | collective-permute-start | bytes 983048 | tf_op jit(solution)/shard_map/ppermute | solution.py:20
  70.3 10.6 %copy-start.23 = (f32[2]{0:T(128)S(1)}, f32[2]{0:T(128)}, u32[]{:S(2)}) copy-start(f32[2]{0:T(128)} %param.22) | copy-start | bytes 28
  70.3 10.7 %copy-start.11 = (f32[1280,128]{1,0:T(8,128)S(1)}, f32[1280,128]{1,0:T(8,128)}, u32[]{:S(2)}) copy-start(f32[1280,128]{1,0:T(8,128)} %get-tuple-element.67.refs_1_) | copy-start | bytes 1966084
  70.3 10.7 %copy-start.12 = (f32[1280,128]{1,0:T(8,128)S(1)}, f32[1280,128]{1,0:T(8,128)}, u32[]{:S(2)}) copy-start(f32[1280,128]{1,0:T(8,128)} %get-tuple-element.68.refs_2_) | copy-start | bytes 1966084
  78.7 9.6 %collective-permute-start.12 = (bf16[1280,128]{1,0:T(8,128)(2,1)S(1)}, bf16[1280,128]{1,0:T(8,128)(2,1)S(1)}, u32[]{:S(2)}, u32[]{:S(2)}) collective-permute-start(bf16[1280,128]{1,0:T(8,128)(2,1)S(1)} %get-tuple-element.64.refs_0_), channel_id=1, source_target_pairs={{0,8},{4,12},{8,0},{12,4},{16,24},{20,28},{24,16},{28,20},{1,9},{5... | collective-permute-start | bytes 983048 | tf_op jit(solution)/shard_map/ppermute | solution.py:20
  80.4 9.4 %collective-permute-start.13 = (bf16[1280,128]{1,0:T(8,128)(2,1)S(1)}, bf16[1280,128]{1,0:T(8,128)(2,1)S(1)}, u32[]{:S(2)}, u32[]{:S(2)}) collective-permute-start(bf16[1280,128]{1,0:T(8,128)(2,1)S(1)} %get-tuple-element.77), channel_id=1, source_target_pairs={{0,16},{4,20},{8,24},{12,28},{16,0},{20,4},{24,8},{28,12},{1,17},{... | collective-permute-start | bytes 983048 | tf_op jit(solution)/shard_map/ppermute | solution.py:20
  82.3 9.1 %collective-permute-start.14 = (bf16[640,256]{1,0:T(8,128)(2,1)S(1)}, bf16[640,256]{1,0:T(8,128)(2,1)S(1)}, u32[]{:S(2)}, u32[]{:S(2)}) collective-permute-start(bf16[640,256]{1,0:T(8,128)(2,1)S(1)} %get-tuple-element.74.refs_0_), channel_id=1, source_target_pairs={{0,1},{1,0},{2,3},{3,2},{4,5},{5,4},{6,7},{7,6},{8,9},{9,8},{10,11... | collective-permute-start | bytes 983048 | tf_op jit(solution)/shard_map/ppermute | solution.py:20
  83.6 12.8 %collective-permute-start.17 = (bf16[640,128]{1,0:T(8,128)(2,1)S(1)}, bf16[640,128]{1,0:T(8,128)(2,1)S(1)}, u32[]{:S(2)}, u32[]{:S(2)}) collective-permute-start(bf16[640,128]{1,0:T(8,128)(2,1)S(1)} %get-tuple-element.70.refs_0_), channel_id=1, source_target_pairs={{0,8},{4,12},{8,0},{12,4},{16,24},{20,28},{24,16},{28,20},{1,9},{5... | collective-permute-start | bytes 491528 | tf_op jit(solution)/shard_map/ppermute | solution.py:20
  84.3 14.4 %collective-permute-start.20 = (bf16[160,256]{1,0:T(8,128)(2,1)S(1)}, bf16[160,256]{1,0:T(8,128)(2,1)S(1)}, u32[]{:S(2)}, u32[]{:S(2)}) collective-permute-start(bf16[160,256]{1,0:T(8,128)(2,1)S(1)} %get-tuple-element.66.refs_0_), channel_id=1, source_target_pairs={{0,2},{1,3},{2,0},{3,1},{4,6},{5,7},{6,4},{7,5},{8,10},{9,11},{10,... | collective-permute-start | bytes 245768 | tf_op jit(solution)/shard_map/ppermute | solution.py:20
  88.3 5.3 %collective-permute-start.16 = (bf16[640,128]{1,0:T(8,128)(2,1)S(1)}, bf16[640,128]{1,0:T(8,128)(2,1)S(1)}, u32[]{:S(2)}, u32[]{:S(2)}) collective-permute-start(bf16[640,128]{1,0:T(8,128)(2,1)S(1)} %get-tuple-element.86), channel_id=1, source_target_pairs={{0,16},{4,20},{8,24},{12,28},{16,0},{20,4},{24,8},{28,12},{1,17},{... | collective-permute-start | bytes 491528 | tf_op jit(solution)/shard_map/ppermute | solution.py:20
  90.0 8.0 %collective-permute-start.18 = (bf16[640,128]{1,0:T(8,128)(2,1)S(1)}, bf16[640,128]{1,0:T(8,128)(2,1)S(1)}, u32[]{:S(2)}, u32[]{:S(2)}) collective-permute-start(bf16[640,128]{1,0:T(8,128)(2,1)S(1)} %get-tuple-element.90), channel_id=1, source_target_pairs={{0,16},{4,20},{8,24},{12,28},{16,0},{20,4},{24,8},{28,12},{1,17},{... | collective-permute-start | bytes 491528 | tf_op jit(solution)/shard_map/ppermute | solution.py:20
  90.5 8.2 %copy-start.8 = (f32[160,1024]{1,0:T(8,128)S(1)}, f32[160,1024]{1,0:T(8,128)}, u32[]{:S(2)}) copy-start(f32[160,1024]{1,0:T(8,128)} %refs_2_.9) | copy-start | bytes 1966084
  91.4 6.6 %collective-permute-start.19 = (bf16[640,128]{1,0:T(8,128)(2,1)S(1)}, bf16[640,128]{1,0:T(8,128)(2,1)S(1)}, u32[]{:S(2)}, u32[]{:S(2)}) collective-permute-start(bf16[640,128]{1,0:T(8,128)(2,1)S(1)} %get-tuple-element.78.refs_0_), channel_id=1, source_target_pairs={{0,8},{4,12},{8,0},{12,4},{16,24},{20,28},{24,16},{28,20},{1,9},{5... | collective-permute-start | bytes 491528 | tf_op jit(solution)/shard_map/ppermute | solution.py:20
  93.6 13.1 %collective-permute-start.15 = (bf16[320,256]{1,0:T(8,128)(2,1)S(1)}, bf16[320,256]{1,0:T(8,128)(2,1)S(1)}, u32[]{:S(2)}, u32[]{:S(2)}) collective-permute-start(bf16[320,256]{1,0:T(8,128)(2,1)S(1)} %get-tuple-element.82.refs_0_), channel_id=1, source_target_pairs={{0,2},{1,3},{2,0},{3,1},{4,6},{5,7},{6,4},{7,5},{8,10},{9,11},{10,... | collective-permute-start | bytes 491528 | tf_op jit(solution)/shard_map/ppermute | solution.py:20
  96.4 7.5 %collective-permute-start.21 = (bf16[640,128]{1,0:T(8,128)(2,1)S(1)}, bf16[640,128]{1,0:T(8,128)(2,1)S(1)}, u32[]{:S(2)}, u32[]{:S(2)}) collective-permute-start(bf16[640,128]{1,0:T(8,128)(2,1)S(1)} %get-tuple-element.87.refs_0_), channel_id=1, source_target_pairs={{0,1},{1,0},{2,3},{3,2},{4,5},{5,4},{6,7},{7,6},{8,9},{9,8},{10,11... | collective-permute-start | bytes 491528 | tf_op jit(solution)/shard_map/ppermute | solution.py:20
  98.1 10.1 %collective-permute-start.23 = (bf16[640,128]{1,0:T(8,128)(2,1)S(1)}, bf16[640,128]{1,0:T(8,128)(2,1)S(1)}, u32[]{:S(2)}, u32[]{:S(2)}) collective-permute-start(bf16[640,128]{1,0:T(8,128)(2,1)S(1)} %get-tuple-element.91._), channel_id=1, source_target_pairs={{0,1},{1,0},{2,3},{3,2},{4,5},{5,4},{6,7},{7,6},{8,9},{9,8},{10,11... | collective-permute-start | bytes 491528 | tf_op jit(solution)/shard_map/ppermute | solution.py:20
  100.3 18.6 %copy-start.19 = (bf16[8,256]{1,0:T(8,128)(2,1)S(1)}, bf16[8,256]{1,0:T(8,128)(2,1)}, u32[]{:S(2)}) copy-start(bf16[8,256]{1,0:T(8,128)(2,1)} %param.21) | copy-start | bytes 12292
  100.3 18.5 %all-to-all-start = ((bf16[32,8,256]{2,1,0:T(8,128)(2,1)}), bf16[32,8,256]{2,1,0:T(8,128)(2,1)S(1)}, u32[]{:S(2)}, u32[]{:S(2)}) async-start(bf16[32,8,256]{2,1,0:T(8,128)(2,1)} %convert_element_type.58.refs_0_), calls=%async_computation | async-start | bytes 262144 | tf_op jit(solution)/shard_map/all_to_all | solution.py:688
  104.0 12.3 %collective-permute-start.22 = (bf16[320,128]{1,0:T(8,128)(2,1)S(1)}, bf16[320,128]{1,0:T(8,128)(2,1)S(1)}, u32[]{:S(2)}, u32[]{:S(2)}) collective-permute-start(bf16[320,128]{1,0:T(8,128)(2,1)S(1)} %get-tuple-element.98.refs_0_), channel_id=1, source_target_pairs={{0,2},{1,3},{2,0},{3,1},{4,6},{5,7},{6,4},{7,5},{8,10},{9,11},{10,... | collective-permute-start | bytes 245768 | tf_op jit(solution)/shard_map/ppermute | solution.py:20
  108.2 9.4 %collective-permute-start.24 = (bf16[320,128]{1,0:T(8,128)(2,1)S(1)}, bf16[320,128]{1,0:T(8,128)(2,1)S(1)}, u32[]{:S(2)}, u32[]{:S(2)}) collective-permute-start(bf16[320,128]{1,0:T(8,128)(2,1)S(1)} %get-tuple-element.101._), channel_id=1, source_target_pairs={{0,2},{1,3},{2,0},{3,1},{4,6},{5,7},{6,4},{7,5},{8,10},{9,11},{10,... | collective-permute-start | bytes 245768 | tf_op jit(solution)/shard_map/ppermute | solution.py:20
  (2 other events, 1.6 us)

commit v9 on v7

--- a/solution.py
+++ b/solution.py
@@ -14,6 +14,7 @@
 LANES = 128
 SLAB = 16
 VMEM = 56 << 20
+TOKEN = (8, 128)
 
 
 def exchange(value, axis, mask):
@@ -103,10 +104,10 @@
     count = len(wanted)
     sources = refs[:4]
     if tail:
-        appended, refs = refs[4], refs[:4] + refs[5:]
+        appended, refs = refs[4:6], refs[:4] + refs[6:]
     outs = refs[4 : 4 + count]
     left, right, sems = refs[4 + count : 7 + count]
-    stages, given = refs[7 + count : -1] if staged else outs, []
+    stages, given = refs[7 + count : 7 + 2 * count] if staged else outs, []
     tokens = left.shape[1] // 2
     per_block = left.shape[0] // blocks
     units_block = per_block // rows
@@ -131,14 +132,11 @@
             )
             lefts[block, at].start()
     if tail:
-        given.append(
+        addends, addend_sems = refs[-2:]
+        for at in range(2):
             pltpu.make_async_copy(
-                appended.at[pl.ds(tail, tail)],
-                outs[0].at[pl.ds(len(wanted[0][0]) * rows, tail)],
-                refs[-1].at[blocks, 0],
-            )
-        )
-        given[0].start()
+                appended[at].at[pl.ds(tail, tail)], addends.at[at], addend_sems.at[at]
+            ).start()
     for copy in grads:
         copy.wait()
     for block in needed:
@@ -155,10 +153,23 @@
             if staged and here:
                 span = pl.ds(units.index(here[0]) * rows, len(here) * rows)
                 copy = pltpu.make_async_copy(
-                    stages[at].at[span], outs[at].at[span], refs[-1].at[block, at]
+                    stages[at].at[span], outs[at].at[span], refs[7 + 2 * count].at[block, at]
                 )
                 copy.start()
                 given.append(copy)
+    if tail:
+        for at in range(2):
+            pltpu.make_async_copy(
+                appended[at].at[pl.ds(tail, tail)], addends.at[at], addend_sems.at[at]
+            ).wait()
+        low = len(wanted[0][0]) * rows
+        stages[0][low : low + tail, :] = addends[0] + addends[1]
+        span = pl.ds(low, tail)
+        copy = pltpu.make_async_copy(
+            stages[0].at[span], outs[0].at[span], refs[7 + 2 * count].at[blocks, 0]
+        )
+        copy.start()
+        given.append(copy)
     for copy in given:
         copy.wait()
 
@@ -181,24 +192,28 @@
             for units, first, last, kind in wanted
         ]
         if appended is not None:
-            results[0] = jnp.concatenate([results[0], appended[appended.shape[0] // 2 :]])
+            both = appended[0] + appended[1]
+            results[0] = jnp.concatenate([results[0], both[both.shape[0] // 2 :]])
         return results
-    tail = 0 if appended is None else appended.shape[0] // 2
+    tail = 0 if appended is None else appended[0].shape[0] // 2
     shapes = [
         jax.ShapeDtypeStruct((len(units) * rows, last - first), kind)
         for units, first, last, kind in wanted
     ]
+    if tail:
+        grown = (shapes[0].shape[0] + tail, shapes[0].shape[1])
+        shapes[0] = jax.ShapeDtypeStruct(grown, shapes[0].dtype)
     staging = []
     if staged:
         staging = [pltpu.VMEM(shape.shape, shape.dtype) for shape in shapes]
         staging.append(pltpu.SemaphoreType.DMA((blocks + 1, len(shapes))))
     if tail:
-        grown = (shapes[0].shape[0] + tail, shapes[0].shape[1])
-        shapes[0] = jax.ShapeDtypeStruct(grown, shapes[0].dtype)
+        staging.append(pltpu.VMEM((2, tail, shapes[0].shape[1]), shapes[0].dtype))
+        staging.append(pltpu.SemaphoreType.DMA((2,)))
     return pl.pallas_call(
         functools.partial(multiply, wanted, rows, blocks, base, staged, tail),
         out_shape=shapes,
-        in_specs=[pl.BlockSpec(memory_space=pltpu.HBM)] * (5 if tail else 4),
+        in_specs=[pl.BlockSpec(memory_space=pltpu.HBM)] * (6 if tail else 4),
         out_specs=[pl.BlockSpec(memory_space=pltpu.HBM if staged else pltpu.VMEM)] * len(shapes),
         scratch_shapes=[
             pltpu.VMEM((total, 2 * tokens), lefts[0].dtype),
@@ -206,9 +221,9 @@
             pltpu.SemaphoreType.DMA((2 + 2 * blocks,)),
         ]
         + staging,
-        compiler_params=pltpu.CompilerParams(vmem_limit_bytes=127 << 19 if staged else VMEM // 2),
+        compiler_params=pltpu.CompilerParams(vmem_limit_bytes=VMEM // 2),
         cost_estimate=pl.CostEstimate(flops=1, bytes_accessed=1, transcendentals=0),
-    )(*lefts, *grads, *([appended] if tail else []))
+    )(*lefts, *grads, *(appended or []))
 
 
 def pick_rows(arranged, units, place, table, tail, *refs):
@@ -269,8 +284,9 @@
                 )
 
 
-def add_and_split(plans, arrays, merged, *refs):
-    refs = list(refs)
+def add_and_split(plans, arrays, merged, _, *refs):
+    refs, done = list(refs[:-1]), refs[-1]
+    done[...] = jnp.zeros_like(done)
     takes = [[refs.pop(0) for _ in plan] for plan in plans]
     inbox = [refs.pop(0) for _ in range(arrays)]
     gives = [[refs.pop(0) for _ in plan] for plan in plans]
@@ -303,7 +319,7 @@
             put += go * size
 
 
-def combine(plans, values, got, merged):
+def combine(plans, values, got, merged, after):
     columns = [parts[0].shape[1] for parts in values]
     totals = [sum(size * go for size, _, go, _, _ in plan) for plan in plans]
     outs = [
@@ -316,21 +332,23 @@
     else:
         for total, width in zip(totals, columns):
             outs.append(jax.ShapeDtypeStruct((total, width), jnp.bfloat16))
+    outs.append(jax.ShapeDtypeStruct(TOKEN, jnp.float32))
     arrays = [array for parts in values for array in parts] + list(got)
     results = pl.pallas_call(
         functools.partial(add_and_split, plans, len(got), merged),
-        in_specs=[pl.BlockSpec(memory_space=pltpu.VMEM)] * len(arrays),
+        in_specs=[pl.BlockSpec(memory_space=pl.ANY)]
+        + [pl.BlockSpec(memory_space=pltpu.VMEM)] * len(arrays),
         out_specs=[pl.BlockSpec(memory_space=pltpu.VMEM)] * len(outs),
         out_shape=outs,
         compiler_params=pltpu.CompilerParams(vmem_limit_bytes=VMEM // 4),
         cost_estimate=pl.CostEstimate(flops=1, bytes_accessed=1, transcendentals=0),
-    )(*arrays)
-    results = list(results)
+    )(after, *arrays)
+    *results, done = results
     kept = [[results.pop(0) for _ in plan] for plan in plans]
-    return kept, results, totals
-
-
-def own_share(coef, spans, plans, rows, tokens, blocks, *refs):
+    return kept, results, totals, done
+
+
+def own_share(coef, spans, plans, rows, tokens, blocks, _, *refs):
     emb, master, out = refs[0], refs[1], refs[-1]
     arrays = refs[2:-1]
     lanes = emb.shape[1] // blocks
@@ -523,17 +541,17 @@
         return dict(zip(which, products(lefts, grads, wanted, rows, uppers, sent, appended)))
 
     theirs, ours = lookup(embed_table, token_ids, arranged, count_tp, block, eighth)
-    asked = ours + exchange(theirs, "fsdp", 1)
+    asked = [ours, exchange(theirs, "fsdp", 1)]
     pairs = [(r, low) for low in range(2) for r in arranged]
     going = compute([0, 1], True)
     got = {index: send(value, orders[index][0]) for index, value in going.items()}
     going |= compute([2, 3, 4], True, asked)
     got |= {index: send(going[index], orders[index][0]) for index in (3, 4, 2)}
-    token = going[4]
     values = compute([0, 1, 2], False)
     values |= compute([3, 4], False)
     values = {index: [value] for index, value in values.items()}
-    values[2].append(asked[: asked.shape[0] // 2].astype(jnp.float32))
+    halves = [array[: array.shape[0] // 2].astype(jnp.float32) for array in asked]
+    values[2].append(halves[0] + halves[1])
     sizes = {index: [rows] for index in range(5)}
     sizes[2].append(lines)
     held = {index: [split(places, orders[index][0])[1]] for index in range(5)}
@@ -571,7 +589,7 @@
     rows_f = tokens_new // count_fsdp
     col_width = columns // count_tp
 
-    def share_of(sums, emb):
+    def share_of(sums, emb, after):
         if plain:
             lefts_own = [
                 unfold_unit(emb[:, at * eighth : (at + 1) * eighth], rows) for at in range(2)
@@ -597,12 +615,13 @@
         plans = [[(2 * index, [0]), (2 * index + 1, [1])] for index in range(5)]
         return pl.pallas_call(
             functools.partial(own_share, coef, spans, plans, rows, tokens_new, 2),
-            in_specs=[pl.BlockSpec(memory_space=pltpu.VMEM)] * (2 + len(arrays)),
+            in_specs=[pl.BlockSpec(memory_space=pl.ANY)]
+            + [pl.BlockSpec(memory_space=pltpu.VMEM)] * (2 + len(arrays)),
             out_specs=pl.BlockSpec(memory_space=pltpu.VMEM),
             out_shape=jax.ShapeDtypeStruct((devices_all, rows_f, col_width), jnp.float32),
             compiler_params=pltpu.CompilerParams(vmem_limit_bytes=VMEM // 4),
             cost_estimate=pl.CostEstimate(flops=1, bytes_accessed=1, transcendentals=0),
-        )(emb, master_w, *arrays).astype(jnp.bfloat16)
+        )(after, emb, master_w, *arrays).astype(jnp.bfloat16)
 
     plain = rows % 32 or lines % 16 or block % LANES or eighth % tokens_new
     groups = ((0, 1), (2,), (3, 4))
@@ -610,63 +629,62 @@
     totals = {}
     sums = {}
     steps = len(one)
-    for at in range(steps):
+    events = [(group, at) for at in range(steps) for group in groups]
+    if steps == 4:
+        first, second, third = groups
+        events = [(first, 0), (second, 0), (third, 0), (first, 1), (second, 1), (first, 2)]
+        events += [(third, 1), (second, 2), (third, 2), (second, 3), (first, 3), (third, 3)]
+    done = jnp.zeros(TOKEN, jnp.float32)
+    for group, at in events:
         last = at + 1 == steps
-        for group in ((2,), (0, 1), (3, 4)) if last else groups:
-            *inbox[group], token = lax.optimization_barrier(inbox[group] + [token])
-            if plain or last:
-                if len(inbox[group]) < len(group):
-                    whole = inbox[group][0]
-                    cuts = [sum(totals[group][:place]) for place in range(len(group) + 1)]
-                    inbox[group] = [whole[low:high] for low, high in zip(cuts[:-1], cuts[1:])]
-                for index, arrived in zip(group, inbox[group]):
-                    receive(index, orders[index][at], arrived)
-            if last:
-                token = values[group[-1]][0]
-                if group == (2,):
-                    parts_own, token = lax.optimization_barrier(
-                        (share_of(sums, values[2][1]), token)
-                    )
-                    token = parts_own
-                    parts_own = lax.all_to_all(
-                        parts_own, ("fsdp", "tp"), split_axis=0, concat_axis=0
-                    )
-                continue
-            if plain:
-                outgoing = []
-                for index in group:
-                    pieces = []
-                    for part, (go, keep) in enumerate(onward(index, orders[index][at + 1])):
-                        value, size = values[index][part], sizes[index][part]
-                        pieces.append(take(value, held[index][part], go, size))
-                        values[index][part] = take(value, held[index][part], keep, size)
-                    outgoing.append(jnp.concatenate(pieces).astype(jnp.bfloat16))
-                totals[group] = [value.shape[0] for value in outgoing]
-                merged = False
-            else:
-                plans = [forward(i, orders[i][at], orders[i][at + 1]) for i in group]
-                merged = len({orders[i][at + 1] for i in group}) == 1
-                kept, outgoing, totals[group] = combine(
-                    plans, [values[i] for i in group], inbox[group], merged
+        if plain or last:
+            if len(inbox[group]) < len(group):
+                whole = inbox[group][0]
+                cuts = [sum(totals[group][:place]) for place in range(len(group) + 1)]
+                inbox[group] = [whole[low:high] for low, high in zip(cuts[:-1], cuts[1:])]
+            for index, arrived in zip(group, inbox[group]):
+                receive(index, orders[index][at], arrived)
+        if last:
+            if group == (2,):
+                parts_own = lax.all_to_all(
+                    share_of(sums, values[2][1], done),
+                    ("fsdp", "tp"),
+                    split_axis=0,
+                    concat_axis=0,
                 )
-                values |= dict(zip(group, kept))
-            for number, index in enumerate(group):
-                now = onward(index, orders[index][at + 1])
-                gone[index], held[index] = [list(parts) for parts in zip(*now)]
-                if at + 2 == steps:
-                    low = sum(totals[group][:number]) if merged else 0
-                    sent = outgoing[0 if merged else number]
-                    sums[index] = [values[index][0], sent[low : low + rows]]
-            outgoing = lax.optimization_barrier(outgoing)
-            token = outgoing[-1]
-            inbox[group] = [
-                send(value, orders[index][at + 1]) for index, value in zip(group, outgoing)
-            ]
-            if at == 1 and group == groups[0]:
-                queries, new_key, lengths, token = lax.optimization_barrier(
-                    (queries, new_key, lengths, token)
-                )
-    parts_own, _ = lax.optimization_barrier((parts_own, values[4][0]))
+            continue
+        if plain:
+            outgoing = []
+            for index in group:
+                pieces = []
+                for part, (go, keep) in enumerate(onward(index, orders[index][at + 1])):
+                    value, size = values[index][part], sizes[index][part]
+                    pieces.append(take(value, held[index][part], go, size))
+                    values[index][part] = take(value, held[index][part], keep, size)
+                outgoing.append(jnp.concatenate(pieces).astype(jnp.bfloat16))
+            totals[group] = [value.shape[0] for value in outgoing]
+            merged = False
+        else:
+            plans = [forward(i, orders[i][at], orders[i][at + 1]) for i in group]
+            merged = len({orders[i][at + 1] for i in group}) == 1
+            kept, outgoing, totals[group], done = combine(
+                plans, [values[i] for i in group], inbox[group], merged, done
+            )
+            values |= dict(zip(group, kept))
+        for number, index in enumerate(group):
+            now = onward(index, orders[index][at + 1])
+            gone[index], held[index] = [list(parts) for parts in zip(*now)]
+            if at + 2 == steps:
+                low = sum(totals[group][:number]) if merged else 0
+                sent = outgoing[0 if merged else number]
+                sums[index] = [values[index][0], sent[low : low + rows]]
+        inbox[group] = [
+            send(value, orders[index][at + 1]) for index, value in zip(group, outgoing)
+        ]
+        if at == 1 and group == groups[0]:
+            queries, new_key, lengths, outgoing[0] = lax.optimization_barrier(
+                (queries, new_key, lengths, outgoing[0])
+            )
     own_value = jnp.sum(parts_own.astype(jnp.float32), axis=0)
     w_next = jnp.concatenate(
         [master_w[:, low:high] - coef * values[at][0] for at, (low, high) in enumerate(spans)],

time: 101 us -> 99.5 us (0.985)
  local copies, waits for them, and re-layouts: 6.04 us -> 2.52 us
  starting transfers between devices: 26.8 us -> 29.1 us
  waiting for transfers between devices: 27.7 us -> 26.3 us
    unnamed x33 -> x25, local copies, waits for them, and re-layouts: 5.94 us -> 2.42 us
    ppermute x19, starting transfers between devices: 23 us -> 26.2 us  [exchange(): lax.ppermute(value, axis, [(i, i ^ mask) for i in range(lax.axis_size(axi...]
    pallas_call x4, Pallas kernels: 20 us -> 22.3 us  [products(): pl.pallas_call(functools.partial(multiply, wanted, rows, blocks, base, st...]
    unnamed x5, other arithmetic: 0.19 us -> 2.33 us
    all_to_all x1, waiting for transfers between devices: 8.21 us -> 6.39 us  [per_device(): lax.all_to_all(share_of(sums, values[2][1], done), ('fsdp', 'tp'), split_...]
    add x1, other arithmetic: 1.83 us -> 0.03 us  [per_device(): values[2].append(halves[0] + halves[1])]
    pallas_call x9, Pallas kernels: 2.18 us -> 0.8 us  [combine(): pl.pallas_call(functools.partial(add_and_split, plans, len(got), merged),...]
  transfers between devices with their start and end apart: 20 -> 20, of which waited for: 7 -> 9; matrix products, arithmetic and copies ran while one was open for 4% -> 5% of each run, Pallas kernels for 30% -> 31%
where the time goes in v9:
time: 99.5 us; the launch traced here: 99.1 us
  Pallas kernels  33.6 us (34%)
  starting transfers between devices  29.1 us (29%)
  waiting for transfers between devices  26.3 us (26%)
  other arithmetic  4.72 us (5%)
  local copies, waits for them, and re-layouts  2.52 us (3%)
  matrix products  1.95 us (2%)
    ppermute x19, starting transfers between devices, exchange(): lax.ppermute(value, axis, [(i, i ^ mask) for i in range(lax.axis_size(axi...  26.2 us
    pallas_call x4, Pallas kernels, products(): pl.pallas_call(functools.partial(multiply, wanted, rows, blocks, base, st...  22.3 us
    ppermute x19, waiting for transfers between devices, exchange(): lax.ppermute(value, axis, [(i, i ^ mask) for i in range(lax.axis_size(axi...  19.9 us
    all_to_all x1, waiting for transfers between devices, per_device(): lax.all_to_all(share_of(sums, values[2][1], done), ('fsdp', 'tp'), split_...  6.39 us
    pallas_call x2, Pallas kernels, pack(): pl.pallas_call(functools.partial(transpose_blocks, arranged, mine, units)...  6.27 us
    pallas_call x1, Pallas kernels, lookup(): pl.pallas_call(functools.partial(pick_rows, arranged, units), grid=(1,),...  3.63 us
    all_to_all x1, starting transfers between devices, per_device(): lax.all_to_all(share_of(sums, values[2][1], done), ('fsdp', 'tp'), split_...  2.88 us
    unnamed x25, local copies, waits for them, and re-layouts  2.42 us
  transfers between devices with their start and end apart: 20, of which 9 were waited for; matrix products, arithmetic and copies ran while one was open for 5% of the time, Pallas kernels for 31%

profile of v9, /device:TPU:0, one launch (start us, length us, event | category | flops | bytes accessed | tf_op | source)
XLA Modules:
  0.0 99.1 jit_solution(16591208561373617354)
XLA Ops:
  0.7 3.2 %shard_map.140 = bf16[2560,512]{1,0:T(8,128)(2,1)} custom-call(bf16[512,5120]{1,0:T(8,128)(2,1)} %source.3), custom_call_target="tpu_custom_call" | custom-call | bytes 5242880 | tf_op jit(solution)/shard_map/pallas_call | solution.py:75
  3.9 0.5 collective-permute-start
  4.5 3.6 %shard_map.144 = (bf16[640,256]{1,0:T(8,128)(2,1)S(1)}, bf16[640,256]{1,0:T(8,128)(2,1)S(1)}) custom-call(s32[64]{0:T(128)S(1)} %and_select_fusion.place, bf16[4748,5120]{1,0:T(8,128)(2,1)} %tail.1, bf16[4748,5120]{1,0:T(8,128)(2,1)} %tail.1), custom_call_target="tpu_custom_call" | custom-call | flops 1 | bytes 1 | tf_op jit(solution)/shard_map/pallas_call | solution.py:443
  8.1 1.1 %collective-permute-start.4 = (bf16[640,256]{1,0:T(8,128)(2,1)S(1)}, bf16[640,256]{1,0:T(8,128)(2,1)S(1)}, u32[]{:S(2)}, u32[]{:S(2)}) collective-permute-start(bf16[640,256]{1,0:T(8,128)(2,1)S(1)} %get-tuple-element.63), channel_id=1, source_target_pairs={{0,4},{4,0},{8,12},{12,8},{16,20},{20,16},{24,28},{28,24},{1,5},{5... | collective-permute-start | bytes 983048 | tf_op jit(solution)/shard_map/ppermute | solution.py:21
  9.3 3.1 %shard_map.139.refs_0_ = bf16[2560,512]{1,0:T(8,128)(2,1)} custom-call(bf16[512,5120]{1,0:T(8,128)(2,1)} %source.3), custom_call_target="tpu_custom_call" | custom-call | bytes 5242880 | tf_op jit(solution)/shard_map/pallas_call | solution.py:75
  12.4 1.7 %copy-done.1 = bf16[2560,512]{1,0:T(8,128)(2,1)S(1)} copy-done((bf16[2560,512]{1,0:T(8,128)(2,1)S(1)}, bf16[2560,512]{1,0:T(8,128)(2,1)}, u32[]{:S(2)}) %copy-start.1) | copy-done | bytes 2621464
  14.1 5.2 %shard_map.142 = (bf16[1280,256]{1,0:T(8,128)(2,1)S(1)}, bf16[1280,256]{1,0:T(8,128)(2,1)S(1)}) custom-call(bf16[2560,512]{1,0:T(8,128)(2,1)S(1)} %copy-done.1, bf16[2560,512]{1,0:T(8,128)(2,1)} %collective-permute-done.refs_1_, bf16[512,1024]{1,0:T(8,128)(2,1)S(1)} %copy-done.2, bf16[512,1024]{1,0:T(8,128)(2,1)} %collective-permute-done.1.refs_3_), custom_call_target="tpu_custom_call" | custom-call | flops 1 | bytes 1 | tf_op jit(solution)/shard_map/pallas_call | solution.py:213
  19.3 2.9 %collective-permute-start.2 = (bf16[1280,256]{1,0:T(8,128)(2,1)S(1)}, bf16[1280,256]{1,0:T(8,128)(2,1)S(1)}, u32[]{:S(2)}, u32[]{:S(2)}) collective-permute-start(bf16[1280,256]{1,0:T(8,128)(2,1)S(1)} %get-tuple-element.58), channel_id=1, source_target_pairs={{0,8},{4,12},{8,0},{12,4},{16,24},{20,28},{24,16},{28,20},{1,9},{5... | collective-permute-start | bytes 1966088 | tf_op jit(solution)/shard_map/ppermute | solution.py:21
  22.2 1.3 %collective-permute-start.3 = (bf16[1280,256]{1,0:T(8,128)(2,1)S(1)}, bf16[1280,256]{1,0:T(8,128)(2,1)S(1)}, u32[]{:S(2)}, u32[]{:S(2)}) collective-permute-start(bf16[1280,256]{1,0:T(8,128)(2,1)S(1)} %get-tuple-element.59), channel_id=1, source_target_pairs={{0,16},{4,20},{8,24},{12,28},{16,0},{20,4},{24,8},{28,12},{1,17},{... | collective-permute-start | bytes 1966088 | tf_op jit(solution)/shard_map/ppermute | solution.py:21
  23.5 8.4 %shard_map.145 = (bf16[1600,256]{1,0:T(8,128)(2,1)S(1)}, bf16[1280,128]{1,0:T(8,128)(2,1)S(1)}, bf16[1280,128]{1,0:T(8,128)(2,1)S(1)}) custom-call(bf16[2560,512]{1,0:T(8,128)(2,1)S(1)} %copy-done.1, bf16[2560,512]{1,0:T(8,128)(2,1)} %collective-permute-done.refs_1_, bf16[512,1024]{1,0:T(8,128)(2,1)S(1)} %copy-done.2, ...), custom_call_target="tpu_custom_call" | custom-call | flops 1 | bytes 1 | tf_op jit(solution)/shard_map/pallas_call | solution.py:213
  31.9 1.8 %collective-permute-start.5 = (bf16[1600,256]{1,0:T(8,128)(2,1)S(1)}, bf16[1600,256]{1,0:T(8,128)(2,1)S(1)}, u32[]{:S(2)}, u32[]{:S(2)}) collective-permute-start(bf16[1600,256]{1,0:T(8,128)(2,1)S(1)} %get-tuple-element.64), channel_id=1, source_target_pairs={{0,1},{1,0},{2,3},{3,2},{4,5},{5,4},{6,7},{7,6},{8,9},{9,8},{10,11... | collective-permute-start | bytes 2457608 | tf_op jit(solution)/shard_map/ppermute | solution.py:21
  33.8 0.5 collective-permute-start.6
  34.3 0.5 collective-permute-start.7
  34.7 4.9 %shard_map.141 = (f32[1280,256]{1,0:T(8,128)S(1)}, f32[1280,256]{1,0:T(8,128)S(1)}, f32[1280,256]{1,0:T(8,128)S(1)}) custom-call(bf16[2560,512]{1,0:T(8,128)(2,1)S(1)} %copy-done.1, bf16[2560,512]{1,0:T(8,128)(2,1)} %collective-permute-done.refs_1_, bf16[512,1024]{1,0:T(8,128)(2,1)S(1)} %copy-done.2, bf16[512,1024]{1,0:T(8,128)(2,1)} %collective-permute-done.1.refs_3_), custom_call_target="tpu_custom_call" | custom-call | flops 1 | bytes 1 | tf_op jit(solution)/shard_map/pallas_call | solution.py:213
  39.6 0.2 collective-permute-done.3.refs_3_
  39.8 0.2 shard_map.143
  40.0 1.5 %collective-permute-start.8 = (bf16[640,256]{1,0:T(8,128)(2,1)S(1)}, bf16[640,256]{1,0:T(8,128)(2,1)S(1)}, u32[]{:S(2)}, u32[]{:S(2)}) collective-permute-start(bf16[640,256]{1,0:T(8,128)(2,1)S(1)} %get-tuple-element.73), channel_id=1, source_target_pairs={{0,16},{4,20},{8,24},{12,28},{16,0},{20,4},{24,8},{28,12},{1,17},{... | collective-permute-start | bytes 983048 | tf_op jit(solution)/shard_map/ppermute | solution.py:21
  41.5 1.5 %collective-permute-start.9 = (bf16[640,256]{1,0:T(8,128)(2,1)S(1)}, bf16[640,256]{1,0:T(8,128)(2,1)S(1)}, u32[]{:S(2)}, u32[]{:S(2)}) collective-permute-start(bf16[640,256]{1,0:T(8,128)(2,1)S(1)} %get-tuple-element.74), channel_id=1, source_target_pairs={{0,8},{4,12},{8,0},{12,4},{16,24},{20,28},{24,16},{28,20},{1,9},{5... | collective-permute-start | bytes 983048 | tf_op jit(solution)/shard_map/ppermute | solution.py:21
  43.1 3.8 %shard_map.147 = (f32[1280,128]{1,0:T(8,128)S(1)}, f32[1280,128]{1,0:T(8,128)S(1)}) custom-call(bf16[2560,512]{1,0:T(8,128)(2,1)S(1)} %copy-done.1, bf16[2560,512]{1,0:T(8,128)(2,1)} %collective-permute-done.refs_1_, bf16[512,1024]{1,0:T(8,128)(2,1)S(1)} %copy-done.2, bf16[512,1024]{1,0:T(8,128)(2,1)} %collective-permute-done.1.refs_3_), custom_call_target="tpu_custom_call" | custom-call | flops 1 | bytes 1 | tf_op jit(solution)/shard_map/pallas_call | solution.py:213
  47.0 5.1 %collective-permute-done.5.refs_2_ = bf16[1600,256]{1,0:T(8,128)(2,1)S(1)} collective-permute-done((bf16[1600,256]{1,0:T(8,128)(2,1)S(1)}, bf16[1600,256]{1,0:T(8,128)(2,1)S(1)}, u32[]{:S(2)}, u32[]{:S(2)}) %collective-permute-start.5) | collective-permute-done | bytes 819232 | tf_op jit(solution)/shard_map/ppermute | solution.py:21
  52.2 0.5 collective-permute-start.10
  52.8 0.8 collective-permute-start.13
  53.6 1.7 %collective-permute-start.14 = (bf16[640,128]{1,0:T(8,128)(2,1)S(1)}, bf16[640,128]{1,0:T(8,128)(2,1)S(1)}, u32[]{:S(2)}, u32[]{:S(2)}) collective-permute-start(bf16[640,128]{1,0:T(8,128)(2,1)S(1)} %get-tuple-element.90), channel_id=1, source_target_pairs={{0,8},{4,12},{8,0},{12,4},{16,24},{20,28},{24,16},{28,20},{1,9},{5... | collective-permute-start | bytes 491528 | tf_op jit(solution)/shard_map/ppermute | solution.py:21
  55.4 1.4 %collective-permute-start.11 = (bf16[640,256]{1,0:T(8,128)(2,1)S(1)}, bf16[640,256]{1,0:T(8,128)(2,1)S(1)}, u32[]{:S(2)}, u32[]{:S(2)}) collective-permute-start(bf16[640,256]{1,0:T(8,128)(2,1)S(1)} %get-tuple-element.82), channel_id=1, source_target_pairs={{0,1},{1,0},{2,3},{3,2},{4,5},{5,4},{6,7},{7,6},{8,9},{9,8},{10,11... | collective-permute-start | bytes 983048 | tf_op jit(solution)/shard_map/ppermute | solution.py:21
  57.0 0.7 fusion.25
  57.8 0.2 fusion.12
  58.0 1.1 %fusion = f32[8,2,8,128]{3,2,1,0:T(8,128)} fusion(f32[8,2,8,512]{3,2,1,0:T(8,128)S(1)} %get-tuple-element.120, f32[8,2,8]{2,1,0:T(2,128)S(1)} %get-tuple-element.118, f32[8,2,8]{2,1,0:T(2,128)S(1)} %multiply_maximum_fusion, bf16[8,512,256]{2,1,0:T(8,128)(2,1)S(1)} %copy-done.8), kind=kOutput, calls=%fused_computation | convolution fusion | flops 16973824 | bytes 2425856 | tf_op jit(solution)/shard_map/rkgc,rckd->rkgd/dot_general | solution.py:721
  59.1 5.4 %collective-permute-done.10.refs_2_ = bf16[800,256]{1,0:T(8,128)(2,1)S(1)} collective-permute-done((bf16[800,256]{1,0:T(8,128)(2,1)S(1)}, bf16[800,256]{1,0:T(8,128)(2,1)S(1)}, u32[]{:S(2)}, u32[]{:S(2)}) %collective-permute-start.10) | collective-permute-done | bytes 409632 | tf_op jit(solution)/shard_map/ppermute | solution.py:21
  64.5 0.8 collective-permute-start.15
  65.4 0.8 collective-permute-done.14.refs_3_
  66.3 1.8 %collective-permute-start.17 = (bf16[640,128]{1,0:T(8,128)(2,1)S(1)}, bf16[640,128]{1,0:T(8,128)(2,1)S(1)}, u32[]{:S(2)}, u32[]{:S(2)}) collective-permute-start(bf16[640,128]{1,0:T(8,128)(2,1)S(1)} %get-tuple-element.100), channel_id=1, source_target_pairs={{0,1},{1,0},{2,3},{3,2},{4,5},{5,4},{6,7},{7,6},{8,9},{9,8},{10,11... | collective-permute-start | bytes 491528 | tf_op jit(solution)/shard_map/ppermute | solution.py:21
  68.1 1.9 %collective-permute-start.12 = (bf16[320,256]{1,0:T(8,128)(2,1)S(1)}, bf16[320,256]{1,0:T(8,128)(2,1)S(1)}, u32[]{:S(2)}, u32[]{:S(2)}) collective-permute-start(bf16[320,256]{1,0:T(8,128)(2,1)S(1)} %get-tuple-element.84), channel_id=1, source_target_pairs={{0,2},{1,3},{2,0},{3,1},{4,6},{5,7},{6,4},{7,5},{8,10},{9,11},{10,... | collective-permute-start | bytes 491528 | tf_op jit(solution)/shard_map/ppermute | solution.py:21
  70.0 0.4 collective-permute-done.15.refs_2_
  70.4 2.8 %collective-permute-start.16 = (bf16[240,256]{1,0:T(8,128)(2,1)S(1)}, bf16[240,256]{1,0:T(8,128)(2,1)S(1)}, u32[]{:S(2)}, u32[]{:S(2)}) collective-permute-start(bf16[240,256]{1,0:T(8,128)(2,1)S(1)} %get-tuple-element.96), channel_id=1, source_target_pairs={{0,2},{1,3},{2,0},{3,1},{4,6},{5,7},{6,4},{7,5},{8,10},{9,11},{10,... | collective-permute-start | bytes 368648 | tf_op jit(solution)/shard_map/ppermute | solution.py:21
  73.3 0.2 collective-permute-done.17.refs_2_
  73.5 2.8 %collective-permute-start.18 = (bf16[320,128]{1,0:T(8,128)(2,1)S(1)}, bf16[320,128]{1,0:T(8,128)(2,1)S(1)}, u32[]{:S(2)}, u32[]{:S(2)}) collective-permute-start(bf16[320,128]{1,0:T(8,128)(2,1)S(1)} %get-tuple-element.102), channel_id=1, source_target_pairs={{0,2},{1,3},{2,0},{3,1},{4,6},{5,7},{6,4},{7,5},{8,10},{9,11},{10,... | collective-permute-start | bytes 245768 | tf_op jit(solution)/shard_map/ppermute | solution.py:21
  76.3 6.4 %collective-permute-done.12 = bf16[320,256]{1,0:T(8,128)(2,1)S(1)} collective-permute-done((bf16[320,256]{1,0:T(8,128)(2,1)S(1)}, bf16[320,256]{1,0:T(8,128)(2,1)S(1)}, u32[]{:S(2)}, u32[]{:S(2)}) %collective-permute-start.12) | collective-permute-done | bytes 163872 | tf_op jit(solution)/shard_map/ppermute | solution.py:21
  82.8 1.5 %collective-permute-done.16 = bf16[240,256]{1,0:T(8,128)(2,1)S(1)} collective-permute-done((bf16[240,256]{1,0:T(8,128)(2,1)S(1)}, bf16[240,256]{1,0:T(8,128)(2,1)S(1)}, u32[]{:S(2)}, u32[]{:S(2)}) %collective-permute-start.16) | collective-permute-done | bytes 122912 | tf_op jit(solution)/shard_map/ppermute | solution.py:21
  84.3 0.6 shard_map.155
  84.9 0.7 convert_element_type.69
  85.6 2.9 %all-to-all-start = ((bf16[32,8,256]{2,1,0:T(8,128)(2,1)}), bf16[32,8,256]{2,1,0:T(8,128)(2,1)S(1)}, u32[]{:S(2)}, u32[]{:S(2)}) async-start(bf16[32,8,256]{2,1,0:T(8,128)(2,1)} %convert_element_type.69), calls=%async_computation | async-start | bytes 262144 | tf_op jit(solution)/shard_map/all_to_all | solution.py:649
  88.5 0.7 subtract_dynamic-update-slice_fusion
  89.2 0.7 subtract_dynamic-update-slice_fusion.4
  89.8 0.7 subtract_dynamic-update-slice_fusion.3
  90.5 6.4 %all-to-all-done = bf16[32,8,256]{2,1,0:T(8,128)(2,1)S(1)} async-done(((bf16[32,8,256]{2,1,0:T(8,128)(2,1)}), bf16[32,8,256]{2,1,0:T(8,128)(2,1)S(1)}, u32[]{:S(2)}, u32[]{:S(2)}) %all-to-all-start) | async-done | bytes 131104 | tf_op jit(solution)/shard_map/all_to_all | solution.py:649
  96.9 0.6 bitcast_convert_fusion
  97.6 0.9 fusion.15
  98.5 0.6 copy.47
  (61 shorter events, 1.3 us)
Async XLA Ops:
  0.6 56.4 %copy-start = (bf16[8,512,256]{2,1,0:T(8,128)(2,1)S(1)}, bf16[8,512,256]{2,1,0:T(8,128)(2,1)}, u32[]{:S(2)}) copy-start(bf16[8,512,256]{2,1,0:T(8,128)(2,1)} %param.18) | copy-start | bytes 6291460
  0.6 3.8 %copy-start.2 = (bf16[512,1024]{1,0:T(8,128)(2,1)S(1)}, bf16[512,1024]{1,0:T(8,128)(2,1)}, u32[]{:S(2)}) copy-start(bf16[512,1024]{1,0:T(8,128)(2,1)} %refs_2_.7) | copy-start | bytes 3145732
  0.7 3.8 %copy-start.10 = (s32[64]{0:T(128)S(1)}, s32[64]{0:T(128)}, u32[]{:S(2)}) copy-start(s32[64]{0:T(128)} %param.16) | copy-start | bytes 772
  3.9 8.5 %collective-permute-start = (bf16[2560,512]{1,0:T(8,128)(2,1)}, bf16[2560,512]{1,0:T(8,128)(2,1)}, u32[]{:S(2)}, u32[]{:S(2)}) collective-permute-start(bf16[2560,512]{1,0:T(8,128)(2,1)} %shard_map.140), channel_id=1, source_target_pairs={{0,4},{4,0},{8,12},{12,8},{16,20},{20,16},{24,28},{28,24},{1,5},{5... | collective-permute-start | bytes 7864328 | tf_op jit(solution)/shard_map/ppermute | solution.py:21
  4.4 7.9 %collective-permute-start.1 = (bf16[512,1024]{1,0:T(8,128)(2,1)S(1)}, bf16[512,1024]{1,0:T(8,128)(2,1)}, u32[]{:S(2)}, u32[]{:S(2)}) collective-permute-start(bf16[512,1024]{1,0:T(8,128)(2,1)S(1)} %copy-done.2), channel_id=1, source_target_pairs={{0,4},{4,0},{8,12},{12,8},{16,20},{20,16},{24,28},{28,24},{1,5},{5... | collective-permute-start | bytes 3145736 | tf_op jit(solution)/shard_map/ppermute | solution.py:21
  8.1 15.4 %collective-permute-start.4 = (bf16[640,256]{1,0:T(8,128)(2,1)S(1)}, bf16[640,256]{1,0:T(8,128)(2,1)S(1)}, u32[]{:S(2)}, u32[]{:S(2)}) collective-permute-start(bf16[640,256]{1,0:T(8,128)(2,1)S(1)} %get-tuple-element.63), channel_id=1, source_target_pairs={{0,4},{4,0},{8,12},{12,8},{16,20},{20,16},{24,28},{28,24},{1,5},{5... | collective-permute-start | bytes 983048 | tf_op jit(solution)/shard_map/ppermute | solution.py:21
  12.3 1.7 %copy-start.1 = (bf16[2560,512]{1,0:T(8,128)(2,1)S(1)}, bf16[2560,512]{1,0:T(8,128)(2,1)}, u32[]{:S(2)}) copy-start(bf16[2560,512]{1,0:T(8,128)(2,1)} %shard_map.139.refs_0_) | copy-start | bytes 7864324
  19.3 20.3 %collective-permute-start.2 = (bf16[1280,256]{1,0:T(8,128)(2,1)S(1)}, bf16[1280,256]{1,0:T(8,128)(2,1)S(1)}, u32[]{:S(2)}, u32[]{:S(2)}) collective-permute-start(bf16[1280,256]{1,0:T(8,128)(2,1)S(1)} %get-tuple-element.58), channel_id=1, source_target_pairs={{0,8},{4,12},{8,0},{12,4},{16,24},{20,28},{24,16},{28,20},{1,9},{5... | collective-permute-start | bytes 1966088 | tf_op jit(solution)/shard_map/ppermute | solution.py:21
  22.2 17.6 %collective-permute-start.3 = (bf16[1280,256]{1,0:T(8,128)(2,1)S(1)}, bf16[1280,256]{1,0:T(8,128)(2,1)S(1)}, u32[]{:S(2)}, u32[]{:S(2)}) collective-permute-start(bf16[1280,256]{1,0:T(8,128)(2,1)S(1)} %get-tuple-element.59), channel_id=1, source_target_pairs={{0,16},{4,20},{8,24},{12,28},{16,0},{20,4},{24,8},{28,12},{1,17},{... | collective-permute-start | bytes 1966088 | tf_op jit(solution)/shard_map/ppermute | solution.py:21
  23.5 10.2 %copy-start.11 = (f32[2]{0:T(128)S(1)}, f32[2]{0:T(128)}, u32[]{:S(2)}) copy-start(f32[2]{0:T(128)} %param.22) | copy-start | bytes 28
  31.9 20.1 %collective-permute-start.5 = (bf16[1600,256]{1,0:T(8,128)(2,1)S(1)}, bf16[1600,256]{1,0:T(8,128)(2,1)S(1)}, u32[]{:S(2)}, u32[]{:S(2)}) collective-permute-start(bf16[1600,256]{1,0:T(8,128)(2,1)S(1)} %get-tuple-element.64), channel_id=1, source_target_pairs={{0,1},{1,0},{2,3},{3,2},{4,5},{5,4},{6,7},{7,6},{8,9},{9,8},{10,11... | collective-permute-start | bytes 2457608 | tf_op jit(solution)/shard_map/ppermute | solution.py:21
  33.8 18.9 %collective-permute-start.6 = (bf16[1280,128]{1,0:T(8,128)(2,1)S(1)}, bf16[1280,128]{1,0:T(8,128)(2,1)S(1)}, u32[]{:S(2)}, u32[]{:S(2)}) collective-permute-start(bf16[1280,128]{1,0:T(8,128)(2,1)S(1)} %get-tuple-element.68), channel_id=1, source_target_pairs={{0,8},{4,12},{8,0},{12,4},{16,24},{20,28},{24,16},{28,20},{1,9},{5... | collective-permute-start | bytes 983048 | tf_op jit(solution)/shard_map/ppermute | solution.py:21
  34.3 18.4 %collective-permute-start.7 = (bf16[1280,128]{1,0:T(8,128)(2,1)S(1)}, bf16[1280,128]{1,0:T(8,128)(2,1)S(1)}, u32[]{:S(2)}, u32[]{:S(2)}) collective-permute-start(bf16[1280,128]{1,0:T(8,128)(2,1)S(1)} %get-tuple-element.69), channel_id=1, source_target_pairs={{0,16},{4,20},{8,24},{12,28},{16,0},{20,4},{24,8},{28,12},{1,17},{... | collective-permute-start | bytes 983048 | tf_op jit(solution)/shard_map/ppermute | solution.py:21
  40.0 15.2 %collective-permute-start.8 = (bf16[640,256]{1,0:T(8,128)(2,1)S(1)}, bf16[640,256]{1,0:T(8,128)(2,1)S(1)}, u32[]{:S(2)}, u32[]{:S(2)}) collective-permute-start(bf16[640,256]{1,0:T(8,128)(2,1)S(1)} %get-tuple-element.73), channel_id=1, source_target_pairs={{0,16},{4,20},{8,24},{12,28},{16,0},{20,4},{24,8},{28,12},{1,17},{... | collective-permute-start | bytes 983048 | tf_op jit(solution)/shard_map/ppermute | solution.py:21
  41.5 13.7 %collective-permute-start.9 = (bf16[640,256]{1,0:T(8,128)(2,1)S(1)}, bf16[640,256]{1,0:T(8,128)(2,1)S(1)}, u32[]{:S(2)}, u32[]{:S(2)}) collective-permute-start(bf16[640,256]{1,0:T(8,128)(2,1)S(1)} %get-tuple-element.74), channel_id=1, source_target_pairs={{0,8},{4,12},{8,0},{12,4},{16,24},{20,28},{24,16},{28,20},{1,9},{5... | collective-permute-start | bytes 983048 | tf_op jit(solution)/shard_map/ppermute | solution.py:21
  52.2 4.6 %copy-start.7 = (s32[8]{0:T(128)S(1)}, s32[8]{0:T(128)}, u32[]{:S(2)}) copy-start(s32[8]{0:T(128)} %param.23) | copy-start | bytes 100
  52.2 4.7 %copy-start.5 = (bf16[8,2048]{1,0:T(8,128)(2,1)S(1)}, bf16[8,2048]{1,0:T(8,128)(2,1)}, u32[]{:S(2)}) copy-start(bf16[8,2048]{1,0:T(8,128)(2,1)} %param.17) | copy-start | bytes 98308
  52.2 4.7 %copy-start.9 = (bf16[8,256]{1,0:T(8,128)(2,1)S(1)}, bf16[8,256]{1,0:T(8,128)(2,1)}, u32[]{:S(2)}) copy-start(bf16[8,256]{1,0:T(8,128)(2,1)} %param.20) | copy-start | bytes 12292
  52.2 12.2 %collective-permute-start.10 = (bf16[800,256]{1,0:T(8,128)(2,1)S(1)}, bf16[800,256]{1,0:T(8,128)(2,1)S(1)}, u32[]{:S(2)}, u32[]{:S(2)}) collective-permute-start(bf16[800,256]{1,0:T(8,128)(2,1)S(1)} %get-tuple-element.78), channel_id=1, source_target_pairs={{0,8},{4,12},{8,0},{12,4},{16,24},{20,28},{24,16},{28,20},{1,9},{5... | collective-permute-start | bytes 1228808 | tf_op jit(solution)/shard_map/ppermute | solution.py:21
  52.8 12.6 %collective-permute-start.13 = (bf16[640,128]{1,0:T(8,128)(2,1)S(1)}, bf16[640,128]{1,0:T(8,128)(2,1)S(1)}, u32[]{:S(2)}, u32[]{:S(2)}) collective-permute-start(bf16[640,128]{1,0:T(8,128)(2,1)S(1)} %get-tuple-element.89), channel_id=1, source_target_pairs={{0,16},{4,20},{8,24},{12,28},{16,0},{20,4},{24,8},{28,12},{1,17},{... | collective-permute-start | bytes 491528 | tf_op jit(solution)/shard_map/ppermute | solution.py:21
  53.6 12.6 %collective-permute-start.14 = (bf16[640,128]{1,0:T(8,128)(2,1)S(1)}, bf16[640,128]{1,0:T(8,128)(2,1)S(1)}, u32[]{:S(2)}, u32[]{:S(2)}) collective-permute-start(bf16[640,128]{1,0:T(8,128)(2,1)S(1)} %get-tuple-element.90), channel_id=1, source_target_pairs={{0,8},{4,12},{8,0},{12,4},{16,24},{20,28},{24,16},{28,20},{1,9},{5... | collective-permute-start | bytes 491528 | tf_op jit(solution)/shard_map/ppermute | solution.py:21
  55.2 2.8 %copy-start.8 = (bf16[8,512,256]{2,1,0:T(8,128)(2,1)S(1)}, bf16[8,512,256]{2,1,0:T(8,128)(2,1)}, u32[]{:S(2)}) copy-start(bf16[8,512,256]{2,1,0:T(8,128)(2,1)} %param.19) | copy-start | bytes 6291460
  55.4 10.0 %collective-permute-start.11 = (bf16[640,256]{1,0:T(8,128)(2,1)S(1)}, bf16[640,256]{1,0:T(8,128)(2,1)S(1)}, u32[]{:S(2)}, u32[]{:S(2)}) collective-permute-start(bf16[640,256]{1,0:T(8,128)(2,1)S(1)} %get-tuple-element.82), channel_id=1, source_target_pairs={{0,1},{1,0},{2,3},{3,2},{4,5},{5,4},{6,7},{7,6},{8,9},{9,8},{10,11... | collective-permute-start | bytes 983048 | tf_op jit(solution)/shard_map/ppermute | solution.py:21
  64.5 18.2 %copy-start.3 = (f32[160,1024]{1,0:T(8,128)S(1)}, f32[160,1024]{1,0:T(8,128)}, u32[]{:S(2)}) copy-start(f32[160,1024]{1,0:T(8,128)} %refs_1_.1) | copy-start | bytes 1966084
  64.5 5.8 %collective-permute-start.15 = (bf16[400,256]{1,0:T(8,128)(2,1)S(1)}, bf16[400,256]{1,0:T(8,128)(2,1)S(1)}, u32[]{:S(2)}, u32[]{:S(2)}) collective-permute-start(bf16[400,256]{1,0:T(8,128)(2,1)S(1)} %get-tuple-element.94), channel_id=1, source_target_pairs={{0,16},{4,20},{8,24},{12,28},{16,0},{20,4},{24,8},{28,12},{1,17},{... | collective-permute-start | bytes 614408 | tf_op jit(solution)/shard_map/ppermute | solution.py:21
  66.3 7.2 %collective-permute-start.17 = (bf16[640,128]{1,0:T(8,128)(2,1)S(1)}, bf16[640,128]{1,0:T(8,128)(2,1)S(1)}, u32[]{:S(2)}, u32[]{:S(2)}) collective-permute-start(bf16[640,128]{1,0:T(8,128)(2,1)S(1)} %get-tuple-element.100), channel_id=1, source_target_pairs={{0,1},{1,0},{2,3},{3,2},{4,5},{5,4},{6,7},{7,6},{8,9},{9,8},{10,11... | collective-permute-start | bytes 491528 | tf_op jit(solution)/shard_map/ppermute | solution.py:21
  68.1 14.7 %collective-permute-start.12 = (bf16[320,256]{1,0:T(8,128)(2,1)S(1)}, bf16[320,256]{1,0:T(8,128)(2,1)S(1)}, u32[]{:S(2)}, u32[]{:S(2)}) collective-permute-start(bf16[320,256]{1,0:T(8,128)(2,1)S(1)} %get-tuple-element.84), channel_id=1, source_target_pairs={{0,2},{1,3},{2,0},{3,1},{4,6},{5,7},{6,4},{7,5},{8,10},{9,11},{10,... | collective-permute-start | bytes 491528 | tf_op jit(solution)/shard_map/ppermute | solution.py:21
  70.4 13.9 %collective-permute-start.16 = (bf16[240,256]{1,0:T(8,128)(2,1)S(1)}, bf16[240,256]{1,0:T(8,128)(2,1)S(1)}, u32[]{:S(2)}, u32[]{:S(2)}) collective-permute-start(bf16[240,256]{1,0:T(8,128)(2,1)S(1)} %get-tuple-element.96), channel_id=1, source_target_pairs={{0,2},{1,3},{2,0},{3,1},{4,6},{5,7},{6,4},{7,5},{8,10},{9,11},{10,... | collective-permute-start | bytes 368648 | tf_op jit(solution)/shard_map/ppermute | solution.py:21
  73.5 15.7 %collective-permute-start.18 = (bf16[320,128]{1,0:T(8,128)(2,1)S(1)}, bf16[320,128]{1,0:T(8,128)(2,1)S(1)}, u32[]{:S(2)}, u32[]{:S(2)}) collective-permute-start(bf16[320,128]{1,0:T(8,128)(2,1)S(1)} %get-tuple-element.102), channel_id=1, source_target_pairs={{0,2},{1,3},{2,0},{3,1},{4,6},{5,7},{6,4},{7,5},{8,10},{9,11},{10,... | collective-permute-start | bytes 245768 | tf_op jit(solution)/shard_map/ppermute | solution.py:21
  82.8 2.1 %copy-start.4 = (f32[160,1024]{1,0:T(8,128)}, f32[160,1024]{1,0:T(8,128)S(1)}, u32[]{:S(2)}) copy-start(f32[160,1024]{1,0:T(8,128)S(1)} %subtract_dynamic-update-slice_fusion.1) | copy-start | bytes 1966084
  84.3 12.6 %copy-start.6 = (bf16[8,256]{1,0:T(8,128)(2,1)S(1)}, bf16[8,256]{1,0:T(8,128)(2,1)}, u32[]{:S(2)}) copy-start(bf16[8,256]{1,0:T(8,128)(2,1)} %param.21) | copy-start | bytes 12292
  85.6 11.3 %all-to-all-start = ((bf16[32,8,256]{2,1,0:T(8,128)(2,1)}), bf16[32,8,256]{2,1,0:T(8,128)(2,1)S(1)}, u32[]{:S(2)}, u32[]{:S(2)}) async-start(bf16[32,8,256]{2,1,0:T(8,128)(2,1)} %convert_element_type.69), calls=%async_computation | async-start | bytes 262144 | tf_op jit(solution)/shard_map/all_to_all | solution.py:649

commit v10 on v9

--- a/solution.py
+++ b/solution.py
@@ -137,6 +137,19 @@
             pltpu.make_async_copy(
                 appended[at].at[pl.ds(tail, tail)], addends.at[at], addend_sems.at[at]
             ).start()
+    if tail:
+        for at in range(2):
+            pltpu.make_async_copy(
+                appended[at].at[pl.ds(tail, tail)], addends.at[at], addend_sems.at[at]
+            ).wait()
+        low = len(wanted[0][0]) * rows
+        stages[0][low : low + tail, :] = addends[0] + addends[1]
+        span = pl.ds(low, tail)
+        copy = pltpu.make_async_copy(
+            stages[0].at[span], outs[0].at[span], refs[7 + 2 * count].at[blocks, 0]
+        )
+        copy.start()
+        given.append(copy)
     for copy in grads:
         copy.wait()
     for block in needed:
@@ -157,19 +170,6 @@
                 )
                 copy.start()
                 given.append(copy)
-    if tail:
-        for at in range(2):
-            pltpu.make_async_copy(
-                appended[at].at[pl.ds(tail, tail)], addends.at[at], addend_sems.at[at]
-            ).wait()
-        low = len(wanted[0][0]) * rows
-        stages[0][low : low + tail, :] = addends[0] + addends[1]
-        span = pl.ds(low, tail)
-        copy = pltpu.make_async_copy(
-            stages[0].at[span], outs[0].at[span], refs[7 + 2 * count].at[blocks, 0]
-        )
-        copy.start()
-        given.append(copy)
     for copy in given:
         copy.wait()
 
@@ -543,10 +543,10 @@
     theirs, ours = lookup(embed_table, token_ids, arranged, count_tp, block, eighth)
     asked = [ours, exchange(theirs, "fsdp", 1)]
     pairs = [(r, low) for low in range(2) for r in arranged]
-    going = compute([0, 1], True)
-    got = {index: send(value, orders[index][0]) for index, value in going.items()}
-    going |= compute([2, 3, 4], True, asked)
-    got |= {index: send(going[index], orders[index][0]) for index in (3, 4, 2)}
+    going = compute([2, 0, 1], True, asked)
+    got = {index: send(going[index], orders[index][0]) for index in (0, 1, 2)}
+    going |= compute([3, 4], True)
+    got |= {index: send(going[index], orders[index][0]) for index in (3, 4)}
     values = compute([0, 1, 2], False)
     values |= compute([3, 4], False)
     values = {index: [value] for index, value in values.items()}

time: 99.5 us -> 103 us (1.035)
  waiting for transfers between devices: 26.3 us -> 28.5 us
  other arithmetic: 4.72 us -> 6.05 us
    ppermute x19, waiting for transfers between devices: 19.9 us -> 22.1 us  [exchange(): lax.ppermute(value, axis, [(i, i ^ mask) for i in range(lax.axis_size(axi...]
    unnamed x5, other arithmetic: 2.33 us -> 3.67 us
    unnamed x25 -> x23, local copies, waits for them, and re-layouts: 2.42 us -> 2.41 us
  transfers between devices with their start and end apart: 20 -> 20, of which waited for: 9 -> 10; matrix products, arithmetic and copies ran while one was open for 5% -> 6% of each run, Pallas kernels for 31% -> 22%
where the time goes in v10:
time: 103 us
  Pallas kernels  33.3 us (32%)
  starting transfers between devices  29.7 us (29%)
  waiting for transfers between devices  28.5 us (28%)
  other arithmetic  6.05 us (6%)
  local copies, waits for them, and re-layouts  2.52 us (2%)
  matrix products  1.95 us (2%)
    ppermute x19, starting transfers between devices, exchange(): lax.ppermute(value, axis, [(i, i ^ mask) for i in range(lax.axis_size(axi...  26.2 us
    pallas_call x4, Pallas kernels, products(): pl.pallas_call(functools.partial(multiply, wanted, rows, blocks, base, st...  22.1 us
    ppermute x19, waiting for transfers between devices, exchange(): lax.ppermute(value, axis, [(i, i ^ mask) for i in range(lax.axis_size(axi...  22.1 us
    all_to_all x1, waiting for transfers between devices, per_device(): lax.all_to_all(share_of(sums, values[2][1], done), ('fsdp', 'tp'), split_...  6.39 us
    pallas_call x2, Pallas kernels, pack(): pl.pallas_call(functools.partial(transpose_blocks, arranged, mine, units)...  6.25 us
    unnamed x5, other arithmetic  3.67 us
    pallas_call x1, Pallas kernels, lookup(): pl.pallas_call(functools.partial(pick_rows, arranged, units), grid=(1,),...  3.63 us
    all_to_all x1, starting transfers between devices, per_device(): lax.all_to_all(share_of(sums, values[2][1], done), ('fsdp', 'tp'), split_...  3.46 us
  transfers between devices with their start and end apart: 20, of which 10 were waited for; matrix products, arithmetic and copies ran while one was open for 6% of the time, Pallas kernels for 22%

profile of v10, /device:TPU:0, one launch (start us, length us, event | category | flops | bytes accessed | tf_op | source)
XLA Modules:
  0.0 102.9 jit_solution(10133544859305294483)
XLA Ops:
  0.7 3.2 %shard_map.140 = bf16[2560,512]{1,0:T(8,128)(2,1)} custom-call(bf16[512,5120]{1,0:T(8,128)(2,1)} %source.3), custom_call_target="tpu_custom_call" | custom-call | bytes 5242880 | tf_op jit(solution)/shard_map/pallas_call | solution.py:75
  3.9 0.5 collective-permute-start
  4.5 3.6 %shard_map.142 = (bf16[640,256]{1,0:T(8,128)(2,1)S(1)}, bf16[640,256]{1,0:T(8,128)(2,1)S(1)}) custom-call(s32[64]{0:T(128)S(1)} %and_select_fusion.place, bf16[4748,5120]{1,0:T(8,128)(2,1)} %tail.1, bf16[4748,5120]{1,0:T(8,128)(2,1)} %tail.1), custom_call_target="tpu_custom_call" | custom-call | flops 1 | bytes 1 | tf_op jit(solution)/shard_map/pallas_call | solution.py:443
  8.1 1.2 %collective-permute-start.2 = (bf16[640,256]{1,0:T(8,128)(2,1)S(1)}, bf16[640,256]{1,0:T(8,128)(2,1)S(1)}, u32[]{:S(2)}, u32[]{:S(2)}) collective-permute-start(bf16[640,256]{1,0:T(8,128)(2,1)S(1)} %get-tuple-element.59), channel_id=1, source_target_pairs={{0,4},{4,0},{8,12},{12,8},{16,20},{20,16},{24,28},{28,24},{1,5},{5... | collective-permute-start | bytes 983048 | tf_op jit(solution)/shard_map/ppermute | solution.py:21
  9.3 3.1 %shard_map.139.refs_0_ = bf16[2560,512]{1,0:T(8,128)(2,1)} custom-call(bf16[512,5120]{1,0:T(8,128)(2,1)} %source.3), custom_call_target="tpu_custom_call" | custom-call | bytes 5242880 | tf_op jit(solution)/shard_map/pallas_call | solution.py:75
  12.5 1.7 %copy-done.1 = bf16[2560,512]{1,0:T(8,128)(2,1)S(1)} copy-done((bf16[2560,512]{1,0:T(8,128)(2,1)S(1)}, bf16[2560,512]{1,0:T(8,128)(2,1)}, u32[]{:S(2)}) %copy-start.1) | copy-done | bytes 2621464
  14.2 7.9 %shard_map.143 = (bf16[1600,256]{1,0:T(8,128)(2,1)S(1)}, bf16[1280,256]{1,0:T(8,128)(2,1)S(1)}, bf16[1280,256]{1,0:T(8,128)(2,1)S(1)}) custom-call(bf16[2560,512]{1,0:T(8,128)(2,1)S(1)} %copy-done.1, bf16[2560,512]{1,0:T(8,128)(2,1)} %collective-permute-done.refs_1_, bf16[512,1024]{1,0:T(8,128)(2,1)S(1)} %copy-done.2, ...), custom_call_target="tpu_custom_call" | custom-call | flops 1 | bytes 1 | tf_op jit(solution)/shard_map/pallas_call | solution.py:213
  22.1 2.7 %collective-permute-start.3 = (bf16[1280,256]{1,0:T(8,128)(2,1)S(1)}, bf16[1280,256]{1,0:T(8,128)(2,1)S(1)}, u32[]{:S(2)}, u32[]{:S(2)}) collective-permute-start(bf16[1280,256]{1,0:T(8,128)(2,1)S(1)} %get-tuple-element.60), channel_id=1, source_target_pairs={{0,8},{4,12},{8,0},{12,4},{16,24},{20,28},{24,16},{28,20},{1,9},{5... | collective-permute-start | bytes 1966088 | tf_op jit(solution)/shard_map/ppermute | solution.py:21
  24.8 1.6 %collective-permute-start.4 = (bf16[1280,256]{1,0:T(8,128)(2,1)S(1)}, bf16[1280,256]{1,0:T(8,128)(2,1)S(1)}, u32[]{:S(2)}, u32[]{:S(2)}) collective-permute-start(bf16[1280,256]{1,0:T(8,128)(2,1)S(1)} %get-tuple-element.61), channel_id=1, source_target_pairs={{0,16},{4,20},{8,24},{12,28},{16,0},{20,4},{24,8},{28,12},{1,17},{... | collective-permute-start | bytes 1966088 | tf_op jit(solution)/shard_map/ppermute | solution.py:21
  26.4 1.4 %collective-permute-start.5 = (bf16[1600,256]{1,0:T(8,128)(2,1)S(1)}, bf16[1600,256]{1,0:T(8,128)(2,1)S(1)}, u32[]{:S(2)}, u32[]{:S(2)}) collective-permute-start(bf16[1600,256]{1,0:T(8,128)(2,1)S(1)} %get-tuple-element.64), channel_id=1, source_target_pairs={{0,1},{1,0},{2,3},{3,2},{4,5},{5,4},{6,7},{7,6},{8,9},{9,8},{10,11... | collective-permute-start | bytes 2457608 | tf_op jit(solution)/shard_map/ppermute | solution.py:21
  27.8 5.5 %shard_map.147 = (bf16[1280,128]{1,0:T(8,128)(2,1)S(1)}, bf16[1280,128]{1,0:T(8,128)(2,1)S(1)}) custom-call(bf16[2560,512]{1,0:T(8,128)(2,1)S(1)} %copy-done.1, bf16[2560,512]{1,0:T(8,128)(2,1)} %collective-permute-done.refs_1_, bf16[512,1024]{1,0:T(8,128)(2,1)S(1)} %copy-done.2, bf16[512,1024]{1,0:T(8,128)(2,1)} %collective-permute-done.1.refs_3_), custom_call_target="tpu_custom_call" | custom-call | flops 1 | bytes 1 | tf_op jit(solution)/shard_map/pallas_call | solution.py:213
  33.4 0.7 collective-permute-start.6
  34.0 0.6 collective-permute-start.7
  34.6 4.9 %shard_map.141 = (f32[1280,256]{1,0:T(8,128)S(1)}, f32[1280,256]{1,0:T(8,128)S(1)}, f32[1280,256]{1,0:T(8,128)S(1)}) custom-call(bf16[2560,512]{1,0:T(8,128)(2,1)S(1)} %copy-done.1, bf16[2560,512]{1,0:T(8,128)(2,1)} %collective-permute-done.refs_1_, bf16[512,1024]{1,0:T(8,128)(2,1)S(1)} %copy-done.2, bf16[512,1024]{1,0:T(8,128)(2,1)} %collective-permute-done.1.refs_3_), custom_call_target="tpu_custom_call" | custom-call | flops 1 | bytes 1 | tf_op jit(solution)/shard_map/pallas_call | solution.py:213
  39.5 0.9 collective-permute-done.3.refs_2_
  40.4 2.0 %collective-permute-done.4.refs_3_ = bf16[1280,256]{1,0:T(8,128)(2,1)S(1)} collective-permute-done((bf16[1280,256]{1,0:T(8,128)(2,1)S(1)}, bf16[1280,256]{1,0:T(8,128)(2,1)S(1)}, u32[]{:S(2)}, u32[]{:S(2)}) %collective-permute-start.4) | collective-permute-done | bytes 655392 | tf_op jit(solution)/shard_map/ppermute | solution.py:21
  42.6 1.6 %collective-permute-start.8 = (bf16[640,256]{1,0:T(8,128)(2,1)S(1)}, bf16[640,256]{1,0:T(8,128)(2,1)S(1)}, u32[]{:S(2)}, u32[]{:S(2)}) collective-permute-start(bf16[640,256]{1,0:T(8,128)(2,1)S(1)} %get-tuple-element.73), channel_id=1, source_target_pairs={{0,16},{4,20},{8,24},{12,28},{16,0},{20,4},{24,8},{28,12},{1,17},{... | collective-permute-start | bytes 983048 | tf_op jit(solution)/shard_map/ppermute | solution.py:21
  44.6 3.8 %shard_map.146 = (f32[1280,128]{1,0:T(8,128)S(1)}, f32[1280,128]{1,0:T(8,128)S(1)}) custom-call(bf16[2560,512]{1,0:T(8,128)(2,1)S(1)} %copy-done.1, bf16[2560,512]{1,0:T(8,128)(2,1)} %collective-permute-done.refs_1_, bf16[512,1024]{1,0:T(8,128)(2,1)S(1)} %copy-done.2, bf16[512,1024]{1,0:T(8,128)(2,1)} %collective-permute-done.1.refs_3_), custom_call_target="tpu_custom_call" | custom-call | flops 1 | bytes 1 | tf_op jit(solution)/shard_map/pallas_call | solution.py:213
  48.6 0.8 collective-permute-done.7.refs_3_
  49.5 1.6 %collective-permute-start.13 = (bf16[640,128]{1,0:T(8,128)(2,1)S(1)}, bf16[640,128]{1,0:T(8,128)(2,1)S(1)}, u32[]{:S(2)}, u32[]{:S(2)}) collective-permute-start(bf16[640,128]{1,0:T(8,128)(2,1)S(1)} %get-tuple-element.89), channel_id=1, source_target_pairs={{0,16},{4,20},{8,24},{12,28},{16,0},{20,4},{24,8},{28,12},{1,17},{... | collective-permute-start | bytes 491528 | tf_op jit(solution)/shard_map/ppermute | solution.py:21
  51.1 0.2 collective-permute-start.14
  51.4 1.8 %collective-permute-start.10 = (bf16[800,256]{1,0:T(8,128)(2,1)S(1)}, bf16[800,256]{1,0:T(8,128)(2,1)S(1)}, u32[]{:S(2)}, u32[]{:S(2)}) collective-permute-start(bf16[800,256]{1,0:T(8,128)(2,1)S(1)} %get-tuple-element.78), channel_id=1, source_target_pairs={{0,8},{4,12},{8,0},{12,4},{16,24},{20,28},{24,16},{28,20},{1,9},{5... | collective-permute-start | bytes 1228808 | tf_op jit(solution)/shard_map/ppermute | solution.py:21
  53.2 3.2 %collective-permute-done.8.refs_2_ = bf16[640,256]{1,0:T(8,128)(2,1)S(1)} collective-permute-done((bf16[640,256]{1,0:T(8,128)(2,1)S(1)}, bf16[640,256]{1,0:T(8,128)(2,1)S(1)}, u32[]{:S(2)}, u32[]{:S(2)}) %collective-permute-start.8) | collective-permute-done | bytes 327712 | tf_op jit(solution)/shard_map/ppermute | solution.py:21
  56.5 1.6 %collective-permute-start.11 = (bf16[640,256]{1,0:T(8,128)(2,1)S(1)}, bf16[640,256]{1,0:T(8,128)(2,1)S(1)}, u32[]{:S(2)}, u32[]{:S(2)}) collective-permute-start(bf16[640,256]{1,0:T(8,128)(2,1)S(1)} %get-tuple-element.82), channel_id=1, source_target_pairs={{0,1},{1,0},{2,3},{3,2},{4,5},{5,4},{6,7},{7,6},{8,9},{9,8},{10,11... | collective-permute-start | bytes 983048 | tf_op jit(solution)/shard_map/ppermute | solution.py:21
  58.4 0.7 fusion.25
  59.4 1.1 %fusion = f32[8,2,8,128]{3,2,1,0:T(8,128)} fusion(f32[8,2,8,512]{3,2,1,0:T(8,128)S(1)} %get-tuple-element.120, f32[8,2,8]{2,1,0:T(2,128)S(1)} %get-tuple-element.118, f32[8,2,8]{2,1,0:T(2,128)S(1)} %multiply_maximum_fusion, bf16[8,512,256]{2,1,0:T(8,128)(2,1)S(1)} %copy-done.7), kind=kOutput, calls=%fused_computation | convolution fusion | flops 16973824 | bytes 2425856 | tf_op jit(solution)/shard_map/rkgc,rckd->rkgd/dot_general | solution.py:721
  60.4 6.1 %collective-permute-done.10.refs_2_ = bf16[800,256]{1,0:T(8,128)(2,1)S(1)} collective-permute-done((bf16[800,256]{1,0:T(8,128)(2,1)S(1)}, bf16[800,256]{1,0:T(8,128)(2,1)S(1)}, u32[]{:S(2)}, u32[]{:S(2)}) %collective-permute-start.10) | collective-permute-done | bytes 409632 | tf_op jit(solution)/shard_map/ppermute | solution.py:21
  66.6 1.6 %collective-permute-start.15 = (bf16[400,256]{1,0:T(8,128)(2,1)S(1)}, bf16[400,256]{1,0:T(8,128)(2,1)S(1)}, u32[]{:S(2)}, u32[]{:S(2)}) collective-permute-start(bf16[400,256]{1,0:T(8,128)(2,1)S(1)} %get-tuple-element.94), channel_id=1, source_target_pairs={{0,16},{4,20},{8,24},{12,28},{16,0},{20,4},{24,8},{28,12},{1,17},{... | collective-permute-start | bytes 614408 | tf_op jit(solution)/shard_map/ppermute | solution.py:21
  68.4 1.6 %collective-permute-start.17 = (bf16[640,128]{1,0:T(8,128)(2,1)S(1)}, bf16[640,128]{1,0:T(8,128)(2,1)S(1)}, u32[]{:S(2)}, u32[]{:S(2)}) collective-permute-start(bf16[640,128]{1,0:T(8,128)(2,1)S(1)} %get-tuple-element.100), channel_id=1, source_target_pairs={{0,1},{1,0},{2,3},{3,2},{4,5},{5,4},{6,7},{7,6},{8,9},{9,8},{10,11... | collective-permute-start | bytes 491528 | tf_op jit(solution)/shard_map/ppermute | solution.py:21
  70.0 2.6 %collective-permute-start.12 = (bf16[320,256]{1,0:T(8,128)(2,1)S(1)}, bf16[320,256]{1,0:T(8,128)(2,1)S(1)}, u32[]{:S(2)}, u32[]{:S(2)}) collective-permute-start(bf16[320,256]{1,0:T(8,128)(2,1)S(1)} %get-tuple-element.84), channel_id=1, source_target_pairs={{0,2},{1,3},{2,0},{3,1},{4,6},{5,7},{6,4},{7,5},{8,10},{9,11},{10,... | collective-permute-start | bytes 491528 | tf_op jit(solution)/shard_map/ppermute | solution.py:21
  72.7 0.5 collective-permute-done.15.refs_2_
  73.3 3.0 %collective-permute-start.16 = (bf16[240,256]{1,0:T(8,128)(2,1)S(1)}, bf16[240,256]{1,0:T(8,128)(2,1)S(1)}, u32[]{:S(2)}, u32[]{:S(2)}) collective-permute-start(bf16[240,256]{1,0:T(8,128)(2,1)S(1)} %get-tuple-element.96), channel_id=1, source_target_pairs={{0,2},{1,3},{2,0},{3,1},{4,6},{5,7},{6,4},{7,5},{8,10},{9,11},{10,... | collective-permute-start | bytes 368648 | tf_op jit(solution)/shard_map/ppermute | solution.py:21
  76.2 0.6 collective-permute-done.17.refs_2_
  76.8 1.4 %collective-permute-start.18 = (bf16[320,128]{1,0:T(8,128)(2,1)S(1)}, bf16[320,128]{1,0:T(8,128)(2,1)S(1)}, u32[]{:S(2)}, u32[]{:S(2)}) collective-permute-start(bf16[320,128]{1,0:T(8,128)(2,1)S(1)} %get-tuple-element.102), channel_id=1, source_target_pairs={{0,2},{1,3},{2,0},{3,1},{4,6},{5,7},{6,4},{7,5},{8,10},{9,11},{10,... | collective-permute-start | bytes 245768 | tf_op jit(solution)/shard_map/ppermute | solution.py:21
  78.2 7.0 %collective-permute-done.12 = bf16[320,256]{1,0:T(8,128)(2,1)S(1)} collective-permute-done((bf16[320,256]{1,0:T(8,128)(2,1)S(1)}, bf16[320,256]{1,0:T(8,128)(2,1)S(1)}, u32[]{:S(2)}, u32[]{:S(2)}) %collective-permute-start.12) | collective-permute-done | bytes 163872 | tf_op jit(solution)/shard_map/ppermute | solution.py:21
  85.2 0.7 subtract_dynamic-update-slice_fusion.2
  85.9 0.7 subtract_dynamic-update-slice_fusion.1
  86.6 1.0 collective-permute-done.16
  87.6 0.6 shard_map.155
  88.2 0.7 convert_element_type.69
  88.9 3.5 %all-to-all-start = ((bf16[32,8,256]{2,1,0:T(8,128)(2,1)}), bf16[32,8,256]{2,1,0:T(8,128)(2,1)S(1)}, u32[]{:S(2)}, u32[]{:S(2)}) async-start(bf16[32,8,256]{2,1,0:T(8,128)(2,1)} %convert_element_type.69), calls=%async_computation | async-start | bytes 262144 | tf_op jit(solution)/shard_map/all_to_all | solution.py:649
  92.3 0.7 subtract_dynamic-update-slice_fusion
  93.0 0.7 subtract_dynamic-update-slice_fusion.4
  93.7 0.7 subtract_dynamic-update-slice_fusion.3
  94.3 6.4 %all-to-all-done = bf16[32,8,256]{2,1,0:T(8,128)(2,1)S(1)} async-done(((bf16[32,8,256]{2,1,0:T(8,128)(2,1)}), bf16[32,8,256]{2,1,0:T(8,128)(2,1)S(1)}, u32[]{:S(2)}, u32[]{:S(2)}) %all-to-all-start) | async-done | bytes 131104 | tf_op jit(solution)/shard_map/all_to_all | solution.py:649
  100.8 0.6 bitcast_convert_fusion
  101.4 0.9 fusion.15
  102.3 0.6 copy.47
  (59 shorter events, 1.9 us)
Async XLA Ops:
  0.6 57.7 %copy-start = (bf16[8,512,256]{2,1,0:T(8,128)(2,1)S(1)}, bf16[8,512,256]{2,1,0:T(8,128)(2,1)}, u32[]{:S(2)}) copy-start(bf16[8,512,256]{2,1,0:T(8,128)(2,1)} %param.18) | copy-start | bytes 6291460
  0.6 3.7 %copy-start.2 = (bf16[512,1024]{1,0:T(8,128)(2,1)S(1)}, bf16[512,1024]{1,0:T(8,128)(2,1)}, u32[]{:S(2)}) copy-start(bf16[512,1024]{1,0:T(8,128)(2,1)} %refs_2_.7) | copy-start | bytes 3145732
  0.7 3.8 %copy-start.9 = (s32[64]{0:T(128)S(1)}, s32[64]{0:T(128)}, u32[]{:S(2)}) copy-start(s32[64]{0:T(128)} %param.16) | copy-start | bytes 772
  3.9 8.6 %collective-permute-start = (bf16[2560,512]{1,0:T(8,128)(2,1)}, bf16[2560,512]{1,0:T(8,128)(2,1)}, u32[]{:S(2)}, u32[]{:S(2)}) collective-permute-start(bf16[2560,512]{1,0:T(8,128)(2,1)} %shard_map.140), channel_id=1, source_target_pairs={{0,4},{4,0},{8,12},{12,8},{16,20},{20,16},{24,28},{28,24},{1,5},{5... | collective-permute-start | bytes 7864328 | tf_op jit(solution)/shard_map/ppermute | solution.py:21
  4.4 8.0 %collective-permute-start.1 = (bf16[512,1024]{1,0:T(8,128)(2,1)S(1)}, bf16[512,1024]{1,0:T(8,128)(2,1)}, u32[]{:S(2)}, u32[]{:S(2)}) collective-permute-start(bf16[512,1024]{1,0:T(8,128)(2,1)S(1)} %copy-done.2), channel_id=1, source_target_pairs={{0,4},{4,0},{8,12},{12,8},{16,20},{20,16},{24,28},{28,24},{1,5},{5... | collective-permute-start | bytes 3145736 | tf_op jit(solution)/shard_map/ppermute | solution.py:21
  8.1 4.3 %collective-permute-start.2 = (bf16[640,256]{1,0:T(8,128)(2,1)S(1)}, bf16[640,256]{1,0:T(8,128)(2,1)S(1)}, u32[]{:S(2)}, u32[]{:S(2)}) collective-permute-start(bf16[640,256]{1,0:T(8,128)(2,1)S(1)} %get-tuple-element.59), channel_id=1, source_target_pairs={{0,4},{4,0},{8,12},{12,8},{16,20},{20,16},{24,28},{28,24},{1,5},{5... | collective-permute-start | bytes 983048 | tf_op jit(solution)/shard_map/ppermute | solution.py:21
  12.4 1.7 %copy-start.1 = (bf16[2560,512]{1,0:T(8,128)(2,1)S(1)}, bf16[2560,512]{1,0:T(8,128)(2,1)}, u32[]{:S(2)}) copy-start(bf16[2560,512]{1,0:T(8,128)(2,1)} %shard_map.139.refs_0_) | copy-start | bytes 7864324
  14.2 13.6 %copy-start.10 = (f32[2]{0:T(128)S(1)}, f32[2]{0:T(128)}, u32[]{:S(2)}) copy-start(f32[2]{0:T(128)} %param.22) | copy-start | bytes 28
  22.1 18.3 %collective-permute-start.3 = (bf16[1280,256]{1,0:T(8,128)(2,1)S(1)}, bf16[1280,256]{1,0:T(8,128)(2,1)S(1)}, u32[]{:S(2)}, u32[]{:S(2)}) collective-permute-start(bf16[1280,256]{1,0:T(8,128)(2,1)S(1)} %get-tuple-element.60), channel_id=1, source_target_pairs={{0,8},{4,12},{8,0},{12,4},{16,24},{20,28},{24,16},{28,20},{1,9},{5... | collective-permute-start | bytes 1966088 | tf_op jit(solution)/shard_map/ppermute | solution.py:21
  24.8 17.6 %collective-permute-start.4 = (bf16[1280,256]{1,0:T(8,128)(2,1)S(1)}, bf16[1280,256]{1,0:T(8,128)(2,1)S(1)}, u32[]{:S(2)}, u32[]{:S(2)}) collective-permute-start(bf16[1280,256]{1,0:T(8,128)(2,1)S(1)} %get-tuple-element.61), channel_id=1, source_target_pairs={{0,16},{4,20},{8,24},{12,28},{16,0},{20,4},{24,8},{28,12},{1,17},{... | collective-permute-start | bytes 1966088 | tf_op jit(solution)/shard_map/ppermute | solution.py:21
  26.4 22.0 %collective-permute-start.5 = (bf16[1600,256]{1,0:T(8,128)(2,1)S(1)}, bf16[1600,256]{1,0:T(8,128)(2,1)S(1)}, u32[]{:S(2)}, u32[]{:S(2)}) collective-permute-start(bf16[1600,256]{1,0:T(8,128)(2,1)S(1)} %get-tuple-element.64), channel_id=1, source_target_pairs={{0,1},{1,0},{2,3},{3,2},{4,5},{5,4},{6,7},{7,6},{8,9},{9,8},{10,11... | collective-permute-start | bytes 2457608 | tf_op jit(solution)/shard_map/ppermute | solution.py:21
  33.4 15.2 %collective-permute-start.6 = (bf16[1280,128]{1,0:T(8,128)(2,1)S(1)}, bf16[1280,128]{1,0:T(8,128)(2,1)S(1)}, u32[]{:S(2)}, u32[]{:S(2)}) collective-permute-start(bf16[1280,128]{1,0:T(8,128)(2,1)S(1)} %get-tuple-element.68), channel_id=1, source_target_pairs={{0,8},{4,12},{8,0},{12,4},{16,24},{20,28},{24,16},{28,20},{1,9},{5... | collective-permute-start | bytes 983048 | tf_op jit(solution)/shard_map/ppermute | solution.py:21
  34.0 15.4 %collective-permute-start.7 = (bf16[1280,128]{1,0:T(8,128)(2,1)S(1)}, bf16[1280,128]{1,0:T(8,128)(2,1)S(1)}, u32[]{:S(2)}, u32[]{:S(2)}) collective-permute-start(bf16[1280,128]{1,0:T(8,128)(2,1)S(1)} %get-tuple-element.69), channel_id=1, source_target_pairs={{0,16},{4,20},{8,24},{12,28},{16,0},{20,4},{24,8},{28,12},{1,17},{... | collective-permute-start | bytes 983048 | tf_op jit(solution)/shard_map/ppermute | solution.py:21
  42.6 13.8 %collective-permute-start.8 = (bf16[640,256]{1,0:T(8,128)(2,1)S(1)}, bf16[640,256]{1,0:T(8,128)(2,1)S(1)}, u32[]{:S(2)}, u32[]{:S(2)}) collective-permute-start(bf16[640,256]{1,0:T(8,128)(2,1)S(1)} %get-tuple-element.73), channel_id=1, source_target_pairs={{0,16},{4,20},{8,24},{12,28},{16,0},{20,4},{24,8},{28,12},{1,17},{... | collective-permute-start | bytes 983048 | tf_op jit(solution)/shard_map/ppermute | solution.py:21
  44.2 12.2 %collective-permute-start.9 = (bf16[640,256]{1,0:T(8,128)(2,1)S(1)}, bf16[640,256]{1,0:T(8,128)(2,1)S(1)}, u32[]{:S(2)}, u32[]{:S(2)}) collective-permute-start(bf16[640,256]{1,0:T(8,128)(2,1)S(1)} %get-tuple-element.74), channel_id=1, source_target_pairs={{0,8},{4,12},{8,0},{12,4},{16,24},{20,28},{24,16},{28,20},{1,9},{5... | collective-permute-start | bytes 983048 | tf_op jit(solution)/shard_map/ppermute | solution.py:21
  48.5 9.6 %copy-start.6 = (s32[8]{0:T(128)S(1)}, s32[8]{0:T(128)}, u32[]{:S(2)}) copy-start(s32[8]{0:T(128)} %param.23) | copy-start | bytes 100
  48.6 9.7 %copy-start.4 = (bf16[8,2048]{1,0:T(8,128)(2,1)S(1)}, bf16[8,2048]{1,0:T(8,128)(2,1)}, u32[]{:S(2)}) copy-start(bf16[8,2048]{1,0:T(8,128)(2,1)} %param.17) | copy-start | bytes 98308
  48.6 9.6 %copy-start.8 = (bf16[8,256]{1,0:T(8,128)(2,1)S(1)}, bf16[8,256]{1,0:T(8,128)(2,1)}, u32[]{:S(2)}) copy-start(bf16[8,256]{1,0:T(8,128)(2,1)} %param.20) | copy-start | bytes 12292
  49.5 18.8 %collective-permute-start.13 = (bf16[640,128]{1,0:T(8,128)(2,1)S(1)}, bf16[640,128]{1,0:T(8,128)(2,1)S(1)}, u32[]{:S(2)}, u32[]{:S(2)}) collective-permute-start(bf16[640,128]{1,0:T(8,128)(2,1)S(1)} %get-tuple-element.89), channel_id=1, source_target_pairs={{0,16},{4,20},{8,24},{12,28},{16,0},{20,4},{24,8},{28,12},{1,17},{... | collective-permute-start | bytes 491528 | tf_op jit(solution)/shard_map/ppermute | solution.py:21
  51.1 17.2 %collective-permute-start.14 = (bf16[640,128]{1,0:T(8,128)(2,1)S(1)}, bf16[640,128]{1,0:T(8,128)(2,1)S(1)}, u32[]{:S(2)}, u32[]{:S(2)}) collective-permute-start(bf16[640,128]{1,0:T(8,128)(2,1)S(1)} %get-tuple-element.90), channel_id=1, source_target_pairs={{0,8},{4,12},{8,0},{12,4},{16,24},{20,28},{24,16},{28,20},{1,9},{5... | collective-permute-start | bytes 491528 | tf_op jit(solution)/shard_map/ppermute | solution.py:21
  51.4 15.1 %collective-permute-start.10 = (bf16[800,256]{1,0:T(8,128)(2,1)S(1)}, bf16[800,256]{1,0:T(8,128)(2,1)S(1)}, u32[]{:S(2)}, u32[]{:S(2)}) collective-permute-start(bf16[800,256]{1,0:T(8,128)(2,1)S(1)} %get-tuple-element.78), channel_id=1, source_target_pairs={{0,8},{4,12},{8,0},{12,4},{16,24},{20,28},{24,16},{28,20},{1,9},{5... | collective-permute-start | bytes 1228808 | tf_op jit(solution)/shard_map/ppermute | solution.py:21
  56.4 2.9 %copy-start.7 = (bf16[8,512,256]{2,1,0:T(8,128)(2,1)S(1)}, bf16[8,512,256]{2,1,0:T(8,128)(2,1)}, u32[]{:S(2)}) copy-start(bf16[8,512,256]{2,1,0:T(8,128)(2,1)} %param.19) | copy-start | bytes 6291460
  56.5 11.7 %collective-permute-start.11 = (bf16[640,256]{1,0:T(8,128)(2,1)S(1)}, bf16[640,256]{1,0:T(8,128)(2,1)S(1)}, u32[]{:S(2)}, u32[]{:S(2)}) collective-permute-start(bf16[640,256]{1,0:T(8,128)(2,1)S(1)} %get-tuple-element.82), channel_id=1, source_target_pairs={{0,1},{1,0},{2,3},{3,2},{4,5},{5,4},{6,7},{7,6},{8,9},{9,8},{10,11... | collective-permute-start | bytes 983048 | tf_op jit(solution)/shard_map/ppermute | solution.py:21
  66.6 18.6 %copy-start.3 = (f32[160,1024]{1,0:T(8,128)S(1)}, f32[160,1024]{1,0:T(8,128)}, u32[]{:S(2)}) copy-start(f32[160,1024]{1,0:T(8,128)} %refs_1_.1) | copy-start | bytes 1966084
  66.6 6.6 %collective-permute-start.15 = (bf16[400,256]{1,0:T(8,128)(2,1)S(1)}, bf16[400,256]{1,0:T(8,128)(2,1)S(1)}, u32[]{:S(2)}, u32[]{:S(2)}) collective-permute-start(bf16[400,256]{1,0:T(8,128)(2,1)S(1)} %get-tuple-element.94), channel_id=1, source_target_pairs={{0,16},{4,20},{8,24},{12,28},{16,0},{20,4},{24,8},{28,12},{1,17},{... | collective-permute-start | bytes 614408 | tf_op jit(solution)/shard_map/ppermute | solution.py:21
  68.4 8.4 %collective-permute-start.17 = (bf16[640,128]{1,0:T(8,128)(2,1)S(1)}, bf16[640,128]{1,0:T(8,128)(2,1)S(1)}, u32[]{:S(2)}, u32[]{:S(2)}) collective-permute-start(bf16[640,128]{1,0:T(8,128)(2,1)S(1)} %get-tuple-element.100), channel_id=1, source_target_pairs={{0,1},{1,0},{2,3},{3,2},{4,5},{5,4},{6,7},{7,6},{8,9},{9,8},{10,11... | collective-permute-start | bytes 491528 | tf_op jit(solution)/shard_map/ppermute | solution.py:21
  70.0 15.2 %collective-permute-start.12 = (bf16[320,256]{1,0:T(8,128)(2,1)S(1)}, bf16[320,256]{1,0:T(8,128)(2,1)S(1)}, u32[]{:S(2)}, u32[]{:S(2)}) collective-permute-start(bf16[320,256]{1,0:T(8,128)(2,1)S(1)} %get-tuple-element.84), channel_id=1, source_target_pairs={{0,2},{1,3},{2,0},{3,1},{4,6},{5,7},{6,4},{7,5},{8,10},{9,11},{10,... | collective-permute-start | bytes 491528 | tf_op jit(solution)/shard_map/ppermute | solution.py:21
  73.3 14.4 %collective-permute-start.16 = (bf16[240,256]{1,0:T(8,128)(2,1)S(1)}, bf16[240,256]{1,0:T(8,128)(2,1)S(1)}, u32[]{:S(2)}, u32[]{:S(2)}) collective-permute-start(bf16[240,256]{1,0:T(8,128)(2,1)S(1)} %get-tuple-element.96), channel_id=1, source_target_pairs={{0,2},{1,3},{2,0},{3,1},{4,6},{5,7},{6,4},{7,5},{8,10},{9,11},{10,... | collective-permute-start | bytes 368648 | tf_op jit(solution)/shard_map/ppermute | solution.py:21
  76.8 16.2 %collective-permute-start.18 = (bf16[320,128]{1,0:T(8,128)(2,1)S(1)}, bf16[320,128]{1,0:T(8,128)(2,1)S(1)}, u32[]{:S(2)}, u32[]{:S(2)}) collective-permute-start(bf16[320,128]{1,0:T(8,128)(2,1)S(1)} %get-tuple-element.102), channel_id=1, source_target_pairs={{0,2},{1,3},{2,0},{3,1},{4,6},{5,7},{6,4},{7,5},{8,10},{9,11},{10,... | collective-permute-start | bytes 245768 | tf_op jit(solution)/shard_map/ppermute | solution.py:21
  87.6 13.2 %copy-start.5 = (bf16[8,256]{1,0:T(8,128)(2,1)S(1)}, bf16[8,256]{1,0:T(8,128)(2,1)}, u32[]{:S(2)}) copy-start(bf16[8,256]{1,0:T(8,128)(2,1)} %param.21) | copy-start | bytes 12292
  88.9 11.9 %all-to-all-start = ((bf16[32,8,256]{2,1,0:T(8,128)(2,1)}), bf16[32,8,256]{2,1,0:T(8,128)(2,1)S(1)}, u32[]{:S(2)}, u32[]{:S(2)}) async-start(bf16[32,8,256]{2,1,0:T(8,128)(2,1)} %convert_element_type.69), calls=%async_computation | async-start | bytes 262144 | tf_op jit(solution)/shard_map/all_to_all | solution.py:649

commit v11 on v10

--- a/solution.py
+++ b/solution.py
@@ -100,14 +100,13 @@
     return runs
 
 
-def multiply(wanted, rows, blocks, base, staged, tail, *refs):
+def multiply(wanted, rows, blocks, base, tail, *refs):
     count = len(wanted)
     sources = refs[:4]
     if tail:
         appended, refs = refs[4:6], refs[:4] + refs[6:]
     outs = refs[4 : 4 + count]
     left, right, sems = refs[4 + count : 7 + count]
-    stages, given = refs[7 + count : 7 + 2 * count] if staged else outs, []
     tokens = left.shape[1] // 2
     per_block = left.shape[0] // blocks
     units_block = per_block // rows
@@ -135,21 +134,15 @@
         addends, addend_sems = refs[-2:]
         for at in range(2):
             pltpu.make_async_copy(
-                appended[at].at[pl.ds(tail, tail)], addends.at[at], addend_sems.at[at]
+                appended[at], addends.at[at], addend_sems.at[at]
             ).start()
     if tail:
         for at in range(2):
             pltpu.make_async_copy(
-                appended[at].at[pl.ds(tail, tail)], addends.at[at], addend_sems.at[at]
+                appended[at], addends.at[at], addend_sems.at[at]
             ).wait()
         low = len(wanted[0][0]) * rows
-        stages[0][low : low + tail, :] = addends[0] + addends[1]
-        span = pl.ds(low, tail)
-        copy = pltpu.make_async_copy(
-            stages[0].at[span], outs[0].at[span], refs[7 + 2 * count].at[blocks, 0]
-        )
-        copy.start()
-        given.append(copy)
+        outs[0][low : low + tail, :] = addends[0] + addends[1]
     for copy in grads:
         copy.wait()
     for block in needed:
@@ -162,19 +155,10 @@
                 product = dot32(
                     left[low * rows : high * rows, :], right[:, first - base : last - base]
                 )
-                stages[at][place : place + (high - low) * rows, :] = product.astype(outs[at].dtype)
-            if staged and here:
-                span = pl.ds(units.index(here[0]) * rows, len(here) * rows)
-                copy = pltpu.make_async_copy(
-                    stages[at].at[span], outs[at].at[span], refs[7 + 2 * count].at[block, at]
-                )
-                copy.start()
-                given.append(copy)
-    for copy in given:
-        copy.wait()
-
-
-def products(lefts, grads, wanted, rows, blocks, staged, appended=None):
+                outs[at][place : place + (high - low) * rows, :] = product.astype(outs[at].dtype)
+
+
+def products(lefts, grads, wanted, rows, blocks, appended=None):
     total, tokens = lefts[0].shape
     base = min(first for _, first, _, _ in wanted)
     columns = max(last for _, _, last, _ in wanted) - base
@@ -192,10 +176,9 @@
             for units, first, last, kind in wanted
         ]
         if appended is not None:
-            both = appended[0] + appended[1]
-            results[0] = jnp.concatenate([results[0], both[both.shape[0] // 2 :]])
+            results[0] = jnp.concatenate([results[0], appended[0] + appended[1]])
         return results
-    tail = 0 if appended is None else appended[0].shape[0] // 2
+    tail = 0 if appended is None else appended[0].shape[0]
     shapes = [
         jax.ShapeDtypeStruct((len(units) * rows, last - first), kind)
         for units, first, last, kind in wanted
@@ -204,17 +187,14 @@
         grown = (shapes[0].shape[0] + tail, shapes[0].shape[1])
         shapes[0] = jax.ShapeDtypeStruct(grown, shapes[0].dtype)
     staging = []
-    if staged:
-        staging = [pltpu.VMEM(shape.shape, shape.dtype) for shape in shapes]
-        staging.append(pltpu.SemaphoreType.DMA((blocks + 1, len(shapes))))
     if tail:
         staging.append(pltpu.VMEM((2, tail, shapes[0].shape[1]), shapes[0].dtype))
         staging.append(pltpu.SemaphoreType.DMA((2,)))
     return pl.pallas_call(
-        functools.partial(multiply, wanted, rows, blocks, base, staged, tail),
+        functools.partial(multiply, wanted, rows, blocks, base, tail),
         out_shape=shapes,
         in_specs=[pl.BlockSpec(memory_space=pltpu.HBM)] * (6 if tail else 4),
-        out_specs=[pl.BlockSpec(memory_space=pltpu.HBM if staged else pltpu.VMEM)] * len(shapes),
+        out_specs=[pl.BlockSpec(memory_space=pltpu.VMEM)] * len(shapes),
         scratch_shapes=[
             pltpu.VMEM((total, 2 * tokens), lefts[0].dtype),
             pltpu.VMEM((2 * tokens, columns), grads[0].dtype),
@@ -277,7 +257,7 @@
                     flipped[pl.ds(pl.multiple_of(from_row + fold * lines, 8), lines), :]
                     for fold in range(folds)
                 ]
-                put = ((unit & 1) * len(arranged) + j) * lines
+                put = (2 * j + (unit & 1)) * lines
                 side_lanes = slice((unit >> 1) * lanes, ((unit >> 1) + 1) * lanes)
                 out[put : put + lines, side_lanes] = jnp.concatenate(pieces, axis=1).astype(
                     out.dtype
@@ -433,8 +413,8 @@
                     jnp.concatenate(
                         [folded(r, side, unit) for unit in range(low, units, 2)], axis=1
                     )
+                    for r in arranged
                     for low in range(2)
-                    for r in arranged
                 ]
             )
             for side in (1 - core, core)
@@ -504,14 +484,10 @@
     places = [(r, unit) for r in arranged for unit in range(count_tp)]
     steps_upper = [("fsdp", bit) for bit in range(upper_bits)]
     steps_tp = [("tp", bit) for bit in range(count_tp.bit_length() - 1)]
-    one, two, three = (
-        steps_upper + steps_tp,
-        steps_upper[::-1] + steps_tp,
-        steps_tp[:1] + steps_upper + steps_tp[1:],
-    )
-    edges = [0, quarter, 2 * quarter, 3 * quarter, 3 * quarter + eighth, columns]
-    spans = list(zip(edges[:-1], edges[1:]))
-    orders = [one, two, three, one, two]
+    one, two = steps_upper + steps_tp, steps_upper[::-1] + steps_tp
+    spans = [(at * quarter, (at + 1) * quarter) for at in range(4)]
+    orders = [one, two, one, two]
+    chunks = range(len(spans))
 
     def has(place, step):
         return (place[step[0] == "tp"] >> step[1]) & 1
@@ -538,26 +514,32 @@
             units = [places.index(p) for p in chosen]
             kind = jnp.bfloat16 if sent else jnp.float32
             wanted.append((units, *spans[index], kind))
-        return dict(zip(which, products(lefts, grads, wanted, rows, uppers, sent, appended)))
+        return dict(zip(which, products(lefts, grads, wanted, rows, uppers, appended)))
 
     theirs, ours = lookup(embed_table, token_ids, arranged, count_tp, block, eighth)
     asked = [ours, exchange(theirs, "fsdp", 1)]
-    pairs = [(r, low) for low in range(2) for r in arranged]
-    going = compute([2, 0, 1], True, asked)
-    got = {index: send(going[index], orders[index][0]) for index in (0, 1, 2)}
-    going |= compute([3, 4], True)
-    got |= {index: send(going[index], orders[index][0]) for index in (3, 4)}
-    values = compute([0, 1, 2], False)
-    values |= compute([3, 4], False)
+    pairs = [(r, low) for r in arranged for low in range(2)]
+    pairs_go, pairs_keep = split(pairs, orders[0][0])
+
+    def chosen_pairs(array, wanted):
+        return take(array, pairs, wanted, lines)
+
+    going = compute([0, 1], True, [chosen_pairs(array, pairs_go) for array in asked])
+    got = {index: send(going[index], orders[index][0]) for index in (0, 1)}
+    going |= compute([2, 3], True)
+    got |= {index: send(going[index], orders[index][0]) for index in (2, 3)}
+    values = compute([0, 1], False)
+    values |= compute([2, 3], False)
     values = {index: [value] for index, value in values.items()}
-    halves = [array[: array.shape[0] // 2].astype(jnp.float32) for array in asked]
-    values[2].append(halves[0] + halves[1])
-    sizes = {index: [rows] for index in range(5)}
-    sizes[2].append(lines)
-    held = {index: [split(places, orders[index][0])[1]] for index in range(5)}
-    held[2].append(split(pairs, orders[2][0])[1])
-    gone = {index: [split(places, orders[index][0])[0]] for index in range(5)}
-    gone[2].append(split(pairs, orders[2][0])[0])
+    kept_pairs = [chosen_pairs(array, pairs_keep).astype(jnp.float32) for array in asked]
+    values[0].append(kept_pairs[0] + kept_pairs[1])
+    sizes = {index: [rows] for index in chunks}
+    sizes[0].append(lines)
+    gone, held = [
+        {index: [split(places, orders[index][0])[side]] for index in chunks} for side in range(2)
+    ]
+    gone[0].append(pairs_go)
+    held[0].append(pairs_keep)
 
     def receive(index, step, arrived):
         start = 0
@@ -611,8 +593,8 @@
             out = out.reshape(count_fsdp, rows_f, count_tp, col_width)
             out = out.transpose(0, 2, 1, 3).reshape(devices_all, rows_f, col_width)
             return out.astype(jnp.bfloat16)
-        arrays = [array for index in range(5) for array in sums[index]]
-        plans = [[(2 * index, [0]), (2 * index + 1, [1])] for index in range(5)]
+        arrays = [array for index in chunks for array in sums[index]]
+        plans = [[(2 * index, [0]), (2 * index + 1, [1])] for index in chunks]
         return pl.pallas_call(
             functools.partial(own_share, coef, spans, plans, rows, tokens_new, 2),
             in_specs=[pl.BlockSpec(memory_space=pl.ANY)]
@@ -624,16 +606,13 @@
         )(after, emb, master_w, *arrays).astype(jnp.bfloat16)
 
     plain = rows % 32 or lines % 16 or block % LANES or eighth % tokens_new
-    groups = ((0, 1), (2,), (3, 4))
+    groups = ((0, 1), (2, 3))
     inbox = {group: [got[index] for index in group] for group in groups}
     totals = {}
     sums = {}
     steps = len(one)
     events = [(group, at) for at in range(steps) for group in groups]
-    if steps == 4:
-        first, second, third = groups
-        events = [(first, 0), (second, 0), (third, 0), (first, 1), (second, 1), (first, 2)]
-        events += [(third, 1), (second, 2), (third, 2), (second, 3), (first, 3), (third, 3)]
+    events[-3:-1] = events[-2:-4:-1]
     done = jnp.zeros(TOKEN, jnp.float32)
     for group, at in events:
         last = at + 1 == steps
@@ -645,13 +624,7 @@
             for index, arrived in zip(group, inbox[group]):
                 receive(index, orders[index][at], arrived)
         if last:
-            if group == (2,):
-                parts_own = lax.all_to_all(
-                    share_of(sums, values[2][1], done),
-                    ("fsdp", "tp"),
-                    split_axis=0,
-                    concat_axis=0,
-                )
+            done = values[0][1]
             continue
         if plain:
             outgoing = []
@@ -681,6 +654,10 @@
         inbox[group] = [
             send(value, orders[index][at + 1]) for index, value in zip(group, outgoing)
         ]
+        if group == groups[1] and at + 2 == steps:
+            parts_own = lax.all_to_all(
+                share_of(sums, values[0][1], done), ("fsdp", "tp"), split_axis=0, concat_axis=0
+            )
         if at == 1 and group == groups[0]:
             queries, new_key, lengths, outgoing[0] = lax.optimization_barrier(
                 (queries, new_key, lengths, outgoing[0])

time: 103 us -> 105 us (1.019)
  waiting for transfers between devices: 28.5 us -> 36.7 us
  Pallas kernels: 33.3 us -> 29 us
  starting transfers between devices: 29.7 us -> 26.3 us
  local copies, waits for them, and re-layouts: 2.52 us -> 4.76 us
    ppermute x19 -> x15, waiting for transfers between devices: 22.1 us -> 30.4 us  [exchange(): lax.ppermute(value, axis, [(i, i ^ mask) for i in range(lax.axis_size(axi...]
    pallas_call x4, Pallas kernels: 22.1 us -> 15.7 us  [products(): pl.pallas_call(functools.partial(multiply, wanted, rows, blocks, base, ta...]
    ppermute x19 -> x15, starting transfers between devices: 26.2 us -> 21.2 us  [exchange(): lax.ppermute(value, axis, [(i, i ^ mask) for i in range(lax.axis_size(axi...]
    unnamed x5 -> x1, other arithmetic: 3.67 us -> 0.92 us
    all_to_all x1, starting transfers between devices: 3.46 us -> 5.02 us  [per_device(): lax.all_to_all(share_of(sums, values[0][1], done), ('fsdp', 'tp'), split_...]
    pallas_call x9 -> x6, Pallas kernels: 0.78 us -> 2.12 us  [combine(): pl.pallas_call(functools.partial(add_and_split, plans, len(got), merged),...]
    sub x0 -> x1, other arithmetic: none -> 1.14 us  [per_device(): master_w[:, low:high] - coef * values[at][0]]
    unnamed x23 -> x25, local copies, waits for them, and re-layouts: 2.41 us -> 3.09 us
  transfers between devices with their start and end apart: 20 -> 16, of which waited for: 10 -> 10; matrix products, arithmetic and copies ran while one was open for 6% -> 6% of each run, Pallas kernels for 22% -> 20%
where the time goes in v11:
time: 105 us
  waiting for transfers between devices  36.7 us (35%)
  Pallas kernels  29 us (28%)
  starting transfers between devices  26.3 us (25%)
  other arithmetic  5.39 us (5%)
  local copies, waits for them, and re-layouts  4.76 us (5%)
  matrix products  1.95 us (2%)
    ppermute x15, waiting for transfers between devices, exchange(): lax.ppermute(value, axis, [(i, i ^ mask) for i in range(lax.axis_size(axi...  30.4 us
    ppermute x15, starting transfers between devices, exchange(): lax.ppermute(value, axis, [(i, i ^ mask) for i in range(lax.axis_size(axi...  21.2 us
    pallas_call x4, Pallas kernels, products(): pl.pallas_call(functools.partial(multiply, wanted, rows, blocks, base, ta...  15.7 us
    all_to_all x1, waiting for transfers between devices, per_device(): lax.all_to_all(share_of(sums, values[0][1], done), ('fsdp', 'tp'), split_...  6.33 us
    pallas_call x2, Pallas kernels, pack(): pl.pallas_call(functools.partial(transpose_blocks, arranged, mine, units)...  6.26 us
    all_to_all x1, starting transfers between devices, per_device(): lax.all_to_all(share_of(sums, values[0][1], done), ('fsdp', 'tp'), split_...  5.02 us
    pallas_call x1, Pallas kernels, lookup(): pl.pallas_call(functools.partial(pick_rows, arranged, units), grid=(1,),...  4.41 us
    unnamed x25, local copies, waits for them, and re-layouts  3.09 us
  transfers between devices with their start and end apart: 16, of which 10 were waited for; matrix products, arithmetic and copies ran while one was open for 6% of the time, Pallas kernels for 20%

profile of v11, /device:TPU:0, one launch (start us, length us, event | category | flops | bytes accessed | tf_op | source)
XLA Modules:
  0.0 105.0 jit_solution(9137355377038770240)
XLA Ops:
  0.7 3.2 %shard_map.140 = bf16[2560,512]{1,0:T(8,128)(2,1)} custom-call(bf16[512,5120]{1,0:T(8,128)(2,1)} %source.3), custom_call_target="tpu_custom_call" | custom-call | bytes 5242880 | tf_op jit(solution)/shard_map/pallas_call | solution.py:75
  3.9 0.5 collective-permute-start
  4.5 4.4 %shard_map.142 = (bf16[640,256]{1,0:T(8,128)(2,1)S(1)}, bf16[640,256]{1,0:T(8,128)(2,1)S(1)}) custom-call(s32[64]{0:T(128)S(1)} %and_select_fusion.place, bf16[4748,5120]{1,0:T(8,128)(2,1)} %tail.1, bf16[4748,5120]{1,0:T(8,128)(2,1)} %tail.1), custom_call_target="tpu_custom_call" | custom-call | flops 1 | bytes 1 | tf_op jit(solution)/shard_map/pallas_call | solution.py:423
  8.9 0.6 collective-permute-start.2
  9.5 3.1 %shard_map.139.refs_0_ = bf16[2560,512]{1,0:T(8,128)(2,1)} custom-call(bf16[512,5120]{1,0:T(8,128)(2,1)} %source.3), custom_call_target="tpu_custom_call" | custom-call | bytes 5242880 | tf_op jit(solution)/shard_map/pallas_call | solution.py:75
  12.6 1.7 %copy-done.1 = bf16[2560,512]{1,0:T(8,128)(2,1)S(1)} copy-done((bf16[2560,512]{1,0:T(8,128)(2,1)S(1)}, bf16[2560,512]{1,0:T(8,128)(2,1)}, u32[]{:S(2)}) %copy-start.1) | copy-done | bytes 2621464
  14.3 3.9 %shard_map.143 = (bf16[1600,256]{1,0:T(8,128)(2,1)S(1)}, bf16[1280,256]{1,0:T(8,128)(2,1)S(1)}) custom-call(bf16[2560,512]{1,0:T(8,128)(2,1)S(1)} %copy-done.1, bf16[2560,512]{1,0:T(8,128)(2,1)} %collective-permute-done.refs_1_, bf16[512,1024]{1,0:T(8,128)(2,1)S(1)} %copy-done.2, bf16[512,1024]{1,0:T(8,128)(2,1)} %collective-permute-done.1.refs_3_, ...), custom_call_target="tpu_custom_call" | custom-call | flops 1 | bytes 1 | tf_op jit(solution)/shard_map/pallas_call | solution.py:193
  18.3 2.4 %collective-permute-start.3 = (bf16[1600,256]{1,0:T(8,128)(2,1)S(1)}, bf16[1600,256]{1,0:T(8,128)(2,1)S(1)}, u32[]{:S(2)}, u32[]{:S(2)}) collective-permute-start(bf16[1600,256]{1,0:T(8,128)(2,1)S(1)} %get-tuple-element.48), channel_id=1, source_target_pairs={{0,8},{4,12},{8,0},{12,4},{16,24},{20,28},{24,16},{28,20},{1,9},{5... | collective-permute-start | bytes 2457608 | tf_op jit(solution)/shard_map/ppermute | solution.py:21
  20.7 0.9 collective-permute-start.4
  21.6 3.9 %shard_map.146 = (bf16[1280,256]{1,0:T(8,128)(2,1)S(1)}, bf16[1280,256]{1,0:T(8,128)(2,1)S(1)}) custom-call(bf16[2560,512]{1,0:T(8,128)(2,1)S(1)} %copy-done.1, bf16[2560,512]{1,0:T(8,128)(2,1)} %collective-permute-done.refs_1_, bf16[512,1024]{1,0:T(8,128)(2,1)S(1)} %copy-done.2, bf16[512,1024]{1,0:T(8,128)(2,1)} %collective-permute-done.1.refs_3_), custom_call_target="tpu_custom_call" | custom-call | flops 1 | bytes 1 | tf_op jit(solution)/shard_map/pallas_call | solution.py:193
  25.6 1.3 %collective-permute-start.5 = (bf16[1280,256]{1,0:T(8,128)(2,1)S(1)}, bf16[1280,256]{1,0:T(8,128)(2,1)S(1)}, u32[]{:S(2)}, u32[]{:S(2)}) collective-permute-start(bf16[1280,256]{1,0:T(8,128)(2,1)S(1)} %get-tuple-element.53), channel_id=1, source_target_pairs={{0,8},{4,12},{8,0},{12,4},{16,24},{20,28},{24,16},{28,20},{1,9},{5... | collective-permute-start | bytes 1966088 | tf_op jit(solution)/shard_map/ppermute | solution.py:21
  26.9 3.9 %shard_map.141 = (f32[1280,256]{1,0:T(8,128)S(1)}, f32[1280,256]{1,0:T(8,128)S(1)}) custom-call(bf16[2560,512]{1,0:T(8,128)(2,1)S(1)} %copy-done.1, bf16[2560,512]{1,0:T(8,128)(2,1)} %collective-permute-done.refs_1_, bf16[512,1024]{1,0:T(8,128)(2,1)S(1)} %copy-done.2, bf16[512,1024]{1,0:T(8,128)(2,1)} %collective-permute-done.1.refs_3_), custom_call_target="tpu_custom_call" | custom-call | flops 1 | bytes 1 | tf_op jit(solution)/shard_map/pallas_call | solution.py:193
  30.9 7.4 %collective-permute-done.4.refs_4_ = bf16[1280,256]{1,0:T(8,128)(2,1)S(1)} collective-permute-done((bf16[1280,256]{1,0:T(8,128)(2,1)S(1)}, bf16[1280,256]{1,0:T(8,128)(2,1)S(1)}, u32[]{:S(2)}, u32[]{:S(2)}) %collective-permute-start.4) | collective-permute-done | bytes 655392 | tf_op jit(solution)/shard_map/ppermute | solution.py:21
  38.3 1.5 %collective-permute-done.3.refs_3_ = bf16[1600,256]{1,0:T(8,128)(2,1)S(1)} collective-permute-done((bf16[1600,256]{1,0:T(8,128)(2,1)S(1)}, bf16[1600,256]{1,0:T(8,128)(2,1)S(1)}, u32[]{:S(2)}, u32[]{:S(2)}) %collective-permute-start.3) | collective-permute-done | bytes 819232 | tf_op jit(solution)/shard_map/ppermute | solution.py:21
  39.8 0.2 shard_map.144
  40.0 2.1 %collective-permute-start.7 = (bf16[800,256]{1,0:T(8,128)(2,1)S(1)}, bf16[800,256]{1,0:T(8,128)(2,1)S(1)}, u32[]{:S(2)}, u32[]{:S(2)}) collective-permute-start(bf16[800,256]{1,0:T(8,128)(2,1)S(1)} %get-tuple-element.59), channel_id=1, source_target_pairs={{0,16},{4,20},{8,24},{12,28},{16,0},{20,4},{24,8},{28,12},{1,17},{... | collective-permute-start | bytes 1228808 | tf_op jit(solution)/shard_map/ppermute | solution.py:21
  42.2 0.8 collective-permute-start.8
  43.0 0.6 broadcast_bitcast_fusion
  43.7 3.9 %shard_map.145 = (f32[1280,256]{1,0:T(8,128)S(1)}, f32[1280,256]{1,0:T(8,128)S(1)}) custom-call(bf16[2560,512]{1,0:T(8,128)(2,1)S(1)} %copy-done.1, bf16[2560,512]{1,0:T(8,128)(2,1)} %collective-permute-done.refs_1_, bf16[512,1024]{1,0:T(8,128)(2,1)S(1)} %copy-done.2, bf16[512,1024]{1,0:T(8,128)(2,1)} %collective-permute-done.1.refs_3_), custom_call_target="tpu_custom_call" | custom-call | flops 1 | bytes 1 | tf_op jit(solution)/shard_map/pallas_call | solution.py:193
  47.6 6.2 %collective-permute-done.5.refs_2_ = bf16[1280,256]{1,0:T(8,128)(2,1)S(1)} collective-permute-done((bf16[1280,256]{1,0:T(8,128)(2,1)S(1)}, bf16[1280,256]{1,0:T(8,128)(2,1)S(1)}, u32[]{:S(2)}, u32[]{:S(2)}) %collective-permute-start.5) | collective-permute-done | bytes 655392 | tf_op jit(solution)/shard_map/ppermute | solution.py:21
  53.8 0.3 shard_map.147
  54.2 2.0 %collective-permute-start.10 = (bf16[640,256]{1,0:T(8,128)(2,1)S(1)}, bf16[640,256]{1,0:T(8,128)(2,1)S(1)}, u32[]{:S(2)}, u32[]{:S(2)}) collective-permute-start(bf16[640,256]{1,0:T(8,128)(2,1)S(1)} %get-tuple-element.65), channel_id=1, source_target_pairs={{0,8},{4,12},{8,0},{12,4},{16,24},{20,28},{24,16},{28,20},{1,9},{5... | collective-permute-start | bytes 983048 | tf_op jit(solution)/shard_map/ppermute | solution.py:21
  56.2 0.9 collective-permute-start.9
  57.1 3.8 %collective-permute-done.8.refs_4_ = bf16[640,256]{1,0:T(8,128)(2,1)S(1)} collective-permute-done((bf16[640,256]{1,0:T(8,128)(2,1)S(1)}, bf16[640,256]{1,0:T(8,128)(2,1)S(1)}, u32[]{:S(2)}, u32[]{:S(2)}) %collective-permute-start.8) | collective-permute-done | bytes 327712 | tf_op jit(solution)/shard_map/ppermute | solution.py:21
  60.9 0.2 collective-permute-done.7.refs_3_
  61.2 2.1 %collective-permute-start.11 = (bf16[720,256]{1,0:T(8,128)(2,1)S(1)}, bf16[720,256]{1,0:T(8,128)(2,1)S(1)}, u32[]{:S(2)}, u32[]{:S(2)}) collective-permute-start(bf16[720,256]{1,0:T(8,128)(2,1)S(1)} %get-tuple-element.70), channel_id=1, source_target_pairs={{0,1},{1,0},{2,3},{3,2},{4,5},{5,4},{6,7},{7,6},{8,9},{9,8},{10,11... | collective-permute-start | bytes 1105928 | tf_op jit(solution)/shard_map/ppermute | solution.py:21
  63.6 0.7 fusion.27
  64.6 3.1 %collective-permute-done.10.refs_3_ = bf16[640,256]{1,0:T(8,128)(2,1)S(1)} collective-permute-done((bf16[640,256]{1,0:T(8,128)(2,1)S(1)}, bf16[640,256]{1,0:T(8,128)(2,1)S(1)}, u32[]{:S(2)}, u32[]{:S(2)}) %collective-permute-start.10) | collective-permute-done | bytes 327712 | tf_op jit(solution)/shard_map/ppermute | solution.py:21
  67.8 1.1 %fusion = f32[8,2,8,128]{3,2,1,0:T(8,128)} fusion(f32[8,2,8,512]{3,2,1,0:T(8,128)S(1)} %get-tuple-element.106, f32[8,2,8]{2,1,0:T(2,128)S(1)} %get-tuple-element.104, f32[8,2,8]{2,1,0:T(2,128)S(1)} %multiply_maximum_fusion, bf16[8,512,256]{2,1,0:T(8,128)(2,1)S(1)} %copy-done.8), kind=kOutput, calls=%fused_computation | convolution fusion | flops 16973824 | bytes 2425856 | tf_op jit(solution)/shard_map/rkgc,rckd->rkgd/dot_general | solution.py:698
  68.9 1.8 %collective-permute-start.13 = (bf16[640,256]{1,0:T(8,128)(2,1)S(1)}, bf16[640,256]{1,0:T(8,128)(2,1)S(1)}, u32[]{:S(2)}, u32[]{:S(2)}) collective-permute-start(bf16[640,256]{1,0:T(8,128)(2,1)S(1)} %get-tuple-element.77), channel_id=1, source_target_pairs={{0,1},{1,0},{2,3},{3,2},{4,5},{5,4},{6,7},{7,6},{8,9},{9,8},{10,11... | collective-permute-start | bytes 983048 | tf_op jit(solution)/shard_map/ppermute | solution.py:21
  70.7 0.5 collective-permute-done.11.refs_3_
  71.2 0.6 shard_map.150
  71.9 2.7 %collective-permute-start.12 = (bf16[400,256]{1,0:T(8,128)(2,1)S(1)}, bf16[400,256]{1,0:T(8,128)(2,1)S(1)}, u32[]{:S(2)}, u32[]{:S(2)}) collective-permute-start(bf16[400,256]{1,0:T(8,128)(2,1)S(1)} %get-tuple-element.72), channel_id=1, source_target_pairs={{0,2},{1,3},{2,0},{3,1},{4,6},{5,7},{6,4},{7,5},{8,10},{9,11},{10,... | collective-permute-start | bytes 614408 | tf_op jit(solution)/shard_map/ppermute | solution.py:21
  74.6 7.1 %collective-permute-done.12 = bf16[400,256]{1,0:T(8,128)(2,1)S(1)} collective-permute-done((bf16[400,256]{1,0:T(8,128)(2,1)S(1)}, bf16[400,256]{1,0:T(8,128)(2,1)S(1)}, u32[]{:S(2)}, u32[]{:S(2)}) %collective-permute-start.12) | collective-permute-done | bytes 204832 | tf_op jit(solution)/shard_map/ppermute | solution.py:21
  81.7 0.7 copy-done.4
  82.4 0.4 collective-permute-done.13.refs_2_
  82.8 0.7 shard_map.151
  83.5 3.0 %collective-permute-start.14 = (bf16[320,256]{1,0:T(8,128)(2,1)}, bf16[320,256]{1,0:T(8,128)(2,1)}, u32[]{:S(2)}, u32[]{:S(2)}) collective-permute-start(bf16[320,256]{1,0:T(8,128)(2,1)} %get-tuple-element.79), channel_id=1, source_target_pairs={{0,2},{1,3},{2,0},{3,1},{4,6},{5,7},{6,4},{7,5},{8,10},{9,11},{10,... | collective-permute-start | bytes 491528 | tf_op jit(solution)/shard_map/ppermute | solution.py:21
  86.5 1.0 fusion.26
  87.5 0.5 shard_map.152
  88.1 0.7 convert_element_type.65
  88.7 5.0 %all-to-all-start = ((bf16[32,8,256]{2,1,0:T(8,128)(2,1)}), bf16[32,8,256]{2,1,0:T(8,128)(2,1)S(1)}, u32[]{:S(2)}, u32[]{:S(2)}) async-start(bf16[32,8,256]{2,1,0:T(8,128)(2,1)} %convert_element_type.65), calls=%async_computation | async-start | bytes 262144 | tf_op jit(solution)/shard_map/all_to_all | solution.py:658
  93.8 1.1 %multiply_subtract_fusion.3 = (f32[160,256]{1,0:T(8,128)S(1)}, f32[160,256]{1,0:T(8,128)S(1)}, f32[160,256]{1,0:T(8,128)S(1)}, f32[160,256]{1,0:T(8,128)S(1)}) fusion(f32[160,256]{1,0:T(8,128)S(1)} %get-tuple-element.71.refs_2_, f32[160,1024]{1,0:T(8,128)S(1)} %copy-done.3, bf16[400,256]{1,0:T(8,128)(2,1)} %copy-done.4, ...), kind=kLoop, calls=%fused_computation.17 | loop fusion | flops 655360 | bytes 2293760 | tf_op jit(solution)/shard_map/sub | solution.py:667
  94.9 0.9 pad_maximum_fusion
  95.8 6.3 %all-to-all-done = bf16[32,8,256]{2,1,0:T(8,128)(2,1)S(1)} async-done(((bf16[32,8,256]{2,1,0:T(8,128)(2,1)}), bf16[32,8,256]{2,1,0:T(8,128)(2,1)S(1)}, u32[]{:S(2)}, u32[]{:S(2)}) %all-to-all-start) | async-done | bytes 131104 | tf_op jit(solution)/shard_map/all_to_all | solution.py:658
  102.2 1.3 %bitcast_convert_fusion = (f32[8,2,128]{2,0,1:T(8,128)S(1)}, bf16[8,256]{1,0:T(8,128)(2,1)}) fusion(bf16[8,256]{1,0:T(8,128)(2,1)S(1)} %copy-done.6, f32[256]{0:T(256)S(1)} %bitcast_subtract_fusion, f32[8,256]{1,0:T(8,128)S(1)} %convert_reduce_fusion, f32[256]{0:T(256)} %broadcast_bitcast_fusion), kind=kLoop, calls=%fused_computation.33 | loop fusion | flops 12288 | bytes 26624 | tf_op jit(solution)/shard_map/convert_element_type | solution.py:701
  103.5 0.9 fusion.15
  104.4 0.6 copy.47
  (50 shorter events, 1.1 us)
Async XLA Ops:
  0.6 62.9 %copy-start = (bf16[8,512,256]{2,1,0:T(8,128)(2,1)S(1)}, bf16[8,512,256]{2,1,0:T(8,128)(2,1)}, u32[]{:S(2)}) copy-start(bf16[8,512,256]{2,1,0:T(8,128)(2,1)} %param.18) | copy-start | bytes 6291460
  0.6 3.7 %copy-start.2 = (bf16[512,1024]{1,0:T(8,128)(2,1)S(1)}, bf16[512,1024]{1,0:T(8,128)(2,1)}, u32[]{:S(2)}) copy-start(bf16[512,1024]{1,0:T(8,128)(2,1)} %refs_2_.7) | copy-start | bytes 3145732
  0.7 3.8 %copy-start.10 = (s32[64]{0:T(128)S(1)}, s32[64]{0:T(128)}, u32[]{:S(2)}) copy-start(s32[64]{0:T(128)} %param.16) | copy-start | bytes 772
  3.9 8.7 %collective-permute-start = (bf16[2560,512]{1,0:T(8,128)(2,1)}, bf16[2560,512]{1,0:T(8,128)(2,1)}, u32[]{:S(2)}, u32[]{:S(2)}) collective-permute-start(bf16[2560,512]{1,0:T(8,128)(2,1)} %shard_map.140), channel_id=1, source_target_pairs={{0,4},{4,0},{8,12},{12,8},{16,20},{20,16},{24,28},{28,24},{1,5},{5... | collective-permute-start | bytes 7864328 | tf_op jit(solution)/shard_map/ppermute | solution.py:21
  4.4 8.2 %collective-permute-start.1 = (bf16[512,1024]{1,0:T(8,128)(2,1)S(1)}, bf16[512,1024]{1,0:T(8,128)(2,1)}, u32[]{:S(2)}, u32[]{:S(2)}) collective-permute-start(bf16[512,1024]{1,0:T(8,128)(2,1)S(1)} %copy-done.2), channel_id=1, source_target_pairs={{0,4},{4,0},{8,12},{12,8},{16,20},{20,16},{24,28},{28,24},{1,5},{5... | collective-permute-start | bytes 3145736 | tf_op jit(solution)/shard_map/ppermute | solution.py:21
  8.9 3.7 %collective-permute-start.2 = (bf16[640,256]{1,0:T(8,128)(2,1)S(1)}, bf16[640,256]{1,0:T(8,128)(2,1)S(1)}, u32[]{:S(2)}, u32[]{:S(2)}) collective-permute-start(bf16[640,256]{1,0:T(8,128)(2,1)S(1)} %get-tuple-element.46), channel_id=1, source_target_pairs={{0,4},{4,0},{8,12},{12,8},{16,20},{20,16},{24,28},{28,24},{1,5},{5... | collective-permute-start | bytes 983048 | tf_op jit(solution)/shard_map/ppermute | solution.py:21
  12.6 1.7 %copy-start.1 = (bf16[2560,512]{1,0:T(8,128)(2,1)S(1)}, bf16[2560,512]{1,0:T(8,128)(2,1)}, u32[]{:S(2)}) copy-start(bf16[2560,512]{1,0:T(8,128)(2,1)} %shard_map.139.refs_0_) | copy-start | bytes 7864324
  18.3 21.5 %collective-permute-start.3 = (bf16[1600,256]{1,0:T(8,128)(2,1)S(1)}, bf16[1600,256]{1,0:T(8,128)(2,1)S(1)}, u32[]{:S(2)}, u32[]{:S(2)}) collective-permute-start(bf16[1600,256]{1,0:T(8,128)(2,1)S(1)} %get-tuple-element.48), channel_id=1, source_target_pairs={{0,8},{4,12},{8,0},{12,4},{16,24},{20,28},{24,16},{28,20},{1,9},{5... | collective-permute-start | bytes 2457608 | tf_op jit(solution)/shard_map/ppermute | solution.py:21
  20.7 17.6 %collective-permute-start.4 = (bf16[1280,256]{1,0:T(8,128)(2,1)S(1)}, bf16[1280,256]{1,0:T(8,128)(2,1)S(1)}, u32[]{:S(2)}, u32[]{:S(2)}) collective-permute-start(bf16[1280,256]{1,0:T(8,128)(2,1)S(1)} %get-tuple-element.49), channel_id=1, source_target_pairs={{0,16},{4,20},{8,24},{12,28},{16,0},{20,4},{24,8},{28,12},{1,17},{... | collective-permute-start | bytes 1966088 | tf_op jit(solution)/shard_map/ppermute | solution.py:21
  25.6 28.3 %collective-permute-start.5 = (bf16[1280,256]{1,0:T(8,128)(2,1)S(1)}, bf16[1280,256]{1,0:T(8,128)(2,1)S(1)}, u32[]{:S(2)}, u32[]{:S(2)}) collective-permute-start(bf16[1280,256]{1,0:T(8,128)(2,1)S(1)} %get-tuple-element.53), channel_id=1, source_target_pairs={{0,8},{4,12},{8,0},{12,4},{16,24},{20,28},{24,16},{28,20},{1,9},{5... | collective-permute-start | bytes 1966088 | tf_op jit(solution)/shard_map/ppermute | solution.py:21
  26.9 27.0 %collective-permute-start.6 = (bf16[1280,256]{1,0:T(8,128)(2,1)S(1)}, bf16[1280,256]{1,0:T(8,128)(2,1)S(1)}, u32[]{:S(2)}, u32[]{:S(2)}) collective-permute-start(bf16[1280,256]{1,0:T(8,128)(2,1)S(1)} %get-tuple-element.54), channel_id=1, source_target_pairs={{0,16},{4,20},{8,24},{12,28},{16,0},{20,4},{24,8},{28,12},{1,17},{... | collective-permute-start | bytes 1966088 | tf_op jit(solution)/shard_map/ppermute | solution.py:21
  39.8 3.2 %copy-start.11 = (f32[2]{0:T(128)S(1)}, f32[2]{0:T(128)}, u32[]{:S(2)}) copy-start(f32[2]{0:T(128)} %param.22) | copy-start | bytes 28
  40.0 21.1 %collective-permute-start.7 = (bf16[800,256]{1,0:T(8,128)(2,1)S(1)}, bf16[800,256]{1,0:T(8,128)(2,1)S(1)}, u32[]{:S(2)}, u32[]{:S(2)}) collective-permute-start(bf16[800,256]{1,0:T(8,128)(2,1)S(1)} %get-tuple-element.59), channel_id=1, source_target_pairs={{0,16},{4,20},{8,24},{12,28},{16,0},{20,4},{24,8},{28,12},{1,17},{... | collective-permute-start | bytes 1228808 | tf_op jit(solution)/shard_map/ppermute | solution.py:21
  42.2 18.7 %collective-permute-start.8 = (bf16[640,256]{1,0:T(8,128)(2,1)S(1)}, bf16[640,256]{1,0:T(8,128)(2,1)S(1)}, u32[]{:S(2)}, u32[]{:S(2)}) collective-permute-start(bf16[640,256]{1,0:T(8,128)(2,1)S(1)} %get-tuple-element.60), channel_id=1, source_target_pairs={{0,8},{4,12},{8,0},{12,4},{16,24},{20,28},{24,16},{28,20},{1,9},{5... | collective-permute-start | bytes 983048 | tf_op jit(solution)/shard_map/ppermute | solution.py:21
  54.1 9.2 %copy-start.7 = (s32[8]{0:T(128)S(1)}, s32[8]{0:T(128)}, u32[]{:S(2)}) copy-start(s32[8]{0:T(128)} %param.23) | copy-start | bytes 100
  54.1 9.3 %copy-start.5 = (bf16[8,2048]{1,0:T(8,128)(2,1)S(1)}, bf16[8,2048]{1,0:T(8,128)(2,1)}, u32[]{:S(2)}) copy-start(bf16[8,2048]{1,0:T(8,128)(2,1)} %param.17) | copy-start | bytes 98308
  54.2 9.3 %copy-start.9 = (bf16[8,256]{1,0:T(8,128)(2,1)S(1)}, bf16[8,256]{1,0:T(8,128)(2,1)}, u32[]{:S(2)}) copy-start(bf16[8,256]{1,0:T(8,128)(2,1)} %param.20) | copy-start | bytes 12292
  54.2 13.5 %collective-permute-start.10 = (bf16[640,256]{1,0:T(8,128)(2,1)S(1)}, bf16[640,256]{1,0:T(8,128)(2,1)S(1)}, u32[]{:S(2)}, u32[]{:S(2)}) collective-permute-start(bf16[640,256]{1,0:T(8,128)(2,1)S(1)} %get-tuple-element.65), channel_id=1, source_target_pairs={{0,8},{4,12},{8,0},{12,4},{16,24},{20,28},{24,16},{28,20},{1,9},{5... | collective-permute-start | bytes 983048 | tf_op jit(solution)/shard_map/ppermute | solution.py:21
  56.2 11.5 %collective-permute-start.9 = (bf16[640,256]{1,0:T(8,128)(2,1)S(1)}, bf16[640,256]{1,0:T(8,128)(2,1)S(1)}, u32[]{:S(2)}, u32[]{:S(2)}) collective-permute-start(bf16[640,256]{1,0:T(8,128)(2,1)S(1)} %get-tuple-element.64), channel_id=1, source_target_pairs={{0,16},{4,20},{8,24},{12,28},{16,0},{20,4},{24,8},{28,12},{1,17},{... | collective-permute-start | bytes 983048 | tf_op jit(solution)/shard_map/ppermute | solution.py:21
  61.2 10.0 %collective-permute-start.11 = (bf16[720,256]{1,0:T(8,128)(2,1)S(1)}, bf16[720,256]{1,0:T(8,128)(2,1)S(1)}, u32[]{:S(2)}, u32[]{:S(2)}) collective-permute-start(bf16[720,256]{1,0:T(8,128)(2,1)S(1)} %get-tuple-element.70), channel_id=1, source_target_pairs={{0,1},{1,0},{2,3},{3,2},{4,5},{5,4},{6,7},{7,6},{8,9},{9,8},{10,11... | collective-permute-start | bytes 1105928 | tf_op jit(solution)/shard_map/ppermute | solution.py:21
  63.6 4.2 %copy-start.8 = (bf16[8,512,256]{2,1,0:T(8,128)(2,1)S(1)}, bf16[8,512,256]{2,1,0:T(8,128)(2,1)}, u32[]{:S(2)}) copy-start(bf16[8,512,256]{2,1,0:T(8,128)(2,1)} %param.19) | copy-start | bytes 6291460
  68.9 18.6 %copy-start.3 = (f32[160,1024]{1,0:T(8,128)S(1)}, f32[160,1024]{1,0:T(8,128)}, u32[]{:S(2)}) copy-start(f32[160,1024]{1,0:T(8,128)} %refs_1_.1) | copy-start | bytes 1966084
  68.9 13.9 %collective-permute-start.13 = (bf16[640,256]{1,0:T(8,128)(2,1)S(1)}, bf16[640,256]{1,0:T(8,128)(2,1)S(1)}, u32[]{:S(2)}, u32[]{:S(2)}) collective-permute-start(bf16[640,256]{1,0:T(8,128)(2,1)S(1)} %get-tuple-element.77), channel_id=1, source_target_pairs={{0,1},{1,0},{2,3},{3,2},{4,5},{5,4},{6,7},{7,6},{8,9},{9,8},{10,11... | collective-permute-start | bytes 983048 | tf_op jit(solution)/shard_map/ppermute | solution.py:21
  71.9 9.8 %collective-permute-start.12 = (bf16[400,256]{1,0:T(8,128)(2,1)S(1)}, bf16[400,256]{1,0:T(8,128)(2,1)S(1)}, u32[]{:S(2)}, u32[]{:S(2)}) collective-permute-start(bf16[400,256]{1,0:T(8,128)(2,1)S(1)} %get-tuple-element.72), channel_id=1, source_target_pairs={{0,2},{1,3},{2,0},{3,1},{4,6},{5,7},{6,4},{7,5},{8,10},{9,11},{10,... | collective-permute-start | bytes 614408 | tf_op jit(solution)/shard_map/ppermute | solution.py:21
  81.7 0.7 copy-start.4
  83.5 10.2 %collective-permute-start.14 = (bf16[320,256]{1,0:T(8,128)(2,1)}, bf16[320,256]{1,0:T(8,128)(2,1)}, u32[]{:S(2)}, u32[]{:S(2)}) collective-permute-start(bf16[320,256]{1,0:T(8,128)(2,1)} %get-tuple-element.79), channel_id=1, source_target_pairs={{0,2},{1,3},{2,0},{3,1},{4,6},{5,7},{6,4},{7,5},{8,10},{9,11},{10,... | collective-permute-start | bytes 491528 | tf_op jit(solution)/shard_map/ppermute | solution.py:21
  88.7 13.5 %copy-start.6 = (bf16[8,256]{1,0:T(8,128)(2,1)S(1)}, bf16[8,256]{1,0:T(8,128)(2,1)}, u32[]{:S(2)}) copy-start(bf16[8,256]{1,0:T(8,128)(2,1)} %param.21) | copy-start | bytes 12292
  88.7 13.4 %all-to-all-start = ((bf16[32,8,256]{2,1,0:T(8,128)(2,1)}), bf16[32,8,256]{2,1,0:T(8,128)(2,1)S(1)}, u32[]{:S(2)}, u32[]{:S(2)}) async-start(bf16[32,8,256]{2,1,0:T(8,128)(2,1)} %convert_element_type.65), calls=%async_computation | async-start | bytes 262144 | tf_op jit(solution)/shard_map/all_to_all | solution.py:658

commit v12 on v10

--- a/solution.py
+++ b/solution.py
@@ -100,14 +100,13 @@
     return runs
 
 
-def multiply(wanted, rows, blocks, base, staged, tail, *refs):
+def multiply(wanted, rows, blocks, base, tail, *refs):
     count = len(wanted)
     sources = refs[:4]
     if tail:
         appended, refs = refs[4:6], refs[:4] + refs[6:]
     outs = refs[4 : 4 + count]
     left, right, sems = refs[4 + count : 7 + count]
-    stages, given = refs[7 + count : 7 + 2 * count] if staged else outs, []
     tokens = left.shape[1] // 2
     per_block = left.shape[0] // blocks
     units_block = per_block // rows
@@ -143,13 +142,7 @@
                 appended[at].at[pl.ds(tail, tail)], addends.at[at], addend_sems.at[at]
             ).wait()
         low = len(wanted[0][0]) * rows
-        stages[0][low : low + tail, :] = addends[0] + addends[1]
-        span = pl.ds(low, tail)
-        copy = pltpu.make_async_copy(
-            stages[0].at[span], outs[0].at[span], refs[7 + 2 * count].at[blocks, 0]
-        )
-        copy.start()
-        given.append(copy)
+        outs[0][low : low + tail, :] = addends[0] + addends[1]
     for copy in grads:
         copy.wait()
     for block in needed:
@@ -162,19 +155,10 @@
                 product = dot32(
                     left[low * rows : high * rows, :], right[:, first - base : last - base]
                 )
-                stages[at][place : place + (high - low) * rows, :] = product.astype(outs[at].dtype)
-            if staged and here:
-                span = pl.ds(units.index(here[0]) * rows, len(here) * rows)
-                copy = pltpu.make_async_copy(
-                    stages[at].at[span], outs[at].at[span], refs[7 + 2 * count].at[block, at]
-                )
-                copy.start()
-                given.append(copy)
-    for copy in given:
-        copy.wait()
-
-
-def products(lefts, grads, wanted, rows, blocks, staged, appended=None):
+                outs[at][place : place + (high - low) * rows, :] = product.astype(outs[at].dtype)
+
+
+def products(lefts, grads, wanted, rows, blocks, appended=None):
     total, tokens = lefts[0].shape
     base = min(first for _, first, _, _ in wanted)
     columns = max(last for _, _, last, _ in wanted) - base
@@ -204,17 +188,14 @@
         grown = (shapes[0].shape[0] + tail, shapes[0].shape[1])
         shapes[0] = jax.ShapeDtypeStruct(grown, shapes[0].dtype)
     staging = []
-    if staged:
-        staging = [pltpu.VMEM(shape.shape, shape.dtype) for shape in shapes]
-        staging.append(pltpu.SemaphoreType.DMA((blocks + 1, len(shapes))))
     if tail:
         staging.append(pltpu.VMEM((2, tail, shapes[0].shape[1]), shapes[0].dtype))
         staging.append(pltpu.SemaphoreType.DMA((2,)))
     return pl.pallas_call(
-        functools.partial(multiply, wanted, rows, blocks, base, staged, tail),
+        functools.partial(multiply, wanted, rows, blocks, base, tail),
         out_shape=shapes,
         in_specs=[pl.BlockSpec(memory_space=pltpu.HBM)] * (6 if tail else 4),
-        out_specs=[pl.BlockSpec(memory_space=pltpu.HBM if staged else pltpu.VMEM)] * len(shapes),
+        out_specs=[pl.BlockSpec(memory_space=pltpu.VMEM)] * len(shapes),
         scratch_shapes=[
             pltpu.VMEM((total, 2 * tokens), lefts[0].dtype),
             pltpu.VMEM((2 * tokens, columns), grads[0].dtype),
@@ -538,15 +519,15 @@
             units = [places.index(p) for p in chosen]
             kind = jnp.bfloat16 if sent else jnp.float32
             wanted.append((units, *spans[index], kind))
-        return dict(zip(which, products(lefts, grads, wanted, rows, uppers, sent, appended)))
+        return dict(zip(which, products(lefts, grads, wanted, rows, uppers, appended)))
 
     theirs, ours = lookup(embed_table, token_ids, arranged, count_tp, block, eighth)
     asked = [ours, exchange(theirs, "fsdp", 1)]
     pairs = [(r, low) for low in range(2) for r in arranged]
-    going = compute([2, 0, 1], True, asked)
-    got = {index: send(going[index], orders[index][0]) for index in (0, 1, 2)}
-    going |= compute([3, 4], True)
-    got |= {index: send(going[index], orders[index][0]) for index in (3, 4)}
+    going = compute([0, 1], True)
+    got = {index: send(value, orders[index][0]) for index, value in going.items()}
+    going |= compute([2, 3, 4], True, asked)
+    got |= {index: send(going[index], orders[index][0]) for index in (3, 4, 2)}
     values = compute([0, 1, 2], False)
     values |= compute([3, 4], False)
     values = {index: [value] for index, value in values.items()}

time: 103 us -> 99.1 us (0.962)
  Pallas kernels: 33.3 us -> 29.4 us
  waiting for transfers between devices: 28.5 us -> 30.8 us
  starting transfers between devices: 29.7 us -> 28.3 us
  other arithmetic: 6.05 us -> 4.72 us
    pallas_call x4, Pallas kernels: 22.1 us -> 17.4 us  [products(): pl.pallas_call(functools.partial(multiply, wanted, rows, blocks, base, ta...]
    ppermute x19, starting transfers between devices: 26.2 us -> 23.5 us  [exchange(): lax.ppermute(value, axis, [(i, i ^ mask) for i in range(lax.axis_size(axi...]
    ppermute x19, waiting for transfers between devices: 22.1 us -> 24.4 us  [exchange(): lax.ppermute(value, axis, [(i, i ^ mask) for i in range(lax.axis_size(axi...]
    unnamed x5, other arithmetic: 3.67 us -> 2.33 us
    all_to_all x1, starting transfers between devices: 3.46 us -> 4.8 us  [per_device(): lax.all_to_all(share_of(sums, values[2][1], done), ('fsdp', 'tp'), split_...]
    unnamed x23 -> x25, local copies, waits for them, and re-layouts: 2.41 us -> 2.42 us
  transfers between devices with their start and end apart: 20 -> 20, of which waited for: 10 -> 10; matrix products, arithmetic and copies ran while one was open for 6% -> 5% of each run, Pallas kernels for 22% -> 27%
where the time goes in v12:
time: 99.1 us; the launch traced here: 98.7 us
  waiting for transfers between devices  30.8 us (31%)
  Pallas kernels  29.4 us (30%)
  starting transfers between devices  28.3 us (29%)
  other arithmetic  4.72 us (5%)
  local copies, waits for them, and re-layouts  2.52 us (3%)
  matrix products  1.95 us (2%)
    ppermute x19, waiting for transfers between devices, exchange(): lax.ppermute(value, axis, [(i, i ^ mask) for i in range(lax.axis_size(axi...  24.4 us
    ppermute x19, starting transfers between devices, exchange(): lax.ppermute(value, axis, [(i, i ^ mask) for i in range(lax.axis_size(axi...  23.5 us
    pallas_call x4, Pallas kernels, products(): pl.pallas_call(functools.partial(multiply, wanted, rows, blocks, base, ta...  17.4 us
    all_to_all x1, waiting for transfers between devices, per_device(): lax.all_to_all(share_of(sums, values[2][1], done), ('fsdp', 'tp'), split_...  6.39 us
    pallas_call x2, Pallas kernels, pack(): pl.pallas_call(functools.partial(transpose_blocks, arranged, mine, units)...  6.27 us
    all_to_all x1, starting transfers between devices, per_device(): lax.all_to_all(share_of(sums, values[2][1], done), ('fsdp', 'tp'), split_...  4.8 us
    pallas_call x1, Pallas kernels, lookup(): pl.pallas_call(functools.partial(pick_rows, arranged, units), grid=(1,),...  4.39 us
    unnamed x25, local copies, waits for them, and re-layouts  2.42 us
  transfers between devices with their start and end apart: 20, of which 10 were waited for; matrix products, arithmetic and copies ran while one was open for 5% of the time, Pallas kernels for 27%

profile of v12, /device:TPU:0, one launch (start us, length us, event | category | flops | bytes accessed | tf_op | source)
XLA Modules:
  0.0 98.7 jit_solution(8044026815009387003)
XLA Ops:
  0.7 3.2 %shard_map.140 = bf16[2560,512]{1,0:T(8,128)(2,1)} custom-call(bf16[512,5120]{1,0:T(8,128)(2,1)} %source.3), custom_call_target="tpu_custom_call" | custom-call | bytes 5242880 | tf_op jit(solution)/shard_map/pallas_call | solution.py:75
  3.9 0.5 collective-permute-start
  4.5 4.4 %shard_map.144 = (bf16[640,256]{1,0:T(8,128)(2,1)S(1)}, bf16[640,256]{1,0:T(8,128)(2,1)S(1)}) custom-call(s32[64]{0:T(128)S(1)} %and_select_fusion.place, bf16[4748,5120]{1,0:T(8,128)(2,1)} %tail.1, bf16[4748,5120]{1,0:T(8,128)(2,1)} %tail.1), custom_call_target="tpu_custom_call" | custom-call | flops 1 | bytes 1 | tf_op jit(solution)/shard_map/pallas_call | solution.py:424
  8.9 0.4 collective-permute-start.4
  9.3 3.1 %shard_map.139.refs_0_ = bf16[2560,512]{1,0:T(8,128)(2,1)} custom-call(bf16[512,5120]{1,0:T(8,128)(2,1)} %source.3), custom_call_target="tpu_custom_call" | custom-call | bytes 5242880 | tf_op jit(solution)/shard_map/pallas_call | solution.py:75
  12.4 1.7 %copy-done.1 = bf16[2560,512]{1,0:T(8,128)(2,1)S(1)} copy-done((bf16[2560,512]{1,0:T(8,128)(2,1)S(1)}, bf16[2560,512]{1,0:T(8,128)(2,1)}, u32[]{:S(2)}) %copy-start.1) | copy-done | bytes 2621464
  14.1 3.9 %shard_map.142 = (bf16[1280,256]{1,0:T(8,128)(2,1)S(1)}, bf16[1280,256]{1,0:T(8,128)(2,1)S(1)}) custom-call(bf16[2560,512]{1,0:T(8,128)(2,1)S(1)} %copy-done.1, bf16[2560,512]{1,0:T(8,128)(2,1)} %collective-permute-done.refs_1_, bf16[512,1024]{1,0:T(8,128)(2,1)S(1)} %copy-done.2, bf16[512,1024]{1,0:T(8,128)(2,1)} %collective-permute-done.1.refs_3_), custom_call_target="tpu_custom_call" | custom-call | flops 1 | bytes 1 | tf_op jit(solution)/shard_map/pallas_call | solution.py:194
  18.1 2.7 %collective-permute-start.2 = (bf16[1280,256]{1,0:T(8,128)(2,1)S(1)}, bf16[1280,256]{1,0:T(8,128)(2,1)S(1)}, u32[]{:S(2)}, u32[]{:S(2)}) collective-permute-start(bf16[1280,256]{1,0:T(8,128)(2,1)S(1)} %get-tuple-element.58), channel_id=1, source_target_pairs={{0,8},{4,12},{8,0},{12,4},{16,24},{20,28},{24,16},{28,20},{1,9},{5... | collective-permute-start | bytes 1966088 | tf_op jit(solution)/shard_map/ppermute | solution.py:21
  20.8 1.5 %collective-permute-start.3 = (bf16[1280,256]{1,0:T(8,128)(2,1)S(1)}, bf16[1280,256]{1,0:T(8,128)(2,1)S(1)}, u32[]{:S(2)}, u32[]{:S(2)}) collective-permute-start(bf16[1280,256]{1,0:T(8,128)(2,1)S(1)} %get-tuple-element.59), channel_id=1, source_target_pairs={{0,16},{4,20},{8,24},{12,28},{16,0},{20,4},{24,8},{28,12},{1,17},{... | collective-permute-start | bytes 1966088 | tf_op jit(solution)/shard_map/ppermute | solution.py:21
  22.2 4.8 %shard_map.145 = (bf16[1600,256]{1,0:T(8,128)(2,1)S(1)}, bf16[1280,128]{1,0:T(8,128)(2,1)S(1)}, bf16[1280,128]{1,0:T(8,128)(2,1)S(1)}) custom-call(bf16[2560,512]{1,0:T(8,128)(2,1)S(1)} %copy-done.1, bf16[2560,512]{1,0:T(8,128)(2,1)} %collective-permute-done.refs_1_, bf16[512,1024]{1,0:T(8,128)(2,1)S(1)} %copy-done.2, ...), custom_call_target="tpu_custom_call" | custom-call | flops 1 | bytes 1 | tf_op jit(solution)/shard_map/pallas_call | solution.py:194
  27.1 1.8 %collective-permute-start.5 = (bf16[1600,256]{1,0:T(8,128)(2,1)S(1)}, bf16[1600,256]{1,0:T(8,128)(2,1)S(1)}, u32[]{:S(2)}, u32[]{:S(2)}) collective-permute-start(bf16[1600,256]{1,0:T(8,128)(2,1)S(1)} %get-tuple-element.64), channel_id=1, source_target_pairs={{0,1},{1,0},{2,3},{3,2},{4,5},{5,4},{6,7},{7,6},{8,9},{9,8},{10,11... | collective-permute-start | bytes 2457608 | tf_op jit(solution)/shard_map/ppermute | solution.py:21
  28.9 0.6 collective-permute-start.6
  29.5 0.4 collective-permute-start.7
  29.9 4.9 %shard_map.141 = (f32[1280,256]{1,0:T(8,128)S(1)}, f32[1280,256]{1,0:T(8,128)S(1)}, f32[1280,256]{1,0:T(8,128)S(1)}) custom-call(bf16[2560,512]{1,0:T(8,128)(2,1)S(1)} %copy-done.1, bf16[2560,512]{1,0:T(8,128)(2,1)} %collective-permute-done.refs_1_, bf16[512,1024]{1,0:T(8,128)(2,1)S(1)} %copy-done.2, bf16[512,1024]{1,0:T(8,128)(2,1)} %collective-permute-done.1.refs_3_), custom_call_target="tpu_custom_call" | custom-call | flops 1 | bytes 1 | tf_op jit(solution)/shard_map/pallas_call | solution.py:194
  34.8 1.5 %collective-permute-done.2.refs_2_ = bf16[1280,256]{1,0:T(8,128)(2,1)S(1)} collective-permute-done((bf16[1280,256]{1,0:T(8,128)(2,1)S(1)}, bf16[1280,256]{1,0:T(8,128)(2,1)S(1)}, u32[]{:S(2)}, u32[]{:S(2)}) %collective-permute-start.2) | collective-permute-done | bytes 655392 | tf_op jit(solution)/shard_map/ppermute | solution.py:21
  36.4 2.0 %collective-permute-done.3.refs_3_ = bf16[1280,256]{1,0:T(8,128)(2,1)S(1)} collective-permute-done((bf16[1280,256]{1,0:T(8,128)(2,1)S(1)}, bf16[1280,256]{1,0:T(8,128)(2,1)S(1)}, u32[]{:S(2)}, u32[]{:S(2)}) %collective-permute-start.3) | collective-permute-done | bytes 655392 | tf_op jit(solution)/shard_map/ppermute | solution.py:21
  38.4 0.2 shard_map.143
  38.6 1.6 %collective-permute-start.8 = (bf16[640,256]{1,0:T(8,128)(2,1)S(1)}, bf16[640,256]{1,0:T(8,128)(2,1)S(1)}, u32[]{:S(2)}, u32[]{:S(2)}) collective-permute-start(bf16[640,256]{1,0:T(8,128)(2,1)S(1)} %get-tuple-element.73), channel_id=1, source_target_pairs={{0,16},{4,20},{8,24},{12,28},{16,0},{20,4},{24,8},{28,12},{1,17},{... | collective-permute-start | bytes 983048 | tf_op jit(solution)/shard_map/ppermute | solution.py:21
  40.1 0.4 collective-permute-start.9
  40.7 3.8 %shard_map.147 = (f32[1280,128]{1,0:T(8,128)S(1)}, f32[1280,128]{1,0:T(8,128)S(1)}) custom-call(bf16[2560,512]{1,0:T(8,128)(2,1)S(1)} %copy-done.1, bf16[2560,512]{1,0:T(8,128)(2,1)} %collective-permute-done.refs_1_, bf16[512,1024]{1,0:T(8,128)(2,1)S(1)} %copy-done.2, bf16[512,1024]{1,0:T(8,128)(2,1)} %collective-permute-done.1.refs_3_), custom_call_target="tpu_custom_call" | custom-call | flops 1 | bytes 1 | tf_op jit(solution)/shard_map/pallas_call | solution.py:194
  44.5 2.6 %collective-permute-done.5.refs_2_ = bf16[1600,256]{1,0:T(8,128)(2,1)S(1)} collective-permute-done((bf16[1600,256]{1,0:T(8,128)(2,1)S(1)}, bf16[1600,256]{1,0:T(8,128)(2,1)S(1)}, u32[]{:S(2)}, u32[]{:S(2)}) %collective-permute-start.5) | collective-permute-done | bytes 819232 | tf_op jit(solution)/shard_map/ppermute | solution.py:21
  47.3 0.6 collective-permute-start.10
  48.0 0.5 collective-permute-start.13
  48.5 1.7 %collective-permute-start.14 = (bf16[640,128]{1,0:T(8,128)(2,1)S(1)}, bf16[640,128]{1,0:T(8,128)(2,1)S(1)}, u32[]{:S(2)}, u32[]{:S(2)}) collective-permute-start(bf16[640,128]{1,0:T(8,128)(2,1)S(1)} %get-tuple-element.90), channel_id=1, source_target_pairs={{0,8},{4,12},{8,0},{12,4},{16,24},{20,28},{24,16},{28,20},{1,9},{5... | collective-permute-start | bytes 491528 | tf_op jit(solution)/shard_map/ppermute | solution.py:21
  50.2 2.2 %collective-permute-done.8.refs_2_ = bf16[640,256]{1,0:T(8,128)(2,1)S(1)} collective-permute-done((bf16[640,256]{1,0:T(8,128)(2,1)S(1)}, bf16[640,256]{1,0:T(8,128)(2,1)S(1)}, u32[]{:S(2)}, u32[]{:S(2)}) %collective-permute-start.8) | collective-permute-done | bytes 327712 | tf_op jit(solution)/shard_map/ppermute | solution.py:21
  52.5 1.7 %collective-permute-start.11 = (bf16[640,256]{1,0:T(8,128)(2,1)S(1)}, bf16[640,256]{1,0:T(8,128)(2,1)S(1)}, u32[]{:S(2)}, u32[]{:S(2)}) collective-permute-start(bf16[640,256]{1,0:T(8,128)(2,1)S(1)} %get-tuple-element.82), channel_id=1, source_target_pairs={{0,1},{1,0},{2,3},{3,2},{4,5},{5,4},{6,7},{7,6},{8,9},{9,8},{10,11... | collective-permute-start | bytes 983048 | tf_op jit(solution)/shard_map/ppermute | solution.py:21
  54.5 0.7 fusion.25
  55.5 1.1 %fusion = f32[8,2,8,128]{3,2,1,0:T(8,128)} fusion(f32[8,2,8,512]{3,2,1,0:T(8,128)S(1)} %get-tuple-element.120, f32[8,2,8]{2,1,0:T(2,128)S(1)} %get-tuple-element.118, f32[8,2,8]{2,1,0:T(2,128)S(1)} %multiply_maximum_fusion, bf16[8,512,256]{2,1,0:T(8,128)(2,1)S(1)} %copy-done.8), kind=kOutput, calls=%fused_computation | convolution fusion | flops 16973824 | bytes 2425856 | tf_op jit(solution)/shard_map/rkgc,rckd->rkgd/dot_general | solution.py:702
  56.5 3.2 %collective-permute-done.10.refs_2_ = bf16[800,256]{1,0:T(8,128)(2,1)S(1)} collective-permute-done((bf16[800,256]{1,0:T(8,128)(2,1)S(1)}, bf16[800,256]{1,0:T(8,128)(2,1)S(1)}, u32[]{:S(2)}, u32[]{:S(2)}) %collective-permute-start.10) | collective-permute-done | bytes 409632 | tf_op jit(solution)/shard_map/ppermute | solution.py:21
  59.9 1.3 %collective-permute-start.15 = (bf16[400,256]{1,0:T(8,128)(2,1)S(1)}, bf16[400,256]{1,0:T(8,128)(2,1)S(1)}, u32[]{:S(2)}, u32[]{:S(2)}) collective-permute-start(bf16[400,256]{1,0:T(8,128)(2,1)S(1)} %get-tuple-element.94), channel_id=1, source_target_pairs={{0,16},{4,20},{8,24},{12,28},{16,0},{20,4},{24,8},{28,12},{1,17},{... | collective-permute-start | bytes 614408 | tf_op jit(solution)/shard_map/ppermute | solution.py:21
  61.3 1.2 %collective-permute-done.14.refs_3_ = bf16[640,128]{1,0:T(8,128)(2,1)S(1)} collective-permute-done((bf16[640,128]{1,0:T(8,128)(2,1)S(1)}, bf16[640,128]{1,0:T(8,128)(2,1)S(1)}, u32[]{:S(2)}, u32[]{:S(2)}) %collective-permute-start.14) | collective-permute-done | bytes 163872 | tf_op jit(solution)/shard_map/ppermute | solution.py:21
  62.5 1.7 %collective-permute-start.17 = (bf16[640,128]{1,0:T(8,128)(2,1)S(1)}, bf16[640,128]{1,0:T(8,128)(2,1)S(1)}, u32[]{:S(2)}, u32[]{:S(2)}) collective-permute-start(bf16[640,128]{1,0:T(8,128)(2,1)S(1)} %get-tuple-element.100), channel_id=1, source_target_pairs={{0,1},{1,0},{2,3},{3,2},{4,5},{5,4},{6,7},{7,6},{8,9},{9,8},{10,11... | collective-permute-start | bytes 491528 | tf_op jit(solution)/shard_map/ppermute | solution.py:21
  64.3 2.7 %collective-permute-start.12 = (bf16[320,256]{1,0:T(8,128)(2,1)S(1)}, bf16[320,256]{1,0:T(8,128)(2,1)S(1)}, u32[]{:S(2)}, u32[]{:S(2)}) collective-permute-start(bf16[320,256]{1,0:T(8,128)(2,1)S(1)} %get-tuple-element.84), channel_id=1, source_target_pairs={{0,2},{1,3},{2,0},{3,1},{4,6},{5,7},{6,4},{7,5},{8,10},{9,11},{10,... | collective-permute-start | bytes 491528 | tf_op jit(solution)/shard_map/ppermute | solution.py:21
  67.0 1.4 %collective-permute-start.16 = (bf16[240,256]{1,0:T(8,128)(2,1)S(1)}, bf16[240,256]{1,0:T(8,128)(2,1)S(1)}, u32[]{:S(2)}, u32[]{:S(2)}) collective-permute-start(bf16[240,256]{1,0:T(8,128)(2,1)S(1)} %get-tuple-element.96), channel_id=1, source_target_pairs={{0,2},{1,3},{2,0},{3,1},{4,6},{5,7},{6,4},{7,5},{8,10},{9,11},{10,... | collective-permute-start | bytes 368648 | tf_op jit(solution)/shard_map/ppermute | solution.py:21
  68.5 2.2 %collective-permute-done.17.refs_2_ = bf16[640,128]{1,0:T(8,128)(2,1)S(1)} collective-permute-done((bf16[640,128]{1,0:T(8,128)(2,1)S(1)}, bf16[640,128]{1,0:T(8,128)(2,1)S(1)}, u32[]{:S(2)}, u32[]{:S(2)}) %collective-permute-start.17) | collective-permute-done | bytes 163872 | tf_op jit(solution)/shard_map/ppermute | solution.py:21
  70.7 1.8 %collective-permute-start.18 = (bf16[320,128]{1,0:T(8,128)(2,1)S(1)}, bf16[320,128]{1,0:T(8,128)(2,1)S(1)}, u32[]{:S(2)}, u32[]{:S(2)}) collective-permute-start(bf16[320,128]{1,0:T(8,128)(2,1)S(1)} %get-tuple-element.102), channel_id=1, source_target_pairs={{0,2},{1,3},{2,0},{3,1},{4,6},{5,7},{6,4},{7,5},{8,10},{9,11},{10,... | collective-permute-start | bytes 245768 | tf_op jit(solution)/shard_map/ppermute | solution.py:21
  72.6 7.3 %collective-permute-done.12 = bf16[320,256]{1,0:T(8,128)(2,1)S(1)} collective-permute-done((bf16[320,256]{1,0:T(8,128)(2,1)S(1)}, bf16[320,256]{1,0:T(8,128)(2,1)S(1)}, u32[]{:S(2)}, u32[]{:S(2)}) %collective-permute-start.12) | collective-permute-done | bytes 163872 | tf_op jit(solution)/shard_map/ppermute | solution.py:21
  80.0 2.0 %collective-permute-done.16 = bf16[240,256]{1,0:T(8,128)(2,1)S(1)} collective-permute-done((bf16[240,256]{1,0:T(8,128)(2,1)S(1)}, bf16[240,256]{1,0:T(8,128)(2,1)S(1)}, u32[]{:S(2)}, u32[]{:S(2)}) %collective-permute-start.16) | collective-permute-done | bytes 122912 | tf_op jit(solution)/shard_map/ppermute | solution.py:21
  82.0 0.6 shard_map.155
  82.6 0.7 convert_element_type.69
  83.3 4.8 %all-to-all-start = ((bf16[32,8,256]{2,1,0:T(8,128)(2,1)}), bf16[32,8,256]{2,1,0:T(8,128)(2,1)S(1)}, u32[]{:S(2)}, u32[]{:S(2)}) async-start(bf16[32,8,256]{2,1,0:T(8,128)(2,1)} %convert_element_type.69), calls=%async_computation | async-start | bytes 262144 | tf_op jit(solution)/shard_map/all_to_all | solution.py:630
  88.1 0.7 subtract_dynamic-update-slice_fusion
  88.8 0.7 subtract_dynamic-update-slice_fusion.4
  89.5 0.7 subtract_dynamic-update-slice_fusion.3
  90.1 6.4 %all-to-all-done = bf16[32,8,256]{2,1,0:T(8,128)(2,1)S(1)} async-done(((bf16[32,8,256]{2,1,0:T(8,128)(2,1)}), bf16[32,8,256]{2,1,0:T(8,128)(2,1)S(1)}, u32[]{:S(2)}, u32[]{:S(2)}) %all-to-all-start) | async-done | bytes 131104 | tf_op jit(solution)/shard_map/all_to_all | solution.py:630
  96.6 0.6 bitcast_convert_fusion
  97.2 0.9 fusion.15
  98.1 0.6 copy.47
  (61 shorter events, 1.5 us)
Async XLA Ops:
  0.6 53.8 %copy-start = (bf16[8,512,256]{2,1,0:T(8,128)(2,1)S(1)}, bf16[8,512,256]{2,1,0:T(8,128)(2,1)}, u32[]{:S(2)}) copy-start(bf16[8,512,256]{2,1,0:T(8,128)(2,1)} %param.18) | copy-start | bytes 6291460
  0.6 3.8 %copy-start.2 = (bf16[512,1024]{1,0:T(8,128)(2,1)S(1)}, bf16[512,1024]{1,0:T(8,128)(2,1)}, u32[]{:S(2)}) copy-start(bf16[512,1024]{1,0:T(8,128)(2,1)} %refs_2_.7) | copy-start | bytes 3145732
  0.7 3.8 %copy-start.10 = (s32[64]{0:T(128)S(1)}, s32[64]{0:T(128)}, u32[]{:S(2)}) copy-start(s32[64]{0:T(128)} %param.16) | copy-start | bytes 772
  3.9 8.5 %collective-permute-start = (bf16[2560,512]{1,0:T(8,128)(2,1)}, bf16[2560,512]{1,0:T(8,128)(2,1)}, u32[]{:S(2)}, u32[]{:S(2)}) collective-permute-start(bf16[2560,512]{1,0:T(8,128)(2,1)} %shard_map.140), channel_id=1, source_target_pairs={{0,4},{4,0},{8,12},{12,8},{16,20},{20,16},{24,28},{28,24},{1,5},{5... | collective-permute-start | bytes 7864328 | tf_op jit(solution)/shard_map/ppermute | solution.py:21
  4.4 8.0 %collective-permute-start.1 = (bf16[512,1024]{1,0:T(8,128)(2,1)S(1)}, bf16[512,1024]{1,0:T(8,128)(2,1)}, u32[]{:S(2)}, u32[]{:S(2)}) collective-permute-start(bf16[512,1024]{1,0:T(8,128)(2,1)S(1)} %copy-done.2), channel_id=1, source_target_pairs={{0,4},{4,0},{8,12},{12,8},{16,20},{20,16},{24,28},{28,24},{1,5},{5... | collective-permute-start | bytes 3145736 | tf_op jit(solution)/shard_map/ppermute | solution.py:21
  8.9 13.3 %collective-permute-start.4 = (bf16[640,256]{1,0:T(8,128)(2,1)S(1)}, bf16[640,256]{1,0:T(8,128)(2,1)S(1)}, u32[]{:S(2)}, u32[]{:S(2)}) collective-permute-start(bf16[640,256]{1,0:T(8,128)(2,1)S(1)} %get-tuple-element.63), channel_id=1, source_target_pairs={{0,4},{4,0},{8,12},{12,8},{16,20},{20,16},{24,28},{28,24},{1,5},{5... | collective-permute-start | bytes 983048 | tf_op jit(solution)/shard_map/ppermute | solution.py:21
  12.4 1.7 %copy-start.1 = (bf16[2560,512]{1,0:T(8,128)(2,1)S(1)}, bf16[2560,512]{1,0:T(8,128)(2,1)}, u32[]{:S(2)}) copy-start(bf16[2560,512]{1,0:T(8,128)(2,1)} %shard_map.139.refs_0_) | copy-start | bytes 7864324
  18.1 18.3 %collective-permute-start.2 = (bf16[1280,256]{1,0:T(8,128)(2,1)S(1)}, bf16[1280,256]{1,0:T(8,128)(2,1)S(1)}, u32[]{:S(2)}, u32[]{:S(2)}) collective-permute-start(bf16[1280,256]{1,0:T(8,128)(2,1)S(1)} %get-tuple-element.58), channel_id=1, source_target_pairs={{0,8},{4,12},{8,0},{12,4},{16,24},{20,28},{24,16},{28,20},{1,9},{5... | collective-permute-start | bytes 1966088 | tf_op jit(solution)/shard_map/ppermute | solution.py:21
  20.8 17.6 %collective-permute-start.3 = (bf16[1280,256]{1,0:T(8,128)(2,1)S(1)}, bf16[1280,256]{1,0:T(8,128)(2,1)S(1)}, u32[]{:S(2)}, u32[]{:S(2)}) collective-permute-start(bf16[1280,256]{1,0:T(8,128)(2,1)S(1)} %get-tuple-element.59), channel_id=1, source_target_pairs={{0,16},{4,20},{8,24},{12,28},{16,0},{20,4},{24,8},{28,12},{1,17},{... | collective-permute-start | bytes 1966088 | tf_op jit(solution)/shard_map/ppermute | solution.py:21
  22.2 6.6 %copy-start.11 = (f32[2]{0:T(128)S(1)}, f32[2]{0:T(128)}, u32[]{:S(2)}) copy-start(f32[2]{0:T(128)} %param.22) | copy-start | bytes 28
  27.1 20.1 %collective-permute-start.5 = (bf16[1600,256]{1,0:T(8,128)(2,1)S(1)}, bf16[1600,256]{1,0:T(8,128)(2,1)S(1)}, u32[]{:S(2)}, u32[]{:S(2)}) collective-permute-start(bf16[1600,256]{1,0:T(8,128)(2,1)S(1)} %get-tuple-element.64), channel_id=1, source_target_pairs={{0,1},{1,0},{2,3},{3,2},{4,5},{5,4},{6,7},{7,6},{8,9},{9,8},{10,11... | collective-permute-start | bytes 2457608 | tf_op jit(solution)/shard_map/ppermute | solution.py:21
  28.9 19.0 %collective-permute-start.6 = (bf16[1280,128]{1,0:T(8,128)(2,1)S(1)}, bf16[1280,128]{1,0:T(8,128)(2,1)S(1)}, u32[]{:S(2)}, u32[]{:S(2)}) collective-permute-start(bf16[1280,128]{1,0:T(8,128)(2,1)S(1)} %get-tuple-element.68), channel_id=1, source_target_pairs={{0,8},{4,12},{8,0},{12,4},{16,24},{20,28},{24,16},{28,20},{1,9},{5... | collective-permute-start | bytes 983048 | tf_op jit(solution)/shard_map/ppermute | solution.py:21
  29.5 18.4 %collective-permute-start.7 = (bf16[1280,128]{1,0:T(8,128)(2,1)S(1)}, bf16[1280,128]{1,0:T(8,128)(2,1)S(1)}, u32[]{:S(2)}, u32[]{:S(2)}) collective-permute-start(bf16[1280,128]{1,0:T(8,128)(2,1)S(1)} %get-tuple-element.69), channel_id=1, source_target_pairs={{0,16},{4,20},{8,24},{12,28},{16,0},{20,4},{24,8},{28,12},{1,17},{... | collective-permute-start | bytes 983048 | tf_op jit(solution)/shard_map/ppermute | solution.py:21
  38.6 13.8 %collective-permute-start.8 = (bf16[640,256]{1,0:T(8,128)(2,1)S(1)}, bf16[640,256]{1,0:T(8,128)(2,1)S(1)}, u32[]{:S(2)}, u32[]{:S(2)}) collective-permute-start(bf16[640,256]{1,0:T(8,128)(2,1)S(1)} %get-tuple-element.73), channel_id=1, source_target_pairs={{0,16},{4,20},{8,24},{12,28},{16,0},{20,4},{24,8},{28,12},{1,17},{... | collective-permute-start | bytes 983048 | tf_op jit(solution)/shard_map/ppermute | solution.py:21
  40.1 12.3 %collective-permute-start.9 = (bf16[640,256]{1,0:T(8,128)(2,1)S(1)}, bf16[640,256]{1,0:T(8,128)(2,1)S(1)}, u32[]{:S(2)}, u32[]{:S(2)}) collective-permute-start(bf16[640,256]{1,0:T(8,128)(2,1)S(1)} %get-tuple-element.74), channel_id=1, source_target_pairs={{0,8},{4,12},{8,0},{12,4},{16,24},{20,28},{24,16},{28,20},{1,9},{5... | collective-permute-start | bytes 983048 | tf_op jit(solution)/shard_map/ppermute | solution.py:21
  47.3 7.0 %copy-start.7 = (s32[8]{0:T(128)S(1)}, s32[8]{0:T(128)}, u32[]{:S(2)}) copy-start(s32[8]{0:T(128)} %param.23) | copy-start | bytes 100
  47.3 7.0 %copy-start.5 = (bf16[8,2048]{1,0:T(8,128)(2,1)S(1)}, bf16[8,2048]{1,0:T(8,128)(2,1)}, u32[]{:S(2)}) copy-start(bf16[8,2048]{1,0:T(8,128)(2,1)} %param.17) | copy-start | bytes 98308
  47.3 7.0 %copy-start.9 = (bf16[8,256]{1,0:T(8,128)(2,1)S(1)}, bf16[8,256]{1,0:T(8,128)(2,1)}, u32[]{:S(2)}) copy-start(bf16[8,256]{1,0:T(8,128)(2,1)} %param.20) | copy-start | bytes 12292
  47.3 12.5 %collective-permute-start.10 = (bf16[800,256]{1,0:T(8,128)(2,1)S(1)}, bf16[800,256]{1,0:T(8,128)(2,1)S(1)}, u32[]{:S(2)}, u32[]{:S(2)}) collective-permute-start(bf16[800,256]{1,0:T(8,128)(2,1)S(1)} %get-tuple-element.78), channel_id=1, source_target_pairs={{0,8},{4,12},{8,0},{12,4},{16,24},{20,28},{24,16},{28,20},{1,9},{5... | collective-permute-start | bytes 1228808 | tf_op jit(solution)/shard_map/ppermute | solution.py:21
  48.0 13.2 %collective-permute-start.13 = (bf16[640,128]{1,0:T(8,128)(2,1)S(1)}, bf16[640,128]{1,0:T(8,128)(2,1)S(1)}, u32[]{:S(2)}, u32[]{:S(2)}) collective-permute-start(bf16[640,128]{1,0:T(8,128)(2,1)S(1)} %get-tuple-element.89), channel_id=1, source_target_pairs={{0,16},{4,20},{8,24},{12,28},{16,0},{20,4},{24,8},{28,12},{1,17},{... | collective-permute-start | bytes 491528 | tf_op jit(solution)/shard_map/ppermute | solution.py:21
  48.5 14.0 %collective-permute-start.14 = (bf16[640,128]{1,0:T(8,128)(2,1)S(1)}, bf16[640,128]{1,0:T(8,128)(2,1)S(1)}, u32[]{:S(2)}, u32[]{:S(2)}) collective-permute-start(bf16[640,128]{1,0:T(8,128)(2,1)S(1)} %get-tuple-element.90), channel_id=1, source_target_pairs={{0,8},{4,12},{8,0},{12,4},{16,24},{20,28},{24,16},{28,20},{1,9},{5... | collective-permute-start | bytes 491528 | tf_op jit(solution)/shard_map/ppermute | solution.py:21
  52.4 3.1 %copy-start.8 = (bf16[8,512,256]{2,1,0:T(8,128)(2,1)S(1)}, bf16[8,512,256]{2,1,0:T(8,128)(2,1)}, u32[]{:S(2)}) copy-start(bf16[8,512,256]{2,1,0:T(8,128)(2,1)} %param.19) | copy-start | bytes 6291460
  52.5 8.7 %collective-permute-start.11 = (bf16[640,256]{1,0:T(8,128)(2,1)S(1)}, bf16[640,256]{1,0:T(8,128)(2,1)S(1)}, u32[]{:S(2)}, u32[]{:S(2)}) collective-permute-start(bf16[640,256]{1,0:T(8,128)(2,1)S(1)} %get-tuple-element.82), channel_id=1, source_target_pairs={{0,1},{1,0},{2,3},{3,2},{4,5},{5,4},{6,7},{7,6},{8,9},{9,8},{10,11... | collective-permute-start | bytes 983048 | tf_op jit(solution)/shard_map/ppermute | solution.py:21
  59.9 20.1 %copy-start.3 = (f32[160,1024]{1,0:T(8,128)S(1)}, f32[160,1024]{1,0:T(8,128)}, u32[]{:S(2)}) copy-start(f32[160,1024]{1,0:T(8,128)} %refs_1_.1) | copy-start | bytes 1966084
  59.9 7.1 %collective-permute-start.15 = (bf16[400,256]{1,0:T(8,128)(2,1)S(1)}, bf16[400,256]{1,0:T(8,128)(2,1)S(1)}, u32[]{:S(2)}, u32[]{:S(2)}) collective-permute-start(bf16[400,256]{1,0:T(8,128)(2,1)S(1)} %get-tuple-element.94), channel_id=1, source_target_pairs={{0,16},{4,20},{8,24},{12,28},{16,0},{20,4},{24,8},{28,12},{1,17},{... | collective-permute-start | bytes 614408 | tf_op jit(solution)/shard_map/ppermute | solution.py:21
  62.5 8.2 %collective-permute-start.17 = (bf16[640,128]{1,0:T(8,128)(2,1)S(1)}, bf16[640,128]{1,0:T(8,128)(2,1)S(1)}, u32[]{:S(2)}, u32[]{:S(2)}) collective-permute-start(bf16[640,128]{1,0:T(8,128)(2,1)S(1)} %get-tuple-element.100), channel_id=1, source_target_pairs={{0,1},{1,0},{2,3},{3,2},{4,5},{5,4},{6,7},{7,6},{8,9},{9,8},{10,11... | collective-permute-start | bytes 491528 | tf_op jit(solution)/shard_map/ppermute | solution.py:21
  64.3 15.7 %collective-permute-start.12 = (bf16[320,256]{1,0:T(8,128)(2,1)S(1)}, bf16[320,256]{1,0:T(8,128)(2,1)S(1)}, u32[]{:S(2)}, u32[]{:S(2)}) collective-permute-start(bf16[320,256]{1,0:T(8,128)(2,1)S(1)} %get-tuple-element.84), channel_id=1, source_target_pairs={{0,2},{1,3},{2,0},{3,1},{4,6},{5,7},{6,4},{7,5},{8,10},{9,11},{10,... | collective-permute-start | bytes 491528 | tf_op jit(solution)/shard_map/ppermute | solution.py:21
  67.0 15.0 %collective-permute-start.16 = (bf16[240,256]{1,0:T(8,128)(2,1)S(1)}, bf16[240,256]{1,0:T(8,128)(2,1)S(1)}, u32[]{:S(2)}, u32[]{:S(2)}) collective-permute-start(bf16[240,256]{1,0:T(8,128)(2,1)S(1)} %get-tuple-element.96), channel_id=1, source_target_pairs={{0,2},{1,3},{2,0},{3,1},{4,6},{5,7},{6,4},{7,5},{8,10},{9,11},{10,... | collective-permute-start | bytes 368648 | tf_op jit(solution)/shard_map/ppermute | solution.py:21
  70.7 18.1 %collective-permute-start.18 = (bf16[320,128]{1,0:T(8,128)(2,1)S(1)}, bf16[320,128]{1,0:T(8,128)(2,1)S(1)}, u32[]{:S(2)}, u32[]{:S(2)}) collective-permute-start(bf16[320,128]{1,0:T(8,128)(2,1)S(1)} %get-tuple-element.102), channel_id=1, source_target_pairs={{0,2},{1,3},{2,0},{3,1},{4,6},{5,7},{6,4},{7,5},{8,10},{9,11},{10,... | collective-permute-start | bytes 245768 | tf_op jit(solution)/shard_map/ppermute | solution.py:21
  80.0 2.6 %copy-start.4 = (f32[160,1024]{1,0:T(8,128)}, f32[160,1024]{1,0:T(8,128)S(1)}, u32[]{:S(2)}) copy-start(f32[160,1024]{1,0:T(8,128)S(1)} %subtract_dynamic-update-slice_fusion.1) | copy-start | bytes 1966084
  82.0 14.5 %copy-start.6 = (bf16[8,256]{1,0:T(8,128)(2,1)S(1)}, bf16[8,256]{1,0:T(8,128)(2,1)}, u32[]{:S(2)}) copy-start(bf16[8,256]{1,0:T(8,128)(2,1)} %param.21) | copy-start | bytes 12292
  83.3 13.2 %all-to-all-start = ((bf16[32,8,256]{2,1,0:T(8,128)(2,1)}), bf16[32,8,256]{2,1,0:T(8,128)(2,1)S(1)}, u32[]{:S(2)}, u32[]{:S(2)}) async-start(bf16[32,8,256]{2,1,0:T(8,128)(2,1)} %convert_element_type.69), calls=%async_computation | async-start | bytes 262144 | tf_op jit(solution)/shard_map/all_to_all | solution.py:630

commit v13 on v12

--- a/solution.py
+++ b/solution.py
@@ -329,6 +329,26 @@
     return kept, results, totals, done
 
 
+def end_chunk(coef, spans, _, arrived, master, *refs):
+    rows = master.shape[0]
+    for at, (first, last) in enumerate(spans):
+        value, out = refs[at], refs[len(spans) + at]
+        grad = value[...] + arrived[at * rows : (at + 1) * rows, :].astype(jnp.float32)
+        out[...] = master[:, first:last] - coef * grad
+
+
+def finish(coef, spans, values, arrived, master_w, after):
+    return pl.pallas_call(
+        functools.partial(end_chunk, coef, spans),
+        in_specs=[pl.BlockSpec(memory_space=pl.ANY)]
+        + [pl.BlockSpec(memory_space=pltpu.VMEM)] * (2 + len(values)),
+        out_specs=[pl.BlockSpec(memory_space=pltpu.VMEM)] * len(values),
+        out_shape=[jax.ShapeDtypeStruct(value.shape, jnp.float32) for value in values],
+        compiler_params=pltpu.CompilerParams(vmem_limit_bytes=VMEM // 4),
+        cost_estimate=pl.CostEstimate(flops=1, bytes_accessed=1, transcendentals=0),
+    )(after, arrived, master_w, *values)
+
+
 def own_share(coef, spans, plans, rows, tokens, blocks, _, *refs):
     emb, master, out = refs[0], refs[1], refs[-1]
     arrays = refs[2:-1]
@@ -613,11 +633,27 @@
     events = [(group, at) for at in range(steps) for group in groups]
     if steps == 4:
         first, second, third = groups
-        events = [(first, 0), (second, 0), (third, 0), (first, 1), (second, 1), (first, 2)]
-        events += [(third, 1), (second, 2), (third, 2), (second, 3), (first, 3), (third, 3)]
+        events = [(first, 0), (second, 0), (third, 0), (first, 1), (second, 1), (third, 1)]
+        events += [(second, 2), (first, 2), (third, 2), (second, 3), (first, 3), (third, 3)]
+    ended = {}
     done = jnp.zeros(TOKEN, jnp.float32)
     for group, at in events:
         last = at + 1 == steps
+        if last and not plain and group != (2,):
+            ended |= dict(
+                zip(
+                    group,
+                    finish(
+                        coef,
+                        [spans[index] for index in group],
+                        [values[index][0] for index in group],
+                        inbox[group][0],
+                        master_w,
+                        own_blocks,
+                    ),
+                )
+            )
+            continue
         if plain or last:
             if len(inbox[group]) < len(group):
                 whole = inbox[group][0]
@@ -627,11 +663,9 @@
                 receive(index, orders[index][at], arrived)
         if last:
             if group == (2,):
+                own_blocks = share_of(sums, values[2][1], done)
                 parts_own = lax.all_to_all(
-                    share_of(sums, values[2][1], done),
-                    ("fsdp", "tp"),
-                    split_axis=0,
-                    concat_axis=0,
+                    own_blocks, ("fsdp", "tp"), split_axis=0, concat_axis=0
                 )
             continue
         if plain:
@@ -668,7 +702,10 @@
             )
     own_value = jnp.sum(parts_own.astype(jnp.float32), axis=0)
     w_next = jnp.concatenate(
-        [master_w[:, low:high] - coef * values[at][0] for at, (low, high) in enumerate(spans)],
+        [
+            ended[at] if at in ended else master_w[:, low:high] - coef * values[at][0]
+            for at, (low, high) in enumerate(spans)
+        ],
         axis=1,
     )
 

time: 99.1 us -> 97.6 us (0.985)
  waiting for transfers between devices: 30.8 us -> 22.4 us
  local copies, waits for them, and re-layouts: 2.52 us -> 7.56 us
  Pallas kernels: 29.4 us -> 31.9 us
    ppermute x19, waiting for transfers between devices: 24.4 us -> 18.5 us  [exchange(): lax.ppermute(value, axis, [(i, i ^ mask) for i in range(lax.axis_size(axi...]
    all_to_all x1, waiting for transfers between devices: 6.39 us -> 3.96 us  [per_device(): lax.all_to_all(own_blocks, ('fsdp', 'tp'), split_axis=0, concat_axis=0)]
    unnamed x25 -> x36, local copies, waits for them, and re-layouts: 2.42 us -> 4.47 us
    slice x3, local copies, waits for them, and re-layouts: 0.03 us -> 1.8 us  [per_device(): sums[index] = [values[index][0], sent[low:low + rows]]]
    unnamed x5 -> x2, other arithmetic: 2.33 us -> 0.78 us
    pallas_call x9, Pallas kernels: 0.8 us -> 2.08 us  [combine(): pl.pallas_call(functools.partial(add_and_split, plans, len(got), merged),...]
    pallas_call x0 -> x2, Pallas kernels: none -> 1 us  [finish(): pl.pallas_call(functools.partial(end_chunk, coef, spans), in_specs=[pl.Bl...]
  transfers between devices with their start and end apart: 20 -> 20, of which waited for: 10 -> 9; matrix products, arithmetic and copies ran while one was open for 5% -> 10% of each run, Pallas kernels for 27% -> 30%
where the time goes in v13:
time: 97.6 us; the launch traced here: 97.1 us
  Pallas kernels  31.9 us (33%)
  starting transfers between devices  28.4 us (29%)
  waiting for transfers between devices  22.4 us (23%)
  local copies, waits for them, and re-layouts  7.56 us (8%)
  other arithmetic  4.57 us (5%)
  matrix products  1.31 us (1%)
  between operations  0.98 us (1%)
    ppermute x19, starting transfers between devices, exchange(): lax.ppermute(value, axis, [(i, i ^ mask) for i in range(lax.axis_size(axi...  23.5 us
    ppermute x19, waiting for transfers between devices, exchange(): lax.ppermute(value, axis, [(i, i ^ mask) for i in range(lax.axis_size(axi...  18.5 us
    pallas_call x4, Pallas kernels, products(): pl.pallas_call(functools.partial(multiply, wanted, rows, blocks, base, ta...  17.4 us
    pallas_call x2, Pallas kernels, pack(): pl.pallas_call(functools.partial(transpose_blocks, arranged, mine, units)...  6.28 us
    all_to_all x1, starting transfers between devices, per_device(): lax.all_to_all(own_blocks, ('fsdp', 'tp'), split_axis=0, concat_axis=0)  4.91 us
    pallas_call x1, Pallas kernels, lookup(): pl.pallas_call(functools.partial(pick_rows, arranged, units), grid=(1,),...  4.53 us
    unnamed x36, local copies, waits for them, and re-layouts  4.47 us
    all_to_all x1, waiting for transfers between devices, per_device(): lax.all_to_all(own_blocks, ('fsdp', 'tp'), split_axis=0, concat_axis=0)  3.96 us
  transfers between devices with their start and end apart: 20, of which 9 were waited for; matrix products, arithmetic and copies ran while one was open for 10% of the time, Pallas kernels for 30%

profile of v13, /device:TPU:0, one launch (start us, length us, event | category | flops | bytes accessed | tf_op | source)
XLA Modules:
  0.0 97.1 jit_solution(15884417662715333734)
XLA Ops:
  0.7 3.2 %shard_map.140 = bf16[2560,512]{1,0:T(8,128)(2,1)} custom-call(bf16[512,5120]{1,0:T(8,128)(2,1)} %source.3), custom_call_target="tpu_custom_call" | custom-call | bytes 5242880 | tf_op jit(solution)/shard_map/pallas_call | solution.py:75
  4.5 4.5 %shard_map.144 = (bf16[640,256]{1,0:T(8,128)(2,1)S(1)}, bf16[640,256]{1,0:T(8,128)(2,1)S(1)}) custom-call(s32[64]{0:T(128)S(1)} %and_select_fusion.place, bf16[4748,5120]{1,0:T(8,128)(2,1)} %tail.1, bf16[4748,5120]{1,0:T(8,128)(2,1)} %tail.1), custom_call_target="tpu_custom_call" | custom-call | flops 1 | bytes 1 | tf_op jit(solution)/shard_map/pallas_call | solution.py:444
  9.3 3.1 %shard_map.139.refs_0_ = bf16[2560,512]{1,0:T(8,128)(2,1)} custom-call(bf16[512,5120]{1,0:T(8,128)(2,1)} %source.3), custom_call_target="tpu_custom_call" | custom-call | bytes 5242880 | tf_op jit(solution)/shard_map/pallas_call | solution.py:75
  12.4 1.7 %copy-done.1 = bf16[2560,512]{1,0:T(8,128)(2,1)S(1)} copy-done((bf16[2560,512]{1,0:T(8,128)(2,1)S(1)}, bf16[2560,512]{1,0:T(8,128)(2,1)}, u32[]{:S(2)}) %copy-start.1) | copy-done | bytes 2621464
  14.1 3.9 %shard_map.142 = (bf16[1280,256]{1,0:T(8,128)(2,1)S(1)}, bf16[1280,256]{1,0:T(8,128)(2,1)S(1)}) custom-call(bf16[2560,512]{1,0:T(8,128)(2,1)S(1)} %copy-done.1, bf16[2560,512]{1,0:T(8,128)(2,1)} %collective-permute-done.refs_1_, bf16[512,1024]{1,0:T(8,128)(2,1)S(1)} %copy-done.2, bf16[512,1024]{1,0:T(8,128)(2,1)} %collective-permute-done.1.refs_3_), custom_call_target="tpu_custom_call" | custom-call | flops 1 | bytes 1 | tf_op jit(solution)/shard_map/pallas_call | solution.py:194
  18.1 2.8 %collective-permute-start.2 = (bf16[1280,256]{1,0:T(8,128)(2,1)S(1)}, bf16[1280,256]{1,0:T(8,128)(2,1)S(1)}, u32[]{:S(2)}, u32[]{:S(2)}) collective-permute-start(bf16[1280,256]{1,0:T(8,128)(2,1)S(1)} %get-tuple-element.62), channel_id=1, source_target_pairs={{0,8},{4,12},{8,0},{12,4},{16,24},{20,28},{24,16},{28,20},{1,9},{5... | collective-permute-start | bytes 1966088 | tf_op jit(solution)/shard_map/ppermute | solution.py:21
  20.9 1.4 %collective-permute-start.3 = (bf16[1280,256]{1,0:T(8,128)(2,1)S(1)}, bf16[1280,256]{1,0:T(8,128)(2,1)S(1)}, u32[]{:S(2)}, u32[]{:S(2)}) collective-permute-start(bf16[1280,256]{1,0:T(8,128)(2,1)S(1)} %get-tuple-element.63), channel_id=1, source_target_pairs={{0,16},{4,20},{8,24},{12,28},{16,0},{20,4},{24,8},{28,12},{1,17},{... | collective-permute-start | bytes 1966088 | tf_op jit(solution)/shard_map/ppermute | solution.py:21
  22.3 4.8 %shard_map.145 = (bf16[1600,256]{1,0:T(8,128)(2,1)S(1)}, bf16[1280,128]{1,0:T(8,128)(2,1)S(1)}, bf16[1280,128]{1,0:T(8,128)(2,1)S(1)}) custom-call(bf16[2560,512]{1,0:T(8,128)(2,1)S(1)} %copy-done.1, bf16[2560,512]{1,0:T(8,128)(2,1)} %collective-permute-done.refs_1_, bf16[512,1024]{1,0:T(8,128)(2,1)S(1)} %copy-done.2, ...), custom_call_target="tpu_custom_call" | custom-call | flops 1 | bytes 1 | tf_op jit(solution)/shard_map/pallas_call | solution.py:194
  27.1 1.6 %collective-permute-start.5 = (bf16[1600,256]{1,0:T(8,128)(2,1)S(1)}, bf16[1600,256]{1,0:T(8,128)(2,1)S(1)}, u32[]{:S(2)}, u32[]{:S(2)}) collective-permute-start(bf16[1600,256]{1,0:T(8,128)(2,1)S(1)} %get-tuple-element.68), channel_id=1, source_target_pairs={{0,1},{1,0},{2,3},{3,2},{4,5},{5,4},{6,7},{7,6},{8,9},{9,8},{10,11... | collective-permute-start | bytes 2457608 | tf_op jit(solution)/shard_map/ppermute | solution.py:21
  28.8 0.6 bitcast_subtract_fusion
  30.4 4.9 %shard_map.141 = (f32[1280,256]{1,0:T(8,128)S(1)}, f32[1280,256]{1,0:T(8,128)S(1)}, f32[1280,256]{1,0:T(8,128)S(1)}) custom-call(bf16[2560,512]{1,0:T(8,128)(2,1)S(1)} %copy-done.1, bf16[2560,512]{1,0:T(8,128)(2,1)} %collective-permute-done.refs_1_, bf16[512,1024]{1,0:T(8,128)(2,1)S(1)} %copy-done.2, bf16[512,1024]{1,0:T(8,128)(2,1)} %collective-permute-done.1.refs_3_), custom_call_target="tpu_custom_call" | custom-call | flops 1 | bytes 1 | tf_op jit(solution)/shard_map/pallas_call | solution.py:194
  35.3 1.2 %collective-permute-done.2.refs_2_ = bf16[1280,256]{1,0:T(8,128)(2,1)S(1)} collective-permute-done((bf16[1280,256]{1,0:T(8,128)(2,1)S(1)}, bf16[1280,256]{1,0:T(8,128)(2,1)S(1)}, u32[]{:S(2)}, u32[]{:S(2)}) %collective-permute-start.2) | collective-permute-done | bytes 655392 | tf_op jit(solution)/shard_map/ppermute | solution.py:21
  36.5 2.0 %collective-permute-done.3.refs_3_ = bf16[1280,256]{1,0:T(8,128)(2,1)S(1)} collective-permute-done((bf16[1280,256]{1,0:T(8,128)(2,1)S(1)}, bf16[1280,256]{1,0:T(8,128)(2,1)S(1)}, u32[]{:S(2)}, u32[]{:S(2)}) %collective-permute-start.3) | collective-permute-done | bytes 655392 | tf_op jit(solution)/shard_map/ppermute | solution.py:21
  38.7 1.6 %collective-permute-start.8 = (bf16[640,256]{1,0:T(8,128)(2,1)S(1)}, bf16[640,256]{1,0:T(8,128)(2,1)S(1)}, u32[]{:S(2)}, u32[]{:S(2)}) collective-permute-start(bf16[640,256]{1,0:T(8,128)(2,1)S(1)} %get-tuple-element.77), channel_id=1, source_target_pairs={{0,16},{4,20},{8,24},{12,28},{16,0},{20,4},{24,8},{28,12},{1,17},{... | collective-permute-start | bytes 983048 | tf_op jit(solution)/shard_map/ppermute | solution.py:21
  40.2 0.6 collective-permute-start.9
  40.8 0.6 broadcast_bitcast_fusion
  41.5 3.8 %shard_map.147 = (f32[1280,128]{1,0:T(8,128)S(1)}, f32[1280,128]{1,0:T(8,128)S(1)}) custom-call(bf16[2560,512]{1,0:T(8,128)(2,1)S(1)} %copy-done.1, bf16[2560,512]{1,0:T(8,128)(2,1)} %collective-permute-done.refs_1_, bf16[512,1024]{1,0:T(8,128)(2,1)S(1)} %copy-done.2, bf16[512,1024]{1,0:T(8,128)(2,1)} %collective-permute-done.1.refs_3_), custom_call_target="tpu_custom_call" | custom-call | flops 1 | bytes 1 | tf_op jit(solution)/shard_map/pallas_call | solution.py:194
  45.3 1.7 %collective-permute-done.5.refs_2_ = bf16[1600,256]{1,0:T(8,128)(2,1)S(1)} collective-permute-done((bf16[1600,256]{1,0:T(8,128)(2,1)S(1)}, bf16[1600,256]{1,0:T(8,128)(2,1)S(1)}, u32[]{:S(2)}, u32[]{:S(2)}) %collective-permute-start.5) | collective-permute-done | bytes 819232 | tf_op jit(solution)/shard_map/ppermute | solution.py:21
  47.3 0.8 collective-permute-start.10
  48.6 1.7 %collective-permute-start.12 = (bf16[640,128]{1,0:T(8,128)(2,1)S(1)}, bf16[640,128]{1,0:T(8,128)(2,1)S(1)}, u32[]{:S(2)}, u32[]{:S(2)}) collective-permute-start(bf16[640,128]{1,0:T(8,128)(2,1)S(1)} %get-tuple-element.87), channel_id=1, source_target_pairs={{0,8},{4,12},{8,0},{12,4},{16,24},{20,28},{24,16},{28,20},{1,9},{5... | collective-permute-start | bytes 491528 | tf_op jit(solution)/shard_map/ppermute | solution.py:21
  50.3 2.2 %collective-permute-done.8.refs_2_ = bf16[640,256]{1,0:T(8,128)(2,1)S(1)} collective-permute-done((bf16[640,256]{1,0:T(8,128)(2,1)S(1)}, bf16[640,256]{1,0:T(8,128)(2,1)S(1)}, u32[]{:S(2)}, u32[]{:S(2)}) %collective-permute-start.8) | collective-permute-done | bytes 327712 | tf_op jit(solution)/shard_map/ppermute | solution.py:21
  52.6 1.5 %collective-permute-start.14 = (bf16[640,256]{1,0:T(8,128)(2,1)S(1)}, bf16[640,256]{1,0:T(8,128)(2,1)S(1)}, u32[]{:S(2)}, u32[]{:S(2)}) collective-permute-start(bf16[640,256]{1,0:T(8,128)(2,1)S(1)} %get-tuple-element.95), channel_id=1, source_target_pairs={{0,1},{1,0},{2,3},{3,2},{4,5},{5,4},{6,7},{7,6},{8,9},{9,8},{10,11... | collective-permute-start | bytes 983048 | tf_op jit(solution)/shard_map/ppermute | solution.py:21
  54.3 0.7 fusion.25
  55.3 0.6 fusion.20
  55.9 3.7 %collective-permute-done.10.refs_2_ = bf16[800,256]{1,0:T(8,128)(2,1)S(1)} collective-permute-done((bf16[800,256]{1,0:T(8,128)(2,1)S(1)}, bf16[800,256]{1,0:T(8,128)(2,1)S(1)}, u32[]{:S(2)}, u32[]{:S(2)}) %collective-permute-start.10) | collective-permute-done | bytes 409632 | tf_op jit(solution)/shard_map/ppermute | solution.py:21
  59.7 1.7 %collective-permute-start.13 = (bf16[400,256]{1,0:T(8,128)(2,1)S(1)}, bf16[400,256]{1,0:T(8,128)(2,1)S(1)}, u32[]{:S(2)}, u32[]{:S(2)}) collective-permute-start(bf16[400,256]{1,0:T(8,128)(2,1)S(1)} %get-tuple-element.91), channel_id=1, source_target_pairs={{0,16},{4,20},{8,24},{12,28},{16,0},{20,4},{24,8},{28,12},{1,17},{... | collective-permute-start | bytes 614408 | tf_op jit(solution)/shard_map/ppermute | solution.py:21
  61.9 0.7 collective-permute-done.12.refs_3_
  62.7 1.8 %collective-permute-start.15 = (bf16[640,128]{1,0:T(8,128)(2,1)S(1)}, bf16[640,128]{1,0:T(8,128)(2,1)S(1)}, u32[]{:S(2)}, u32[]{:S(2)}) collective-permute-start(bf16[640,128]{1,0:T(8,128)(2,1)S(1)} %get-tuple-element.99), channel_id=1, source_target_pairs={{0,1},{1,0},{2,3},{3,2},{4,5},{5,4},{6,7},{7,6},{8,9},{9,8},{10,11... | collective-permute-start | bytes 491528 | tf_op jit(solution)/shard_map/ppermute | solution.py:21
  64.4 1.3 %collective-permute-done.13.refs_2_ = bf16[400,256]{1,0:T(8,128)(2,1)S(1)} collective-permute-done((bf16[400,256]{1,0:T(8,128)(2,1)S(1)}, bf16[400,256]{1,0:T(8,128)(2,1)S(1)}, u32[]{:S(2)}, u32[]{:S(2)}) %collective-permute-start.13) | collective-permute-done | bytes 204832 | tf_op jit(solution)/shard_map/ppermute | solution.py:21
  65.8 2.7 %collective-permute-start.16 = (bf16[240,256]{1,0:T(8,128)(2,1)S(1)}, bf16[240,256]{1,0:T(8,128)(2,1)S(1)}, u32[]{:S(2)}, u32[]{:S(2)}) collective-permute-start(bf16[240,256]{1,0:T(8,128)(2,1)S(1)} %get-tuple-element.102), channel_id=1, source_target_pairs={{0,2},{1,3},{2,0},{3,1},{4,6},{5,7},{6,4},{7,5},{8,10},{9,11},{10,... | collective-permute-start | bytes 368648 | tf_op jit(solution)/shard_map/ppermute | solution.py:21
  68.5 0.7 shard_map.153
  69.5 1.0 fusion.22
  70.5 0.7 shard_map.154
  71.1 2.7 %collective-permute-start.18 = (bf16[320,128]{1,0:T(8,128)(2,1)}, bf16[320,128]{1,0:T(8,128)(2,1)S(1)}, u32[]{:S(2)}, u32[]{:S(2)}) collective-permute-start(bf16[320,128]{1,0:T(8,128)(2,1)} %get-tuple-element.108), channel_id=1, source_target_pairs={{0,2},{1,3},{2,0},{3,1},{4,6},{5,7},{6,4},{7,5},{8,10},{9,11},{10,... | collective-permute-start | bytes 245768 | tf_op jit(solution)/shard_map/ppermute | solution.py:21
  73.8 0.8 fusion.24
  74.6 5.6 %collective-permute-done.16 = bf16[240,256]{1,0:T(8,128)(2,1)S(1)} collective-permute-done((bf16[240,256]{1,0:T(8,128)(2,1)S(1)}, bf16[240,256]{1,0:T(8,128)(2,1)S(1)}, u32[]{:S(2)}, u32[]{:S(2)}) %collective-permute-start.16) | collective-permute-done | bytes 122912 | tf_op jit(solution)/shard_map/ppermute | solution.py:21
  80.8 0.7 convert_element_type.52._
  81.5 4.9 %all-to-all-start = ((bf16[32,8,256]{2,1,0:T(8,128)(2,1)}), bf16[32,8,256]{2,1,0:T(8,128)(2,1)}, u32[]{:S(2)}, u32[]{:S(2)}) async-start(bf16[32,8,256]{2,1,0:T(8,128)(2,1)} %convert_element_type.52._), calls=%async_computation | async-start | bytes 262144 | tf_op jit(solution)/shard_map/all_to_all | solution.py:667
  86.5 1.0 shard_map.156
  87.5 0.7 constant_dynamic-update-slice_fusion.3
  88.2 0.7 constant_dynamic-update-slice_fusion.2
  88.9 0.7 subtract_dynamic-update-slice_fusion
  89.6 0.6 constant_dynamic-update-slice_fusion.1
  90.2 0.6 constant_dynamic-update-slice_fusion
  90.8 4.0 %all-to-all-done = bf16[32,8,256]{2,1,0:T(8,128)(2,1)} async-done(((bf16[32,8,256]{2,1,0:T(8,128)(2,1)}), bf16[32,8,256]{2,1,0:T(8,128)(2,1)}, u32[]{:S(2)}, u32[]{:S(2)}) %all-to-all-start) | async-done | bytes 131104 | tf_op jit(solution)/shard_map/all_to_all | solution.py:667
  94.8 0.9 convert_reduce_fusion
  95.8 0.6 bitcast_convert_fusion
  96.5 0.6 copy.47
  (71 shorter events, 5.1 us)
Async XLA Ops:
  0.6 53.7 %copy-start = (bf16[8,512,256]{2,1,0:T(8,128)(2,1)S(1)}, bf16[8,512,256]{2,1,0:T(8,128)(2,1)}, u32[]{:S(2)}) copy-start(bf16[8,512,256]{2,1,0:T(8,128)(2,1)} %param.18) | copy-start | bytes 6291460
  0.6 3.8 %copy-start.2 = (bf16[512,1024]{1,0:T(8,128)(2,1)S(1)}, bf16[512,1024]{1,0:T(8,128)(2,1)}, u32[]{:S(2)}) copy-start(bf16[512,1024]{1,0:T(8,128)(2,1)} %refs_2_.7) | copy-start | bytes 3145732
  0.7 3.8 %copy-start.14 = (s32[64]{0:T(128)S(1)}, s32[64]{0:T(128)}, u32[]{:S(2)}) copy-start(s32[64]{0:T(128)} %param.16) | copy-start | bytes 772
  3.9 8.5 %collective-permute-start = (bf16[2560,512]{1,0:T(8,128)(2,1)}, bf16[2560,512]{1,0:T(8,128)(2,1)}, u32[]{:S(2)}, u32[]{:S(2)}) collective-permute-start(bf16[2560,512]{1,0:T(8,128)(2,1)} %shard_map.140), channel_id=1, source_target_pairs={{0,4},{4,0},{8,12},{12,8},{16,20},{20,16},{24,28},{28,24},{1,5},{5... | collective-permute-start | bytes 7864328 | tf_op jit(solution)/shard_map/ppermute | solution.py:21
  4.4 8.0 %collective-permute-start.1 = (bf16[512,1024]{1,0:T(8,128)(2,1)S(1)}, bf16[512,1024]{1,0:T(8,128)(2,1)}, u32[]{:S(2)}, u32[]{:S(2)}) collective-permute-start(bf16[512,1024]{1,0:T(8,128)(2,1)S(1)} %copy-done.2), channel_id=1, source_target_pairs={{0,4},{4,0},{8,12},{12,8},{16,20},{20,16},{24,28},{28,24},{1,5},{5... | collective-permute-start | bytes 3145736 | tf_op jit(solution)/shard_map/ppermute | solution.py:21
  9.0 13.3 %collective-permute-start.4 = (bf16[640,256]{1,0:T(8,128)(2,1)S(1)}, bf16[640,256]{1,0:T(8,128)(2,1)S(1)}, u32[]{:S(2)}, u32[]{:S(2)}) collective-permute-start(bf16[640,256]{1,0:T(8,128)(2,1)S(1)} %get-tuple-element.67), channel_id=1, source_target_pairs={{0,4},{4,0},{8,12},{12,8},{16,20},{20,16},{24,28},{28,24},{1,5},{5... | collective-permute-start | bytes 983048 | tf_op jit(solution)/shard_map/ppermute | solution.py:21
  12.4 1.7 %copy-start.1 = (bf16[2560,512]{1,0:T(8,128)(2,1)S(1)}, bf16[2560,512]{1,0:T(8,128)(2,1)}, u32[]{:S(2)}) copy-start(bf16[2560,512]{1,0:T(8,128)(2,1)} %shard_map.139.refs_0_) | copy-start | bytes 7864324
  18.1 18.4 %collective-permute-start.2 = (bf16[1280,256]{1,0:T(8,128)(2,1)S(1)}, bf16[1280,256]{1,0:T(8,128)(2,1)S(1)}, u32[]{:S(2)}, u32[]{:S(2)}) collective-permute-start(bf16[1280,256]{1,0:T(8,128)(2,1)S(1)} %get-tuple-element.62), channel_id=1, source_target_pairs={{0,8},{4,12},{8,0},{12,4},{16,24},{20,28},{24,16},{28,20},{1,9},{5... | collective-permute-start | bytes 1966088 | tf_op jit(solution)/shard_map/ppermute | solution.py:21
  20.9 17.6 %collective-permute-start.3 = (bf16[1280,256]{1,0:T(8,128)(2,1)S(1)}, bf16[1280,256]{1,0:T(8,128)(2,1)S(1)}, u32[]{:S(2)}, u32[]{:S(2)}) collective-permute-start(bf16[1280,256]{1,0:T(8,128)(2,1)S(1)} %get-tuple-element.63), channel_id=1, source_target_pairs={{0,16},{4,20},{8,24},{12,28},{16,0},{20,4},{24,8},{28,12},{1,17},{... | collective-permute-start | bytes 1966088 | tf_op jit(solution)/shard_map/ppermute | solution.py:21
  22.3 6.4 %copy-start.15 = (f32[2]{0:T(128)S(1)}, f32[2]{0:T(128)}, u32[]{:S(2)}) copy-start(f32[2]{0:T(128)} %param.22) | copy-start | bytes 28
  27.1 19.9 %collective-permute-start.5 = (bf16[1600,256]{1,0:T(8,128)(2,1)S(1)}, bf16[1600,256]{1,0:T(8,128)(2,1)S(1)}, u32[]{:S(2)}, u32[]{:S(2)}) collective-permute-start(bf16[1600,256]{1,0:T(8,128)(2,1)S(1)} %get-tuple-element.68), channel_id=1, source_target_pairs={{0,1},{1,0},{2,3},{3,2},{4,5},{5,4},{6,7},{7,6},{8,9},{9,8},{10,11... | collective-permute-start | bytes 2457608 | tf_op jit(solution)/shard_map/ppermute | solution.py:21
  29.4 18.6 %collective-permute-start.6 = (bf16[1280,128]{1,0:T(8,128)(2,1)S(1)}, bf16[1280,128]{1,0:T(8,128)(2,1)S(1)}, u32[]{:S(2)}, u32[]{:S(2)}) collective-permute-start(bf16[1280,128]{1,0:T(8,128)(2,1)S(1)} %get-tuple-element.72), channel_id=1, source_target_pairs={{0,8},{4,12},{8,0},{12,4},{16,24},{20,28},{24,16},{28,20},{1,9},{5... | collective-permute-start | bytes 983048 | tf_op jit(solution)/shard_map/ppermute | solution.py:21
  29.9 18.1 %collective-permute-start.7 = (bf16[1280,128]{1,0:T(8,128)(2,1)S(1)}, bf16[1280,128]{1,0:T(8,128)(2,1)S(1)}, u32[]{:S(2)}, u32[]{:S(2)}) collective-permute-start(bf16[1280,128]{1,0:T(8,128)(2,1)S(1)} %get-tuple-element.73), channel_id=1, source_target_pairs={{0,16},{4,20},{8,24},{12,28},{16,0},{20,4},{24,8},{28,12},{1,17},{... | collective-permute-start | bytes 983048 | tf_op jit(solution)/shard_map/ppermute | solution.py:21
  38.7 13.8 %collective-permute-start.8 = (bf16[640,256]{1,0:T(8,128)(2,1)S(1)}, bf16[640,256]{1,0:T(8,128)(2,1)S(1)}, u32[]{:S(2)}, u32[]{:S(2)}) collective-permute-start(bf16[640,256]{1,0:T(8,128)(2,1)S(1)} %get-tuple-element.77), channel_id=1, source_target_pairs={{0,16},{4,20},{8,24},{12,28},{16,0},{20,4},{24,8},{28,12},{1,17},{... | collective-permute-start | bytes 983048 | tf_op jit(solution)/shard_map/ppermute | solution.py:21
  40.2 12.3 %collective-permute-start.9 = (bf16[640,256]{1,0:T(8,128)(2,1)S(1)}, bf16[640,256]{1,0:T(8,128)(2,1)S(1)}, u32[]{:S(2)}, u32[]{:S(2)}) collective-permute-start(bf16[640,256]{1,0:T(8,128)(2,1)S(1)} %get-tuple-element.78), channel_id=1, source_target_pairs={{0,8},{4,12},{8,0},{12,4},{16,24},{20,28},{24,16},{28,20},{1,9},{5... | collective-permute-start | bytes 983048 | tf_op jit(solution)/shard_map/ppermute | solution.py:21
  47.2 6.9 %copy-start.11 = (s32[8]{0:T(128)S(1)}, s32[8]{0:T(128)}, u32[]{:S(2)}) copy-start(s32[8]{0:T(128)} %param.23) | copy-start | bytes 100
  47.2 7.0 %copy-start.6 = (bf16[8,2048]{1,0:T(8,128)(2,1)S(1)}, bf16[8,2048]{1,0:T(8,128)(2,1)}, u32[]{:S(2)}) copy-start(bf16[8,2048]{1,0:T(8,128)(2,1)} %param.17) | copy-start | bytes 98308
  47.2 7.0 %copy-start.13 = (bf16[8,256]{1,0:T(8,128)(2,1)S(1)}, bf16[8,256]{1,0:T(8,128)(2,1)}, u32[]{:S(2)}) copy-start(bf16[8,256]{1,0:T(8,128)(2,1)} %param.20) | copy-start | bytes 12292
  47.3 12.4 %collective-permute-start.10 = (bf16[800,256]{1,0:T(8,128)(2,1)S(1)}, bf16[800,256]{1,0:T(8,128)(2,1)S(1)}, u32[]{:S(2)}, u32[]{:S(2)}) collective-permute-start(bf16[800,256]{1,0:T(8,128)(2,1)S(1)} %get-tuple-element.82), channel_id=1, source_target_pairs={{0,8},{4,12},{8,0},{12,4},{16,24},{20,28},{24,16},{28,20},{1,9},{5... | collective-permute-start | bytes 1228808 | tf_op jit(solution)/shard_map/ppermute | solution.py:21
  48.1 13.7 %collective-permute-start.11 = (bf16[640,128]{1,0:T(8,128)(2,1)S(1)}, bf16[640,128]{1,0:T(8,128)(2,1)S(1)}, u32[]{:S(2)}, u32[]{:S(2)}) collective-permute-start(bf16[640,128]{1,0:T(8,128)(2,1)S(1)} %get-tuple-element.86), channel_id=1, source_target_pairs={{0,16},{4,20},{8,24},{12,28},{16,0},{20,4},{24,8},{28,12},{1,17},{... | collective-permute-start | bytes 491528 | tf_op jit(solution)/shard_map/ppermute | solution.py:21
  48.6 14.0 %collective-permute-start.12 = (bf16[640,128]{1,0:T(8,128)(2,1)S(1)}, bf16[640,128]{1,0:T(8,128)(2,1)S(1)}, u32[]{:S(2)}, u32[]{:S(2)}) collective-permute-start(bf16[640,128]{1,0:T(8,128)(2,1)S(1)} %get-tuple-element.87), channel_id=1, source_target_pairs={{0,8},{4,12},{8,0},{12,4},{16,24},{20,28},{24,16},{28,20},{1,9},{5... | collective-permute-start | bytes 491528 | tf_op jit(solution)/shard_map/ppermute | solution.py:21
  52.6 8.8 %copy-start.12 = (bf16[8,512,256]{2,1,0:T(8,128)(2,1)S(1)}, bf16[8,512,256]{2,1,0:T(8,128)(2,1)}, u32[]{:S(2)}) copy-start(bf16[8,512,256]{2,1,0:T(8,128)(2,1)} %param.19) | copy-start | bytes 6291460
  52.6 15.9 %collective-permute-start.14 = (bf16[640,256]{1,0:T(8,128)(2,1)S(1)}, bf16[640,256]{1,0:T(8,128)(2,1)S(1)}, u32[]{:S(2)}, u32[]{:S(2)}) collective-permute-start(bf16[640,256]{1,0:T(8,128)(2,1)S(1)} %get-tuple-element.95), channel_id=1, source_target_pairs={{0,1},{1,0},{2,3},{3,2},{4,5},{5,4},{6,7},{7,6},{8,9},{9,8},{10,11... | collective-permute-start | bytes 983048 | tf_op jit(solution)/shard_map/ppermute | solution.py:21
  59.7 6.0 %collective-permute-start.13 = (bf16[400,256]{1,0:T(8,128)(2,1)S(1)}, bf16[400,256]{1,0:T(8,128)(2,1)S(1)}, u32[]{:S(2)}, u32[]{:S(2)}) collective-permute-start(bf16[400,256]{1,0:T(8,128)(2,1)S(1)} %get-tuple-element.91), channel_id=1, source_target_pairs={{0,16},{4,20},{8,24},{12,28},{16,0},{20,4},{24,8},{28,12},{1,17},{... | collective-permute-start | bytes 614408 | tf_op jit(solution)/shard_map/ppermute | solution.py:21
  61.9 18.3 %copy-start.3 = (f32[160,1024]{1,0:T(8,128)S(1)}, f32[160,1024]{1,0:T(8,128)}, u32[]{:S(2)}) copy-start(f32[160,1024]{1,0:T(8,128)} %master.3) | copy-start | bytes 1966084
  62.7 7.8 %collective-permute-start.15 = (bf16[640,128]{1,0:T(8,128)(2,1)S(1)}, bf16[640,128]{1,0:T(8,128)(2,1)S(1)}, u32[]{:S(2)}, u32[]{:S(2)}) collective-permute-start(bf16[640,128]{1,0:T(8,128)(2,1)S(1)} %get-tuple-element.99), channel_id=1, source_target_pairs={{0,1},{1,0},{2,3},{3,2},{4,5},{5,4},{6,7},{7,6},{8,9},{9,8},{10,11... | collective-permute-start | bytes 491528 | tf_op jit(solution)/shard_map/ppermute | solution.py:21
  65.8 14.4 %collective-permute-start.16 = (bf16[240,256]{1,0:T(8,128)(2,1)S(1)}, bf16[240,256]{1,0:T(8,128)(2,1)S(1)}, u32[]{:S(2)}, u32[]{:S(2)}) collective-permute-start(bf16[240,256]{1,0:T(8,128)(2,1)S(1)} %get-tuple-element.102), channel_id=1, source_target_pairs={{0,2},{1,3},{2,0},{3,1},{4,6},{5,7},{6,4},{7,5},{8,10},{9,11},{10,... | collective-permute-start | bytes 368648 | tf_op jit(solution)/shard_map/ppermute | solution.py:21
  69.2 17.3 %collective-permute-start.17 = (bf16[320,256]{1,0:T(8,128)(2,1)}, bf16[320,256]{1,0:T(8,128)(2,1)}, u32[]{:S(2)}, u32[]{:S(2)}) collective-permute-start(bf16[320,256]{1,0:T(8,128)(2,1)} %get-tuple-element.104), channel_id=1, source_target_pairs={{0,2},{1,3},{2,0},{3,1},{4,6},{5,7},{6,4},{7,5},{8,10},{9,11},{10,... | collective-permute-start | bytes 491528 | tf_op jit(solution)/shard_map/ppermute | solution.py:21
  71.1 15.3 %collective-permute-start.18 = (bf16[320,128]{1,0:T(8,128)(2,1)}, bf16[320,128]{1,0:T(8,128)(2,1)S(1)}, u32[]{:S(2)}, u32[]{:S(2)}) collective-permute-start(bf16[320,128]{1,0:T(8,128)(2,1)} %get-tuple-element.108), channel_id=1, source_target_pairs={{0,2},{1,3},{2,0},{3,1},{4,6},{5,7},{6,4},{7,5},{8,10},{9,11},{10,... | collective-permute-start | bytes 245768 | tf_op jit(solution)/shard_map/ppermute | solution.py:21
  80.2 0.6 copy-start.4
  81.5 13.3 %all-to-all-start = ((bf16[32,8,256]{2,1,0:T(8,128)(2,1)}), bf16[32,8,256]{2,1,0:T(8,128)(2,1)}, u32[]{:S(2)}, u32[]{:S(2)}) async-start(bf16[32,8,256]{2,1,0:T(8,128)(2,1)} %convert_element_type.52._), calls=%async_computation | async-start | bytes 262144 | tf_op jit(solution)/shard_map/all_to_all | solution.py:667
  86.4 2.4 %copy-start.5 = (bf16[240,256]{1,0:T(8,128)(2,1)S(1)}, bf16[240,256]{1,0:T(8,128)(2,1)}, u32[]{:S(2)}) copy-start(bf16[240,256]{1,0:T(8,128)(2,1)} %copy-done.4) | copy-start | bytes 368644
  86.5 9.3 %copy-start.8 = (bf16[8,256]{1,0:T(8,128)(2,1)S(1)}, bf16[8,256]{1,0:T(8,128)(2,1)}, u32[]{:S(2)}) copy-start(bf16[8,256]{1,0:T(8,128)(2,1)} %param.21) | copy-start | bytes 12292
  86.5 9.3 %copy-start.9 = (f32[256]{0:T(256)S(1)}, f32[256]{0:T(256)}, u32[]{:S(2)}) copy-start(f32[256]{0:T(256)} %bitcast_subtract_fusion) | copy-start | bytes 3076
  86.5 9.3 %copy-start.10 = (f32[256]{0:T(256)S(1)}, f32[256]{0:T(256)}, u32[]{:S(2)}) copy-start(f32[256]{0:T(256)} %broadcast_bitcast_fusion) | copy-start | bytes 3076
  86.5 9.9 %copy-start.7 = (f32[8,2,8]{2,1,0:T(2,128)S(1)}, f32[8,2,8]{2,1,0:T(2,128)}, u32[]{:S(2)}) copy-start(f32[8,2,8]{2,1,0:T(2,128)} %get-tuple-element.125) | copy-start | bytes 1540
